TPU v7x, 32 devices: a whole 2x2x4 slice. The times are simulated.
32 devices in a mesh: dp: 8 (over z, x), emb: 4 (over y, core).
Axes of the slice: x: 2, y: 2, z: 4, core: 2. Of those that a mesh axis runs over, the one named last changes fastest.
Arguments:
- stem_rows: bfloat16 [1024, 4, 64, 128], P(('dp', 'emb')), may hold values from -6 to 6
- emb_ids: int32 [1024, 1], P(('dp', 'emb')), may hold values from 0 to 3; in each aligned block of 32 rows (0 to 31, 32 to 63, ...) at most 16 rows name the same one
- segments: int32 [1024, 4], P(('dp', 'emb')), may hold values from 0 to 3, as said below
- cotangent: bfloat16 [1024, 128, 128], P(('dp', 'emb')), may hold values from -6 to 6
- trunk_mats: float32 [128, 1024], replicated
- mats_momentum: float32 [128, 1024], replicated
- mats_average: float32 [128, 1024], replicated, may hold values from -0.5 to 0.5
- trunk_down: float32 [512, 128], replicated, may hold values from -0.25 to 0.25
- down_momentum: float32 [512, 128], replicated
- down_average: float32 [512, 128], replicated, may hold values from -0.25 to 0.25
- trunk_vectors: float32 [9, 128], replicated
- vectors_momentum: float32 [9, 128], replicated
- vectors_average: float32 [9, 128], replicated
- stem_mats: float32 [4, 128, 384], P('emb')
- stem_momentum: float32 [4, 128, 384], P('emb')
- stem_average: float32 [4, 128, 384], P('emb'), may hold values from -0.5 to 0.5
- stem_queries: float32 [4, 32, 128], P('emb'), may hold values from -6 to 6
- queries_momentum: float32 [4, 32, 128], P('emb')
- queries_average: float32 [4, 32, 128], P('emb'), may hold values from -6 to 6
Outputs:
- trunk_out: bfloat16 [1024, 128, 128], P(('dp', 'emb'))
- rows_grad: bfloat16 [1024, 4, 64, 128], P(('dp', 'emb'))
- mats_moment: float32 [128, 1024], replicated
- mats_mean: float32 [128, 1024], replicated
- mats_new: float32 [128, 1024], replicated
- mats_copy: bfloat16 [128, 1024], replicated
- down_moment: float32 [512, 128], replicated
- down_mean: float32 [512, 128], replicated
- down_new: float32 [512, 128], replicated
- down_copy: bfloat16 [512, 128], replicated
- vectors_moment: float32 [9, 128], replicated
- vectors_mean: float32 [9, 128], replicated
- vectors_new: float32 [9, 128], replicated
- stem_moment: float32 [4, 128, 384], P('emb')
- stem_mean: float32 [4, 128, 384], P('emb')
- stem_new: float32 [4, 128, 384], P('emb')
- stem_copy: bfloat16 [4, 128, 384], P('emb')
- queries_moment: float32 [4, 32, 128], P('emb')
- queries_mean: float32 [4, 32, 128], P('emb')
- queries_new: float32 [4, 32, 128], P('emb')
- queries_copy: bfloat16 [4, 32, 128], P('emb')
- action_stats: float32 [2, 128], replicated
Inputs may be any that keep to these rules, and one draw needn't show every extreme that they name: `emb_ids`: among the 32 sequences of one device at most 16 have the same embodiment. `segments`: each row starts at 0 and rises by 0 or 1 from one step to the next; a sample is the run of steps with one id.
All inputs are finite; a program needn't handle non-finite values.
Results may differ from a plain program's by a relative error of at most 0.017.
Values may be sent and summed in bfloat16 or wider, within the bound.
No kernel may reach another device: no remote copies, remote signals or barrier semaphores. Data moves between devices by JAX's collectives and lax.ppermute only.
A program may use at most 256 MiB of HBM per device.

v0:
```python
import math

import jax
import jax.numpy as jnp
from jax import lax
from jax.sharding import PartitionSpec as P

D = 128
FF = 512
HEADS = 8
HEAD_DIM = 16
QUERIES = 32
STEP = 4
CAP = 16
TOK_SEQ = 128


NORM_EPSILON = 1e-05
MOMENTUM_DECAY = 0.9
BASE_RATE = 0.1
MASKED_SCORE = -1000000000.0


def heads_of(value):
    return value.reshape(value.shape[:-1] + (HEADS, HEAD_DIM))


def norm_ahead(value, gain, bias):
    row_mean = jnp.mean(value, axis=-1, keepdims=True)
    centered = value - row_mean
    inverse = lax.rsqrt(jnp.mean(centered * centered, axis=-1, keepdims=True) + NORM_EPSILON)
    unit_value = centered * inverse
    return (unit_value * gain + bias, (unit_value, inverse))


def norm_back(gradient, gain, kept_parts):
    unit_value, inverse = kept_parts
    grad_unit = gradient * gain
    grad_value = inverse * (
        grad_unit
        - jnp.mean(grad_unit, axis=-1, keepdims=True)
        - unit_value * jnp.mean(grad_unit * unit_value, axis=-1, keepdims=True)
    )
    return (grad_value, jnp.sum(gradient * unit_value, axis=(0, 1)), jnp.sum(gradient, axis=(0, 1)))


def stem_ahead(step_rows, kv_weight, out_weight, queries):
    seq_count, step_count = step_rows.shape[:2]
    score_scale = 1.0 / math.sqrt(HEAD_DIM)
    key_value = jnp.einsum(
        "bsrd,bde->bsre", step_rows, kv_weight, preferred_element_type=jnp.float32
    ).astype(jnp.bfloat16)
    key_heads = heads_of(key_value[..., :D])
    value_heads = heads_of(key_value[..., D:])
    query_heads = heads_of(queries)
    scores = (
        jnp.einsum("bqhc,bsrhc->bshqr", query_heads, key_heads, preferred_element_type=jnp.float32)
        * score_scale
    )
    attend = jax.nn.softmax(scores, axis=-1)
    attend_low = attend.astype(jnp.bfloat16)
    mixed_heads = jnp.einsum(
        "bshqr,bsrhc->bsqhc", attend_low, value_heads, preferred_element_type=jnp.float32
    )
    mixed_low = mixed_heads.reshape(seq_count, step_count, QUERIES, D).astype(jnp.bfloat16)
    result = jnp.einsum(
        "bsqd,bde->bsqe", mixed_low, out_weight, preferred_element_type=jnp.float32
    ).astype(jnp.bfloat16)
    return (
        result.reshape(seq_count, step_count * QUERIES, D),
        (key_value, attend, attend_low, mixed_low),
    )


def stem_back(step_rows, kv_weight, out_weight, queries, kept_parts, grad_result):
    key_value, attend, attend_low, mixed_low = kept_parts
    seq_count, step_count = step_rows.shape[:2]
    score_scale = 1.0 / math.sqrt(HEAD_DIM)
    key_heads = heads_of(key_value[..., :D])
    value_heads = heads_of(key_value[..., D:])
    query_heads = heads_of(queries)
    grad_steps = grad_result.reshape(seq_count, step_count, QUERIES, D)
    grad_outw = jnp.einsum(
        "bsqd,bsqe->bde", mixed_low, grad_steps, preferred_element_type=jnp.float32
    )
    grad_mixed = jnp.einsum(
        "bsqe,bde->bsqd", grad_steps, out_weight, preferred_element_type=jnp.float32
    ).astype(jnp.bfloat16)
    grad_heads = heads_of(grad_mixed)
    grad_attend = jnp.einsum(
        "bsqhc,bsrhc->bshqr", grad_heads, value_heads, preferred_element_type=jnp.float32
    )
    grad_values = jnp.einsum(
        "bshqr,bsqhc->bsrhc", attend_low, grad_heads, preferred_element_type=jnp.float32
    )
    grad_scores = (
        attend * (grad_attend - jnp.sum(attend * grad_attend, axis=-1, keepdims=True))
    ).astype(jnp.bfloat16)
    grad_query = (
        jnp.einsum("bshqr,bsrhc->bqhc", grad_scores, key_heads, preferred_element_type=jnp.float32)
        * score_scale
    )
    grad_keys = (
        jnp.einsum(
            "bshqr,bqhc->bsrhc", grad_scores, query_heads, preferred_element_type=jnp.float32
        )
        * score_scale
    )
    grad_kv = jnp.concatenate(
        [
            grad_keys.reshape(seq_count, step_count, -1, D),
            grad_values.reshape(seq_count, step_count, -1, D),
        ],
        axis=-1,
    ).astype(jnp.bfloat16)
    grad_kvw = jnp.einsum("bsrd,bsre->bde", step_rows, grad_kv, preferred_element_type=jnp.float32)
    grad_rows = jnp.einsum("bsre,bde->bsrd", grad_kv, kv_weight, preferred_element_type=jnp.float32)
    grad_weights = jnp.concatenate([grad_kvw, grad_outw], axis=-1)
    return (grad_weights, grad_query.reshape(seq_count, QUERIES, D), grad_rows)


def trunk_pass(tokens, mats_low, down_low, vectors, seg_tokens, cotangent):
    seq_count = tokens.shape[0]
    score_scale = 1.0 / math.sqrt(HEAD_DIM)
    residual = tokens.astype(jnp.float32)
    normed, kept_one = norm_ahead(residual, vectors[0], vectors[1])
    normed_low = normed.astype(jnp.bfloat16)
    projected = jnp.einsum(
        "btd,de->bte", normed_low, mats_low[:, : 3 * D], preferred_element_type=jnp.float32
    ).astype(jnp.bfloat16)
    query_heads = heads_of(projected[..., :D])
    key_heads = heads_of(projected[..., D : 2 * D])
    value_heads = heads_of(projected[..., 2 * D :])
    visible = (seg_tokens[:, :, None] == seg_tokens[:, None, :])[:, None]
    scores = (
        jnp.einsum("bqhc,bkhc->bhqk", query_heads, key_heads, preferred_element_type=jnp.float32)
        * score_scale
    )
    attend = jax.nn.softmax(jnp.where(visible, scores, MASKED_SCORE), axis=-1)
    attend_low = attend.astype(jnp.bfloat16)
    mixed_heads = jnp.einsum(
        "bhqk,bkhc->bqhc", attend_low, value_heads, preferred_element_type=jnp.float32
    )
    mixed_low = mixed_heads.reshape(seq_count, -1, D).astype(jnp.bfloat16)
    hidden = residual + jnp.einsum(
        "btd,de->bte", mixed_low, mats_low[:, 3 * D : 4 * D], preferred_element_type=jnp.float32
    )
    normed_two, kept_two = norm_ahead(hidden, vectors[2], vectors[3])
    normed_two_low = normed_two.astype(jnp.bfloat16)
    inner_act = jnp.einsum(
        "btd,df->btf", normed_two_low, mats_low[:, 4 * D :], preferred_element_type=jnp.float32
    ) + vectors[5:].reshape(FF)
    active, gelu_back = jax.vjp(lambda point: jax.nn.gelu(point, approximate=True), inner_act)
    active_low = active.astype(jnp.bfloat16)
    output = (
        hidden
        + jnp.einsum("btf,fd->btd", active_low, down_low, preferred_element_type=jnp.float32)
        + vectors[4]
    )
    grad_out = cotangent.astype(jnp.float32)
    grad_down = jnp.einsum("btf,btd->fd", active_low, cotangent, preferred_element_type=jnp.float32)
    grad_active = jnp.einsum("btd,fd->btf", cotangent, down_low, preferred_element_type=jnp.float32)
    grad_inner = gelu_back(grad_active)[0].astype(jnp.bfloat16)
    grad_win = jnp.einsum(
        "btd,btf->df", normed_two_low, grad_inner, preferred_element_type=jnp.float32
    )
    grad_bias_in = jnp.sum(grad_inner.astype(jnp.float32), axis=(0, 1))
    grad_normed_two = jnp.einsum(
        "btf,df->btd", grad_inner, mats_low[:, 4 * D :], preferred_element_type=jnp.float32
    )
    grad_hidden_norm, grad_gain_two, grad_bias_two = norm_back(
        grad_normed_two, vectors[2], kept_two
    )
    grad_hidden = grad_out + grad_hidden_norm
    grad_branch = grad_hidden.astype(jnp.bfloat16)
    grad_wout = jnp.einsum(
        "btd,bte->de", mixed_low, grad_branch, preferred_element_type=jnp.float32
    )
    grad_mixed = jnp.einsum(
        "bte,de->btd", grad_branch, mats_low[:, 3 * D : 4 * D], preferred_element_type=jnp.float32
    ).astype(jnp.bfloat16)
    grad_heads = heads_of(grad_mixed)
    grad_attend = jnp.einsum(
        "bqhc,bkhc->bhqk", grad_heads, value_heads, preferred_element_type=jnp.float32
    )
    grad_values = jnp.einsum(
        "bhqk,bqhc->bkhc", attend_low, grad_heads, preferred_element_type=jnp.float32
    )
    grad_scores = (
        attend * (grad_attend - jnp.sum(attend * grad_attend, axis=-1, keepdims=True))
    ).astype(jnp.bfloat16)
    grad_queries = (
        jnp.einsum("bhqk,bkhc->bqhc", grad_scores, key_heads, preferred_element_type=jnp.float32)
        * score_scale
    )
    grad_keys = (
        jnp.einsum("bhqk,bqhc->bkhc", grad_scores, query_heads, preferred_element_type=jnp.float32)
        * score_scale
    )
    grad_projected = jnp.concatenate(
        [
            grad_queries.reshape(seq_count, -1, D),
            grad_keys.reshape(seq_count, -1, D),
            grad_values.reshape(seq_count, -1, D),
        ],
        axis=-1,
    ).astype(jnp.bfloat16)
    grad_wqkv = jnp.einsum(
        "btd,bte->de", normed_low, grad_projected, preferred_element_type=jnp.float32
    )
    grad_normed = jnp.einsum(
        "bte,de->btd", grad_projected, mats_low[:, : 3 * D], preferred_element_type=jnp.float32
    )
    grad_resid_norm, grad_gain_one, grad_bias_one = norm_back(grad_normed, vectors[0], kept_one)
    grad_tokens = (grad_hidden + grad_resid_norm).astype(jnp.bfloat16)
    grad_mats = jnp.concatenate([grad_wqkv, grad_wout, grad_win], axis=1)
    grad_vectors = jnp.concatenate(
        [
            jnp.stack(
                [
                    grad_gain_one,
                    grad_bias_one,
                    grad_gain_two,
                    grad_bias_two,
                    jnp.sum(grad_out, axis=(0, 1)),
                ]
            ),
            grad_bias_in.reshape(-1, D),
        ],
        axis=0,
    )
    return (output.astype(jnp.bfloat16), grad_tokens, grad_mats, grad_down, grad_vectors)


def renew(weight, moment, average, gradient, step_rate):
    new_moment = MOMENTUM_DECAY * moment + gradient
    new_weight = weight - step_rate * (gradient + MOMENTUM_DECAY * new_moment)
    new_average = average + (new_weight - average) / (STEP + 1)
    return (new_moment, new_average, new_weight)


def local(
    stem_rows,
    emb_ids,
    segments,
    cotangent,
    trunk_mats,
    mats_momentum,
    mats_average,
    trunk_down,
    down_momentum,
    down_average,
    trunk_vectors,
    vectors_momentum,
    vectors_average,
    stem_mats,
    stem_momentum,
    stem_average,
    stem_queries,
    queries_momentum,
    queries_average,
):
    seq_local = stem_rows.shape[0]
    emb_count = lax.axis_size("emb")
    slot_count = emb_count * CAP
    seg_tokens = jnp.repeat(segments, QUERIES, axis=1)
    owners = emb_ids[:, 0][:, None] == jnp.arange(emb_count, dtype=jnp.int32)[None, :]
    owner_float = owners.astype(jnp.float32)
    stem_low = stem_mats.astype(jnp.bfloat16)
    queries_low = stem_queries.astype(jnp.bfloat16)
    mats_low = trunk_mats.astype(jnp.bfloat16)
    down_low = trunk_down.astype(jnp.bfloat16)
    earlier = jnp.cumsum(owner_float, axis=0) - owner_float
    position_in = jnp.sum(earlier * owner_float, axis=1).astype(jnp.int32)
    slot_index = emb_ids[:, 0] * CAP + position_in
    placing = (slot_index[:, None] == jnp.arange(slot_count, dtype=jnp.int32)[None, :]).astype(
        jnp.bfloat16
    )
    outgoing = jnp.dot(
        placing.T, stem_rows.reshape(seq_local, -1), preferred_element_type=jnp.float32
    ).astype(jnp.bfloat16)
    arrived = lax.all_to_all(
        outgoing.reshape(emb_count, -1, D), "emb", split_axis=0, concat_axis=0, tiled=True
    )
    arrived = arrived.reshape((slot_count,) + stem_rows.shape[1:])
    kv_weight = jnp.broadcast_to(stem_low[:, :, : 2 * D], (slot_count, D, 2 * D))
    out_weight = jnp.broadcast_to(stem_low[:, :, 2 * D :], (slot_count, D, D))
    query_weight = jnp.broadcast_to(queries_low, (slot_count, QUERIES, D))
    stem_made, kept_parts = stem_ahead(arrived, kv_weight, out_weight, query_weight)
    returned = lax.all_to_all(
        stem_made.reshape(emb_count, -1, D), "emb", split_axis=0, concat_axis=0, tiled=True
    )
    tokens = jnp.dot(placing, returned.reshape(slot_count, -1), preferred_element_type=jnp.float32)
    tokens = tokens.astype(jnp.bfloat16).reshape(seq_local, -1, D)
    output, grad_tokens, grad_mats, grad_down, grad_vectors = trunk_pass(
        tokens, mats_low, down_low, trunk_vectors, seg_tokens, cotangent
    )
    outgoing_grad = jnp.dot(
        placing.T, grad_tokens.reshape(seq_local, -1), preferred_element_type=jnp.float32
    ).astype(jnp.bfloat16)
    arrived_grad = lax.all_to_all(
        outgoing_grad.reshape(emb_count, -1, D), "emb", split_axis=0, concat_axis=0, tiled=True
    )
    arrived_grad = arrived_grad.reshape(stem_made.shape)
    grad_each, grad_query_each, grad_rows = stem_back(
        arrived, kv_weight, out_weight, query_weight, kept_parts, arrived_grad
    )
    grad_stem = jnp.sum(grad_each, axis=0, keepdims=True)
    grad_query = jnp.sum(grad_query_each, axis=0, keepdims=True)
    back_rows = lax.all_to_all(
        grad_rows.astype(jnp.bfloat16).reshape(emb_count, -1, D),
        "emb",
        split_axis=0,
        concat_axis=0,
        tiled=True,
    )
    rows_grad = jnp.dot(
        placing, back_rows.reshape(slot_count, -1), preferred_element_type=jnp.float32
    )
    rows_grad = rows_grad.astype(jnp.bfloat16).reshape(stem_rows.shape)
    out_values = output.astype(jnp.float32).reshape(-1, D)
    feature_sums = jnp.stack(
        [jnp.sum(out_values, axis=0), jnp.sum(out_values * out_values, axis=0)]
    )
    grad_stem, grad_query = (
        lax.psum(grad_stem.astype(jnp.bfloat16), "dp").astype(jnp.float32),
        lax.psum(grad_query.astype(jnp.bfloat16), "dp").astype(jnp.float32),
    )
    grad_mats, grad_down, grad_vectors, feature_sums = lax.psum(
        (grad_mats, grad_down, grad_vectors, feature_sums), ("dp", "emb")
    )
    token_total = seq_local * TOK_SEQ * lax.axis_size("dp") * emb_count
    feature_mean = feature_sums[0] / token_total
    feature_var = feature_sums[1] / token_total - feature_mean * feature_mean
    action_stats = jnp.stack([feature_mean, feature_var])
    step_rate = BASE_RATE / math.sqrt(token_total)
    mats_moment, mats_mean, mats_new = renew(
        trunk_mats, mats_momentum, mats_average, grad_mats, step_rate
    )
    down_moment, down_mean, down_new = renew(
        trunk_down, down_momentum, down_average, grad_down, step_rate
    )
    vectors_moment, vectors_mean, vectors_new = renew(
        trunk_vectors, vectors_momentum, vectors_average, grad_vectors, step_rate
    )
    stem_moment, stem_mean, stem_new = renew(
        stem_mats, stem_momentum, stem_average, grad_stem, step_rate
    )
    queries_moment, queries_mean, queries_new = renew(
        stem_queries, queries_momentum, queries_average, grad_query, step_rate
    )
    return (
        output,
        rows_grad,
        mats_moment,
        mats_mean,
        mats_new,
        mats_new.astype(jnp.bfloat16),
        down_moment,
        down_mean,
        down_new,
        down_new.astype(jnp.bfloat16),
        vectors_moment,
        vectors_mean,
        vectors_new,
        stem_moment,
        stem_mean,
        stem_new,
        stem_new.astype(jnp.bfloat16),
        queries_moment,
        queries_mean,
        queries_new,
        queries_new.astype(jnp.bfloat16),
        action_stats,
    )


def solution(mesh):
    in_specs = (
        P(("dp", "emb"), None, None, None),
        P(("dp", "emb"), None),
        P(("dp", "emb"), None),
        P(("dp", "emb"), None, None),
        P(),
        P(),
        P(),
        P(),
        P(),
        P(),
        P(),
        P(),
        P(),
        P("emb", None, None),
        P("emb", None, None),
        P("emb", None, None),
        P("emb", None, None),
        P("emb", None, None),
        P("emb", None, None),
    )
    out_specs = (
        P(("dp", "emb"), None, None),
        P(("dp", "emb"), None, None, None),
        P(),
        P(),
        P(),
        P(),
        P(),
        P(),
        P(),
        P(),
        P(),
        P(),
        P(),
        P("emb", None, None),
        P("emb", None, None),
        P("emb", None, None),
        P("emb", None, None),
        P("emb", None, None),
        P("emb", None, None),
        P("emb", None, None),
        P("emb", None, None),
        P(),
    )
    return jax.shard_map(local, mesh=mesh, in_specs=in_specs, out_specs=out_specs, check_vma=False)
```

profile of v0, /device:TPU:0, one launch (start us, length us, event | category | flops | bytes accessed | tf_op | source)
XLA Modules:
  0.0 752.2 jit_solution(1588468770832413394)
XLA Ops:
  10.3 5.1 convolution_convert_fusion
  15.5 7.4 reshape.217
  22.8 5.1 all-to-all-start
  28.2 48.7 %all-to-all-done = bf16[4,4096,128]{2,1,0:T(8,128)(2,1)} async-done(((bf16[4,4096,128]{2,1,0:T(8,128)(2,1)}), bf16[4,4096,128]{2,1,0:T(8,128)(2,1)}, u32[]{:S(2)}, u32[]{:S(2)}) %all-to-all-start) | async-done | bytes 4194336 | tf_op jit(solution)/shard_map/all_to_all | solution.py:282
  76.9 4.5 convolution_convert_fusion.4
  81.4 4.3 fusion.122
  85.7 8.4 %copy.122 = bf16[64,4,64,128]{2,3,1,0:T(8,128)(2,1)} copy(bf16[64,4,64,128]{3,2,1,0:T(8,128)(2,1)} %get-tuple-element.73) | data formatting | bytes 8388608 | tf_op jit(solution)/shard_map/slice | solution.py:53
  94.1 8.4 %copy.121 = bf16[64,4,64,128]{2,3,1,0:T(8,128)(2,1)} copy(bf16[64,4,64,128]{3,2,1,0:T(8,128)(2,1)} %get-tuple-element.74) | data formatting | bytes 8388608 | tf_op jit(solution)/shard_map/slice | solution.py:54
  102.5 15.3 %fusion.30 = f32[64,8,4,64,32]{3,4,2,1,0:T(8,128)} fusion(bf16[64,4,64,8,16]{2,4,3,1,0:T(8,128)(2,1)} %bitcast.216, bf16[32,8,16]{0,2,1:T(8,128)(2,1)S(1)} %bitcast.246), kind=kOutput, calls=%fused_computation.49 | convolution fusion | flops 134217728 | bytes 20979712 | tf_op jit(solution)/shard_map/bqhc,bsrhc->bshqr/dot_general | solution.py:57
  117.7 37.1 %fusion.124 = (f32[64,4,8,32]{3,1,2,0:T(4,128)S(1)}, f32[64,4,8,32,64]{4,3,1,2,0:T(8,128)}) fusion(f32[64,8,4,64,32]{3,4,2,1,0:T(8,128)} %fusion.30), kind=kOutput, calls=%fused_computation.200 | output fusion | flops 16777280 | bytes 33816576 | tf_op jit(solution)/shard_map/sub | solution.py:60
  154.8 17.7 %fusion.115 = bf16[64,4,8,32,64]{4,3,1,2,0:T(8,128)(2,1)} fusion(f32[64,4,8,32,64]{4,3,1,2,0:T(8,128)} %get-tuple-element.88, f32[64,4,8,32]{3,1,2,0:T(4,128)S(1)} %get-tuple-element.87), kind=kLoop, calls=%fused_computation.193 | loop fusion | flops 8388608 | bytes 25427968 | tf_op jit(solution)/shard_map/convert_element_type | solution.py:61
  172.5 13.4 %fusion.32 = bf16[64,4,8,16,32]{4,3,2,1,0:T(8,128)(2,1)S(1)} fusion(bf16[64,4,64,8,16]{2,4,3,1,0:T(8,128)(2,1)} %bitcast.223, bf16[64,4,8,32,64]{4,3,1,2,0:T(8,128)(2,1)} %fusion.115), kind=kOutput, calls=%fused_computation.52 | convolution fusion | flops 135266304 | bytes 14680064 | tf_op jit(solution)/shard_map/bshqr,bsrhc->bsqhc/dot_general | solution.py:62
  185.9 4.1 fusion.65
  190.0 3.8 all-to-all-start.1
  196.1 23.3 %all-to-all-done.1 = bf16[4,2048,128]{2,1,0:T(8,128)(2,1)S(1)} async-done(((bf16[4,2048,128]{2,1,0:T(8,128)(2,1)}), bf16[4,2048,128]{2,1,0:T(8,128)(2,1)S(1)}, u32[]{:S(2)}, u32[]{:S(2)}) %all-to-all-start.1) | async-done | bytes 2097184 | tf_op jit(solution)/shard_map/all_to_all | solution.py:290
  219.4 2.3 reshape.221
  221.7 2.1 fusion.73
  229.7 2.1 fusion.123
  233.4 2.3 copy.129
  235.7 2.3 copy.127
  237.9 11.2 %fusion.125 = (f32[32,8,128]{2,1,0:T(8,128)}, f32[32,8,128,128]{2,3,1,0:T(8,128)}) fusion(pred[32,128,128]{1,2,0:T(8,128)(4,1)} %broadcast_compare_fusion, bf16[32,128,8,16]{1,3,2,0:T(8,128)(2,1)} %bitcast.234, bf16[32,128,8,16]{1,3,2,0:T(8,128)(2,1)S(1)} %bitcast.228), kind=kOutput, calls=%fused_computation.201 | convolution fusion | flops 150995072 | bytes 19529728 | tf_op jit(solution)/shard_map/sub | solution.py:139
  249.1 8.3 %fusion.75 = bf16[32,8,16,128]{3,2,1,0:T(8,128)(2,1)S(1)} fusion(bf16[32,128,8,16]{1,3,2,0:T(8,128)(2,1)} %bitcast.243, f32[32,8,128,128]{2,3,1,0:T(8,128)} %get-tuple-element.90, f32[32,8,128]{2,1,0:T(8,128)} %get-tuple-element.89), kind=kOutput, calls=%fused_computation.109 | convolution fusion | flops 143130624 | bytes 19005440 | tf_op jit(solution)/shard_map/bhqk,bkhc->bqhc/dot_general | solution.py:141
  259.7 6.2 multiply_convert_fusion.3
  265.9 7.3 convert_reduce_fusion
  273.2 2.5 convolution_bitcast_fusion.2
  275.7 2.6 multiply_reduce_fusion.2
  278.3 3.0 convert_reduce_fusion.2
  283.0 11.4 %fusion.78 = bf16[32,8,16,128]{3,2,1,0:T(8,128)(2,1)} fusion(bf16[32,128,8,16]{1,3,2,0:T(8,128)(2,1)S(1)} %bitcast.241, f32[32,8,128,128]{2,3,1,0:T(8,128)} %get-tuple-element.90, f32[32,8,128]{2,1,0:T(8,128)S(1)} %copy-done.38), kind=kOutput, calls=%fused_computation.110 | convolution fusion | flops 143130624 | bytes 19005440 | tf_op jit(solution)/shard_map/bhqk,bqhc->bkhc/dot_general | solution.py:186
  294.4 11.0 %multiply_reduce_fusion.1 = (f32[32,8,128]{2,1,0:T(8,128)S(1)}, f32[32,8,128,128]{2,3,1,0:T(8,128)}) fusion(f32[32,8,128,128]{2,3,1,0:T(8,128)} %get-tuple-element.90, f32[32,8,128]{2,1,0:T(8,128)S(1)} %copy-done.38, bf16[32,128,8,16]{1,3,2,0:T(8,128)(2,1)S(1)} %bitcast.242, bf16[32,128,8,16]{1,3,2,0:T(8,128)(2,1)S(1)} %bitcast.244), kind=kOutput, calls=%fused_computation.16 | convolution fusion | flops 146767872 | bytes 35913728 | tf_op jit(solution)/shard_map/bqhc,bkhc->bhqk/dot_general | solution.py:183
  305.4 12.2 %multiply_convert_fusion.2 = bf16[32,8,128,128]{2,3,1,0:T(8,128)(2,1)S(1)} fusion(f32[32,8,128,128]{2,3,1,0:T(8,128)} %get-tuple-element.97, f32[32,8,128]{2,1,0:T(8,128)S(1)} %get-tuple-element.96, f32[32,8,128,128]{2,3,1,0:T(8,128)} %get-tuple-element.90, f32[32,8,128]{2,1,0:T(8,128)S(1)} %copy-done.38), kind=kLoop, calls=%fused_computation.15 | loop fusion | flops 16777216 | bytes 42205184 | tf_op jit(solution)/shard_map/convert_element_type | solution.py:191
  317.7 5.4 multiply_convert_fusion.4
  323.1 3.3 multiply_convert_fusion.5
  326.4 2.4 copy.138
  328.8 2.3 copy.136
  332.6 3.7 fusion.83
  336.4 3.9 multiply_reduce_fusion.3
  340.4 2.0 convolution_bitcast_fusion.1
  342.4 2.7 convert_reduce_fusion.1
  345.1 2.6 add_convert_fusion
  348.8 2.3 reshape.230
  351.1 3.7 all-to-all-start.2
  357.6 59.9 %all-reduce = (f32[9,128]{1,0:T(8,128)S(1)}, f32[2,128]{1,0:T(2,128)S(1)}) all-reduce(f32[9,128]{1,0:T(8,128)S(1)} %concatenate.20, f32[2,128]{1,0:T(2,128)S(1)} %pad_maximum_fusion.13), channel_id=1, replica_groups=mesh['dp'=8,'emb'=4] {'dp','emb'}, use_global_device_ids=true, to_apply=%region_24.25 | all-reduce | flops 1408 | bytes 11264 | tf_op jit(solution)/shard_map/psum | solution.py:329
  418.6 75.2 %all-reduce.7.cloned.1.call-done = (f32[128,1024]{1,0:T(8,128)}, f32[512,128]{1,0:T(8,128)}) async-done(((f32[128,1024]{1,0:T(8,128)}, f32[512,128]{1,0:T(8,128)}), (f32[128,1024]{1,0:T(8,128)}, f32[512,128]{1,0:T(8,128)})) %all-reduce.7.cloned.1.call-update) | async-done | bytes 786448 | tf_op jit(solution)/shard_map/psum | solution.py:329
  493.9 1.9 fusion.120
  496.6 2.2 fusion.121
  500.5 2.9 fusion.68
  503.4 7.8 %copy.180 = bf16[64,4,32,128]{2,3,1,0:T(8,128)(2,1)} copy(bf16[64,4,32,128]{3,2,1,0:T(8,128)(2,1)} %fusion.68) | data formatting | bytes 4194304 | tf_op jit(solution)/shard_map/reshape | solution.py:25
  511.1 13.2 %fusion.35 = bf16[64,4,8,16,64]{4,3,2,1,0:T(8,128)(2,1)} fusion(bf16[64,4,32,8,16]{2,4,3,1,0:T(8,128)(2,1)} %bitcast.220, bf16[64,4,8,32,64]{4,3,1,2,0:T(8,128)(2,1)} %fusion.115), kind=kOutput, calls=%fused_computation.53 | convolution fusion | flops 136314880 | bytes 14680064 | tf_op jit(solution)/shard_map/bshqr,bsqhc->bsrhc/dot_general | solution.py:93
  524.3 30.8 %multiply_reduce_fusion = (f32[64,4,8,32]{3,1,2,0:T(4,128)S(1)}, f32[64,4,8,32,64]{4,3,1,2,0:T(8,128)}) fusion(f32[64,4,8,32,64]{4,3,1,2,0:T(8,128)} %get-tuple-element.88, f32[64,4,8,32]{3,1,2,0:T(4,128)S(1)} %copy-done.9, bf16[64,4,64,8,16]{2,4,3,1,0:T(8,128)(2,1)} %bitcast.224, bf16[64,4,32,8,16]{2,4,3,1,0:T(8,128)(2,1)} %bitcast.221), kind=kOutput, calls=%fused_computation.9 | convolution fusion | flops 146735104 | bytes 40370176 | tf_op jit(solution)/shard_map/bsqhc,bsrhc->bshqr/dot_general | solution.py:90
  555.1 8.5 %copy.147 = bf16[64,4,64,128]{3,2,1,0:T(8,128)(2,1)} copy(bf16[64,4,64,128]{2,3,1,0:T(8,128)(2,1)} %bitcast.222) | data formatting | bytes 8388608 | tf_op jit(solution)/shard_map/reshape | solution.py:112
  563.6 27.3 %multiply_convert_fusion = bf16[64,4,8,32,64]{4,3,1,2,0:T(8,128)(2,1)} fusion(f32[64,4,8,32,64]{4,3,1,2,0:T(8,128)} %get-tuple-element.100, f32[64,4,8,32]{3,1,2,0:T(4,128)S(1)} %get-tuple-element.99, f32[64,4,8,32,64]{4,3,1,2,0:T(8,128)} %get-tuple-element.88, f32[64,4,8,32]{3,1,2,0:T(4,128)S(1)} %copy-done.9), kind=kLoop, calls=%fused_computation.8 | loop fusion | flops 16777216 | bytes 42467328 | tf_op jit(solution)/shard_map/convert_element_type | solution.py:98
  591.0 11.3 %fusion.21 = bf16[64,4,64,8,16]{2,4,1,3,0:T(8,128)(2,1)} fusion(bf16[64,4,8,32,64]{4,3,1,2,0:T(8,128)(2,1)} %multiply_convert_fusion, bf16[32,8,16]{0,2,1:T(8,128)(2,1)S(1)} %bitcast.247), kind=kOutput, calls=%fused_computation.36 | convolution fusion | flops 138412032 | bytes 12591104 | tf_op jit(solution)/shard_map/bshqr,bqhc->bsrhc/dot_general | solution.py:104
  602.3 9.0 %copy.143 = bf16[64,4,64,8,16]{2,4,3,1,0:T(8,128)(2,1)} copy(bf16[64,4,64,8,16]{2,4,1,3,0:T(8,128)(2,1)} %fusion.21) | data formatting | bytes 8388608 | tf_op jit(solution)/shard_map/mul | solution.py:104
  611.3 8.5 %copy.146 = bf16[64,4,64,128]{3,2,1,0:T(8,128)(2,1)} copy(bf16[64,4,64,128]{2,3,1,0:T(8,128)(2,1)} %bitcast.225) | data formatting | bytes 8388608 | tf_op jit(solution)/shard_map/reshape | solution.py:111
  619.9 7.7 %fusion.54 = bf16[64,4,64,128]{3,2,1,0:T(8,128)(2,1)} fusion(bf16[64,4,64,128]{3,2,1,0:T(8,128)(2,1)} %copy.147, bf16[64,4,64,128]{3,2,1,0:T(8,128)(2,1)} %copy.146, bf16[128,256]{1,0:T(8,128)(2,1)S(1)} %copy-done.34), kind=kOutput, calls=%fused_computation.72 | convolution fusion | flops 1092616192 | bytes 12648448 | tf_op jit(solution)/shard_map/bsre,bde->bsrd/dot_general | solution.py:117
  627.6 4.8 all-to-all-start.3
  632.5 11.2 %fusion.42 = bf16[8,16,32]{2,1,0:T(8,128)(2,1)S(1)} fusion(bf16[64,4,8,32,64]{4,3,1,2,0:T(8,128)(2,1)} %multiply_convert_fusion, bf16[64,4,64,8,16]{2,4,3,1,0:T(8,128)(2,1)} %bitcast.217), kind=kOutput, calls=%fused_computation.59 | convolution fusion | flops 134737920 | bytes 12591104 | tf_op jit(solution)/shard_map/bshqr,bsrhc->bqhc/dot_general | solution.py:100
  643.8 6.3 fusion.47
  650.2 6.7 convolution_bitcast_fusion
  656.9 3.7 maximum_reduce_fusion
  660.6 20.6 %psum.46 = bf16[1,32,128]{2,1,0:T(8,128)(2,1)S(1)} all-reduce(bf16[1,32,128]{2,1,0:T(8,128)(2,1)S(1)} %copy.157), channel_id=1, replica_groups=mesh['dp'=8,'emb'=4] {'dp'}, use_global_device_ids=true, to_apply=%region_28.29 | all-reduce | flops 4096 | bytes 16384 | tf_op jit(solution)/shard_map/psum | solution.py:327
  682.4 47.6 %all-reduce.5.cloned.1.call-done = bf16[1,128,384]{2,1,0:T(8,128)(2,1)} async-done(((bf16[1,128,384]{2,1,0:T(8,128)(2,1)}), bf16[1,128,384]{2,1,0:T(8,128)(2,1)}) %all-reduce.5.cloned.1.call-update) | async-done | bytes 98320 | tf_op jit(solution)/shard_map/psum | solution.py:326
  732.5 7.3 reshape.235
  739.8 2.9 fusion.74
  (168 shorter events, 30.5 us)
Async XLA Ops:
  10.3 337.5 %copy-start.47 = (s32[32]{0:T(128)}, s32[32]{0:T(128)S(1)}, u32[]{:S(2)}) copy-start(s32[32]{0:T(128)S(1)} %fusion.107) | copy-start | bytes 388
  22.8 5.1 copy-start.39
  22.8 5.3 copy-start.27
  22.8 54.0 %all-to-all-start = ((bf16[4,4096,128]{2,1,0:T(8,128)(2,1)}), bf16[4,4096,128]{2,1,0:T(8,128)(2,1)}, u32[]{:S(2)}, u32[]{:S(2)}) async-start(bf16[4,4096,128]{2,1,0:T(8,128)(2,1)} %reshape.217), calls=%async_computation | async-start | bytes 8388608 | tf_op jit(solution)/shard_map/all_to_all | solution.py:282
  28.1 74.3 %copy-start.25 = (bf16[1,32,128]{1,2,0:T(8,128)(2,1)}, bf16[1,32,128]{1,2,0:T(8,128)(2,1)S(1)}, u32[]{:S(2)}) copy-start(bf16[1,32,128]{1,2,0:T(8,128)(2,1)S(1)} %copy.123) | copy-start | bytes 24580
  28.2 53.2 %copy-start.33 = (bf16[128,256]{1,0:T(8,128)(2,1)}, bf16[128,256]{1,0:T(8,128)(2,1)S(1)}, u32[]{:S(2)}) copy-start(bf16[128,256]{1,0:T(8,128)(2,1)S(1)} %slice_bitcast_fusion.6) | copy-start | bytes 196612
  154.8 17.7 %copy-start.8 = (f32[64,4,8,32]{3,1,2,0:T(4,128)}, f32[64,4,8,32]{3,1,2,0:T(4,128)S(1)}, u32[]{:S(2)}) copy-start(f32[64,4,8,32]{3,1,2,0:T(4,128)S(1)} %get-tuple-element.87) | copy-start | bytes 786436
  185.9 4.1 copy-start
  190.0 3.8 copy-start.54
  190.0 4.1 copy-start.16
  190.0 4.1 copy-start.42
  190.0 29.4 %all-to-all-start.1 = ((bf16[4,2048,128]{2,1,0:T(8,128)(2,1)}), bf16[4,2048,128]{2,1,0:T(8,128)(2,1)S(1)}, u32[]{:S(2)}, u32[]{:S(2)}) async-start(bf16[4,2048,128]{2,1,0:T(8,128)(2,1)} %bitcast.231), calls=%async_computation.1 | async-start | bytes 4194304 | tf_op jit(solution)/shard_map/all_to_all | solution.py:290
  194.1 63.3 %copy-start.30 = (bf16[128,1024]{1,0:T(8,128)(2,1)}, bf16[128,1024]{1,0:T(8,128)(2,1)S(1)}, u32[]{:S(2)}) copy-start(bf16[128,1024]{1,0:T(8,128)(2,1)S(1)} %convert_element_type.192) | copy-start | bytes 786436
  194.7 31.6 %copy-start.49 = (f32[128]{0:T(128)}, f32[128]{0:T(128)S(1)}, u32[]{:S(2)}) copy-start(f32[128]{0:T(128)S(1)} %get-tuple-element.84) | copy-start | bytes 1540
  227.7 1.0 copy-start.12
  258.3 20.0 %copy-start.1 = (f32[32,128,128]{2,1,0:T(8,128)}, f32[32,128,128]{2,1,0:T(8,128)S(1)}, u32[]{:S(2)}) copy-start(f32[32,128,128]{2,1,0:T(8,128)S(1)} %get-tuple-element.92) | copy-start | bytes 6291460
  259.7 6.2 copy-start.13
  259.7 6.2 copy-start.22
  273.2 2.6 copy-start.31
  281.3 1.3 copy-start.3
  281.3 1.8 copy-start.38
  283.0 11.4 %copy-start.18 = (bf16[32,128,128]{1,2,0:T(8,128)(2,1)S(1)}, bf16[32,128,128]{1,2,0:T(8,128)(2,1)}, u32[]{:S(2)}) copy-start(bf16[32,128,128]{1,2,0:T(8,128)(2,1)} %copy.127) | copy-start | bytes 3145732
  305.4 12.2 %copy-start.10 = (bf16[32,128,128]{1,2,0:T(8,128)(2,1)S(1)}, bf16[32,128,128]{1,2,0:T(8,128)(2,1)}, u32[]{:S(2)}) copy-start(bf16[32,128,128]{1,2,0:T(8,128)(2,1)} %copy.129) | copy-start | bytes 3145732
  326.4 4.6 copy-start.11
  332.6 3.8 copy-start.19
  332.6 3.8 copy-start.20
  332.6 3.8 copy-start.21
  332.6 3.8 copy-start.50
  336.4 4.0 copy-start.7
  336.4 4.0 copy-start.14
  340.4 2.0 copy-start.2
  340.4 2.0 copy-start.51
  342.4 2.8 copy-start.4
  348.7 6.2 copy-start.53
  348.7 6.2 copy-start.24
  348.7 8.0 %copy-start.52 = (f32[128]{0:T(128)S(1)}, f32[128]{0:T(128)}, u32[]{:S(2)}) copy-start(f32[128]{0:T(128)} %get-tuple-element.78) | copy-start | bytes 1540
  348.7 8.0 %copy-start.55 = (f32[512]{0:T(512)S(1)}, f32[512]{0:T(512)}, u32[]{:S(2)}) copy-start(f32[512]{0:T(512)} %get-tuple-element.101) | copy-start | bytes 6148
  348.7 8.0 %copy-start.56 = (f32[128]{0:T(128)S(1)}, f32[128]{0:T(128)}, u32[]{:S(2)}) copy-start(f32[128]{0:T(128)} %get-tuple-element.44) | copy-start | bytes 1540
  348.8 69.3 %copy-start.45 = (f32[9,128]{1,0:T(8,128)S(1)}, f32[9,128]{1,0:T(8,128)}, u32[]{:S(2)}) copy-start(f32[9,128]{1,0:T(8,128)} %param.31) | copy-start | bytes 13828
  348.8 69.2 %copy-start.46 = (f32[9,128]{1,0:T(8,128)S(1)}, f32[9,128]{1,0:T(8,128)}, u32[]{:S(2)}) copy-start(f32[9,128]{1,0:T(8,128)} %param.30) | copy-start | bytes 13828
  351.1 144.6 %copy-start.35 = (f32[512,128]{1,0:T(8,128)S(1)}, f32[512,128]{1,0:T(8,128)}, u32[]{:S(2)}) copy-start(f32[512,128]{1,0:T(8,128)} %param.28) | copy-start | bytes 786436
  351.1 145.4 %copy-start.17 = (f32[128,1024]{1,0:T(8,128)S(1)}, f32[128,1024]{1,0:T(8,128)}, u32[]{:S(2)}) copy-start(f32[128,1024]{1,0:T(8,128)} %param.23) | copy-start | bytes 1572868
  351.1 149.3 %all-to-all-start.2 = ((bf16[4,2048,128]{2,1,0:T(8,128)(2,1)}), bf16[4,2048,128]{2,1,0:T(8,128)(2,1)S(1)}, u32[]{:S(2)}, u32[]{:S(2)}) async-start(bf16[4,2048,128]{2,1,0:T(8,128)(2,1)} %reshape.230), calls=%async_computation.2 | async-start | bytes 4194304 | tf_op jit(solution)/shard_map/all_to_all | solution.py:301
  354.9 139.0 %all-reduce.7.cloned.1.call-start = ((), (), s32[]{:S(2)}) async-start(), calls=%async_computation.5 | async-start | bytes 1572864 | tf_op jit(solution)/shard_map/psum | solution.py:329
  493.9 5.7 copy-start.32
  495.8 7.6 %copy-start.23 = (f32[512,128]{1,0:T(8,128)}, f32[512,128]{1,0:T(8,128)S(1)}, u32[]{:S(2)}) copy-start(f32[512,128]{1,0:T(8,128)S(1)} %get-tuple-element.68) | copy-start | bytes 786436
  498.8 0.8 copy-start.15
  500.5 10.7 %copy-start.5 = (bf16[4,2048,128]{2,1,0:T(8,128)(2,1)}, bf16[4,2048,128]{2,1,0:T(8,128)(2,1)S(1)}, u32[]{:S(2)}) copy-start(bf16[4,2048,128]{2,1,0:T(8,128)(2,1)S(1)} %all-to-all-done.2) | copy-start | bytes 6291460
  511.1 13.2 %copy-start.9 = (f32[64,4,8,32]{3,1,2,0:T(4,128)S(1)}, f32[64,4,8,32]{3,1,2,0:T(4,128)}, u32[]{:S(2)}) copy-start(f32[64,4,8,32]{3,1,2,0:T(4,128)} %copy-done.8) | copy-start | bytes 786436
  563.6 27.4 %copy-start.26 = (bf16[1,32,128]{1,2,0:T(8,128)(2,1)S(1)}, bf16[1,32,128]{1,2,0:T(8,128)(2,1)}, u32[]{:S(2)}) copy-start(bf16[1,32,128]{1,2,0:T(8,128)(2,1)} %copy-done.25) | copy-start | bytes 24580
  611.3 8.5 %copy-start.34 = (bf16[128,256]{1,0:T(8,128)(2,1)S(1)}, bf16[128,256]{1,0:T(8,128)(2,1)}, u32[]{:S(2)}) copy-start(bf16[128,256]{1,0:T(8,128)(2,1)} %copy-done.33) | copy-start | bytes 196612
  627.6 104.9 %all-to-all-start.3 = ((bf16[4,4096,128]{2,1,0:T(8,128)(2,1)}), bf16[4,4096,128]{2,1,0:T(8,128)(2,1)}, u32[]{:S(2)}, u32[]{:S(2)}) async-start(bf16[4,4096,128]{2,1,0:T(8,128)(2,1)} %bitcast.237), calls=%async_computation.3 | async-start | bytes 8388608 | tf_op jit(solution)/shard_map/all_to_all | solution.py:310
  632.4 97.6 %all-reduce.5.cloned.1.call-start = ((), (), s32[]{:S(2)}) async-start(), calls=%async_computation.4 | async-start | bytes 196608 | tf_op jit(solution)/shard_map/psum | solution.py:326
  643.8 6.4 copy-start.6
  656.9 24.3 %copy-start.40 = (f32[1,32,128]{2,1,0:T(8,128)S(1)}, f32[1,32,128]{2,1,0:T(8,128)}, u32[]{:S(2)}) copy-start(f32[1,32,128]{2,1,0:T(8,128)} %param.35) | copy-start | bytes 49156
  656.9 24.3 %copy-start.43 = (f32[1,32,128]{2,1,0:T(8,128)S(1)}, f32[1,32,128]{2,1,0:T(8,128)}, u32[]{:S(2)}) copy-start(f32[1,32,128]{2,1,0:T(8,128)} %param.36) | copy-start | bytes 49156
  656.9 25.0 %copy-start.44 = (f32[1,32,128]{2,1,0:T(8,128)S(1)}, f32[1,32,128]{2,1,0:T(8,128)}, u32[]{:S(2)}) copy-start(f32[1,32,128]{2,1,0:T(8,128)} %param.37) | copy-start | bytes 49156
  656.9 73.2 %copy-start.28 = (f32[1,128,384]{2,1,0:T(8,128)S(1)}, f32[1,128,384]{2,1,0:T(8,128)}, u32[]{:S(2)}) copy-start(f32[1,128,384]{2,1,0:T(8,128)} %param.32) | copy-start | bytes 589828
  656.9 73.2 %copy-start.37 = (f32[1,128,384]{2,1,0:T(8,128)S(1)}, f32[1,128,384]{2,1,0:T(8,128)}, u32[]{:S(2)}) copy-start(f32[1,128,384]{2,1,0:T(8,128)} %param.33) | copy-start | bytes 589828
  656.9 74.9 %copy-start.36 = (f32[1,128,384]{2,1,0:T(8,128)S(1)}, f32[1,128,384]{2,1,0:T(8,128)}, u32[]{:S(2)}) copy-start(f32[1,128,384]{2,1,0:T(8,128)} %param.34) | copy-start | bytes 589828
  681.8 58.0 %copy-start.41 = (f32[1,32,128]{2,1,0:T(8,128)}, f32[1,32,128]{2,1,0:T(8,128)S(1)}, u32[]{:S(2)}) copy-start(f32[1,32,128]{2,1,0:T(8,128)S(1)} %get-tuple-element.59) | copy-start | bytes 49156
  731.7 8.0 %copy-start.29 = (f32[1,128,384]{2,1,0:T(8,128)}, f32[1,128,384]{2,1,0:T(8,128)S(1)}, u32[]{:S(2)}) copy-start(f32[1,128,384]{2,1,0:T(8,128)S(1)} %get-tuple-element.62) | copy-start | bytes 589828
  732.5 7.3 copy-start.48
Sparse Core Ops, SparseCore 0:
  362.1 131.6 all-reduce.6
Sparse Core Ops, SparseCore 1:
  660.6 69.4 all-reduce.4
where the time goes:
time: 757 us; the launch traced here: 752 us
  matrix products  223 us (29%)
  waiting for transfers between devices  195 us (26%)
  other arithmetic  124 us (16%)
  local copies, waits for them, and re-layouts  95.4 us (13%)
  blocking collectives  80.5 us (11%)
  starting transfers between devices  17.5 us (2%)
  between operations  16.5 us (2%)
    psum x1, waiting for transfers between devices, local(): lax.psum((grad_mats, grad_down, grad_vectors, feature_sums), ('dp', 'emb'))  75.2 us
    psum x1, blocking collectives, local(): lax.psum((grad_mats, grad_down, grad_vectors, feature_sums), ('dp', 'emb'))  59.9 us
    all_to_all x1, waiting for transfers between devices, local(): lax.all_to_all(outgoing.reshape(emb_count, -1, D), 'emb', split_axis=0, c...  48.7 us
    psum x1, waiting for transfers between devices, local(): lax.psum(grad_stem.astype(jnp.bfloat16), 'dp').astype(jnp.float32)  47.6 us
    sub x1, other arithmetic, stem_ahead(): attend = jax.nn.softmax(scores, axis=-1)  37.1 us
    dot_general x1, matrix products, stem_back(): jnp.einsum('bsqhc,bsrhc->bshqr', grad_heads, value_heads, preferred_eleme...  30.8 us
    convert_element_type x1, other arithmetic, stem_back(): grad_scores = (attend * (grad_attend - jnp.sum(attend * grad_attend, axis...  27.3 us
    all_to_all x1, waiting for transfers between devices, local(): lax.all_to_all(stem_made.reshape(emb_count, -1, D), 'emb', split_axis=0,...  23.3 us
  transfers between devices with their start and end apart: 6, of which 4 were waited for; matrix products, arithmetic and copies ran while one was open for 6% of the time, Pallas kernels for 0%

commit v1 on v0

v1 whole, which is shorter than its diff:
```python
import functools
import math

import jax
import jax.numpy as jnp
from jax import lax
from jax.experimental import pallas as pl
from jax.experimental.pallas import tpu as pltpu
from jax.sharding import PartitionSpec as P

D = 128
FF = 512
HEADS = 8
HEAD_DIM = 16
QUERIES = 32
STEPS = 4
STEP = 4
TOK_SEQ = 128
ROWS_SEQ = 256
PAIRS = HEADS // 2

NORM_EPSILON = 1e-05
MOMENTUM_DECAY = 0.9
BASE_RATE = 0.1
HIDDEN_SCORE = -1e30
SCALE = 1.0 / math.sqrt(HEAD_DIM)

TRUNK_ROWS = 384
STEM_ROWS = 416
VEC_ROWS = 32
SEND_ROWS = TRUNK_ROWS + STEM_ROWS + VEC_ROWS

BF = jnp.bfloat16
F32 = jnp.float32
VMEM_LIMIT = 56 * 1024 * 1024


def mm(a, b):
    return lax.dot_general(a, b, (((1,), (0,)), ((), ())), preferred_element_type=F32)


def mm_nt(a, b):
    return lax.dot_general(a, b, (((1,), (1,)), ((), ())), preferred_element_type=F32)


def norm_ahead(value, gain, bias):
    centered = value - jnp.mean(value, axis=0, keepdims=True)
    inverse = lax.rsqrt(jnp.mean(centered * centered, axis=0, keepdims=True) + NORM_EPSILON)
    unit = centered * inverse
    return unit * gain + bias, unit, inverse


def norm_back(gradient, gain, unit, inverse):
    grad_unit = gradient * gain
    mean_one = jnp.mean(grad_unit, axis=0, keepdims=True)
    mean_two = jnp.mean(grad_unit * unit, axis=0, keepdims=True)
    return inverse * (grad_unit - mean_one - unit * mean_two)


def softmax_rows(scores, axis):
    top = jnp.max(scores, axis=axis, keepdims=True)
    raised = jnp.exp(scores - top)
    return raised * (1.0 / jnp.sum(raised, axis=axis, keepdims=True))


def scores_back(probs, grad, axis):
    product = probs * grad
    return (product - probs * jnp.sum(product, axis=axis, keepdims=True)).astype(BF)


def head_pair(source, j):
    pieces = []
    if j:
        pieces.append(jnp.zeros((32 * j, 256), BF))
    zero = jnp.zeros((16, 128), BF)
    one = source[32 * j : 32 * j + 16]
    two = source[32 * j + 16 : 32 * j + 32]
    pieces.append(jnp.concatenate([one, zero], axis=1))
    pieces.append(jnp.concatenate([zero, two], axis=1))
    if j < PAIRS - 1:
        pieces.append(jnp.zeros((128 - 32 * j - 32, 256), BF))
    return jnp.concatenate(pieces, axis=0)


def pair_rows(source, j):
    zero = jnp.zeros((16, 128), BF)
    one = source[32 * j : 32 * j + 16]
    two = source[32 * j + 16 : 32 * j + 32]
    return jnp.concatenate(
        [jnp.concatenate([one, zero], axis=1), jnp.concatenate([zero, two], axis=1)], axis=0
    )


def pair_pick(both):
    return jnp.concatenate([both[:16, :128], both[16:, 128:]], axis=0)


def fold_lanes(value, group):
    total = value[:, :128]
    for b in range(1, group):
        total = total + value[:, 128 * b : 128 * b + 128]
    return total


def main_kernel(
    group,
    rel_ref,
    seg_ref,
    pos_ref,
    rows_ref,
    cot_ref,
    own_ref,
    one_ref,
    two_ref,
    three_ref,
    mats_ref,
    down_ref,
    vec_ref,
    out_ref,
    rgrad_ref,
    send_ref,
    vsend_ref,
    s_kv,
    s_kvT,
    s_out,
    s_outT,
    s_qb,
    t_qkvT,
    t_qkv,
    t_o,
    t_oT,
    t_in,
    t_inT,
    t_dn,
    t_dnT,
    bias_in,
    vecs,
    a_qkv,
    a_o,
    a_in,
    a_dn,
    a_bin,
    a_vec,
    a_kv,
    a_out,
    a_q,
):
    step = pl.program_id(0)

    @pl.when(step == 0)
    def _():
        head_mask = (
            lax.broadcasted_iota(jnp.int32, (256, 128), 0) // 32
            == lax.broadcasted_iota(jnp.int32, (256, 128), 1) // 16
        )
        for k, ref in enumerate((own_ref, one_ref, two_ref, three_ref)):
            wk, wv, wo = ref[0:128], ref[128:256], ref[256:384]
            s_kv[k] = jnp.concatenate([wk, wv], axis=1)
            s_kvT[k] = jnp.concatenate([wk.T, wv.T], axis=0)
            s_out[k] = wo
            s_outT[k] = wo.T
            queries = ref[384:416].astype(F32) * SCALE
            tiled = jnp.where(head_mask, jnp.concatenate([queries] * HEADS, axis=0), 0.0)
            s_qb[k] = tiled.T.astype(BF)
        mats = mats_ref[...].astype(BF)
        t_qkv[...] = mats[:, :384]
        t_qkvT[0:128] = (mats[:, 0:128].astype(F32) * SCALE).astype(BF).T
        t_qkvT[128:256] = mats[:, 128:256].T
        t_qkvT[256:384] = mats[:, 256:384].T
        t_o[...] = mats[:, 384:512]
        t_oT[...] = mats[:, 384:512].T
        t_in[...] = mats[:, 512:]
        down = down_ref[...].astype(BF)
        t_dn[...] = down
        for c in range(4):
            t_inT[128 * c : 128 * c + 128] = mats[:, 512 + 128 * c : 640 + 128 * c].T
            t_dnT[:, 128 * c : 128 * c + 128] = down[128 * c : 128 * c + 128].T
            bias_in[128 * c : 128 * c + 128] = jnp.broadcast_to(
                vec_ref[5 + c : 6 + c], (128, 128)
            ).T
        for c in range(5):
            vecs[c] = jnp.broadcast_to(vec_ref[c : c + 1], (128, 128)).T
        for ref in (a_qkv, a_o, a_in, a_dn, a_bin, a_vec, a_kv, a_out, a_q):
            ref[...] = jnp.zeros_like(ref)

    lane_block = lax.broadcasted_iota(jnp.int32, (1, 128), 1) // 32
    rels = [rel_ref[step * group + b] for b in range(group)]

    kept = []
    token_list = []
    for b in range(group):
        e = rels[b]
        rows = rows_ref[b]
        rows_T = rows.T
        kv = mm(rows, s_kv[e]).astype(BF)
        kv_T = mm(s_kvT[e], rows_T).astype(BF)
        query_block = s_qb[e]
        scores = mm(kv[:, :128], query_block)
        probs = softmax_rows(scores.reshape(STEPS, 64, 256), 1)
        probs_low = probs.astype(BF).reshape(256, 256)
        value_T = kv_T[128:]
        mixed = [jnp.zeros((16, 128), F32)] * HEADS
        half = (lax.broadcasted_iota(jnp.int32, (1, 128), 1) < 64).astype(BF)
        for t in range(2):
            both = value_T[:, 128 * t : 128 * t + 128]
            left = both * half
            made = mm(
                jnp.concatenate([left, both - left], axis=0), probs_low[128 * t : 128 * t + 128]
            )
            for u in range(2):
                s = 2 * t + u
                for h in range(HEADS):
                    c = h % 4
                    piece = made[
                        128 * u + 16 * h : 128 * u + 16 * h + 16,
                        128 * (h // 4) : 128 * (h // 4) + 128,
                    ]
                    turn = (s - c) % 4
                    if turn:
                        piece = pltpu.roll(piece, 32 * turn, 1)
                    mixed[h] = jnp.where(lane_block == s, piece, mixed[h])
        mixed_T = jnp.concatenate(mixed, axis=0).astype(BF)
        token_list.append(mm(s_outT[e], mixed_T).astype(BF))
        kept.append((rows_T, kv, kv_T, query_block, probs, probs_low, mixed_T))

    def wide(index):
        return jnp.concatenate([vecs[index]] * group, axis=1)

    residual = jnp.concatenate(token_list, axis=1).astype(F32)
    gain_one, gain_two = wide(0), wide(2)
    normed, unit_one, inverse_one = norm_ahead(residual, gain_one, wide(1))
    normed = normed.astype(BF)
    projected = mm(t_qkvT[...], normed).astype(BF)
    mixed_list, trunk_kept = [], []
    for b in range(group):
        lanes = slice(128 * b, 128 * b + 128)
        normed_tok = normed[:, lanes].T
        key_value = mm(normed_tok, t_qkv[:, 128:]).astype(BF)
        keys, values = key_value[:, :128], key_value[:, 128:]
        query_T = projected[:128, lanes]
        key_T = projected[128:256, lanes]
        value_T = projected[256:, lanes]
        base = (step * group + b) * STEPS
        marks = [seg_ref[base + s] for s in range(STEPS)]
        lane_marks = jnp.where(
            lane_block == 0,
            marks[0],
            jnp.where(
                lane_block == 1, marks[1], jnp.where(lane_block == 2, marks[2], marks[3])
            ),
        )
        lane_marks = jnp.concatenate([lane_marks] * 2, axis=1)
        hide = jnp.stack([jnp.where(lane_marks == marks[s], 0.0, HIDDEN_SCORE) for s in range(STEPS)])
        probs_list, made_list = [], []
        for j in range(PAIRS):
            scores = mm(keys, head_pair(query_T, j))
            scores = (scores.reshape(STEPS, 32, 256) + hide).reshape(128, 256)
            probs = softmax_rows(scores, 0)
            probs_low = probs.astype(BF)
            made_list.append(pair_pick(mm(value_T[32 * j : 32 * j + 32], probs_low)))
            probs_list.append((probs, probs_low))
        mixed_list.append(jnp.concatenate(made_list, axis=0).astype(BF))
        trunk_kept.append((query_T, key_T, values, probs_list))
    mixed = jnp.concatenate(mixed_list, axis=1)
    hidden = residual + mm(t_oT[...], mixed)
    normed_two, unit_two, inverse_two = norm_ahead(hidden, gain_two, wide(3))
    normed_two = normed_two.astype(BF)
    cot = jnp.concatenate([cot_ref[b].T for b in range(group)], axis=1)
    output = hidden + wide(4)
    grad_normed = jnp.zeros((128, 128 * group), F32)
    inner_const = math.sqrt(2.0 / math.pi)
    for c in range(4):
        part = slice(128 * c, 128 * c + 128)
        bias = jnp.concatenate([bias_in[part]] * group, axis=1)
        inner = mm(t_inT[part], normed_two) + bias
        square = inner * inner
        bend = jnp.tanh(inner * (inner_const + (inner_const * 0.044715) * square))
        rise = 0.5 + 0.5 * bend
        active = (inner * rise).astype(BF)
        slope = rise + (0.5 * inner) * (1.0 - bend * bend) * (
            inner_const + (3.0 * inner_const * 0.044715) * square
        )
        output = output + mm(t_dnT[:, part], active)
        a_dn[:, part] += mm_nt(cot, active)
        grad_inner = mm(t_dn[part], cot) * slope
        a_bin[part] += fold_lanes(grad_inner, group)
        grad_inner = grad_inner.astype(BF)
        a_in[:, part] += mm_nt(normed_two, grad_inner)
        grad_normed = grad_normed + mm(t_in[:, part], grad_inner)
    output = output.astype(BF)
    for b in range(group):
        out_ref[b] = output[:, 128 * b : 128 * b + 128].T
    output = output.astype(F32)
    a_vec[5] += fold_lanes(output, group)
    a_vec[6] += fold_lanes(output * output, group)

    grad_out = cot.astype(F32)
    a_vec[4] += fold_lanes(grad_out, group)
    a_vec[2] += fold_lanes(grad_normed * unit_two, group)
    a_vec[3] += fold_lanes(grad_normed, group)
    grad_hidden = grad_out + norm_back(grad_normed, gain_two, unit_two, inverse_two)
    grad_branch = grad_hidden.astype(BF)
    a_o[...] += mm_nt(mixed, grad_branch)
    grad_mixed = mm(t_o[...], grad_branch).astype(BF)
    grad_list = []
    for b in range(group):
        query_T, key_T, values, probs_list = trunk_kept[b]
        grad_T = grad_mixed[:, 128 * b : 128 * b + 128]
        grad_queries, grad_keys, grad_values = [], [], []
        for j in range(PAIRS):
            probs, probs_low = probs_list[j]
            grad_probs = mm(values, head_pair(grad_T, j))
            grad_scores = scores_back(probs, grad_probs, 0)
            grad_queries.append(pair_pick(mm(key_T[32 * j : 32 * j + 32], grad_scores)))
            grad_keys.append(mm_nt(pair_rows(query_T, j), grad_scores))
            grad_values.append(mm_nt(pair_rows(grad_T, j), probs_low))
        grad_queries = jnp.concatenate(grad_queries, axis=0) * SCALE
        grad_list.append(
            jnp.concatenate([grad_queries] + grad_keys + grad_values, axis=0).astype(BF)
        )
    grad_projected = jnp.concatenate(grad_list, axis=1)
    a_qkv[...] += mm_nt(normed, grad_projected)
    grad_normed = mm(t_qkv[...], grad_projected)
    a_vec[0] += fold_lanes(grad_normed * unit_one, group)
    a_vec[1] += fold_lanes(grad_normed, group)
    grad_tokens = (grad_hidden + norm_back(grad_normed, gain_one, unit_one, inverse_one)).astype(BF)

    for b in range(group):
        e = rels[b]
        rows_T, kv, kv_T, query_block, probs, probs_low, mixed_T = kept[b]
        grad_T = grad_tokens[:, 128 * b : 128 * b + 128]
        a_out[e] += mm_nt(mixed_T, grad_T)
        grad_mixed = mm(s_out[e], grad_T)
        turned = [grad_mixed.astype(BF)] + [
            pltpu.roll(grad_mixed, 32 * k, 1).astype(BF) for k in range(1, 4)
        ]
        masks = [(lane_block == c).astype(BF) for c in range(4)]
        zero = jnp.zeros((16, 128), BF)
        grad_values, grad_scores = [], []
        for s in range(STEPS):
            pieces = []
            for h in range(HEADS):
                c = h % 4
                piece = turned[(c - s) % 4][16 * h : 16 * h + 16] * masks[c]
                pieces.append(
                    jnp.concatenate([piece, zero] if h < 4 else [zero, piece], axis=1)
                )
            spread = jnp.concatenate(pieces, axis=0)
            here = slice(64 * s, 64 * s + 64)
            grad_probs = mm(kv[here, 128:], spread)
            grad_scores.append(scores_back(probs[s], grad_probs, 0))
            grad_values.append(mm_nt(probs_low[here], spread))
        grad_scores = jnp.concatenate(grad_scores, axis=0)
        grad_values = jnp.concatenate(grad_values, axis=0).astype(BF)
        grad_keys = mm_nt(grad_scores, query_block).astype(BF)
        a_q[e] += mm(kv_T[:128], grad_scores)
        grad_kv = jnp.concatenate([grad_keys, grad_values], axis=1)
        a_kv[e] += mm(rows_T, grad_kv)
        rgrad_ref[b] = mm_nt(grad_kv, s_kv[e]).astype(BF)

    @pl.when(step == pl.num_programs(0) - 1)
    def _():
        me = pos_ref[0]
        count = send_ref.shape[0]
        blocks = [a_qkv[:, 128 * c : 128 * c + 128] for c in range(3)]
        blocks.append(a_o[...])
        blocks += [a_in[:, 128 * c : 128 * c + 128] for c in range(4)]
        blocks += [a_dn[:, 128 * c : 128 * c + 128].T for c in range(4)]
        per = len(blocks) // count
        for j in range(count):
            place = lax.rem(j - me + count, count)
            for i in range(per):
                send_ref[place, 128 * i : 128 * i + 128] = blocks[per * j + i].astype(BF)
        head_mask = (
            lax.broadcasted_iota(jnp.int32, (256, 128), 0) // 32
            == lax.broadcasted_iota(jnp.int32, (256, 128), 1) // 16
        )
        sums = [jnp.sum(a_vec[c].T, axis=0, keepdims=True) for c in range(5)]
        sums += [
            jnp.sum(a_bin[128 * c : 128 * c + 128].T, axis=0, keepdims=True) for c in range(4)
        ]
        sums += [jnp.sum(a_vec[c].T, axis=0, keepdims=True) for c in (5, 6)]
        sums.append(jnp.zeros((5, 128), F32))
        sums = jnp.concatenate(sums, axis=0)
        high = sums.astype(BF)
        low = (sums - high.astype(F32)).astype(BF)
        vsend_ref[...] = sums
        for k in range(count):
            send_ref[k, 384:512] = a_kv[k, :, :128].astype(BF)
            send_ref[k, 512:640] = a_kv[k, :, 128:].astype(BF)
            send_ref[k, 640:768] = a_out[k].astype(BF)
            spread = jnp.where(head_mask, a_q[k].T, 0.0)
            query = spread[0:32]
            for h in range(1, HEADS):
                query = query + spread[32 * h : 32 * h + 32]
            send_ref[k, 768:800] = (query * SCALE).astype(BF)
            send_ref[k, 800:816] = high
            send_ref[k, 816:832] = low


def split_sum(sums):
    high = sums.astype(BF)
    return high, (sums - high.astype(F32)).astype(BF)


def owner_kernel(shards, pos_ref, *refs):
    out_ref, scratch = refs[-2], refs[-1]
    total = refs[0][0].astype(F32)
    for ref in refs[1:-2]:
        total = total + ref[...].astype(F32)
    scratch[...] = total
    rows = SEND_ROWS // shards
    sums = scratch[800:816] + scratch[816:832]
    high, low = split_sum(sums)
    me = pos_ref[1]
    for j in range(shards):
        place = lax.rem(j - me + shards, shards)
        out_ref[place, 32 : 32 + rows] = scratch[rows * j : rows * j + rows].astype(BF)
        out_ref[place, 0:16] = high
        out_ref[place, 16:32] = low


def shard_kernel(*refs):
    own_ref, vec_ref = refs[-2:]
    total = refs[0][0].astype(F32)
    for ref in refs[1:-2]:
        total = total + ref[...].astype(F32)
    own_ref[...] = total[32:].astype(BF)
    vec_ref[...] = total[0:16] + total[16:32]


def place_kernel(pos_ref, *refs):
    out_ref = refs[-1]
    shards = len(refs) - 1
    me = pos_ref[1]
    for k, ref in enumerate(refs[:-1]):
        out_ref[lax.rem(me - k + shards, shards)] = ref[...]


def renew(weight, moment, average, gradient, step_rate):
    new_moment = MOMENTUM_DECAY * moment + gradient
    new_weight = weight - step_rate * (gradient + MOMENTUM_DECAY * new_moment)
    new_average = average + (new_weight - average) / (STEP + 1)
    return (new_moment, new_average, new_weight)


def renew_kernel(token_total, pos_ref, *refs):
    trunk_refs, stem_ref, sums_ref = refs[0:4], refs[4], refs[5]
    groups = [refs[6 + 3 * i : 9 + 3 * i] for i in range(5)]
    outs = refs[21:41]
    pieces = refs[41]
    mats_o, down_o, vec_o, stem_o, quer_o = outs[0:4], outs[4:8], outs[8:11], outs[11:15], outs[15:19]
    stats_o = outs[19]
    rate = BASE_RATE / math.sqrt(token_total)
    me = pos_ref[0]
    count = len(trunk_refs)
    for k, ref in enumerate(trunk_refs):
        pieces[lax.rem(me - k + count, count)] = ref[...].astype(F32)

    def block(i):
        return pieces[i // 3, 128 * (i % 3) : 128 * (i % 3) + 128]

    def put(out, where, made):
        out[0][where], out[1][where], out[2][where] = made
        if len(out) > 3:
            out[3][where] = made[2].astype(BF)

    def take(ins, where):
        return [ref[where] for ref in ins]

    for i in range(8):
        where = (slice(None), slice(128 * i, 128 * i + 128))
        put(mats_o, where, renew(*take(groups[0], where), block(i), rate))
    for i in range(4):
        where = (slice(128 * i, 128 * i + 128), slice(None))
        put(down_o, where, renew(*take(groups[1], where), block(8 + i), rate))
    where = (slice(None), slice(None))
    put(vec_o, where, renew(*take(groups[2], where), sums_ref[0:9], rate))
    for i in range(3):
        where = (slice(None), slice(128 * i, 128 * i + 128))
        grad = stem_ref[128 * i : 128 * i + 128].astype(F32)
        put(stem_o, where, renew(*take(groups[3], where), grad, rate))
    where = (slice(None), slice(None))
    put(quer_o, where, renew(*take(groups[4], where), stem_ref[384:416].astype(F32), rate))
    mean = sums_ref[9:10] / token_total
    stats_o[0:1] = mean
    stats_o[1:2] = sums_ref[10:11] / token_total - mean * mean


def vmem_call(kernel, outs, scratch=(), scalars=1):
    in_vmem = pl.BlockSpec(memory_space=pltpu.VMEM)

    def call(*args):
        return pl.pallas_call(
            kernel,
            out_shape=outs,
            in_specs=[pl.BlockSpec(memory_space=pltpu.SMEM)] * scalars
            + [in_vmem] * (len(args) - scalars),
            out_specs=jax.tree.map(lambda _: in_vmem, outs),
            scratch_shapes=list(scratch),
            compiler_params=pltpu.CompilerParams(vmem_limit_bytes=VMEM_LIMIT),
        )(*args)

    return call


def local(
    stem_rows,
    emb_ids,
    segments,
    cotangent,
    trunk_mats,
    mats_momentum,
    mats_average,
    trunk_down,
    down_momentum,
    down_average,
    trunk_vectors,
    vectors_momentum,
    vectors_average,
    stem_mats,
    stem_momentum,
    stem_average,
    stem_queries,
    queries_momentum,
    queries_average,
):
    seqs = stem_rows.shape[0]
    emb_count, dp_count = lax.axis_size("emb"), lax.axis_size("dp")
    emb_me, dp_me = lax.axis_index("emb"), lax.axis_index("dp")
    pos = jnp.stack([emb_me, dp_me]).astype(jnp.int32)
    rel = lax.rem(emb_ids[:, 0] - emb_me + emb_count, emb_count)
    token_total = seqs * TOK_SEQ * dp_count * emb_count

    def shift(value, axis, count, by):
        return lax.ppermute(value, axis, [(i, (i + by) % count) for i in range(count)])

    low = stem_mats[0].astype(BF)
    own = jnp.concatenate(
        [low[:, :D], low[:, D : 2 * D], low[:, 2 * D :], stem_queries[0].astype(BF)], axis=0
    )
    stems = [own] + [shift(own, "emb", emb_count, -k) for k in range(1, emb_count)]

    group = 2
    grid = seqs // group

    def whole(shape):
        return pl.BlockSpec(shape, lambda i, *_: (0,) * len(shape))

    scratch = [
        ((4, 128, 256), BF),
        ((4, 256, 128), BF),
        ((4, 128, 128), BF),
        ((4, 128, 128), BF),
        ((4, 128, 256), BF),
        ((384, 128), BF),
        ((128, 384), BF),
        ((128, 128), BF),
        ((128, 128), BF),
        ((128, 512), BF),
        ((512, 128), BF),
        ((512, 128), BF),
        ((128, 512), BF),
        ((512, 128), F32),
        ((5, 128, 128), F32),
        ((128, 384), F32),
        ((128, 128), F32),
        ((128, 512), F32),
        ((128, 512), F32),
        ((512, 128), F32),
        ((7, 128, 128), F32),
        ((4, 128, 256), F32),
        ((4, 128, 128), F32),
        ((4, 128, 256), F32),
    ]
    output, rows_grad, send, _ = pl.pallas_call(
        functools.partial(main_kernel, group),
        out_shape=(
            jax.ShapeDtypeStruct((seqs, TOK_SEQ, D), BF),
            jax.ShapeDtypeStruct((seqs, ROWS_SEQ, D), BF),
            jax.ShapeDtypeStruct((emb_count, SEND_ROWS, D), BF),
            jax.ShapeDtypeStruct((16, D), F32),
        ),
        grid_spec=pltpu.PrefetchScalarGridSpec(
            num_scalar_prefetch=3,
            grid=(grid,),
            in_specs=[
                pl.BlockSpec((group, ROWS_SEQ, D), lambda i, *_: (i, 0, 0)),
                pl.BlockSpec((group, TOK_SEQ, D), lambda i, *_: (i, 0, 0)),
            ]
            + [whole((STEM_ROWS, D))] * 4
            + [whole((D, 1024)), whole((FF, D)), whole((9, D))],
            out_specs=(
                pl.BlockSpec((group, TOK_SEQ, D), lambda i, *_: (i, 0, 0)),
                pl.BlockSpec((group, ROWS_SEQ, D), lambda i, *_: (i, 0, 0)),
                whole((emb_count, SEND_ROWS, D)),
                whole((16, D)),
            ),
            scratch_shapes=[pltpu.VMEM(shape, dtype) for shape, dtype in scratch],
        ),
        compiler_params=pltpu.CompilerParams(
            vmem_limit_bytes=VMEM_LIMIT, dimension_semantics=("arbitrary",)
        ),
    )(
        rel,
        segments.reshape(-1),
        pos,
        stem_rows.reshape(seqs, ROWS_SEQ, D),
        cotangent,
        *stems,
        trunk_mats,
        trunk_down,
        trunk_vectors,
    )

    shard_rows = SEND_ROWS // dp_count
    arrived = [shift(send[k], "emb", emb_count, k) for k in range(1, emb_count)]
    first = pl.BlockSpec((1, SEND_ROWS, D), lambda i: (0, 0, 0))
    in_vmem = pl.BlockSpec(memory_space=pltpu.VMEM)
    shards = pl.pallas_call(
        functools.partial(owner_kernel, dp_count),
        grid=(1,),
        out_shape=jax.ShapeDtypeStruct((dp_count, 32 + shard_rows, D), BF),
        in_specs=[pl.BlockSpec(memory_space=pltpu.SMEM), first] + [in_vmem] * len(arrived),
        out_specs=in_vmem,
        scratch_shapes=[pltpu.VMEM((SEND_ROWS, D), F32)],
        compiler_params=pltpu.CompilerParams(vmem_limit_bytes=VMEM_LIMIT),
    )(pos, send, *arrived)
    arrived = [shift(shards[k], "dp", dp_count, k) for k in range(1, dp_count)]
    first = pl.BlockSpec((1, 32 + shard_rows, D), lambda i: (0, 0, 0))
    shard, sums = pl.pallas_call(
        shard_kernel,
        grid=(1,),
        out_shape=(
            jax.ShapeDtypeStruct((shard_rows, D), BF),
            jax.ShapeDtypeStruct((16, D), F32),
        ),
        in_specs=[first] + [in_vmem] * len(arrived),
        out_specs=(in_vmem, in_vmem),
        compiler_params=pltpu.CompilerParams(vmem_limit_bytes=VMEM_LIMIT),
    )(shards, *arrived)
    all_shards = [shard] + [shift(shard, "dp", dp_count, k) for k in range(1, dp_count)]
    placed = vmem_call(
        place_kernel, jax.ShapeDtypeStruct((dp_count, shard_rows, D), BF)
    )(pos, *all_shards).reshape(SEND_ROWS, D)
    trunk = placed[:TRUNK_ROWS]
    trunks = [trunk] + [shift(trunk, "emb", emb_count, k) for k in range(1, emb_count)]
    stem = placed[TRUNK_ROWS : TRUNK_ROWS + STEM_ROWS]

    def like(array, copy):
        made = [jax.ShapeDtypeStruct(array.shape, F32)] * 3
        return made + ([jax.ShapeDtypeStruct(array.shape, BF)] if copy else [])

    outs = (
        like(trunk_mats, True)
        + like(trunk_down, True)
        + like(trunk_vectors, False)
        + like(stem_mats[0], True)
        + like(stem_queries[0], True)
        + [jax.ShapeDtypeStruct((2, D), F32)]
    )
    made = vmem_call(
        functools.partial(renew_kernel, token_total),
        outs,
        [pltpu.VMEM((emb_count, TRUNK_ROWS, D), F32)],
    )(
        pos,
        *trunks,
        stem,
        sums,
        trunk_mats,
        mats_momentum,
        mats_average,
        trunk_down,
        down_momentum,
        down_average,
        trunk_vectors,
        vectors_momentum,
        vectors_average,
        stem_mats[0],
        stem_momentum[0],
        stem_average[0],
        stem_queries[0],
        queries_momentum[0],
        queries_average[0],
    )
    made = list(made[:11]) + [part[None] for part in made[11:19]] + [made[19]]
    return (output, rows_grad.reshape(stem_rows.shape), *made)


def solution(mesh):
    split = P(("dp", "emb"))
    stem = P("emb")
    in_specs = (split,) * 4 + (P(),) * 9 + (stem,) * 6
    out_specs = (split,) * 2 + (P(),) * 11 + (stem,) * 8 + (P(),)
    return jax.shard_map(local, mesh=mesh, in_specs=in_specs, out_specs=out_specs, check_vma=False)
```

time: 757 us -> 220 us (0.29)
  matrix products: 223 us -> 0 us
  waiting for transfers between devices: 195 us -> 24.7 us
  Pallas kernels: 0 us -> 151 us
  other arithmetic: 124 us -> 3.49 us
  local copies, waits for them, and re-layouts: 95.4 us -> 9.8 us
  blocking collectives: 80.5 us -> 0 us
  between operations: 16.5 us -> 0.87 us
  starting transfers between devices: 17.5 us -> 29.5 us
    dot_general x33 -> x0, matrix products: 212 us -> none  [the longest x1 30.8 us: stem_back(): jnp.einsum('bsqhc,bsrhc->bshqr', grad_heads, value_heads, preferred_eleme...]
    pallas_call x0 -> x5, Pallas kernels: none -> 151 us  [the longest x1 142 us: local(): pl.pallas_call(functools.partial(main_kernel, group), out_shape=(jax.Shap...]
    psum x2 -> x0, waiting for transfers between devices: 123 us -> none  [the longest x1 75.2 us: local(): lax.psum((grad_mats, grad_down, grad_vectors, feature_sums), ('dp', 'emb'))]
    psum x2 -> x0, blocking collectives: 80.5 us -> none  [the longest x1 59.9 us: local(): lax.psum((grad_mats, grad_down, grad_vectors, feature_sums), ('dp', 'emb'))]
    all_to_all x4 -> x0, waiting for transfers between devices: 72 us -> none  [the longest x1 48.7 us: local(): lax.all_to_all(outgoing.reshape(emb_count, -1, D), 'emb', split_axis=0, c...]
    convert_element_type x12 -> x2, other arithmetic: 68.5 us -> 1.66 us  [the longest x1 0.94 us: local(): low = stem_mats[0].astype(BF)]
    reshape x10 -> x1, local copies, waits for them, and re-layouts: 50.3 us -> 0.62 us  [local(): segments.reshape(-1)]
    sub x1 -> x0, other arithmetic: 37.1 us -> none  [stem_ahead(): attend = jax.nn.softmax(scores, axis=-1)]
  transfers between devices with their start and end apart: 6 -> 23, of which waited for: 4 -> 11; matrix products, arithmetic and copies ran while one was open for 6% -> 2% of each run, Pallas kernels for 0% -> 0%
where the time goes in v1:
time: 220 us
  Pallas kernels  151 us (69%)
  starting transfers between devices  29.5 us (13%)
  waiting for transfers between devices  24.7 us (11%)
  local copies, waits for them, and re-layouts  9.8 us (4%)
  other arithmetic  3.49 us (2%)
    pallas_call x1, Pallas kernels, local(): pl.pallas_call(functools.partial(main_kernel, group), out_shape=(jax.Shap...  142 us
    ppermute x23, starting transfers between devices, shift(): lax.ppermute(value, axis, [(i, (i + by) % count) for i in range(count)])  29.5 us
    ppermute x23, waiting for transfers between devices, shift(): lax.ppermute(value, axis, [(i, (i + by) % count) for i in range(count)])  24.7 us
    pallas_call x2, Pallas kernels, call(): pl.pallas_call(kernel, out_shape=outs, in_specs=[pl.BlockSpec(memory_spac...  5.65 us
    unnamed x51, local copies, waits for them, and re-layouts  4.66 us
  transfers between devices with their start and end apart: 23, of which 11 were waited for; matrix products, arithmetic and copies ran while one was open for 2% of the time, Pallas kernels for 0%

profile of v1, /device:TPU:0, one launch (start us, length us, event | category | flops | bytes accessed | tf_op | source)
XLA Modules:
  0.0 219.8 jit_solution(8264100000709763066)
XLA Ops:
  0.7 0.7 bitcast_convert_fusion
  1.4 0.9 bitcast_convert_fusion.1
  2.4 0.0 copy-start
  2.4 0.5 collective-permute-start.2
  2.9 2.6 %collective-permute-start.1 = (bf16[416,128]{1,0:T(8,128)(2,1)S(1)}, bf16[416,128]{1,0:T(8,128)(2,1)S(1)}, u32[]{:S(2)}, u32[]{:S(2)}) collective-permute-start(bf16[416,128]{1,0:T(8,128)(2,1)S(1)} %pad_maximum_fusion.own_ref), channel_id=1, source_target_pairs={{0,2},{1,3},{2,0},{3,1},{4,6},{5,7},{6,4},{7,5},{8,10},{9,11},{10,... | collective-permute-start | bytes 319496 | tf_op jit(solution)/shard_map/ppermute | solution.py:536
  5.5 1.4 collective-permute-start
  6.9 0.8 copy.42
  7.6 0.6 reshape.60.seg_ref
  8.2 1.2 compare_select_fusion.rel_ref
  9.4 0.6 pad_add_fusion.pos_ref
  10.1 0.0 collective-permute-done.1.two_ref
  10.1 0.0 copy-start.6
  10.1 0.4 collective-permute-done.one_ref
  10.5 0.2 copy-done.5
  10.7 0.0 copy-done.6
  10.8 0.4 copy-done.7
  11.1 142.2 %shard_map.354 = (bf16[32,128,128]{2,1,0:T(8,128)(2,1)}, bf16[32,256,128]{2,1,0:T(8,128)(2,1)}, bf16[4,832,128]{2,1,0:T(8,128)(2,1)}, f32[16,128]{1,0:T(8,128)}) custom-call(s32[32]{0:T(128)} %compare_select_fusion.rel_ref, s32[128]{0:T(128)} %reshape.60.seg_ref, s32[2]{0:T(128)} %pad_add_fusion.pos_ref, bf16[32,256,128]{2,1,0:T(8,128)(2,1)} %bitcast.43, ...), custom_call_target="tpu_custom_call" | custom-call | tf_op jit(solution)/shard_map/pallas_call | solution.py:576
  153.3 1.2 slice_bitcast_fusion
  154.5 2.0 collective-permute-start.5
  156.5 0.0 collective-permute-start.4
  156.5 0.2 collective-permute-start.3
  156.7 5.4 %collective-permute-done.5.refs_3_ = bf16[832,128]{1,0:T(8,128)(2,1)S(1)} collective-permute-done((bf16[832,128]{1,0:T(8,128)(2,1)S(1)}, bf16[832,128]{1,0:T(8,128)(2,1)S(1)}, u32[]{:S(2)}, u32[]{:S(2)}) %collective-permute-start.5) | collective-permute-done | bytes 213024 | tf_op jit(solution)/shard_map/ppermute | solution.py:536
  162.1 4.8 %collective-permute-done.4.refs_2_ = bf16[832,128]{1,0:T(8,128)(2,1)S(1)} collective-permute-done((bf16[832,128]{1,0:T(8,128)(2,1)S(1)}, bf16[832,128]{1,0:T(8,128)(2,1)S(1)}, u32[]{:S(2)}, u32[]{:S(2)}) %collective-permute-start.4) | collective-permute-done | bytes 213024 | tf_op jit(solution)/shard_map/ppermute | solution.py:536
  166.8 0.1 collective-permute-done.3.refs_1_
  166.9 0.6 copy-done.3
  167.5 0.7 copy-done.4
  168.2 2.1 shard_map.355.refs_0_
  170.3 0.9 slice_bitcast_fusion.3
  171.1 4.9 %collective-permute-start.12 = (bf16[136,128]{1,0:T(8,128)(2,1)S(1)}, bf16[136,128]{1,0:T(8,128)(2,1)S(1)}, u32[]{:S(2)}, u32[]{:S(2)}) collective-permute-start(bf16[136,128]{1,0:T(8,128)(2,1)S(1)} %get-tuple-element.75), channel_id=1, source_target_pairs={{0,28},{4,0},{8,4},{12,8},{16,12},{20,16},{24,20},{28,24},{1,29},{... | collective-permute-start | bytes 104456 | tf_op jit(solution)/shard_map/ppermute | solution.py:536
  176.1 0.4 collective-permute-start.11
  176.5 3.0 %collective-permute-start.9 = (bf16[136,128]{1,0:T(8,128)(2,1)S(1)}, bf16[136,128]{1,0:T(8,128)(2,1)S(1)}, u32[]{:S(2)}, u32[]{:S(2)}) collective-permute-start(bf16[136,128]{1,0:T(8,128)(2,1)S(1)} %get-tuple-element.78), channel_id=1, source_target_pairs={{0,16},{4,20},{8,24},{12,28},{16,0},{20,4},{24,8},{28,12},{1,17},{... | collective-permute-start | bytes 104456 | tf_op jit(solution)/shard_map/ppermute | solution.py:536
  179.5 0.0 collective-permute-start.8
  179.5 1.8 collective-permute-start.7
  181.4 1.1 collective-permute-start.6
  182.5 0.0 copy-start.14
  182.5 2.7 %collective-permute-done.8.refs_3_ = bf16[136,128]{1,0:T(8,128)(2,1)S(1)} collective-permute-done((bf16[136,128]{1,0:T(8,128)(2,1)S(1)}, bf16[136,128]{1,0:T(8,128)(2,1)S(1)}, u32[]{:S(2)}, u32[]{:S(2)}) %collective-permute-start.8) | collective-permute-done | bytes 34848 | tf_op jit(solution)/shard_map/ppermute | solution.py:536
  185.3 1.3 collective-permute-done.7.refs_2_
  186.6 1.4 collective-permute-done.6.refs_1_
  188.0 0.0 copy-start.17
  188.1 0.6 copy-done.17
  188.7 1.5 shard_map.356
  190.2 0.3 collective-permute-start.19
  190.5 1.4 collective-permute-start.18
  191.9 1.5 collective-permute-start.17
  193.3 2.4 %collective-permute-start.16 = (bf16[104,128]{1,0:T(8,128)(2,1)}, bf16[104,128]{1,0:T(8,128)(2,1)S(1)}, u32[]{:S(2)}, u32[]{:S(2)}) collective-permute-start(bf16[104,128]{1,0:T(8,128)(2,1)} %get-tuple-element.50.refs_0_), channel_id=1, source_target_pairs={{0,16},{4,20},{8,24},{12,28},{16,0},{20,4},{24,8},{28,12},{1,17},{... | collective-permute-start | bytes 79880 | tf_op jit(solution)/shard_map/ppermute | solution.py:536
  195.8 0.5 collective-permute-start.15
  196.3 1.5 collective-permute-start.14
  197.7 2.0 collective-permute-start.13
  199.8 0.0 copy-start.21
  199.8 1.9 collective-permute-done.15.refs_3_
  201.6 0.5 collective-permute-done.14.refs_2_
  202.1 2.4 %collective-permute-done.13.refs_1_ = bf16[104,128]{1,0:T(8,128)(2,1)S(1)} collective-permute-done((bf16[104,128]{1,0:T(8,128)(2,1)}, bf16[104,128]{1,0:T(8,128)(2,1)S(1)}, u32[]{:S(2)}, u32[]{:S(2)}) %collective-permute-start.13) | collective-permute-done | bytes 26656 | tf_op jit(solution)/shard_map/ppermute | solution.py:536
  204.5 0.0 copy-start.24
  204.6 0.6 copy-done.24
  205.2 1.6 shard_map.357
  206.7 0.9 slice.70.refs_0_
  207.6 0.1 collective-permute-start.22
  207.7 1.7 collective-permute-start.21
  209.4 0.2 collective-permute-start.20
  209.6 1.5 slice.71.refs_4_
  211.1 3.9 %collective-permute-done.21.refs_2_ = bf16[384,128]{1,0:T(8,128)(2,1)S(1)} collective-permute-done((bf16[384,128]{1,0:T(8,128)(2,1)S(1)}, bf16[384,128]{1,0:T(8,128)(2,1)S(1)}, u32[]{:S(2)}, u32[]{:S(2)}) %collective-permute-start.21) | collective-permute-done | bytes 98336 | tf_op jit(solution)/shard_map/ppermute | solution.py:536
  215.0 0.6 copy-done.9
  215.7 0.0 copy-done.10
  215.7 4.1 %shard_map.358 = (f32[128,1024]{1,0:T(8,128)}, f32[128,1024]{1,0:T(8,128)}, f32[128,1024]{1,0:T(8,128)}, bf16[128,1024]{1,0:T(8,128)(2,1)}, f32[512,128]{1,0:T(8...) custom-call(s32[2]{0:T(128)} %pad_add_fusion.pos_ref, ...), custom_call_target="tpu_custom_call" | custom-call | tf_op jit(solution)/shard_map/pallas_call | solution.py:494
  (49 shorter events, 0.1 us)
Async XLA Ops:
  2.4 8.1 %copy-start = (bf16[416,128]{1,0:T(8,128)(2,1)}, bf16[416,128]{1,0:T(8,128)(2,1)S(1)}, u32[]{:S(2)}) copy-start(bf16[416,128]{1,0:T(8,128)(2,1)S(1)} %pad_maximum_fusion.own_ref) | copy-start | bytes 319492
  2.4 7.7 %collective-permute-start.2 = (bf16[416,128]{1,0:T(8,128)(2,1)S(1)}, bf16[416,128]{1,0:T(8,128)(2,1)S(1)}, u32[]{:S(2)}, u32[]{:S(2)}) collective-permute-start(bf16[416,128]{1,0:T(8,128)(2,1)S(1)} %pad_maximum_fusion.own_ref), channel_id=1, source_target_pairs={{0,1},{1,2},{2,3},{3,0},{4,5},{5,6},{6,7},{7,4},{8,9},{9,10},{10,1... | collective-permute-start | bytes 319496 | tf_op jit(solution)/shard_map/ppermute | solution.py:536
  2.9 7.2 %collective-permute-start.1 = (bf16[416,128]{1,0:T(8,128)(2,1)S(1)}, bf16[416,128]{1,0:T(8,128)(2,1)S(1)}, u32[]{:S(2)}, u32[]{:S(2)}) collective-permute-start(bf16[416,128]{1,0:T(8,128)(2,1)S(1)} %pad_maximum_fusion.own_ref), channel_id=1, source_target_pairs={{0,2},{1,3},{2,0},{3,1},{4,6},{5,7},{6,4},{7,5},{8,10},{9,11},{10,... | collective-permute-start | bytes 319496 | tf_op jit(solution)/shard_map/ppermute | solution.py:536
  5.5 5.0 %collective-permute-start = (bf16[416,128]{1,0:T(8,128)(2,1)S(1)}, bf16[416,128]{1,0:T(8,128)(2,1)S(1)}, u32[]{:S(2)}, u32[]{:S(2)}) collective-permute-start(bf16[416,128]{1,0:T(8,128)(2,1)S(1)} %pad_maximum_fusion.own_ref), channel_id=1, source_target_pairs={{0,3},{1,0},{2,1},{3,2},{4,7},{5,4},{6,5},{7,6},{8,11},{9,8},{10,9... | collective-permute-start | bytes 319496 | tf_op jit(solution)/shard_map/ppermute | solution.py:536
  10.1 0.6 copy-start.5
  10.1 0.7 copy-start.6
  10.5 0.6 copy-start.7
  154.5 7.5 %collective-permute-start.5 = (bf16[832,128]{1,0:T(8,128)(2,1)S(1)}, bf16[832,128]{1,0:T(8,128)(2,1)S(1)}, u32[]{:S(2)}, u32[]{:S(2)}) collective-permute-start(bf16[832,128]{1,0:T(8,128)(2,1)S(1)} %get-tuple-element.72), channel_id=1, source_target_pairs={{0,3},{1,0},{2,1},{3,2},{4,7},{5,4},{6,5},{7,6},{8,11},{9,8},{10,9... | collective-permute-start | bytes 638984 | tf_op jit(solution)/shard_map/ppermute | solution.py:536
  156.5 10.3 %collective-permute-start.4 = (bf16[832,128]{1,0:T(8,128)(2,1)S(1)}, bf16[832,128]{1,0:T(8,128)(2,1)S(1)}, u32[]{:S(2)}, u32[]{:S(2)}) collective-permute-start(bf16[832,128]{1,0:T(8,128)(2,1)S(1)} %get-tuple-element.73), channel_id=1, source_target_pairs={{0,2},{1,3},{2,0},{3,1},{4,6},{5,7},{6,4},{7,5},{8,10},{9,11},{10,... | collective-permute-start | bytes 638984 | tf_op jit(solution)/shard_map/ppermute | solution.py:536
  156.5 10.4 %collective-permute-start.3 = (bf16[832,128]{1,0:T(8,128)(2,1)S(1)}, bf16[832,128]{1,0:T(8,128)(2,1)S(1)}, u32[]{:S(2)}, u32[]{:S(2)}) collective-permute-start(bf16[832,128]{1,0:T(8,128)(2,1)S(1)} %get-tuple-element.74), channel_id=1, source_target_pairs={{0,1},{1,2},{2,3},{3,0},{4,5},{5,6},{6,7},{7,4},{8,9},{9,10},{10,1... | collective-permute-start | bytes 638984 | tf_op jit(solution)/shard_map/ppermute | solution.py:536
  162.1 4.8 %copy-start.2 = (bf16[832,128]{1,0:T(8,128)(2,1)}, bf16[832,128]{1,0:T(8,128)(2,1)S(1)}, u32[]{:S(2)}) copy-start(bf16[832,128]{1,0:T(8,128)(2,1)S(1)} %collective-permute-done.5.refs_3_) | copy-start | bytes 638980
  166.8 0.7 copy-start.3
  167.5 0.7 copy-start.4
  171.1 8.4 %collective-permute-start.12 = (bf16[136,128]{1,0:T(8,128)(2,1)S(1)}, bf16[136,128]{1,0:T(8,128)(2,1)S(1)}, u32[]{:S(2)}, u32[]{:S(2)}) collective-permute-start(bf16[136,128]{1,0:T(8,128)(2,1)S(1)} %get-tuple-element.75), channel_id=1, source_target_pairs={{0,28},{4,0},{8,4},{12,8},{16,12},{20,16},{24,20},{28,24},{1,29},{... | collective-permute-start | bytes 104456 | tf_op jit(solution)/shard_map/ppermute | solution.py:536
  176.1 5.3 %collective-permute-start.11 = (bf16[136,128]{1,0:T(8,128)(2,1)S(1)}, bf16[136,128]{1,0:T(8,128)(2,1)S(1)}, u32[]{:S(2)}, u32[]{:S(2)}) collective-permute-start(bf16[136,128]{1,0:T(8,128)(2,1)S(1)} %get-tuple-element.76), channel_id=1, source_target_pairs={{0,24},{4,28},{8,0},{12,4},{16,8},{20,12},{24,16},{28,20},{1,25},{... | collective-permute-start | bytes 104456 | tf_op jit(solution)/shard_map/ppermute | solution.py:536
  176.5 6.0 %collective-permute-start.10 = (bf16[136,128]{1,0:T(8,128)(2,1)S(1)}, bf16[136,128]{1,0:T(8,128)(2,1)S(1)}, u32[]{:S(2)}, u32[]{:S(2)}) collective-permute-start(bf16[136,128]{1,0:T(8,128)(2,1)S(1)} %get-tuple-element.77), channel_id=1, source_target_pairs={{0,20},{4,24},{8,28},{12,0},{16,4},{20,8},{24,12},{28,16},{1,21},{... | collective-permute-start | bytes 104456 | tf_op jit(solution)/shard_map/ppermute | solution.py:536
  176.5 6.0 %collective-permute-start.9 = (bf16[136,128]{1,0:T(8,128)(2,1)S(1)}, bf16[136,128]{1,0:T(8,128)(2,1)S(1)}, u32[]{:S(2)}, u32[]{:S(2)}) collective-permute-start(bf16[136,128]{1,0:T(8,128)(2,1)S(1)} %get-tuple-element.78), channel_id=1, source_target_pairs={{0,16},{4,20},{8,24},{12,28},{16,0},{20,4},{24,8},{28,12},{1,17},{... | collective-permute-start | bytes 104456 | tf_op jit(solution)/shard_map/ppermute | solution.py:536
  179.5 5.7 %collective-permute-start.8 = (bf16[136,128]{1,0:T(8,128)(2,1)S(1)}, bf16[136,128]{1,0:T(8,128)(2,1)S(1)}, u32[]{:S(2)}, u32[]{:S(2)}) collective-permute-start(bf16[136,128]{1,0:T(8,128)(2,1)S(1)} %get-tuple-element.79), channel_id=1, source_target_pairs={{0,12},{4,16},{8,20},{12,24},{16,28},{20,0},{24,4},{28,8},{1,13},{... | collective-permute-start | bytes 104456 | tf_op jit(solution)/shard_map/ppermute | solution.py:536
  179.5 8.5 %copy-start.11 = (bf16[136,128]{1,0:T(8,128)(2,1)}, bf16[136,128]{1,0:T(8,128)(2,1)S(1)}, u32[]{:S(2)}) copy-start(bf16[136,128]{1,0:T(8,128)(2,1)S(1)} %collective-permute-done.12.refs_7_) | copy-start | bytes 104452
  179.5 7.0 %collective-permute-start.7 = (bf16[136,128]{1,0:T(8,128)(2,1)S(1)}, bf16[136,128]{1,0:T(8,128)(2,1)S(1)}, u32[]{:S(2)}, u32[]{:S(2)}) collective-permute-start(bf16[136,128]{1,0:T(8,128)(2,1)S(1)} %get-tuple-element.80), channel_id=1, source_target_pairs={{0,8},{4,12},{8,16},{12,20},{16,24},{20,28},{24,0},{28,4},{1,9},{5... | collective-permute-start | bytes 104456 | tf_op jit(solution)/shard_map/ppermute | solution.py:536
  181.4 6.6 %copy-start.12 = (bf16[136,128]{1,0:T(8,128)(2,1)}, bf16[136,128]{1,0:T(8,128)(2,1)S(1)}, u32[]{:S(2)}) copy-start(bf16[136,128]{1,0:T(8,128)(2,1)S(1)} %collective-permute-done.11.refs_6_) | copy-start | bytes 104452
  181.4 6.6 %collective-permute-start.6 = (bf16[136,128]{1,0:T(8,128)(2,1)S(1)}, bf16[136,128]{1,0:T(8,128)(2,1)S(1)}, u32[]{:S(2)}, u32[]{:S(2)}) collective-permute-start(bf16[136,128]{1,0:T(8,128)(2,1)S(1)} %get-tuple-element.81), channel_id=1, source_target_pairs={{0,4},{4,8},{8,12},{12,16},{16,20},{20,24},{24,28},{28,0},{1,5},{5... | collective-permute-start | bytes 104456 | tf_op jit(solution)/shard_map/ppermute | solution.py:536
  182.5 5.5 %copy-start.13 = (bf16[136,128]{1,0:T(8,128)(2,1)}, bf16[136,128]{1,0:T(8,128)(2,1)S(1)}, u32[]{:S(2)}) copy-start(bf16[136,128]{1,0:T(8,128)(2,1)S(1)} %collective-permute-done.10.refs_5_) | copy-start | bytes 104452
  182.5 5.5 %copy-start.14 = (bf16[136,128]{1,0:T(8,128)(2,1)}, bf16[136,128]{1,0:T(8,128)(2,1)S(1)}, u32[]{:S(2)}) copy-start(bf16[136,128]{1,0:T(8,128)(2,1)S(1)} %collective-permute-done.9.refs_4_) | copy-start | bytes 104452
  185.3 2.8 %copy-start.15 = (bf16[136,128]{1,0:T(8,128)(2,1)}, bf16[136,128]{1,0:T(8,128)(2,1)S(1)}, u32[]{:S(2)}) copy-start(bf16[136,128]{1,0:T(8,128)(2,1)S(1)} %collective-permute-done.8.refs_3_) | copy-start | bytes 104452
  186.6 1.5 copy-start.16
  188.0 0.6 copy-start.17
  190.2 6.1 %collective-permute-start.19 = (bf16[104,128]{1,0:T(8,128)(2,1)}, bf16[104,128]{1,0:T(8,128)(2,1)S(1)}, u32[]{:S(2)}, u32[]{:S(2)}) collective-permute-start(bf16[104,128]{1,0:T(8,128)(2,1)} %get-tuple-element.50.refs_0_), channel_id=1, source_target_pairs={{0,28},{4,0},{8,4},{12,8},{16,12},{20,16},{24,20},{28,24},{1,29},{... | collective-permute-start | bytes 79880 | tf_op jit(solution)/shard_map/ppermute | solution.py:536
  190.5 7.3 %collective-permute-start.18 = (bf16[104,128]{1,0:T(8,128)(2,1)}, bf16[104,128]{1,0:T(8,128)(2,1)S(1)}, u32[]{:S(2)}, u32[]{:S(2)}) collective-permute-start(bf16[104,128]{1,0:T(8,128)(2,1)} %get-tuple-element.50.refs_0_), channel_id=1, source_target_pairs={{0,24},{4,28},{8,0},{12,4},{16,8},{20,12},{24,16},{28,20},{1,25},{... | collective-permute-start | bytes 79880 | tf_op jit(solution)/shard_map/ppermute | solution.py:536
  191.9 7.9 %collective-permute-start.17 = (bf16[104,128]{1,0:T(8,128)(2,1)}, bf16[104,128]{1,0:T(8,128)(2,1)S(1)}, u32[]{:S(2)}, u32[]{:S(2)}) collective-permute-start(bf16[104,128]{1,0:T(8,128)(2,1)} %get-tuple-element.50.refs_0_), channel_id=1, source_target_pairs={{0,20},{4,24},{8,28},{12,0},{16,4},{20,8},{24,12},{28,16},{1,21},{... | collective-permute-start | bytes 79880 | tf_op jit(solution)/shard_map/ppermute | solution.py:536
  193.3 6.4 %collective-permute-start.16 = (bf16[104,128]{1,0:T(8,128)(2,1)}, bf16[104,128]{1,0:T(8,128)(2,1)S(1)}, u32[]{:S(2)}, u32[]{:S(2)}) collective-permute-start(bf16[104,128]{1,0:T(8,128)(2,1)} %get-tuple-element.50.refs_0_), channel_id=1, source_target_pairs={{0,16},{4,20},{8,24},{12,28},{16,0},{20,4},{24,8},{28,12},{1,17},{... | collective-permute-start | bytes 79880 | tf_op jit(solution)/shard_map/ppermute | solution.py:536
  195.8 5.9 %collective-permute-start.15 = (bf16[104,128]{1,0:T(8,128)(2,1)}, bf16[104,128]{1,0:T(8,128)(2,1)S(1)}, u32[]{:S(2)}, u32[]{:S(2)}) collective-permute-start(bf16[104,128]{1,0:T(8,128)(2,1)} %get-tuple-element.50.refs_0_), channel_id=1, source_target_pairs={{0,12},{4,16},{8,20},{12,24},{16,28},{20,0},{24,4},{28,8},{1,13},{... | collective-permute-start | bytes 79880 | tf_op jit(solution)/shard_map/ppermute | solution.py:536
  196.3 8.2 %copy-start.18 = (bf16[104,128]{1,0:T(8,128)(2,1)}, bf16[104,128]{1,0:T(8,128)(2,1)S(1)}, u32[]{:S(2)}) copy-start(bf16[104,128]{1,0:T(8,128)(2,1)S(1)} %collective-permute-done.19.refs_7_) | copy-start | bytes 79876
  196.3 5.9 %collective-permute-start.14 = (bf16[104,128]{1,0:T(8,128)(2,1)}, bf16[104,128]{1,0:T(8,128)(2,1)S(1)}, u32[]{:S(2)}, u32[]{:S(2)}) collective-permute-start(bf16[104,128]{1,0:T(8,128)(2,1)} %get-tuple-element.50.refs_0_), channel_id=1, source_target_pairs={{0,8},{4,12},{8,16},{12,20},{16,24},{20,28},{24,0},{28,4},{1,9},{5... | collective-permute-start | bytes 79880 | tf_op jit(solution)/shard_map/ppermute | solution.py:536
  197.7 6.8 %copy-start.19 = (bf16[104,128]{1,0:T(8,128)(2,1)}, bf16[104,128]{1,0:T(8,128)(2,1)S(1)}, u32[]{:S(2)}) copy-start(bf16[104,128]{1,0:T(8,128)(2,1)S(1)} %collective-permute-done.18.refs_6_) | copy-start | bytes 79876
  197.7 6.8 %collective-permute-start.13 = (bf16[104,128]{1,0:T(8,128)(2,1)}, bf16[104,128]{1,0:T(8,128)(2,1)S(1)}, u32[]{:S(2)}, u32[]{:S(2)}) collective-permute-start(bf16[104,128]{1,0:T(8,128)(2,1)} %get-tuple-element.50.refs_0_), channel_id=1, source_target_pairs={{0,4},{4,8},{8,12},{12,16},{16,20},{20,24},{24,28},{28,0},{1,5},{5... | collective-permute-start | bytes 79880 | tf_op jit(solution)/shard_map/ppermute | solution.py:536
  199.8 4.7 %copy-start.20 = (bf16[104,128]{1,0:T(8,128)(2,1)}, bf16[104,128]{1,0:T(8,128)(2,1)S(1)}, u32[]{:S(2)}) copy-start(bf16[104,128]{1,0:T(8,128)(2,1)S(1)} %collective-permute-done.17.refs_5_) | copy-start | bytes 79876
  199.8 4.7 %copy-start.21 = (bf16[104,128]{1,0:T(8,128)(2,1)}, bf16[104,128]{1,0:T(8,128)(2,1)S(1)}, u32[]{:S(2)}) copy-start(bf16[104,128]{1,0:T(8,128)(2,1)S(1)} %collective-permute-done.16.refs_4_) | copy-start | bytes 79876
  201.6 2.9 %copy-start.22 = (bf16[104,128]{1,0:T(8,128)(2,1)}, bf16[104,128]{1,0:T(8,128)(2,1)S(1)}, u32[]{:S(2)}) copy-start(bf16[104,128]{1,0:T(8,128)(2,1)S(1)} %collective-permute-done.15.refs_3_) | copy-start | bytes 79876
  202.1 2.4 %copy-start.23 = (bf16[104,128]{1,0:T(8,128)(2,1)}, bf16[104,128]{1,0:T(8,128)(2,1)S(1)}, u32[]{:S(2)}) copy-start(bf16[104,128]{1,0:T(8,128)(2,1)S(1)} %collective-permute-done.14.refs_2_) | copy-start | bytes 79876
  204.5 0.6 copy-start.24
  207.6 7.4 %copy-start.1 = (bf16[384,128]{1,0:T(8,128)(2,1)}, bf16[384,128]{1,0:T(8,128)(2,1)S(1)}, u32[]{:S(2)}) copy-start(bf16[384,128]{1,0:T(8,128)(2,1)S(1)} %slice.70.refs_0_) | copy-start | bytes 294916
  207.6 3.5 %collective-permute-start.22 = (bf16[384,128]{1,0:T(8,128)(2,1)S(1)}, bf16[384,128]{1,0:T(8,128)(2,1)S(1)}, u32[]{:S(2)}, u32[]{:S(2)}) collective-permute-start(bf16[384,128]{1,0:T(8,128)(2,1)S(1)} %slice.70.refs_0_), channel_id=1, source_target_pairs={{0,3},{1,0},{2,1},{3,2},{4,7},{5,4},{6,5},{7,6},{8,11},{9,8},{10,9... | collective-permute-start | bytes 294920 | tf_op jit(solution)/shard_map/ppermute | solution.py:536
  207.7 7.3 %collective-permute-start.21 = (bf16[384,128]{1,0:T(8,128)(2,1)S(1)}, bf16[384,128]{1,0:T(8,128)(2,1)S(1)}, u32[]{:S(2)}, u32[]{:S(2)}) collective-permute-start(bf16[384,128]{1,0:T(8,128)(2,1)S(1)} %slice.70.refs_0_), channel_id=1, source_target_pairs={{0,2},{1,3},{2,0},{3,1},{4,6},{5,7},{6,4},{7,5},{8,10},{9,11},{10,... | collective-permute-start | bytes 294920 | tf_op jit(solution)/shard_map/ppermute | solution.py:536
  209.4 5.6 %collective-permute-start.20 = (bf16[384,128]{1,0:T(8,128)(2,1)S(1)}, bf16[384,128]{1,0:T(8,128)(2,1)S(1)}, u32[]{:S(2)}, u32[]{:S(2)}) collective-permute-start(bf16[384,128]{1,0:T(8,128)(2,1)S(1)} %slice.70.refs_0_), channel_id=1, source_target_pairs={{0,1},{1,2},{2,3},{3,0},{4,5},{5,6},{6,7},{7,4},{8,9},{9,10},{10,1... | collective-permute-start | bytes 294920 | tf_op jit(solution)/shard_map/ppermute | solution.py:536
  211.1 3.9 %copy-start.8 = (bf16[384,128]{1,0:T(8,128)(2,1)}, bf16[384,128]{1,0:T(8,128)(2,1)S(1)}, u32[]{:S(2)}) copy-start(bf16[384,128]{1,0:T(8,128)(2,1)S(1)} %collective-permute-done.22.refs_3_) | copy-start | bytes 294916
  215.0 0.6 copy-start.9
  215.0 0.7 copy-start.10

commit v2 on v1

--- a/solution.py
+++ b/solution.py
@@ -24,6 +24,7 @@
 BASE_RATE = 0.1
 HIDDEN_SCORE = -1e30
 SCALE = 1.0 / math.sqrt(HEAD_DIM)
+LOG2E = math.log2(math.e)
 
 TRUNK_ROWS = 384
 STEM_ROWS = 416
@@ -121,7 +122,6 @@
     send_ref,
     vsend_ref,
     s_kv,
-    s_kvT,
     s_out,
     s_outT,
     s_qb,
@@ -139,7 +139,6 @@
     a_o,
     a_in,
     a_dn,
-    a_bin,
     a_vec,
     a_kv,
     a_out,
@@ -156,17 +155,15 @@
         for k, ref in enumerate((own_ref, one_ref, two_ref, three_ref)):
             wk, wv, wo = ref[0:128], ref[128:256], ref[256:384]
             s_kv[k] = jnp.concatenate([wk, wv], axis=1)
-            s_kvT[k] = jnp.concatenate([wk.T, wv.T], axis=0)
             s_out[k] = wo
             s_outT[k] = wo.T
-            queries = ref[384:416].astype(F32) * SCALE
+            queries = ref[384:416].astype(F32) * (SCALE * LOG2E)
             tiled = jnp.where(head_mask, jnp.concatenate([queries] * HEADS, axis=0), 0.0)
             s_qb[k] = tiled.T.astype(BF)
         mats = mats_ref[...].astype(BF)
         t_qkv[...] = mats[:, :384]
-        t_qkvT[0:128] = (mats[:, 0:128].astype(F32) * SCALE).astype(BF).T
-        t_qkvT[128:256] = mats[:, 128:256].T
-        t_qkvT[256:384] = mats[:, 256:384].T
+        for c in range(3):
+            t_qkvT[128 * c : 128 * c + 128] = mats[:, 128 * c : 128 * c + 128].T
         t_o[...] = mats[:, 384:512]
         t_oT[...] = mats[:, 384:512].T
         t_in[...] = mats[:, 512:]
@@ -180,66 +177,78 @@
             ).T
         for c in range(5):
             vecs[c] = jnp.broadcast_to(vec_ref[c : c + 1], (128, 128)).T
-        for ref in (a_qkv, a_o, a_in, a_dn, a_bin, a_vec, a_kv, a_out, a_q):
+        for ref in (a_qkv, a_o, a_in, a_dn, a_vec, a_kv, a_out, a_q):
             ref[...] = jnp.zeros_like(ref)
 
     lane_block = lax.broadcasted_iota(jnp.int32, (1, 128), 1) // 32
     rels = [rel_ref[step * group + b] for b in range(group)]
-
-    kept = []
-    token_list = []
-    for b in range(group):
-        e = rels[b]
-        rows = rows_ref[b]
-        rows_T = rows.T
-        kv = mm(rows, s_kv[e]).astype(BF)
-        kv_T = mm(s_kvT[e], rows_T).astype(BF)
-        query_block = s_qb[e]
-        scores = mm(kv[:, :128], query_block)
-        probs = softmax_rows(scores.reshape(STEPS, 64, 256), 1)
-        probs_low = probs.astype(BF).reshape(256, 256)
-        value_T = kv_T[128:]
-        mixed = [jnp.zeros((16, 128), F32)] * HEADS
-        half = (lax.broadcasted_iota(jnp.int32, (1, 128), 1) < 64).astype(BF)
+    ones = jnp.ones((16, 128), BF)
+
+    every = range(group)
+    kv = [mm(rows_ref[b], s_kv[rels[b]]).astype(BF) for b in every]
+    scores = [
+        [mm(kv[b][64 * s : 64 * s + 64, :128], s_qb[rels[b]]) for s in range(STEPS)] for b in every
+    ]
+    half = (lax.broadcasted_iota(jnp.int32, (1, 128), 1) < 64).astype(BF)
+    value_T = [kv[b][:, 128:].T for b in every]
+    probs, probs_low = [], []
+    for b in every:
+        probs.append([])
+        probs_low.append([])
+        for s in range(STEPS):
+            halves = []
+            for u in range(2):
+                tile = scores[b][s][:, 128 * u : 128 * u + 128]
+                raised = jnp.exp2(tile - jnp.max(tile, axis=0, keepdims=True))
+                halves.append(raised * (1.0 / jnp.sum(raised, axis=0, keepdims=True)))
+            probs[b].append(halves)
+            probs_low[b].append(jnp.concatenate([half.astype(BF) for half in halves], axis=1))
+    made = []
+    for b in every:
+        made.append([])
         for t in range(2):
-            both = value_T[:, 128 * t : 128 * t + 128]
+            both = value_T[b][:, 128 * t : 128 * t + 128]
             left = both * half
-            made = mm(
-                jnp.concatenate([left, both - left], axis=0), probs_low[128 * t : 128 * t + 128]
+            made[b].append(
+                mm(
+                    jnp.concatenate([left, both - left], axis=0),
+                    jnp.concatenate(probs_low[b][2 * t : 2 * t + 2], axis=0),
+                )
             )
-            for u in range(2):
-                s = 2 * t + u
-                for h in range(HEADS):
-                    c = h % 4
-                    piece = made[
-                        128 * u + 16 * h : 128 * u + 16 * h + 16,
-                        128 * (h // 4) : 128 * (h // 4) + 128,
-                    ]
-                    turn = (s - c) % 4
-                    if turn:
-                        piece = pltpu.roll(piece, 32 * turn, 1)
-                    mixed[h] = jnp.where(lane_block == s, piece, mixed[h])
-        mixed_T = jnp.concatenate(mixed, axis=0).astype(BF)
-        token_list.append(mm(s_outT[e], mixed_T).astype(BF))
-        kept.append((rows_T, kv, kv_T, query_block, probs, probs_low, mixed_T))
-
-    def wide(index):
-        return jnp.concatenate([vecs[index]] * group, axis=1)
-
-    residual = jnp.concatenate(token_list, axis=1).astype(F32)
-    gain_one, gain_two = wide(0), wide(2)
-    normed, unit_one, inverse_one = norm_ahead(residual, gain_one, wide(1))
-    normed = normed.astype(BF)
-    projected = mm(t_qkvT[...], normed).astype(BF)
-    mixed_list, trunk_kept = [], []
-    for b in range(group):
-        lanes = slice(128 * b, 128 * b + 128)
-        normed_tok = normed[:, lanes].T
-        key_value = mm(normed_tok, t_qkv[:, 128:]).astype(BF)
-        keys, values = key_value[:, :128], key_value[:, 128:]
-        query_T = projected[:128, lanes]
-        key_T = projected[128:256, lanes]
-        value_T = projected[256:, lanes]
+    stem_mixed = []
+    for b in every:
+        rows = []
+        for h in range(HEADS):
+            c = h % 4
+            row = jnp.zeros((16, 128), F32)
+            for s in range(STEPS):
+                start = 128 * (s % 2) + 16 * h
+                piece = made[b][s // 2][start : start + 16, 128 * (h // 4) : 128 * (h // 4) + 128]
+                turn = (s - c) % 4
+                if turn:
+                    piece = pltpu.roll(piece, 32 * turn, 1)
+                row = jnp.where(lane_block == s, piece, row)
+            rows.append(row)
+        stem_mixed.append(jnp.concatenate(rows, axis=0).astype(BF))
+    tokens = [mm(s_outT[rels[b]], stem_mixed[b]).astype(BF) for b in every]
+
+    residual, normed_list, unit_one, inverse_one = [], [], [], []
+    for b in every:
+        residual.append(tokens[b].astype(F32))
+        ahead, unit, inverse = norm_ahead(residual[b], vecs[0], vecs[1])
+        normed_list.append(ahead.astype(BF))
+        unit_one.append(unit)
+        inverse_one.append(inverse)
+    normed = jnp.concatenate(normed_list, axis=1)
+    projected = mm(t_qkvT[...], normed)
+    lanes = [slice(128 * b, 128 * b + 128) for b in every]
+    query_T = [(projected[:128, lanes[b]] * (LOG2E * SCALE)).astype(BF) for b in every]
+    key_T = [projected[128:256, lanes[b]].astype(BF) for b in every]
+    value_T = [projected[256:, lanes[b]].astype(BF) for b in every]
+    keys = [key_T[b].T for b in every]
+    values = [value_T[b].T for b in every]
+    hide = []
+    for b in every:
         base = (step * group + b) * STEPS
         marks = [seg_ref[base + s] for s in range(STEPS)]
         lane_marks = jnp.where(
@@ -249,94 +258,169 @@
                 lane_block == 1, marks[1], jnp.where(lane_block == 2, marks[2], marks[3])
             ),
         )
-        lane_marks = jnp.concatenate([lane_marks] * 2, axis=1)
-        hide = jnp.stack([jnp.where(lane_marks == marks[s], 0.0, HIDDEN_SCORE) for s in range(STEPS)])
-        probs_list, made_list = [], []
+        hide.append([jnp.where(lane_marks == marks[s], 0.0, HIDDEN_SCORE) for s in range(STEPS)])
+    scores = [[mm(keys[b], head_pair(query_T[b], j)) for j in range(PAIRS)] for b in every]
+    cot_list = [cot_ref[b].T for b in every]
+    raised = []
+    for b in every:
+        raised.append([])
         for j in range(PAIRS):
-            scores = mm(keys, head_pair(query_T, j))
-            scores = (scores.reshape(STEPS, 32, 256) + hide).reshape(128, 256)
-            probs = softmax_rows(scores, 0)
-            probs_low = probs.astype(BF)
-            made_list.append(pair_pick(mm(value_T[32 * j : 32 * j + 32], probs_low)))
-            probs_list.append((probs, probs_low))
-        mixed_list.append(jnp.concatenate(made_list, axis=0).astype(BF))
-        trunk_kept.append((query_T, key_T, values, probs_list))
+            halves = []
+            for u in range(2):
+                tile = scores[b][j][:, 128 * u : 128 * u + 128]
+                tile = jnp.concatenate(
+                    [tile[32 * s : 32 * s + 32] + hide[b][s] for s in range(STEPS)], axis=0
+                )
+                halves.append(
+                    jnp.exp2(tile - jnp.max(tile, axis=0, keepdims=True)).astype(BF)
+                )
+            raised[b].append(jnp.concatenate(halves, axis=1))
+    made = [
+        [
+            mm(jnp.concatenate([value_T[b][32 * j : 32 * j + 32], ones], axis=0), raised[b][j])
+            for j in range(PAIRS)
+        ]
+        for b in every
+    ]
+    head_mixed, head_inverse, mixed_list = [], [], []
+    for b in every:
+        head_mixed.append([])
+        head_inverse.append([])
+        for h in range(HEADS):
+            j, u = divmod(h, 2)
+            here = slice(128 * u, 128 * u + 128)
+            inverse = 1.0 / made[b][j][32:40, here]
+            part = made[b][j][16 * u : 16 * u + 16, here]
+            head_inverse[b].append(inverse)
+            head_mixed[b].append(
+                jnp.concatenate([part[:8] * inverse, part[8:] * inverse], axis=0)
+            )
+        mixed_list.append(jnp.concatenate(head_mixed[b], axis=0).astype(BF))
     mixed = jnp.concatenate(mixed_list, axis=1)
-    hidden = residual + mm(t_oT[...], mixed)
-    normed_two, unit_two, inverse_two = norm_ahead(hidden, gain_two, wide(3))
-    normed_two = normed_two.astype(BF)
-    cot = jnp.concatenate([cot_ref[b].T for b in range(group)], axis=1)
-    output = hidden + wide(4)
-    grad_normed = jnp.zeros((128, 128 * group), F32)
-    inner_const = math.sqrt(2.0 / math.pi)
-    for c in range(4):
-        part = slice(128 * c, 128 * c + 128)
-        bias = jnp.concatenate([bias_in[part]] * group, axis=1)
-        inner = mm(t_inT[part], normed_two) + bias
-        square = inner * inner
-        bend = jnp.tanh(inner * (inner_const + (inner_const * 0.044715) * square))
-        rise = 0.5 + 0.5 * bend
-        active = (inner * rise).astype(BF)
-        slope = rise + (0.5 * inner) * (1.0 - bend * bend) * (
-            inner_const + (3.0 * inner_const * 0.044715) * square
+    branch = mm(t_oT[...], mixed)
+    hidden, normed_list, unit_two, inverse_two = [], [], [], []
+    for b in every:
+        hidden.append(residual[b] + branch[:, lanes[b]])
+        ahead, unit, inverse = norm_ahead(hidden[b], vecs[2], vecs[3])
+        normed_list.append(ahead.astype(BF))
+        unit_two.append(unit)
+        inverse_two.append(inverse)
+    normed_two = jnp.concatenate(
+        [jnp.concatenate(normed_list, axis=1), jnp.ones((16, 128 * group), BF)], axis=0
+    )
+    cot = jnp.concatenate(cot_list, axis=1)
+    c0 = math.sqrt(2.0 / math.pi)
+    c1 = c0 * 0.044715
+    inner_all = mm(t_inT[...], normed_two[:128])
+    grad_all = mm(t_dn[...], cot)
+    active_rows, grad_rows = [], []
+    for r in range(0, FF, 16):
+        bias = bias_in[r : r + 16]
+        active_cols, grad_cols = [], []
+        for b in every:
+            inner = inner_all[r : r + 16, lanes[b]] + bias
+            square = inner * inner
+            bend = jnp.tanh(inner * (c0 + c1 * square))
+            rise = 0.5 + 0.5 * bend
+            active = inner * rise
+            slope = rise + (active - active * rise) * (2.0 * c0 + (6.0 * c1) * square)
+            active_cols.append(active.astype(BF))
+            grad_cols.append((grad_all[r : r + 16, lanes[b]] * slope).astype(BF))
+        active_rows.append(jnp.concatenate(active_cols, axis=1))
+        grad_rows.append(jnp.concatenate(grad_cols, axis=1))
+    active = jnp.concatenate(active_rows, axis=0)
+    grad_inner = jnp.concatenate(grad_rows, axis=0)
+    grad_all = mm(t_in[...], grad_inner)
+    output_all = mm(t_dnT[...], active)
+    a_dn[...] += mm_nt(cot, active)
+    a_in[...] += mm_nt(normed_two, grad_inner)
+
+    grad_hidden = []
+    for b in every:
+        grad_out = cot_list[b].astype(F32)
+        grad_normed = grad_all[:, lanes[b]]
+        a_vec[4] += grad_out
+        a_vec[2] += grad_normed * unit_two[b]
+        a_vec[3] += grad_normed
+        grad_hidden.append(
+            grad_out + norm_back(grad_normed, vecs[2], unit_two[b], inverse_two[b])
         )
-        output = output + mm(t_dnT[:, part], active)
-        a_dn[:, part] += mm_nt(cot, active)
-        grad_inner = mm(t_dn[part], cot) * slope
-        a_bin[part] += fold_lanes(grad_inner, group)
-        grad_inner = grad_inner.astype(BF)
-        a_in[:, part] += mm_nt(normed_two, grad_inner)
-        grad_normed = grad_normed + mm(t_in[:, part], grad_inner)
-    output = output.astype(BF)
-    for b in range(group):
-        out_ref[b] = output[:, 128 * b : 128 * b + 128].T
-    output = output.astype(F32)
-    a_vec[5] += fold_lanes(output, group)
-    a_vec[6] += fold_lanes(output * output, group)
-
-    grad_out = cot.astype(F32)
-    a_vec[4] += fold_lanes(grad_out, group)
-    a_vec[2] += fold_lanes(grad_normed * unit_two, group)
-    a_vec[3] += fold_lanes(grad_normed, group)
-    grad_hidden = grad_out + norm_back(grad_normed, gain_two, unit_two, inverse_two)
-    grad_branch = grad_hidden.astype(BF)
+    grad_branch = jnp.concatenate([part.astype(BF) for part in grad_hidden], axis=1)
+    grad_mixed = mm(t_o[...], grad_branch)
     a_o[...] += mm_nt(mixed, grad_branch)
-    grad_mixed = mm(t_o[...], grad_branch).astype(BF)
+    for b in every:
+        output = (hidden[b] + output_all[:, lanes[b]] + vecs[4]).astype(BF)
+        out_ref[b] = output.T
+        output = output.astype(F32)
+        a_vec[5] += output
+        a_vec[6] += output * output
+    grad_T, drops = [], []
+    for b in every:
+        scaled = []
+        drops.append([])
+        for h in range(HEADS):
+            inverse = head_inverse[b][h]
+            part = grad_mixed[16 * h : 16 * h + 16, lanes[b]]
+            part = jnp.concatenate([part[:8] * inverse, part[8:] * inverse], axis=0).astype(BF)
+            scaled.append(part)
+            drops[b].append(jnp.sum(part.astype(F32) * head_mixed[b][h], axis=0, keepdims=True))
+        grad_T.append(jnp.concatenate(scaled, axis=0))
+    grad_probs = [[mm(values[b], head_pair(grad_T[b], j)) for j in range(PAIRS)] for b in every]
+    grad_values = [
+        [mm_nt(pair_rows(grad_T[b], j), raised[b][j]) for j in range(PAIRS)] for b in every
+    ]
+    grad_scores = []
+    for b in every:
+        grad_scores.append([])
+        for j in range(PAIRS):
+            halves = []
+            for u in range(2):
+                here = slice(128 * u, 128 * u + 128)
+                tile = grad_probs[b][j][:, here] - drops[b][2 * j + u]
+                halves.append(tile.astype(BF) * raised[b][j][:, here])
+            grad_scores[b].append(jnp.concatenate(halves, axis=1))
+    grad_queries = [
+        [pair_pick(mm(key_T[b][32 * j : 32 * j + 32], grad_scores[b][j])) for j in range(PAIRS)]
+        for b in every
+    ]
+    grad_keys = [
+        [mm_nt(pair_rows(query_T[b], j), grad_scores[b][j]) for j in range(PAIRS)] for b in every
+    ]
     grad_list = []
-    for b in range(group):
-        query_T, key_T, values, probs_list = trunk_kept[b]
-        grad_T = grad_mixed[:, 128 * b : 128 * b + 128]
-        grad_queries, grad_keys, grad_values = [], [], []
-        for j in range(PAIRS):
-            probs, probs_low = probs_list[j]
-            grad_probs = mm(values, head_pair(grad_T, j))
-            grad_scores = scores_back(probs, grad_probs, 0)
-            grad_queries.append(pair_pick(mm(key_T[32 * j : 32 * j + 32], grad_scores)))
-            grad_keys.append(mm_nt(pair_rows(query_T, j), grad_scores))
-            grad_values.append(mm_nt(pair_rows(grad_T, j), probs_low))
-        grad_queries = jnp.concatenate(grad_queries, axis=0) * SCALE
+    for b in every:
         grad_list.append(
-            jnp.concatenate([grad_queries] + grad_keys + grad_values, axis=0).astype(BF)
+            jnp.concatenate(
+                [
+                    (jnp.concatenate(grad_queries[b], axis=0) * SCALE).astype(BF),
+                    (jnp.concatenate(grad_keys[b], axis=0) * (1.0 / LOG2E)).astype(BF),
+                    jnp.concatenate(grad_values[b], axis=0).astype(BF),
+                ],
+                axis=0,
+            )
         )
     grad_projected = jnp.concatenate(grad_list, axis=1)
+    grad_all = mm(t_qkv[...], grad_projected)
     a_qkv[...] += mm_nt(normed, grad_projected)
-    grad_normed = mm(t_qkv[...], grad_projected)
-    a_vec[0] += fold_lanes(grad_normed * unit_one, group)
-    a_vec[1] += fold_lanes(grad_normed, group)
-    grad_tokens = (grad_hidden + norm_back(grad_normed, gain_one, unit_one, inverse_one)).astype(BF)
-
-    for b in range(group):
-        e = rels[b]
-        rows_T, kv, kv_T, query_block, probs, probs_low, mixed_T = kept[b]
-        grad_T = grad_tokens[:, 128 * b : 128 * b + 128]
-        a_out[e] += mm_nt(mixed_T, grad_T)
-        grad_mixed = mm(s_out[e], grad_T)
-        turned = [grad_mixed.astype(BF)] + [
-            pltpu.roll(grad_mixed, 32 * k, 1).astype(BF) for k in range(1, 4)
+    grad_tokens = []
+    for b in every:
+        grad_normed = grad_all[:, lanes[b]]
+        a_vec[0] += grad_normed * unit_one[b]
+        a_vec[1] += grad_normed
+        grad_tokens.append(
+            (grad_hidden[b] + norm_back(grad_normed, vecs[0], unit_one[b], inverse_one[b])).astype(BF)
+        )
+
+    grad_mixed = [mm(s_out[rels[b]], grad_tokens[b]) for b in every]
+    for b in every:
+        a_out[rels[b]] += mm_nt(stem_mixed[b], grad_tokens[b])
+    masks = [(lane_block == c).astype(BF) for c in range(4)]
+    zero = jnp.zeros((16, 128), BF)
+    spread = []
+    for b in every:
+        spread.append([])
+        turned = [grad_mixed[b].astype(BF)] + [
+            pltpu.roll(grad_mixed[b], 32 * k, 1).astype(BF) for k in range(1, 4)
         ]
-        masks = [(lane_block == c).astype(BF) for c in range(4)]
-        zero = jnp.zeros((16, 128), BF)
-        grad_values, grad_scores = [], []
         for s in range(STEPS):
             pieces = []
             for h in range(HEADS):
@@ -345,18 +429,42 @@
                 pieces.append(
                     jnp.concatenate([piece, zero] if h < 4 else [zero, piece], axis=1)
                 )
-            spread = jnp.concatenate(pieces, axis=0)
-            here = slice(64 * s, 64 * s + 64)
-            grad_probs = mm(kv[here, 128:], spread)
-            grad_scores.append(scores_back(probs[s], grad_probs, 0))
-            grad_values.append(mm_nt(probs_low[here], spread))
-        grad_scores = jnp.concatenate(grad_scores, axis=0)
-        grad_values = jnp.concatenate(grad_values, axis=0).astype(BF)
-        grad_keys = mm_nt(grad_scores, query_block).astype(BF)
-        a_q[e] += mm(kv_T[:128], grad_scores)
-        grad_kv = jnp.concatenate([grad_keys, grad_values], axis=1)
-        a_kv[e] += mm(rows_T, grad_kv)
-        rgrad_ref[b] = mm_nt(grad_kv, s_kv[e]).astype(BF)
+            spread[b].append(jnp.concatenate(pieces, axis=0))
+    grad_probs = [
+        [mm(kv[b][64 * s : 64 * s + 64, 128:], spread[b][s]) for s in range(STEPS)] for b in every
+    ]
+    grad_values = [
+        jnp.concatenate(
+            [mm_nt(probs_low[b][s], spread[b][s]).astype(BF) for s in range(STEPS)], axis=0
+        )
+        for b in every
+    ]
+    grad_scores = []
+    for b in every:
+        steps = []
+        for s in range(STEPS):
+            steps.append(
+                jnp.concatenate(
+                    [
+                        scores_back(probs[b][s][u], grad_probs[b][s][:, 128 * u : 128 * u + 128], 0)
+                        for u in range(2)
+                    ],
+                    axis=1,
+                )
+            )
+        grad_scores.append(jnp.concatenate(steps, axis=0))
+    grad_keys = [
+        (mm_nt(grad_scores[b], s_qb[rels[b]]) * (1.0 / LOG2E)).astype(BF) for b in every
+    ]
+    keys_T = [kv[b][:, :128].T for b in every]
+    rows_T = [rows_ref[b].T for b in every]
+    for b in every:
+        a_q[rels[b]] += mm(keys_T[b], grad_scores[b])
+    grad_kv = [jnp.concatenate([grad_keys[b], grad_values[b]], axis=1) for b in every]
+    for b in every:
+        rgrad_ref[b] = mm_nt(grad_kv[b], s_kv[rels[b]]).astype(BF)
+    for b in every:
+        a_kv[rels[b]] += mm(rows_T[b], grad_kv[b])
 
     @pl.when(step == pl.num_programs(0) - 1)
     def _():
@@ -364,7 +472,7 @@
         count = send_ref.shape[0]
         blocks = [a_qkv[:, 128 * c : 128 * c + 128] for c in range(3)]
         blocks.append(a_o[...])
-        blocks += [a_in[:, 128 * c : 128 * c + 128] for c in range(4)]
+        blocks += [a_in[0:128, 128 * c : 128 * c + 128] for c in range(4)]
         blocks += [a_dn[:, 128 * c : 128 * c + 128].T for c in range(4)]
         per = len(blocks) // count
         for j in range(count):
@@ -376,9 +484,7 @@
             == lax.broadcasted_iota(jnp.int32, (256, 128), 1) // 16
         )
         sums = [jnp.sum(a_vec[c].T, axis=0, keepdims=True) for c in range(5)]
-        sums += [
-            jnp.sum(a_bin[128 * c : 128 * c + 128].T, axis=0, keepdims=True) for c in range(4)
-        ]
+        sums += [a_in[128:129, 128 * c : 128 * c + 128] for c in range(4)]
         sums += [jnp.sum(a_vec[c].T, axis=0, keepdims=True) for c in (5, 6)]
         sums.append(jnp.zeros((5, 128), F32))
         sums = jnp.concatenate(sums, axis=0)
@@ -541,7 +647,7 @@
     )
     stems = [own] + [shift(own, "emb", emb_count, -k) for k in range(1, emb_count)]
 
-    group = 2
+    group = 4
     grid = seqs // group
 
     def whole(shape):
@@ -549,7 +655,6 @@
 
     scratch = [
         ((4, 128, 256), BF),
-        ((4, 256, 128), BF),
         ((4, 128, 128), BF),
         ((4, 128, 128), BF),
         ((4, 128, 256), BF),
@@ -565,9 +670,8 @@
         ((5, 128, 128), F32),
         ((128, 384), F32),
         ((128, 128), F32),
+        ((144, 512), F32),
         ((128, 512), F32),
-        ((128, 512), F32),
-        ((512, 128), F32),
         ((7, 128, 128), F32),
         ((4, 128, 256), F32),
         ((4, 128, 128), F32),

time: 220 us -> 128 us (0.58)
  Pallas kernels: 151 us -> 59.4 us
    pallas_call x1, Pallas kernels: 142 us -> 50.2 us  [local(): pl.pallas_call(functools.partial(main_kernel, group), out_shape=(jax.Shap...]
  transfers between devices with their start and end apart: 23 -> 23, of which waited for: 11 -> 11; matrix products, arithmetic and copies ran while one was open for 2% -> 4% of each run, Pallas kernels for 0% -> 0%
where the time goes in v2:
time: 128 us
  Pallas kernels  59.4 us (46%)
  starting transfers between devices  29.5 us (23%)
  waiting for transfers between devices  24.7 us (19%)
  local copies, waits for them, and re-layouts  9.78 us (8%)
  other arithmetic  3.49 us (3%)
    pallas_call x1, Pallas kernels, local(): pl.pallas_call(functools.partial(main_kernel, group), out_shape=(jax.Shap...  50.2 us
    ppermute x23, starting transfers between devices, shift(): lax.ppermute(value, axis, [(i, (i + by) % count) for i in range(count)])  29.5 us
    ppermute x23, waiting for transfers between devices, shift(): lax.ppermute(value, axis, [(i, (i + by) % count) for i in range(count)])  24.7 us
    pallas_call x2, Pallas kernels, call(): pl.pallas_call(kernel, out_shape=outs, in_specs=[pl.BlockSpec(memory_spac...  5.65 us
    unnamed x51, local copies, waits for them, and re-layouts  4.64 us
  transfers between devices with their start and end apart: 23, of which 11 were waited for; matrix products, arithmetic and copies ran while one was open for 4% of the time, Pallas kernels for 0%

profile of v2, /device:TPU:0, one launch (start us, length us, event | category | flops | bytes accessed | tf_op | source)
XLA Modules:
  0.0 127.7 jit_solution(18180018248448937312)
XLA Ops:
  0.7 0.7 bitcast_convert_fusion
  1.4 0.9 bitcast_convert_fusion.1
  2.4 0.0 copy-start
  2.4 0.5 collective-permute-start.2
  2.9 2.6 %collective-permute-start.1 = (bf16[416,128]{1,0:T(8,128)(2,1)S(1)}, bf16[416,128]{1,0:T(8,128)(2,1)S(1)}, u32[]{:S(2)}, u32[]{:S(2)}) collective-permute-start(bf16[416,128]{1,0:T(8,128)(2,1)S(1)} %pad_maximum_fusion.own_ref), channel_id=1, source_target_pairs={{0,2},{1,3},{2,0},{3,1},{4,6},{5,7},{6,4},{7,5},{8,10},{9,11},{10,... | collective-permute-start | bytes 319496 | tf_op jit(solution)/shard_map/ppermute | solution.py:642
  5.5 1.4 %collective-permute-start = (bf16[416,128]{1,0:T(8,128)(2,1)S(1)}, bf16[416,128]{1,0:T(8,128)(2,1)S(1)}, u32[]{:S(2)}, u32[]{:S(2)}) collective-permute-start(bf16[416,128]{1,0:T(8,128)(2,1)S(1)} %pad_maximum_fusion.own_ref), channel_id=1, source_target_pairs={{0,3},{1,0},{2,1},{3,2},{4,7},{5,4},{6,5},{7,6},{8,11},{9,8},{10,9... | collective-permute-start | bytes 319496 | tf_op jit(solution)/shard_map/ppermute | solution.py:642
  6.9 0.8 copy.42
  7.6 0.6 reshape.60.seg_ref
  8.2 1.2 compare_select_fusion.rel_ref
  9.4 0.6 pad_add_fusion.pos_ref
  10.1 0.0 collective-permute-done.1.two_ref
  10.1 0.0 copy-start.6
  10.1 0.4 collective-permute-done.one_ref
  10.5 0.2 copy-done.5
  10.7 0.0 copy-done.6
  10.8 0.4 copy-done.7
  11.1 50.2 %shard_map.354 = (bf16[32,128,128]{2,1,0:T(8,128)(2,1)}, bf16[32,256,128]{2,1,0:T(8,128)(2,1)}, bf16[4,832,128]{2,1,0:T(8,128)(2,1)}, f32[16,128]{1,0:T(8,128)}) custom-call(s32[32]{0:T(128)} %compare_select_fusion.rel_ref, s32[128]{0:T(128)} %reshape.60.seg_ref, s32[2]{0:T(128)} %pad_add_fusion.pos_ref, bf16[32,256,128]{2,1,0:T(8,128)(2,1)} %bitcast.43, ...), custom_call_target="tpu_custom_call" | custom-call | tf_op jit(solution)/shard_map/pallas_call | solution.py:680
  61.3 1.2 slice_bitcast_fusion
  62.5 2.0 %collective-permute-start.5 = (bf16[832,128]{1,0:T(8,128)(2,1)S(1)}, bf16[832,128]{1,0:T(8,128)(2,1)S(1)}, u32[]{:S(2)}, u32[]{:S(2)}) collective-permute-start(bf16[832,128]{1,0:T(8,128)(2,1)S(1)} %get-tuple-element.72), channel_id=1, source_target_pairs={{0,3},{1,0},{2,1},{3,2},{4,7},{5,4},{6,5},{7,6},{8,11},{9,8},{10,9... | collective-permute-start | bytes 638984 | tf_op jit(solution)/shard_map/ppermute | solution.py:642
  64.4 0.2 collective-permute-start.3
  64.6 5.4 %collective-permute-done.5.refs_3_ = bf16[832,128]{1,0:T(8,128)(2,1)S(1)} collective-permute-done((bf16[832,128]{1,0:T(8,128)(2,1)S(1)}, bf16[832,128]{1,0:T(8,128)(2,1)S(1)}, u32[]{:S(2)}, u32[]{:S(2)}) %collective-permute-start.5) | collective-permute-done | bytes 213024 | tf_op jit(solution)/shard_map/ppermute | solution.py:642
  70.0 4.7 %collective-permute-done.4.refs_2_ = bf16[832,128]{1,0:T(8,128)(2,1)S(1)} collective-permute-done((bf16[832,128]{1,0:T(8,128)(2,1)S(1)}, bf16[832,128]{1,0:T(8,128)(2,1)S(1)}, u32[]{:S(2)}, u32[]{:S(2)}) %collective-permute-start.4) | collective-permute-done | bytes 213024 | tf_op jit(solution)/shard_map/ppermute | solution.py:642
  74.7 0.1 collective-permute-done.3.refs_1_
  74.8 0.6 copy-done.3
  75.4 0.7 copy-done.4
  76.1 2.1 %shard_map.355.refs_0_ = bf16[8,136,128]{2,1,0:T(8,128)(2,1)} custom-call(s32[2]{0:T(128)} %pad_add_fusion.pos_ref, bf16[4,832,128]{2,1,0:T(8,128)(2,1)} %get-tuple-element.49.refs_0_, bf16[832,128]{1,0:T(8,128)(2,1)} %copy-done.4, bf16[832,128]{1,0:T(8,128)(2,1)} %copy-done.3, bf16[832,128]{1,0:T(8,128)(2,1)} %copy-done.2), custom_call_target="tpu_custom_call" | custom-call | tf_op jit(solution)/shard_map/pallas_call | solution.py:724
  78.2 0.9 slice_bitcast_fusion.3
  79.1 4.9 %collective-permute-start.12 = (bf16[136,128]{1,0:T(8,128)(2,1)S(1)}, bf16[136,128]{1,0:T(8,128)(2,1)S(1)}, u32[]{:S(2)}, u32[]{:S(2)}) collective-permute-start(bf16[136,128]{1,0:T(8,128)(2,1)S(1)} %get-tuple-element.75), channel_id=1, source_target_pairs={{0,28},{4,0},{8,4},{12,8},{16,12},{20,16},{24,20},{28,24},{1,29},{... | collective-permute-start | bytes 104456 | tf_op jit(solution)/shard_map/ppermute | solution.py:642
  84.0 0.4 collective-permute-start.11
  84.5 0.0 collective-permute-start.10
  84.5 3.0 %collective-permute-start.9 = (bf16[136,128]{1,0:T(8,128)(2,1)S(1)}, bf16[136,128]{1,0:T(8,128)(2,1)S(1)}, u32[]{:S(2)}, u32[]{:S(2)}) collective-permute-start(bf16[136,128]{1,0:T(8,128)(2,1)S(1)} %get-tuple-element.78), channel_id=1, source_target_pairs={{0,16},{4,20},{8,24},{12,28},{16,0},{20,4},{24,8},{28,12},{1,17},{... | collective-permute-start | bytes 104456 | tf_op jit(solution)/shard_map/ppermute | solution.py:642
  87.5 0.0 collective-permute-start.8
  87.5 1.8 %collective-permute-start.7 = (bf16[136,128]{1,0:T(8,128)(2,1)S(1)}, bf16[136,128]{1,0:T(8,128)(2,1)S(1)}, u32[]{:S(2)}, u32[]{:S(2)}) collective-permute-start(bf16[136,128]{1,0:T(8,128)(2,1)S(1)} %get-tuple-element.80), channel_id=1, source_target_pairs={{0,8},{4,12},{8,16},{12,20},{16,24},{20,28},{24,0},{28,4},{1,9},{5... | collective-permute-start | bytes 104456 | tf_op jit(solution)/shard_map/ppermute | solution.py:642
  89.3 1.1 collective-permute-start.6
  90.5 0.0 copy-start.14
  90.5 2.8 %collective-permute-done.8.refs_3_ = bf16[136,128]{1,0:T(8,128)(2,1)S(1)} collective-permute-done((bf16[136,128]{1,0:T(8,128)(2,1)S(1)}, bf16[136,128]{1,0:T(8,128)(2,1)S(1)}, u32[]{:S(2)}, u32[]{:S(2)}) %collective-permute-start.8) | collective-permute-done | bytes 34848 | tf_op jit(solution)/shard_map/ppermute | solution.py:642
  93.2 1.3 %collective-permute-done.7.refs_2_ = bf16[136,128]{1,0:T(8,128)(2,1)S(1)} collective-permute-done((bf16[136,128]{1,0:T(8,128)(2,1)S(1)}, bf16[136,128]{1,0:T(8,128)(2,1)S(1)}, u32[]{:S(2)}, u32[]{:S(2)}) %collective-permute-start.7) | collective-permute-done | bytes 34848 | tf_op jit(solution)/shard_map/ppermute | solution.py:642
  94.5 1.4 %collective-permute-done.6.refs_1_ = bf16[136,128]{1,0:T(8,128)(2,1)S(1)} collective-permute-done((bf16[136,128]{1,0:T(8,128)(2,1)S(1)}, bf16[136,128]{1,0:T(8,128)(2,1)S(1)}, u32[]{:S(2)}, u32[]{:S(2)}) %collective-permute-start.6) | collective-permute-done | bytes 34848 | tf_op jit(solution)/shard_map/ppermute | solution.py:642
  96.0 0.0 copy-start.17
  96.0 0.6 copy-done.17
  96.6 1.5 %shard_map.356 = (bf16[104,128]{1,0:T(8,128)(2,1)}, f32[16,128]{1,0:T(8,128)}) custom-call(bf16[8,136,128]{2,1,0:T(8,128)(2,1)} %shard_map.355.refs_0_, bf16[136,128]{1,0:T(8,128)(2,1)} %copy-done.17, bf16[136,128]{1,0:T(8,128)(2,1)} %copy-done.16, bf16[136,128]{1,0:T(8,128)(2,1)} %copy-done.15, bf16[136,128]{1,0:T(8,128)(2,1)} %copy-done.14, ...), custom_call_target="tpu_custom_call" | custom-call | tf_op jit(solution)/shard_map/pallas_call | solution.py:735
  98.1 0.3 collective-permute-start.19
  98.4 1.4 %collective-permute-start.18 = (bf16[104,128]{1,0:T(8,128)(2,1)}, bf16[104,128]{1,0:T(8,128)(2,1)S(1)}, u32[]{:S(2)}, u32[]{:S(2)}) collective-permute-start(bf16[104,128]{1,0:T(8,128)(2,1)} %get-tuple-element.50.refs_0_), channel_id=1, source_target_pairs={{0,24},{4,28},{8,0},{12,4},{16,8},{20,12},{24,16},{28,20},{1,25},{... | collective-permute-start | bytes 79880 | tf_op jit(solution)/shard_map/ppermute | solution.py:642
  99.8 1.5 %collective-permute-start.17 = (bf16[104,128]{1,0:T(8,128)(2,1)}, bf16[104,128]{1,0:T(8,128)(2,1)S(1)}, u32[]{:S(2)}, u32[]{:S(2)}) collective-permute-start(bf16[104,128]{1,0:T(8,128)(2,1)} %get-tuple-element.50.refs_0_), channel_id=1, source_target_pairs={{0,20},{4,24},{8,28},{12,0},{16,4},{20,8},{24,12},{28,16},{1,21},{... | collective-permute-start | bytes 79880 | tf_op jit(solution)/shard_map/ppermute | solution.py:642
  101.3 2.4 %collective-permute-start.16 = (bf16[104,128]{1,0:T(8,128)(2,1)}, bf16[104,128]{1,0:T(8,128)(2,1)S(1)}, u32[]{:S(2)}, u32[]{:S(2)}) collective-permute-start(bf16[104,128]{1,0:T(8,128)(2,1)} %get-tuple-element.50.refs_0_), channel_id=1, source_target_pairs={{0,16},{4,20},{8,24},{12,28},{16,0},{20,4},{24,8},{28,12},{1,17},{... | collective-permute-start | bytes 79880 | tf_op jit(solution)/shard_map/ppermute | solution.py:642
  103.7 0.5 collective-permute-start.15
  104.2 1.5 %collective-permute-start.14 = (bf16[104,128]{1,0:T(8,128)(2,1)}, bf16[104,128]{1,0:T(8,128)(2,1)S(1)}, u32[]{:S(2)}, u32[]{:S(2)}) collective-permute-start(bf16[104,128]{1,0:T(8,128)(2,1)} %get-tuple-element.50.refs_0_), channel_id=1, source_target_pairs={{0,8},{4,12},{8,16},{12,20},{16,24},{20,28},{24,0},{28,4},{1,9},{5... | collective-permute-start | bytes 79880 | tf_op jit(solution)/shard_map/ppermute | solution.py:642
  105.7 2.0 %collective-permute-start.13 = (bf16[104,128]{1,0:T(8,128)(2,1)}, bf16[104,128]{1,0:T(8,128)(2,1)S(1)}, u32[]{:S(2)}, u32[]{:S(2)}) collective-permute-start(bf16[104,128]{1,0:T(8,128)(2,1)} %get-tuple-element.50.refs_0_), channel_id=1, source_target_pairs={{0,4},{4,8},{8,12},{12,16},{16,20},{20,24},{24,28},{28,0},{1,5},{5... | collective-permute-start | bytes 79880 | tf_op jit(solution)/shard_map/ppermute | solution.py:642
  107.7 0.0 copy-start.21
  107.7 1.9 %collective-permute-done.15.refs_3_ = bf16[104,128]{1,0:T(8,128)(2,1)S(1)} collective-permute-done((bf16[104,128]{1,0:T(8,128)(2,1)}, bf16[104,128]{1,0:T(8,128)(2,1)S(1)}, u32[]{:S(2)}, u32[]{:S(2)}) %collective-permute-start.15) | collective-permute-done | bytes 26656 | tf_op jit(solution)/shard_map/ppermute | solution.py:642
  109.6 0.5 collective-permute-done.14.refs_2_
  110.1 2.4 %collective-permute-done.13.refs_1_ = bf16[104,128]{1,0:T(8,128)(2,1)S(1)} collective-permute-done((bf16[104,128]{1,0:T(8,128)(2,1)}, bf16[104,128]{1,0:T(8,128)(2,1)S(1)}, u32[]{:S(2)}, u32[]{:S(2)}) %collective-permute-start.13) | collective-permute-done | bytes 26656 | tf_op jit(solution)/shard_map/ppermute | solution.py:642
  112.5 0.0 copy-start.24
  112.5 0.6 copy-done.24
  113.1 1.6 %shard_map.357 = bf16[8,104,128]{2,1,0:T(8,128)(2,1)} custom-call(s32[2]{0:T(128)} %pad_add_fusion.pos_ref, bf16[104,128]{1,0:T(8,128)(2,1)} %get-tuple-element.50.refs_0_, bf16[104,128]{1,0:T(8,128)(2,1)} %copy-done.24, bf16[104,128]{1,0:T(8,128)(2,1)} %copy-done.23, bf16[104,128]{1,0:T(8,128)(2,1)} %copy-done.22, bf16[104,128]{1,0:T(8,128)(2,1)} %copy-done.21, ...), custom_call_target="tpu_custom_call" | custom-call | tf_op jit(solution)/shard_map/pallas_call | solution.py:600
  114.7 0.9 slice.70.refs_0_
  115.6 0.1 collective-permute-start.22
  115.7 1.7 %collective-permute-start.21 = (bf16[384,128]{1,0:T(8,128)(2,1)S(1)}, bf16[384,128]{1,0:T(8,128)(2,1)S(1)}, u32[]{:S(2)}, u32[]{:S(2)}) collective-permute-start(bf16[384,128]{1,0:T(8,128)(2,1)S(1)} %slice.70.refs_0_), channel_id=1, source_target_pairs={{0,2},{1,3},{2,0},{3,1},{4,6},{5,7},{6,4},{7,5},{8,10},{9,11},{10,... | collective-permute-start | bytes 294920 | tf_op jit(solution)/shard_map/ppermute | solution.py:642
  117.3 0.2 collective-permute-start.20
  117.5 1.5 %slice.71.refs_4_ = bf16[416,128]{1,0:T(8,128)(2,1)} slice(bf16[832,128]{1,0:T(8,128)(2,1)} %bitcast.45), slice={[384:800], [0:128]} | slice | bytes 212992 | tf_op jit(solution)/shard_map/slice | solution.py:752
  119.1 3.9 %collective-permute-done.21.refs_2_ = bf16[384,128]{1,0:T(8,128)(2,1)S(1)} collective-permute-done((bf16[384,128]{1,0:T(8,128)(2,1)S(1)}, bf16[384,128]{1,0:T(8,128)(2,1)S(1)}, u32[]{:S(2)}, u32[]{:S(2)}) %collective-permute-start.21) | collective-permute-done | bytes 98336 | tf_op jit(solution)/shard_map/ppermute | solution.py:642
  123.0 0.6 copy-done.9
  123.6 0.0 copy-done.10
  123.7 4.1 %shard_map.358 = (f32[128,1024]{1,0:T(8,128)}, f32[128,1024]{1,0:T(8,128)}, f32[128,1024]{1,0:T(8,128)}, bf16[128,1024]{1,0:T(8,128)(2,1)}, f32[512,128]{1,0:T(8...) custom-call(s32[2]{0:T(128)} %pad_add_fusion.pos_ref, ...), custom_call_target="tpu_custom_call" | custom-call | tf_op jit(solution)/shard_map/pallas_call | solution.py:600
  (49 shorter events, 0.1 us)
Async XLA Ops:
  2.4 8.1 %copy-start = (bf16[416,128]{1,0:T(8,128)(2,1)}, bf16[416,128]{1,0:T(8,128)(2,1)S(1)}, u32[]{:S(2)}) copy-start(bf16[416,128]{1,0:T(8,128)(2,1)S(1)} %pad_maximum_fusion.own_ref) | copy-start | bytes 319492
  2.4 7.7 %collective-permute-start.2 = (bf16[416,128]{1,0:T(8,128)(2,1)S(1)}, bf16[416,128]{1,0:T(8,128)(2,1)S(1)}, u32[]{:S(2)}, u32[]{:S(2)}) collective-permute-start(bf16[416,128]{1,0:T(8,128)(2,1)S(1)} %pad_maximum_fusion.own_ref), channel_id=1, source_target_pairs={{0,1},{1,2},{2,3},{3,0},{4,5},{5,6},{6,7},{7,4},{8,9},{9,10},{10,1... | collective-permute-start | bytes 319496 | tf_op jit(solution)/shard_map/ppermute | solution.py:642
  2.9 7.2 %collective-permute-start.1 = (bf16[416,128]{1,0:T(8,128)(2,1)S(1)}, bf16[416,128]{1,0:T(8,128)(2,1)S(1)}, u32[]{:S(2)}, u32[]{:S(2)}) collective-permute-start(bf16[416,128]{1,0:T(8,128)(2,1)S(1)} %pad_maximum_fusion.own_ref), channel_id=1, source_target_pairs={{0,2},{1,3},{2,0},{3,1},{4,6},{5,7},{6,4},{7,5},{8,10},{9,11},{10,... | collective-permute-start | bytes 319496 | tf_op jit(solution)/shard_map/ppermute | solution.py:642
  5.5 5.0 %collective-permute-start = (bf16[416,128]{1,0:T(8,128)(2,1)S(1)}, bf16[416,128]{1,0:T(8,128)(2,1)S(1)}, u32[]{:S(2)}, u32[]{:S(2)}) collective-permute-start(bf16[416,128]{1,0:T(8,128)(2,1)S(1)} %pad_maximum_fusion.own_ref), channel_id=1, source_target_pairs={{0,3},{1,0},{2,1},{3,2},{4,7},{5,4},{6,5},{7,6},{8,11},{9,8},{10,9... | collective-permute-start | bytes 319496 | tf_op jit(solution)/shard_map/ppermute | solution.py:642
  10.1 0.6 copy-start.5
  10.1 0.7 copy-start.6
  10.5 0.6 copy-start.7
  62.5 7.5 %collective-permute-start.5 = (bf16[832,128]{1,0:T(8,128)(2,1)S(1)}, bf16[832,128]{1,0:T(8,128)(2,1)S(1)}, u32[]{:S(2)}, u32[]{:S(2)}) collective-permute-start(bf16[832,128]{1,0:T(8,128)(2,1)S(1)} %get-tuple-element.72), channel_id=1, source_target_pairs={{0,3},{1,0},{2,1},{3,2},{4,7},{5,4},{6,5},{7,6},{8,11},{9,8},{10,9... | collective-permute-start | bytes 638984 | tf_op jit(solution)/shard_map/ppermute | solution.py:642
  64.4 10.3 %collective-permute-start.4 = (bf16[832,128]{1,0:T(8,128)(2,1)S(1)}, bf16[832,128]{1,0:T(8,128)(2,1)S(1)}, u32[]{:S(2)}, u32[]{:S(2)}) collective-permute-start(bf16[832,128]{1,0:T(8,128)(2,1)S(1)} %get-tuple-element.73), channel_id=1, source_target_pairs={{0,2},{1,3},{2,0},{3,1},{4,6},{5,7},{6,4},{7,5},{8,10},{9,11},{10,... | collective-permute-start | bytes 638984 | tf_op jit(solution)/shard_map/ppermute | solution.py:642
  64.4 10.4 %collective-permute-start.3 = (bf16[832,128]{1,0:T(8,128)(2,1)S(1)}, bf16[832,128]{1,0:T(8,128)(2,1)S(1)}, u32[]{:S(2)}, u32[]{:S(2)}) collective-permute-start(bf16[832,128]{1,0:T(8,128)(2,1)S(1)} %get-tuple-element.74), channel_id=1, source_target_pairs={{0,1},{1,2},{2,3},{3,0},{4,5},{5,6},{6,7},{7,4},{8,9},{9,10},{10,1... | collective-permute-start | bytes 638984 | tf_op jit(solution)/shard_map/ppermute | solution.py:642
  70.0 4.8 %copy-start.2 = (bf16[832,128]{1,0:T(8,128)(2,1)}, bf16[832,128]{1,0:T(8,128)(2,1)S(1)}, u32[]{:S(2)}) copy-start(bf16[832,128]{1,0:T(8,128)(2,1)S(1)} %collective-permute-done.5.refs_3_) | copy-start | bytes 638980
  74.7 0.7 copy-start.3
  75.4 0.7 copy-start.4
  79.1 8.4 %collective-permute-start.12 = (bf16[136,128]{1,0:T(8,128)(2,1)S(1)}, bf16[136,128]{1,0:T(8,128)(2,1)S(1)}, u32[]{:S(2)}, u32[]{:S(2)}) collective-permute-start(bf16[136,128]{1,0:T(8,128)(2,1)S(1)} %get-tuple-element.75), channel_id=1, source_target_pairs={{0,28},{4,0},{8,4},{12,8},{16,12},{20,16},{24,20},{28,24},{1,29},{... | collective-permute-start | bytes 104456 | tf_op jit(solution)/shard_map/ppermute | solution.py:642
  84.0 5.3 %collective-permute-start.11 = (bf16[136,128]{1,0:T(8,128)(2,1)S(1)}, bf16[136,128]{1,0:T(8,128)(2,1)S(1)}, u32[]{:S(2)}, u32[]{:S(2)}) collective-permute-start(bf16[136,128]{1,0:T(8,128)(2,1)S(1)} %get-tuple-element.76), channel_id=1, source_target_pairs={{0,24},{4,28},{8,0},{12,4},{16,8},{20,12},{24,16},{28,20},{1,25},{... | collective-permute-start | bytes 104456 | tf_op jit(solution)/shard_map/ppermute | solution.py:642
  84.5 6.0 %collective-permute-start.10 = (bf16[136,128]{1,0:T(8,128)(2,1)S(1)}, bf16[136,128]{1,0:T(8,128)(2,1)S(1)}, u32[]{:S(2)}, u32[]{:S(2)}) collective-permute-start(bf16[136,128]{1,0:T(8,128)(2,1)S(1)} %get-tuple-element.77), channel_id=1, source_target_pairs={{0,20},{4,24},{8,28},{12,0},{16,4},{20,8},{24,12},{28,16},{1,21},{... | collective-permute-start | bytes 104456 | tf_op jit(solution)/shard_map/ppermute | solution.py:642
  84.5 6.0 %collective-permute-start.9 = (bf16[136,128]{1,0:T(8,128)(2,1)S(1)}, bf16[136,128]{1,0:T(8,128)(2,1)S(1)}, u32[]{:S(2)}, u32[]{:S(2)}) collective-permute-start(bf16[136,128]{1,0:T(8,128)(2,1)S(1)} %get-tuple-element.78), channel_id=1, source_target_pairs={{0,16},{4,20},{8,24},{12,28},{16,0},{20,4},{24,8},{28,12},{1,17},{... | collective-permute-start | bytes 104456 | tf_op jit(solution)/shard_map/ppermute | solution.py:642
  87.5 5.7 %collective-permute-start.8 = (bf16[136,128]{1,0:T(8,128)(2,1)S(1)}, bf16[136,128]{1,0:T(8,128)(2,1)S(1)}, u32[]{:S(2)}, u32[]{:S(2)}) collective-permute-start(bf16[136,128]{1,0:T(8,128)(2,1)S(1)} %get-tuple-element.79), channel_id=1, source_target_pairs={{0,12},{4,16},{8,20},{12,24},{16,28},{20,0},{24,4},{28,8},{1,13},{... | collective-permute-start | bytes 104456 | tf_op jit(solution)/shard_map/ppermute | solution.py:642
  87.5 8.5 %copy-start.11 = (bf16[136,128]{1,0:T(8,128)(2,1)}, bf16[136,128]{1,0:T(8,128)(2,1)S(1)}, u32[]{:S(2)}) copy-start(bf16[136,128]{1,0:T(8,128)(2,1)S(1)} %collective-permute-done.12.refs_7_) | copy-start | bytes 104452
  87.5 7.0 %collective-permute-start.7 = (bf16[136,128]{1,0:T(8,128)(2,1)S(1)}, bf16[136,128]{1,0:T(8,128)(2,1)S(1)}, u32[]{:S(2)}, u32[]{:S(2)}) collective-permute-start(bf16[136,128]{1,0:T(8,128)(2,1)S(1)} %get-tuple-element.80), channel_id=1, source_target_pairs={{0,8},{4,12},{8,16},{12,20},{16,24},{20,28},{24,0},{28,4},{1,9},{5... | collective-permute-start | bytes 104456 | tf_op jit(solution)/shard_map/ppermute | solution.py:642
  89.3 6.6 %copy-start.12 = (bf16[136,128]{1,0:T(8,128)(2,1)}, bf16[136,128]{1,0:T(8,128)(2,1)S(1)}, u32[]{:S(2)}) copy-start(bf16[136,128]{1,0:T(8,128)(2,1)S(1)} %collective-permute-done.11.refs_6_) | copy-start | bytes 104452
  89.3 6.6 %collective-permute-start.6 = (bf16[136,128]{1,0:T(8,128)(2,1)S(1)}, bf16[136,128]{1,0:T(8,128)(2,1)S(1)}, u32[]{:S(2)}, u32[]{:S(2)}) collective-permute-start(bf16[136,128]{1,0:T(8,128)(2,1)S(1)} %get-tuple-element.81), channel_id=1, source_target_pairs={{0,4},{4,8},{8,12},{12,16},{16,20},{20,24},{24,28},{28,0},{1,5},{5... | collective-permute-start | bytes 104456 | tf_op jit(solution)/shard_map/ppermute | solution.py:642
  90.5 5.5 %copy-start.13 = (bf16[136,128]{1,0:T(8,128)(2,1)}, bf16[136,128]{1,0:T(8,128)(2,1)S(1)}, u32[]{:S(2)}) copy-start(bf16[136,128]{1,0:T(8,128)(2,1)S(1)} %collective-permute-done.10.refs_5_) | copy-start | bytes 104452
  90.5 5.5 %copy-start.14 = (bf16[136,128]{1,0:T(8,128)(2,1)}, bf16[136,128]{1,0:T(8,128)(2,1)S(1)}, u32[]{:S(2)}) copy-start(bf16[136,128]{1,0:T(8,128)(2,1)S(1)} %collective-permute-done.9.refs_4_) | copy-start | bytes 104452
  93.2 2.8 %copy-start.15 = (bf16[136,128]{1,0:T(8,128)(2,1)}, bf16[136,128]{1,0:T(8,128)(2,1)S(1)}, u32[]{:S(2)}) copy-start(bf16[136,128]{1,0:T(8,128)(2,1)S(1)} %collective-permute-done.8.refs_3_) | copy-start | bytes 104452
  94.5 1.5 %copy-start.16 = (bf16[136,128]{1,0:T(8,128)(2,1)}, bf16[136,128]{1,0:T(8,128)(2,1)S(1)}, u32[]{:S(2)}) copy-start(bf16[136,128]{1,0:T(8,128)(2,1)S(1)} %collective-permute-done.7.refs_2_) | copy-start | bytes 104452
  96.0 0.6 copy-start.17
  98.1 6.1 %collective-permute-start.19 = (bf16[104,128]{1,0:T(8,128)(2,1)}, bf16[104,128]{1,0:T(8,128)(2,1)S(1)}, u32[]{:S(2)}, u32[]{:S(2)}) collective-permute-start(bf16[104,128]{1,0:T(8,128)(2,1)} %get-tuple-element.50.refs_0_), channel_id=1, source_target_pairs={{0,28},{4,0},{8,4},{12,8},{16,12},{20,16},{24,20},{28,24},{1,29},{... | collective-permute-start | bytes 79880 | tf_op jit(solution)/shard_map/ppermute | solution.py:642
  98.4 7.3 %collective-permute-start.18 = (bf16[104,128]{1,0:T(8,128)(2,1)}, bf16[104,128]{1,0:T(8,128)(2,1)S(1)}, u32[]{:S(2)}, u32[]{:S(2)}) collective-permute-start(bf16[104,128]{1,0:T(8,128)(2,1)} %get-tuple-element.50.refs_0_), channel_id=1, source_target_pairs={{0,24},{4,28},{8,0},{12,4},{16,8},{20,12},{24,16},{28,20},{1,25},{... | collective-permute-start | bytes 79880 | tf_op jit(solution)/shard_map/ppermute | solution.py:642
  99.8 7.9 %collective-permute-start.17 = (bf16[104,128]{1,0:T(8,128)(2,1)}, bf16[104,128]{1,0:T(8,128)(2,1)S(1)}, u32[]{:S(2)}, u32[]{:S(2)}) collective-permute-start(bf16[104,128]{1,0:T(8,128)(2,1)} %get-tuple-element.50.refs_0_), channel_id=1, source_target_pairs={{0,20},{4,24},{8,28},{12,0},{16,4},{20,8},{24,12},{28,16},{1,21},{... | collective-permute-start | bytes 79880 | tf_op jit(solution)/shard_map/ppermute | solution.py:642
  101.3 6.4 %collective-permute-start.16 = (bf16[104,128]{1,0:T(8,128)(2,1)}, bf16[104,128]{1,0:T(8,128)(2,1)S(1)}, u32[]{:S(2)}, u32[]{:S(2)}) collective-permute-start(bf16[104,128]{1,0:T(8,128)(2,1)} %get-tuple-element.50.refs_0_), channel_id=1, source_target_pairs={{0,16},{4,20},{8,24},{12,28},{16,0},{20,4},{24,8},{28,12},{1,17},{... | collective-permute-start | bytes 79880 | tf_op jit(solution)/shard_map/ppermute | solution.py:642
  103.7 5.9 %collective-permute-start.15 = (bf16[104,128]{1,0:T(8,128)(2,1)}, bf16[104,128]{1,0:T(8,128)(2,1)S(1)}, u32[]{:S(2)}, u32[]{:S(2)}) collective-permute-start(bf16[104,128]{1,0:T(8,128)(2,1)} %get-tuple-element.50.refs_0_), channel_id=1, source_target_pairs={{0,12},{4,16},{8,20},{12,24},{16,28},{20,0},{24,4},{28,8},{1,13},{... | collective-permute-start | bytes 79880 | tf_op jit(solution)/shard_map/ppermute | solution.py:642
  104.2 8.2 %copy-start.18 = (bf16[104,128]{1,0:T(8,128)(2,1)}, bf16[104,128]{1,0:T(8,128)(2,1)S(1)}, u32[]{:S(2)}) copy-start(bf16[104,128]{1,0:T(8,128)(2,1)S(1)} %collective-permute-done.19.refs_7_) | copy-start | bytes 79876
  104.2 5.9 %collective-permute-start.14 = (bf16[104,128]{1,0:T(8,128)(2,1)}, bf16[104,128]{1,0:T(8,128)(2,1)S(1)}, u32[]{:S(2)}, u32[]{:S(2)}) collective-permute-start(bf16[104,128]{1,0:T(8,128)(2,1)} %get-tuple-element.50.refs_0_), channel_id=1, source_target_pairs={{0,8},{4,12},{8,16},{12,20},{16,24},{20,28},{24,0},{28,4},{1,9},{5... | collective-permute-start | bytes 79880 | tf_op jit(solution)/shard_map/ppermute | solution.py:642
  105.7 6.8 %copy-start.19 = (bf16[104,128]{1,0:T(8,128)(2,1)}, bf16[104,128]{1,0:T(8,128)(2,1)S(1)}, u32[]{:S(2)}) copy-start(bf16[104,128]{1,0:T(8,128)(2,1)S(1)} %collective-permute-done.18.refs_6_) | copy-start | bytes 79876
  105.7 6.8 %collective-permute-start.13 = (bf16[104,128]{1,0:T(8,128)(2,1)}, bf16[104,128]{1,0:T(8,128)(2,1)S(1)}, u32[]{:S(2)}, u32[]{:S(2)}) collective-permute-start(bf16[104,128]{1,0:T(8,128)(2,1)} %get-tuple-element.50.refs_0_), channel_id=1, source_target_pairs={{0,4},{4,8},{8,12},{12,16},{16,20},{20,24},{24,28},{28,0},{1,5},{5... | collective-permute-start | bytes 79880 | tf_op jit(solution)/shard_map/ppermute | solution.py:642
  107.7 4.7 %copy-start.20 = (bf16[104,128]{1,0:T(8,128)(2,1)}, bf16[104,128]{1,0:T(8,128)(2,1)S(1)}, u32[]{:S(2)}) copy-start(bf16[104,128]{1,0:T(8,128)(2,1)S(1)} %collective-permute-done.17.refs_5_) | copy-start | bytes 79876
  107.7 4.7 %copy-start.21 = (bf16[104,128]{1,0:T(8,128)(2,1)}, bf16[104,128]{1,0:T(8,128)(2,1)S(1)}, u32[]{:S(2)}) copy-start(bf16[104,128]{1,0:T(8,128)(2,1)S(1)} %collective-permute-done.16.refs_4_) | copy-start | bytes 79876
  109.6 2.9 %copy-start.22 = (bf16[104,128]{1,0:T(8,128)(2,1)}, bf16[104,128]{1,0:T(8,128)(2,1)S(1)}, u32[]{:S(2)}) copy-start(bf16[104,128]{1,0:T(8,128)(2,1)S(1)} %collective-permute-done.15.refs_3_) | copy-start | bytes 79876
  110.1 2.4 %copy-start.23 = (bf16[104,128]{1,0:T(8,128)(2,1)}, bf16[104,128]{1,0:T(8,128)(2,1)S(1)}, u32[]{:S(2)}) copy-start(bf16[104,128]{1,0:T(8,128)(2,1)S(1)} %collective-permute-done.14.refs_2_) | copy-start | bytes 79876
  112.5 0.6 copy-start.24
  115.6 7.4 %copy-start.1 = (bf16[384,128]{1,0:T(8,128)(2,1)}, bf16[384,128]{1,0:T(8,128)(2,1)S(1)}, u32[]{:S(2)}) copy-start(bf16[384,128]{1,0:T(8,128)(2,1)S(1)} %slice.70.refs_0_) | copy-start | bytes 294916
  115.6 3.5 %collective-permute-start.22 = (bf16[384,128]{1,0:T(8,128)(2,1)S(1)}, bf16[384,128]{1,0:T(8,128)(2,1)S(1)}, u32[]{:S(2)}, u32[]{:S(2)}) collective-permute-start(bf16[384,128]{1,0:T(8,128)(2,1)S(1)} %slice.70.refs_0_), channel_id=1, source_target_pairs={{0,3},{1,0},{2,1},{3,2},{4,7},{5,4},{6,5},{7,6},{8,11},{9,8},{10,9... | collective-permute-start | bytes 294920 | tf_op jit(solution)/shard_map/ppermute | solution.py:642
  115.7 7.3 %collective-permute-start.21 = (bf16[384,128]{1,0:T(8,128)(2,1)S(1)}, bf16[384,128]{1,0:T(8,128)(2,1)S(1)}, u32[]{:S(2)}, u32[]{:S(2)}) collective-permute-start(bf16[384,128]{1,0:T(8,128)(2,1)S(1)} %slice.70.refs_0_), channel_id=1, source_target_pairs={{0,2},{1,3},{2,0},{3,1},{4,6},{5,7},{6,4},{7,5},{8,10},{9,11},{10,... | collective-permute-start | bytes 294920 | tf_op jit(solution)/shard_map/ppermute | solution.py:642
  117.3 5.6 %collective-permute-start.20 = (bf16[384,128]{1,0:T(8,128)(2,1)S(1)}, bf16[384,128]{1,0:T(8,128)(2,1)S(1)}, u32[]{:S(2)}, u32[]{:S(2)}) collective-permute-start(bf16[384,128]{1,0:T(8,128)(2,1)S(1)} %slice.70.refs_0_), channel_id=1, source_target_pairs={{0,1},{1,2},{2,3},{3,0},{4,5},{5,6},{6,7},{7,4},{8,9},{9,10},{10,1... | collective-permute-start | bytes 294920 | tf_op jit(solution)/shard_map/ppermute | solution.py:642
  119.1 3.9 %copy-start.8 = (bf16[384,128]{1,0:T(8,128)(2,1)}, bf16[384,128]{1,0:T(8,128)(2,1)S(1)}, u32[]{:S(2)}) copy-start(bf16[384,128]{1,0:T(8,128)(2,1)S(1)} %collective-permute-done.22.refs_3_) | copy-start | bytes 294916
  123.0 0.6 copy-start.9
  123.0 0.7 copy-start.10

commit v3 on v1

v3 whole, which is shorter than its diff:
```python
import functools
import math

import jax
import jax.numpy as jnp
from jax import lax
from jax.experimental import pallas as pl
from jax.experimental.pallas import tpu as pltpu
from jax.sharding import PartitionSpec as P

D = 128
FF = 512
HEADS = 8
HEAD_DIM = 16
QUERIES = 32
STEPS = 4
STEP = 4
TOK_SEQ = 128
ROWS_SEQ = 256
PAIRS = HEADS // 2

NORM_EPSILON = 1e-05
MOMENTUM_DECAY = 0.9
BASE_RATE = 0.1
HIDDEN_SCORE = -1e30
LAG = 1
SCALE = 1.0 / math.sqrt(HEAD_DIM)
LOG2E = math.log2(math.e)

TRUNK_ROWS = 384
STEM_ROWS = 416
VEC_ROWS = 32
PIECE_ROWS = TRUNK_ROWS + STEM_ROWS

BF = jnp.bfloat16
F32 = jnp.float32
VMEM_LIMIT = 56 * 1024 * 1024


def mm(a, b):
    return lax.dot_general(a, b, (((1,), (0,)), ((), ())), preferred_element_type=F32)


def mm_nt(a, b):
    return lax.dot_general(a, b, (((1,), (1,)), ((), ())), preferred_element_type=F32)


def scores_back(probs, grad, axis):
    product = probs * grad
    return (product - probs * jnp.sum(product, axis=axis, keepdims=True)).astype(BF)


def head_pair(source, j):
    pieces = []
    if j:
        pieces.append(jnp.zeros((32 * j, 256), BF))
    zero = jnp.zeros((16, 128), BF)
    one = source[32 * j : 32 * j + 16]
    two = source[32 * j + 16 : 32 * j + 32]
    pieces.append(jnp.concatenate([one, zero], axis=1))
    pieces.append(jnp.concatenate([zero, two], axis=1))
    if j < PAIRS - 1:
        pieces.append(jnp.zeros((128 - 32 * j - 32, 256), BF))
    return jnp.concatenate(pieces, axis=0)


def pair_rows(source, j):
    zero = jnp.zeros((16, 128), BF)
    one = source[32 * j : 32 * j + 16]
    two = source[32 * j + 16 : 32 * j + 32]
    return jnp.concatenate(
        [jnp.concatenate([one, zero], axis=1), jnp.concatenate([zero, two], axis=1)], axis=0
    )


def pair_pick(both):
    return jnp.concatenate([both[:16, :128], both[16:, 128:]], axis=0)


def main_kernel(
    group,
    rel_ref,
    seg_ref,
    pos_ref,
    rows_ref,
    cot_ref,
    own_ref,
    one_ref,
    two_ref,
    three_ref,
    mats_ref,
    down_ref,
    vec_ref,
    out_ref,
    rgrad_ref,
    keep_ref,
    give_ref,
    sums_ref,
    s_k,
    s_qb,
    s_a,
    s_a2,
    s_v,
    s_vT,
    s_out,
    s_outT,
    t_qkvT,
    t_qkv,
    t_o,
    t_oT,
    t_in,
    t_inT,
    t_dn,
    t_dnT,
    vecs,
    a_qkv,
    a_o,
    a_in,
    a_dn,
    a_vec,
    a_a,
    a_v,
    a_out,
):
    step = pl.program_id(0)

    head_mask = (
        lax.broadcasted_iota(jnp.int32, (256, 128), 0) // 32
        == lax.broadcasted_iota(jnp.int32, (256, 128), 1) // 16
    )

    @pl.when(step == 0)
    def _():
        for k, ref in enumerate((own_ref, one_ref, two_ref, three_ref)):
            wk, wv, wo = ref[0:128], ref[128:256], ref[256:384]
            queries = ref[384:416].astype(F32)
            tiled = jnp.where(head_mask, jnp.concatenate([queries] * HEADS, axis=0), 0.0)
            block = tiled.T.astype(BF)
            both = mm(wk, block) * SCALE
            s_k[k] = wk
            s_qb[k] = block
            s_a[k] = both.astype(BF)
            s_a2[k] = (both * LOG2E).astype(BF)
            s_v[k] = wv
            s_vT[k] = wv.T
            s_out[k] = wo
            s_outT[k] = wo.T
        mats = mats_ref[...].astype(BF)
        for c in range(5):
            vecs[c] = jnp.broadcast_to(vec_ref[c : c + 1], (128, 128)).T
        corner = lax.broadcasted_iota(jnp.int32, (128, 16), 1)

        def beside(column):
            column = jnp.broadcast_to(column, (128, 16))
            high = column.astype(BF).astype(F32)
            return jnp.where(corner == 0, high, jnp.where(corner == 1, column - high, 0.0)).astype(BF)

        for c in range(7):
            where = 128 * c if c < 3 else 128 * (c + 1)
            block = mats[:, where : where + 128].astype(F32)
            gain, bias = (vecs[0], vecs[1]) if c < 3 else (vecs[2], vecs[3])
            scaled = (block * gain).astype(BF)
            shift = jnp.sum((block * bias).T, axis=1, keepdims=True)
            if c < 3:
                t_qkv[:, 128 * c : 128 * c + 128] = scaled
                t_qkvT[128 * c : 128 * c + 128, 0:128] = scaled.T
                t_qkvT[128 * c : 128 * c + 128, 128:144] = beside(shift)
            else:
                d = c - 3
                shift = shift + jnp.broadcast_to(vec_ref[5 + d : 6 + d], (128, 128)).T[:, 0:1]
                t_in[:, 128 * d : 128 * d + 128] = scaled
                t_inT[128 * d : 128 * d + 128, 0:128] = scaled.T
                t_inT[128 * d : 128 * d + 128, 128:144] = beside(shift)
        t_o[...] = mats[:, 384:512]
        t_oT[...] = mats[:, 384:512].T
        down = down_ref[...].astype(BF)
        t_dn[...] = down
        for c in range(4):
            t_dnT[:, 128 * c : 128 * c + 128] = down[128 * c : 128 * c + 128].T
        for ref in (a_qkv, a_o, a_in, a_dn, a_vec, a_a, a_v, a_out):
            ref[...] = jnp.zeros_like(ref)

    lane_block = lax.broadcasted_iota(jnp.int32, (1, 128), 1) // 32
    ones = jnp.ones((16, 128), BF)
    zero = jnp.zeros((16, 128), BF)
    c0 = math.sqrt(2.0 / math.pi)
    c1 = c0 * 0.044715
    masks = [(lane_block == c).astype(BF) for c in range(4)]
    at_block = [lane_block == c for c in range(4)]
    kept = {name: [] for name in ("normed", "gradp", "mixed", "branch", "normed2", "inner", "cot", "active", "sums")}

    def flow(seqs):
        every = range(len(seqs))
        rels = [rel_ref[step * group + b] for b in seqs]
        lanes = [slice(128 * b, 128 * b + 128) for b in every]
        scores = [mm(rows_ref[b], s_a2[e]) for b, e in zip(seqs, rels)]
        rows_T = [rows_ref[b].T for b in seqs]
        value_T = [mm(s_vT[e], rows_T[i]).astype(BF) for i, e in enumerate(rels)]
        yield
        probs, probs_low = [], []
        for b in every:
            probs.append([])
            probs_low.append([])
            for s in range(STEPS):
                halves = []
                for u in range(2):
                    tile = scores[b][64 * s : 64 * s + 64, 128 * u : 128 * u + 128]
                    raised = jnp.exp2(tile - jnp.max(tile, axis=0, keepdims=True))
                    halves.append(raised * (1.0 / jnp.sum(raised, axis=0, keepdims=True)))
                probs[b].append(halves)
                probs_low[b].append([half.astype(BF) for half in halves])
        stem_values = [value_T[b].T for b in every]
        yield
        made = []
        gap = jnp.zeros((64, 128), BF)
        for b in every:
            made.append([])
            for t in range(2):
                made[b].append([])
                for u in range(2):
                    block = jnp.concatenate(
                        [
                            jnp.concatenate([probs_low[b][2 * t][u], gap], axis=1),
                            jnp.concatenate([gap, probs_low[b][2 * t + 1][u]], axis=1),
                        ],
                        axis=0,
                    )
                    made[b][t].append(
                        mm(value_T[b][64 * u : 64 * u + 64, 128 * t : 128 * t + 128], block)
                    )
        stem_mixed = []
        for b in every:
            rows = []
            for h in range(HEADS):
                u, c = divmod(h, 4)
                row = None
                for s in range(STEPS):
                    piece = made[b][s // 2][u][
                        16 * c : 16 * c + 16, 128 * (s % 2) : 128 * (s % 2) + 128
                    ]
                    turn = (s - c) % 4
                    if turn:
                        piece = pltpu.roll(piece, 32 * turn, 1)
                    row = piece if row is None else jnp.where(at_block[s], piece, row)
                rows.append(row)
            stem_mixed.append(jnp.concatenate(rows, axis=0).astype(BF))
        yield
        residual = [mm(s_outT[rels[b]], stem_mixed[b]) for b in every]
        yield

        def norm(values):
            units, inverses = [], []
            for value in values:
                centered = value - jnp.mean(value, axis=0, keepdims=True)
                inverse = lax.rsqrt(
                    jnp.mean(centered * centered, axis=0, keepdims=True) + NORM_EPSILON
                )
                units.append(centered * inverse)
                inverses.append(inverse)
            low = jnp.concatenate([unit.astype(BF) for unit in units], axis=1)
            return units, inverses, jnp.concatenate([low, jnp.ones((16, low.shape[1]), BF)], axis=0)

        def norm_back(gradient, unit, inverse):
            mean_one = jnp.mean(gradient, axis=0, keepdims=True)
            mean_two = jnp.mean(gradient * unit, axis=0, keepdims=True)
            return inverse * (gradient - mean_one - unit * mean_two)

        unit_one, inverse_one, normed = norm(residual)
        yield
        projected = mm(t_qkvT[...], normed)
        query_T = [(projected[:128, lanes[b]] * (LOG2E * SCALE)).astype(BF) for b in every]
        key_T = [projected[128:256, lanes[b]].astype(BF) for b in every]
        value_T = [projected[256:, lanes[b]].astype(BF) for b in every]
        keys = [key_T[b].T for b in every]
        values = [value_T[b].T for b in every]
        hide = []
        for b in seqs:
            base = (step * group + b) * STEPS
            marks = [seg_ref[base + s] for s in range(STEPS)]
            lane_marks = jnp.where(
                at_block[0],
                marks[0],
                jnp.where(at_block[1], marks[1], jnp.where(at_block[2], marks[2], marks[3])),
            )
            hide.append([jnp.where(lane_marks == marks[s], 0.0, HIDDEN_SCORE) for s in range(STEPS)])
        yield
        scores = [[mm(keys[b], head_pair(query_T[b], j)) for j in range(PAIRS)] for b in every]
        cot_list = [cot_ref[b].T for b in seqs]
        yield
        raised = []
        for b in every:
            raised.append([])
            for j in range(PAIRS):
                halves = []
                for u in range(2):
                    tile = scores[b][j][:, 128 * u : 128 * u + 128]
                    tile = jnp.concatenate(
                        [tile[32 * s : 32 * s + 32] + hide[b][s] for s in range(STEPS)], axis=0
                    )
                    halves.append(
                        jnp.exp2(tile - jnp.max(tile, axis=0, keepdims=True)).astype(BF)
                    )
                raised[b].append(jnp.concatenate(halves, axis=1))
        yield
        made = [
            [
                mm(jnp.concatenate([value_T[b][32 * j : 32 * j + 32], ones], axis=0), raised[b][j])
                for j in range(PAIRS)
            ]
            for b in every
        ]
        head_mixed, head_inverse, mixed_list = [], [], []
        for b in every:
            head_mixed.append([])
            head_inverse.append([])
            for h in range(HEADS):
                j, u = divmod(h, 2)
                here = slice(128 * u, 128 * u + 128)
                inverse = 1.0 / made[b][j][32:40, here]
                part = made[b][j][16 * u : 16 * u + 16, here]
                head_inverse[b].append(inverse)
                head_mixed[b].append(
                    jnp.concatenate([part[:8] * inverse, part[8:] * inverse], axis=0)
                )
            mixed_list.append(jnp.concatenate(head_mixed[b], axis=0).astype(BF))
        mixed = jnp.concatenate(mixed_list, axis=1)
        yield
        branch = mm(t_oT[...], mixed)
        hidden = [residual[b] + branch[:, lanes[b]] for b in every]
        yield
        unit_two, inverse_two, normed_two = norm(hidden)
        cot = jnp.concatenate(cot_list, axis=1)
        yield
        inner_all = mm(t_inT[...], normed_two)
        grad_all = mm(t_dn[...], cot)
        yield
        active_rows, grad_rows = [], []
        for r in range(0, FF, 16):
            active_cols, grad_cols = [], []
            for b in every:
                inner = inner_all[r : r + 16, lanes[b]]
                square = inner * inner
                bend = jnp.tanh(inner * (c0 + c1 * square))
                rise = 0.5 + 0.5 * bend
                active = inner * rise
                slope = rise + (active - active * rise) * (2.0 * c0 + (6.0 * c1) * square)
                active_cols.append(active.astype(BF))
                grad_cols.append((grad_all[r : r + 16, lanes[b]] * slope).astype(BF))
            active_rows.append(jnp.concatenate(active_cols, axis=1))
            grad_rows.append(jnp.concatenate(grad_cols, axis=1))
        active = jnp.concatenate(active_rows, axis=0)
        grad_inner = jnp.concatenate(grad_rows, axis=0)
        yield
        grad_all = mm(t_in[...], grad_inner)
        output_all = mm(t_dnT[...], active)
        yield

        grad_hidden = []
        for b in every:
            grad_hidden.append(
                cot_list[b].astype(F32)
                + norm_back(grad_all[:, lanes[b]], unit_two[b], inverse_two[b])
            )
        grad_branch = jnp.concatenate([part.astype(BF) for part in grad_hidden], axis=1)
        yield
        grad_mixed = mm(t_o[...], grad_branch)
        sums = [jnp.zeros((128, 128), F32)] * 3
        for i, b in enumerate(seqs):
            output = hidden[i] + output_all[:, lanes[i]] + vecs[4]
            out_ref[b] = output.astype(BF).T
            sums = [
                sums[0] + cot_list[i].astype(F32),
                sums[1] + output,
                sums[2] + output * output,
            ]
        kept["sums"].append(sums)
        grad_T, drops = [], []
        for b in every:
            scaled = []
            drops.append([])
            for h in range(HEADS):
                inverse = head_inverse[b][h]
                part = grad_mixed[16 * h : 16 * h + 16, lanes[b]]
                part = jnp.concatenate([part[:8] * inverse, part[8:] * inverse], axis=0)
                scaled.append(part.astype(BF))
                drops[b].append(jnp.sum(part * head_mixed[b][h], axis=0, keepdims=True))
            grad_T.append(jnp.concatenate(scaled, axis=0))
        yield
        grad_probs = [[mm(values[b], head_pair(grad_T[b], j)) for j in range(PAIRS)] for b in every]
        grad_values = [
            [mm_nt(pair_rows(grad_T[b], j), raised[b][j]) for j in range(PAIRS)] for b in every
        ]
        yield
        grad_scores = []
        for b in every:
            grad_scores.append([])
            for j in range(PAIRS):
                halves = []
                for u in range(2):
                    here = slice(128 * u, 128 * u + 128)
                    tile = grad_probs[b][j][:, here] - drops[b][2 * j + u]
                    halves.append(tile.astype(BF) * raised[b][j][:, here])
                grad_scores[b].append(jnp.concatenate(halves, axis=1))
        yield
        grad_queries = [
            [pair_pick(mm(key_T[b][32 * j : 32 * j + 32], grad_scores[b][j])) for j in range(PAIRS)]
            for b in every
        ]
        grad_keys = [
            [mm_nt(pair_rows(query_T[b], j), grad_scores[b][j]) for j in range(PAIRS)] for b in every
        ]
        grad_list = []
        for b in every:
            grad_list.append(
                jnp.concatenate(
                    [
                        (jnp.concatenate(grad_queries[b], axis=0) * SCALE).astype(BF),
                        (jnp.concatenate(grad_keys[b], axis=0) * (1.0 / LOG2E)).astype(BF),
                        jnp.concatenate(grad_values[b], axis=0).astype(BF),
                    ],
                    axis=0,
                )
            )
        grad_projected = jnp.concatenate(grad_list, axis=1)
        yield
        grad_all = mm(t_qkv[...], grad_projected)
        for name, value in (
            ("normed", normed),
            ("gradp", grad_projected),
            ("mixed", mixed),
            ("branch", grad_branch),
            ("normed2", normed_two),
            ("inner", grad_inner),
            ("cot", cot),
            ("active", active),
        ):
            kept[name].append(value)
        yield
        grad_tokens = [
            (grad_hidden[b] + norm_back(grad_all[:, lanes[b]], unit_one[b], inverse_one[b])).astype(BF)
            for b in every
        ]
        yield

        grad_mixed = [mm(s_out[rels[b]], grad_tokens[b]) for b in every]
        for b in every:
            a_out[rels[b]] += mm_nt(stem_mixed[b], grad_tokens[b])
        yield
        spread = []
        for b in every:
            spread.append([])
            turned = [grad_mixed[b].astype(BF)] + [
                pltpu.roll(grad_mixed[b], 32 * k, 1).astype(BF) for k in range(1, 4)
            ]
            for s in range(STEPS):
                pieces = []
                for h in range(HEADS):
                    c = h % 4
                    piece = turned[(c - s) % 4][16 * h : 16 * h + 16] * masks[c]
                    pieces.append(
                        jnp.concatenate([piece, zero] if h < 4 else [zero, piece], axis=1)
                    )
                spread[b].append(jnp.concatenate(pieces, axis=0))
        yield
        grad_probs = [
            [mm(stem_values[b][64 * s : 64 * s + 64], spread[b][s]) for s in range(STEPS)]
            for b in every
        ]
        grad_values = [
            jnp.concatenate(
                [
                    mm_nt(jnp.concatenate(probs_low[b][s], axis=1), spread[b][s]).astype(BF)
                    for s in range(STEPS)
                ],
                axis=0,
            )
            for b in every
        ]
        yield
        grad_scores = []
        for b in every:
            steps = []
            for s in range(STEPS):
                steps.append(
                    jnp.concatenate(
                        [
                            scores_back(probs[b][s][u], grad_probs[b][s][:, 128 * u : 128 * u + 128], 0)
                            for u in range(2)
                        ],
                        axis=1,
                    )
                )
            grad_scores.append(jnp.concatenate(steps, axis=0))
        yield
        for i, b in enumerate(seqs):
            e = rels[i]
            made = mm_nt(s_a[e], grad_scores[i]) + mm_nt(s_v[e], grad_values[i])
            rgrad_ref[b] = made.astype(BF).T
        yield
        for i, b in enumerate(seqs):
            e = rels[i]
            rows_T = rows_ref[b].T
            a_a[e] += mm(rows_T, grad_scores[i])
            a_v[e] += mm(rows_T, grad_values[i])

    part = 2
    flows = [flow(range(part * g, part * g + part)) for g in range(group // part)]
    live, wave = len(flows), 0
    while live:
        live = 0
        for g, one in enumerate(flows):
            if wave < LAG * g:
                live += 1
                continue
            try:
                next(one)
                live += 1
            except StopIteration:
                pass
        wave += 1

    def side(name):
        return jnp.concatenate(kept[name], axis=1)

    a_dn[...] += mm_nt(side("cot"), side("active"))
    a_in[...] += mm_nt(side("normed2"), side("inner"))
    a_o[...] += mm_nt(side("mixed"), side("branch"))
    a_qkv[...] += mm_nt(side("normed"), side("gradp"))
    for c in range(3):
        total = kept["sums"][0][c]
        for sums in kept["sums"][1:]:
            total = total + sums[c]
        a_vec[c] += total

    @pl.when(step == pl.num_programs(0) - 1)
    def _():
        me = pos_ref[0]

        def exact(left, right):
            high = left.astype(BF)
            return mm(high, right) + mm((left - high.astype(F32)).astype(BF), right)

        mats = mats_ref[...].astype(BF).astype(F32)
        blocks, gains, biases = [], [None, None], [None, None]
        for c in range(8):
            if c == 3:
                blocks.append(a_o[...])
                continue
            n = 0 if c < 3 else 1
            ref, where = (a_qkv, 128 * c) if c < 3 else (a_in, 128 * (c - 4))
            summed = ref[0:128, where : where + 128]
            ones_row = jnp.broadcast_to(ref[128:129, where : where + 128], (128, 128))
            weight = mats[:, 128 * c : 128 * c + 128]
            blocks.append(summed * vecs[2 * n] + ones_row * vecs[2 * n + 1])
            gain, bias = weight * summed, weight * ones_row
            gains[n] = gain if gains[n] is None else gains[n] + gain
            biases[n] = bias if biases[n] is None else biases[n] + bias
        blocks += [a_dn[:, 128 * c : 128 * c + 128].T for c in range(4)]
        count, per = 4, len(blocks) // 4

        def put(place, where, value):
            rows = value.shape[0]
            base = PIECE_ROWS * lax.div(place, 2)

            @pl.when(lax.rem(place, 2) == 0)
            def _():
                keep_ref[pl.ds(base + where, rows)] = value

            @pl.when(lax.rem(place, 2) == 1)
            def _():
                give_ref[pl.ds(base + where, rows)] = value.astype(BF)

        for j in range(count):
            place = jnp.bitwise_xor(me, j)
            for i in range(per):
                put(place, 128 * i, blocks[per * j + i])
        columns = [gains[0], biases[0], gains[1], biases[1], a_vec[0]]
        sums = [jnp.sum(column.T, axis=0, keepdims=True) for column in columns]
        sums += [a_in[128:129, 128 * c : 128 * c + 128] for c in range(4)]
        sums += [jnp.sum(a_vec[c].T, axis=0, keepdims=True) for c in (1, 2)]
        sums.append(jnp.zeros((5, 128), F32))
        sums = jnp.concatenate(sums, axis=0)
        high, low = split_sum(sums)
        sums_ref[...] = sums
        give_ref[2 * PIECE_ROWS : 2 * PIECE_ROWS + 16] = high
        give_ref[2 * PIECE_ROWS + 16 : 2 * PIECE_ROWS + 32] = low
        for k in range(count):
            grad = a_a[k] * SCALE
            grad_high = grad.astype(BF)
            grad_low = (grad - grad_high.astype(F32)).astype(BF)
            key_T = s_k[k].T
            spread = (mm(key_T, grad_high) + mm(key_T, grad_low)).T
            spread = jnp.where(head_mask, spread, 0.0)
            query = spread[0:32]
            for h in range(1, HEADS):
                query = query + spread[32 * h : 32 * h + 32]
            parts = [
                mm_nt(grad_high, s_qb[k]) + mm_nt(grad_low, s_qb[k]),
                a_v[k],
                a_out[k],
                query,
            ]
            base = PIECE_ROWS * (k // 2) + TRUNK_ROWS
            for i, value in enumerate(parts):
                here = slice(base + 128 * i, base + 128 * i + value.shape[0])
                if k % 2:
                    give_ref[here] = value.astype(BF)
                else:
                    keep_ref[here] = value


def split_sum(sums):
    high = sums.astype(BF)
    return high, (sums - high.astype(F32)).astype(BF)


def add_sums(sums_ref, got_ref, start, next_ref, give_ref, give_start):
    total = sums_ref[...] + (
        got_ref[start : start + 16].astype(F32) + got_ref[start + 16 : start + 32].astype(F32)
    )
    next_ref[...] = total
    if give_ref is not None:
        high, low = split_sum(total)
        give_ref[give_start : give_start + 16] = high
        give_ref[give_start + 16 : give_start + 32] = low


def core_kernel(keep_ref, got_ref, sums_ref, own_ref, give_ref, next_ref):
    own_ref[...] = keep_ref[0:PIECE_ROWS] + got_ref[0:PIECE_ROWS].astype(F32)
    give_ref[0:PIECE_ROWS] = (
        keep_ref[PIECE_ROWS : 2 * PIECE_ROWS] + got_ref[PIECE_ROWS : 2 * PIECE_ROWS].astype(F32)
    ).astype(BF)
    add_sums(sums_ref, got_ref, 2 * PIECE_ROWS, next_ref, give_ref, PIECE_ROWS)


def halve_kernel(pos_ref, keep_ref, got_ref, sums_ref, own_ref, give_ref, next_ref):
    odd = lax.rem(pos_ref[1], 2)
    trunk = keep_ref[0:TRUNK_ROWS] + got_ref[0:TRUNK_ROWS].astype(F32)
    stem = keep_ref[TRUNK_ROWS:] + got_ref[TRUNK_ROWS:PIECE_ROWS].astype(F32)
    rest = jnp.zeros((STEM_ROWS - TRUNK_ROWS, D), F32)
    trunk = jnp.concatenate([trunk, rest], axis=0)
    own_ref[...] = jnp.where(odd == 0, trunk, stem)
    give_ref[0:STEM_ROWS] = jnp.where(odd == 0, stem, trunk).astype(BF)
    add_sums(sums_ref, got_ref, PIECE_ROWS, next_ref, give_ref, STEM_ROWS)


def level_kernel(keep_ref, got_ref, sums_ref, own_ref, give_ref, next_ref):
    total = keep_ref[...] + got_ref[0:STEM_ROWS].astype(F32)
    own_ref[...] = total
    give_ref[0:STEM_ROWS] = total.astype(BF)
    add_sums(sums_ref, got_ref, STEM_ROWS, next_ref, give_ref, STEM_ROWS)


def last_kernel(keep_ref, got_ref, sums_ref, own_ref, next_ref):
    own_ref[...] = (keep_ref[...] + got_ref[0:STEM_ROWS].astype(F32)).astype(BF)
    add_sums(sums_ref, got_ref, STEM_ROWS, next_ref, None, 0)


def renew(weight, moment, average, gradient, step_rate):
    new_moment = MOMENTUM_DECAY * moment + gradient
    new_weight = weight - step_rate * (gradient + MOMENTUM_DECAY * new_moment)
    new_average = average + (new_weight - average) / (STEP + 1)
    return (new_moment, new_average, new_weight)


def put_new(outs, where, made):
    outs[0][where], outs[1][where], outs[2][where] = made
    if len(outs) > 3:
        outs[3][where] = made[2].astype(BF)


def renew_stem(token_total, pos_ref, own_ref, got_ref, sums_ref, *refs):
    stem_in, quer_in, vec_in = refs[0:3], refs[3:6], refs[6:9]
    stem_o, quer_o, vec_o, stats_o = refs[9:13], refs[13:17], refs[17:20], refs[20]
    rate = BASE_RATE / math.sqrt(token_total)
    odd = lax.rem(pos_ref[1], 2) == 1
    full = (slice(None), slice(None))
    for i in range(3):
        where = (slice(None), slice(128 * i, 128 * i + 128))
        rows = slice(128 * i, 128 * i + 128)
        grad = jnp.where(odd, own_ref[rows].astype(F32), got_ref[rows].astype(F32))
        put_new(stem_o, where, renew(*[ref[where] for ref in stem_in], grad, rate))
    grad = jnp.where(odd, own_ref[384:416].astype(F32), got_ref[384:416].astype(F32))
    put_new(quer_o, full, renew(*[ref[...] for ref in quer_in], grad, rate))
    put_new(vec_o, full, renew(*[ref[...] for ref in vec_in], sums_ref[0:9], rate))
    mean = sums_ref[9:10] / token_total
    stats_o[0:1] = mean
    stats_o[1:2] = sums_ref[10:11] / token_total - mean * mean


def renew_trunk(token_total, pos_ref, *refs):
    trunk_refs, mats_in, down_in = refs[0:4], refs[4:7], refs[7:10]
    mats_o, down_o, pieces = refs[10:14], refs[14:18], refs[18]
    rate = BASE_RATE / math.sqrt(token_total)
    for k, ref in enumerate(trunk_refs):
        pieces[jnp.bitwise_xor(pos_ref[0], k)] = ref[...].astype(F32)

    def block(i):
        return pieces[i // 3, 128 * (i % 3) : 128 * (i % 3) + 128]

    for i in range(8):
        where = (slice(None), slice(128 * i, 128 * i + 128))
        put_new(mats_o, where, renew(*[ref[where] for ref in mats_in], block(i), rate))
    for i in range(4):
        where = (slice(128 * i, 128 * i + 128), slice(None))
        put_new(down_o, where, renew(*[ref[where] for ref in down_in], block(8 + i), rate))


def vmem_call(kernel, outs, scratch=(), scalars=0):
    in_vmem = pl.BlockSpec(memory_space=pltpu.VMEM)

    def call(*args):
        return pl.pallas_call(
            kernel,
            out_shape=outs,
            in_specs=[pl.BlockSpec(memory_space=pltpu.SMEM)] * scalars
            + [in_vmem] * (len(args) - scalars),
            out_specs=jax.tree.map(lambda _: in_vmem, outs),
            scratch_shapes=list(scratch),
            compiler_params=pltpu.CompilerParams(vmem_limit_bytes=VMEM_LIMIT),
        )(*args)

    return call


def run_main(rel, segments, pos, rows, cot, stems, mats, down, vectors, emb_count):
    seqs = rows.shape[0]
    group = 8
    grid = seqs // group

    def whole(shape):
        return pl.BlockSpec(shape, lambda i, *_: (0,) * len(shape))

    scratch = [
        ((4, 128, 128), BF),
        ((4, 128, 256), BF),
        ((4, 128, 256), BF),
        ((4, 128, 256), BF),
        ((4, 128, 128), BF),
        ((4, 128, 128), BF),
        ((4, 128, 128), BF),
        ((4, 128, 128), BF),
        ((384, 144), BF),
        ((128, 384), BF),
        ((128, 128), BF),
        ((128, 128), BF),
        ((128, 512), BF),
        ((512, 144), BF),
        ((512, 128), BF),
        ((128, 512), BF),
        ((5, 128, 128), F32),
        ((144, 384), F32),
        ((128, 128), F32),
        ((144, 512), F32),
        ((128, 512), F32),
        ((3, 128, 128), F32),
        ((4, 128, 256), F32),
        ((4, 128, 128), F32),
        ((4, 128, 128), F32),
    ]
    return pl.pallas_call(
        functools.partial(main_kernel, group),
        out_shape=(
            jax.ShapeDtypeStruct((seqs, TOK_SEQ, D), BF),
            jax.ShapeDtypeStruct((seqs, ROWS_SEQ, D), BF),
            jax.ShapeDtypeStruct((2 * PIECE_ROWS, D), F32),
            jax.ShapeDtypeStruct((2 * PIECE_ROWS + VEC_ROWS, D), BF),
            jax.ShapeDtypeStruct((16, D), F32),
        ),
        grid_spec=pltpu.PrefetchScalarGridSpec(
            num_scalar_prefetch=3,
            grid=(grid,),
            in_specs=[
                pl.BlockSpec((group, ROWS_SEQ, D), lambda i, *_: (i, 0, 0)),
                pl.BlockSpec((group, TOK_SEQ, D), lambda i, *_: (i, 0, 0)),
            ]
            + [whole((STEM_ROWS, D))] * 4
            + [whole((D, 1024)), whole((FF, D)), whole((9, D))],
            out_specs=(
                pl.BlockSpec((group, TOK_SEQ, D), lambda i, *_: (i, 0, 0)),
                pl.BlockSpec((group, ROWS_SEQ, D), lambda i, *_: (i, 0, 0)),
                whole((2 * PIECE_ROWS, D)),
                whole((2 * PIECE_ROWS + VEC_ROWS, D)),
                whole((16, D)),
            ),
            scratch_shapes=[pltpu.VMEM(shape, dtype) for shape, dtype in scratch],
        ),
        compiler_params=pltpu.CompilerParams(
            vmem_limit_bytes=VMEM_LIMIT, dimension_semantics=("arbitrary",)
        ),
    )(rel, segments, pos, rows, cot, *stems, mats, down, vectors)


def local(
    stem_rows,
    emb_ids,
    segments,
    cotangent,
    trunk_mats,
    mats_momentum,
    mats_average,
    trunk_down,
    down_momentum,
    down_average,
    trunk_vectors,
    vectors_momentum,
    vectors_average,
    stem_mats,
    stem_momentum,
    stem_average,
    stem_queries,
    queries_momentum,
    queries_average,
):
    seqs = stem_rows.shape[0]
    emb_count, dp_count = lax.axis_size("emb"), lax.axis_size("dp")
    emb_me, dp_me = lax.axis_index("emb"), lax.axis_index("dp")
    pos = jnp.stack([emb_me, dp_me]).astype(jnp.int32)
    rel = emb_ids[:, 0] ^ emb_me
    token_total = seqs * TOK_SEQ * dp_count * emb_count

    def swap(value, axis, count, mask):
        return lax.ppermute(value, axis, [(i, i ^ mask) for i in range(count)])

    def spread(value):
        far = swap(value, "emb", emb_count, 2)
        return [value, swap(value, "emb", emb_count, 1), far, swap(far, "emb", emb_count, 1)]

    low = stem_mats[0].astype(BF)
    own = jnp.concatenate(
        [low[:, :D], low[:, D : 2 * D], low[:, 2 * D :], stem_queries[0].astype(BF)], axis=0
    )
    stems = spread(own)

    output, rows_grad, keep, give, sums = run_main(
        rel,
        segments.reshape(-1),
        pos,
        stem_rows.reshape(seqs, ROWS_SEQ, D),
        cotangent,
        stems,
        trunk_mats,
        trunk_down,
        trunk_vectors,
        emb_count,
    )

    f32, bf16 = F32, BF

    def shape(rows, dtype):
        return jax.ShapeDtypeStruct((rows, D), dtype)

    got = swap(give, "emb", emb_count, 1)
    own, give, sums = vmem_call(
        core_kernel, (shape(PIECE_ROWS, f32), shape(PIECE_ROWS + VEC_ROWS, bf16), shape(16, f32))
    )(keep, got, sums)
    got = swap(give, "emb", emb_count, 2)
    half = (shape(STEM_ROWS, f32), shape(STEM_ROWS + VEC_ROWS, bf16), shape(16, f32))
    own, give, sums = vmem_call(halve_kernel, half, scalars=1)(pos, own, got, sums)
    got = swap(give, "dp", dp_count, 1)
    bits = [1 << i for i in range(1, dp_count.bit_length() - 1)]
    if len(bits) == 2:
        bits[1] = bits[0] | bits[1]
    for mask in bits:
        own, give, sums = vmem_call(level_kernel, half)(own, got, sums)
        got = swap(give, "dp", dp_count, mask)
    own, sums = vmem_call(last_kernel, (shape(STEM_ROWS, bf16), shape(16, f32)))(own, got, sums)
    other = swap(own, "dp", dp_count, 1)
    trunk = jnp.where(dp_me % 2 == 0, own[:TRUNK_ROWS], other[:TRUNK_ROWS])
    trunks = spread(trunk)

    def like(array, copy):
        made = [jax.ShapeDtypeStruct(array.shape, F32)] * 3
        return made + ([jax.ShapeDtypeStruct(array.shape, BF)] if copy else [])

    stem_made = vmem_call(
        functools.partial(renew_stem, token_total),
        like(stem_mats[0], True)
        + like(stem_queries[0], True)
        + like(trunk_vectors, False)
        + [jax.ShapeDtypeStruct((2, D), F32)],
        scalars=1,
    )(
        pos,
        own,
        other,
        sums,
        stem_mats[0],
        stem_momentum[0],
        stem_average[0],
        stem_queries[0],
        queries_momentum[0],
        queries_average[0],
        trunk_vectors,
        vectors_momentum,
        vectors_average,
    )
    trunk_made = vmem_call(
        functools.partial(renew_trunk, token_total),
        like(trunk_mats, True) + like(trunk_down, True),
        [pltpu.VMEM((emb_count, TRUNK_ROWS, D), F32)],
        scalars=1,
    )(
        pos,
        *trunks,
        trunk_mats,
        mats_momentum,
        mats_average,
        trunk_down,
        down_momentum,
        down_average,
    )
    stems_new = [part[None] for part in stem_made[:8]]
    return (
        output,
        rows_grad.reshape(stem_rows.shape),
        *trunk_made,
        *stem_made[8:11],
        *stems_new,
        stem_made[11],
    )


def solution(mesh):
    split = P(("dp", "emb"))
    stem = P("emb")
    in_specs = (split,) * 4 + (P(),) * 9 + (stem,) * 6
    out_specs = (split,) * 2 + (P(),) * 11 + (stem,) * 8 + (P(),)
    return jax.shard_map(local, mesh=mesh, in_specs=in_specs, out_specs=out_specs, check_vma=False)
```

time: 220 us -> 113 us (0.51)
  Pallas kernels: 151 us -> 59.8 us
  starting transfers between devices: 29.5 us -> 15.9 us
  local copies, waits for them, and re-layouts: 9.8 us -> 6.65 us
    pallas_call x3 -> x1, Pallas kernels: 146 us -> 44.7 us  [run_main(): pl.pallas_call(functools.partial(main_kernel, group), out_shape=(jax.Shap...]
    ppermute x23 -> x12, starting transfers between devices: 29.5 us -> 15.9 us  [swap(): return lax.ppermute(value, axis, [(i, i ^ mask) for i in range(count)])]
    pallas_call x2 -> x7, Pallas kernels: 5.65 us -> 15.1 us  [call(): pl.pallas_call(kernel, out_shape=outs, in_specs=[pl.BlockSpec(memory_spac...]
    slice x2 -> x0, local copies, waits for them, and re-layouts: 2.44 us -> none  [the longest x1 1.54 us: local(): stem = placed[TRUNK_ROWS:TRUNK_ROWS + STEM_ROWS]]
    unnamed x51 -> x29, local copies, waits for them, and re-layouts: 4.66 us -> 6.02 us
    ppermute x23 -> x12, waiting for transfers between devices: 24.7 us -> 24.9 us  [swap(): return lax.ppermute(value, axis, [(i, i ^ mask) for i in range(count)])]
  transfers between devices with their start and end apart: 23 -> 12, of which waited for: 11 -> 9; matrix products, arithmetic and copies ran while one was open for 2% -> 3% of each run, Pallas kernels for 0% -> 2%
where the time goes in v3:
time: 113 us
  Pallas kernels  59.8 us (53%)
  waiting for transfers between devices  24.9 us (22%)
  starting transfers between devices  15.9 us (14%)
  local copies, waits for them, and re-layouts  6.65 us (6%)
  other arithmetic  4.44 us (4%)
    pallas_call x1, Pallas kernels, run_main(): pl.pallas_call(functools.partial(main_kernel, group), out_shape=(jax.Shap...  44.7 us
    ppermute x12, waiting for transfers between devices, swap(): return lax.ppermute(value, axis, [(i, i ^ mask) for i in range(count)])  24.9 us
    ppermute x12, starting transfers between devices, swap(): return lax.ppermute(value, axis, [(i, i ^ mask) for i in range(count)])  15.9 us
    pallas_call x7, Pallas kernels, call(): pl.pallas_call(kernel, out_shape=outs, in_specs=[pl.BlockSpec(memory_spac...  15.1 us
    unnamed x29, local copies, waits for them, and re-layouts  6.02 us
  transfers between devices with their start and end apart: 12, of which 9 were waited for; matrix products, arithmetic and copies ran while one was open for 3% of the time, Pallas kernels for 2%

profile of v3, /device:TPU:0, one launch (start us, length us, event | category | flops | bytes accessed | tf_op | source)
XLA Modules:
  0.0 112.5 jit_solution(15370000464753349087)
XLA Ops:
  0.7 0.7 bitcast_convert_fusion
  1.4 0.9 bitcast_convert_fusion.1
  2.4 0.0 copy-start
  2.4 0.5 collective-permute-start
  2.9 2.6 %collective-permute-start.1 = (bf16[416,128]{1,0:T(8,128)(2,1)S(1)}, bf16[416,128]{1,0:T(8,128)(2,1)S(1)}, u32[]{:S(2)}, u32[]{:S(2)}) collective-permute-start(bf16[416,128]{1,0:T(8,128)(2,1)S(1)} %pad_maximum_fusion.own_ref), channel_id=1, source_target_pairs={{0,2},{1,3},{2,0},{3,1},{4,6},{5,7},{6,4},{7,5},{8,10},{9,11},{10,... | collective-permute-start | bytes 319496 | tf_op jit(solution)/shard_map/ppermute | solution.py:823
  5.5 1.2 %xor_bitcast_fusion.rel_ref = s32[32]{0:T(128)} fusion(s32[32,1]{0,1:T(1,128)} %param.20, s32[]{:T(128)} %axis_index.22), kind=kLoop, calls=%fused_computation.3 | loop fusion | flops 32 | bytes 260 | tf_op jit(solution)/shard_map/xor | solution.py:819
  6.7 0.8 copy.42
  7.4 0.6 reshape.55.seg_ref
  8.0 1.0 collective-permute-done.1.two_ref
  9.1 0.0 copy-start.9
  9.1 0.0 collective-permute-start.2
  9.1 0.7 pad_add_fusion.pos_ref
  9.7 0.0 collective-permute-done.one_ref
  9.7 0.0 copy-start.8
  9.7 0.7 collective-permute-done.2.three_ref
  10.4 0.0 copy-start.10
  10.4 0.0 copy-done
  10.4 0.0 copy-done.9
  10.4 0.0 copy-done.8
  10.4 0.6 copy-done.10
  11.0 44.7 %shard_map.354 = (bf16[32,128,128]{2,1,0:T(8,128)(2,1)}, bf16[32,256,128]{2,1,0:T(8,128)(2,1)}, f32[1600,128]{1,0:T(8,128)}, bf16[1632,128]{1,0:T(8,128)(2,1)}, f32[16,128]{1,0:T(8,128)}) custom-call(s32[32]{0:T(128)} %xor_bitcast_fusion.rel_ref, s32[128]{0:T(128)} %reshape.55.seg_ref, s32[2]{0:T(128)} %pad_add_fusion.pos_ref, ...), custom_call_target="tpu_custom_call" | custom-call | tf_op jit(solution)/shard_map/pallas_call | solution.py:761
  55.7 0.2 collective-permute-start.3
  56.0 1.8 %collective-permute-done.3.got_ref = bf16[1632,128]{1,0:T(8,128)(2,1)S(1)} collective-permute-done((bf16[1632,128]{1,0:T(8,128)(2,1)}, bf16[1632,128]{1,0:T(8,128)(2,1)S(1)}, u32[]{:S(2)}, u32[]{:S(2)}) %collective-permute-start.3) | collective-permute-done | bytes 417824 | tf_op jit(solution)/shard_map/ppermute | solution.py:823
  57.8 0.0 copy-start.1
  57.8 0.8 copy-done.1
  58.5 2.1 %shard_map.355 = (f32[800,128]{1,0:T(8,128)}, bf16[832,128]{1,0:T(8,128)(2,1)}, f32[16,128]{1,0:T(8,128)}) custom-call(f32[1600,128]{1,0:T(8,128)} %get-tuple-element.63.keep_ref, bf16[1632,128]{1,0:T(8,128)(2,1)} %copy-done.1, f32[16,128]{1,0:T(8,128)} %get-tuple-element.65.sums_ref), custom_call_target="tpu_custom_call" | custom-call | tf_op jit(solution)/shard_map/pallas_call | solution.py:713
  60.7 1.8 %collective-permute-start.4 = (bf16[832,128]{1,0:T(8,128)(2,1)}, bf16[832,128]{1,0:T(8,128)(2,1)S(1)}, u32[]{:S(2)}, u32[]{:S(2)}) collective-permute-start(bf16[832,128]{1,0:T(8,128)(2,1)} %get-tuple-element.67), channel_id=1, source_target_pairs={{0,2},{1,3},{2,0},{3,1},{4,6},{5,7},{6,4},{7,5},{8,10},{9,11},{10,... | collective-permute-start | bytes 638984 | tf_op jit(solution)/shard_map/ppermute | solution.py:823
  62.4 5.8 %collective-permute-done.4.got_ref = bf16[832,128]{1,0:T(8,128)(2,1)S(1)} collective-permute-done((bf16[832,128]{1,0:T(8,128)(2,1)}, bf16[832,128]{1,0:T(8,128)(2,1)S(1)}, u32[]{:S(2)}, u32[]{:S(2)}) %collective-permute-start.4) | collective-permute-done | bytes 213024 | tf_op jit(solution)/shard_map/ppermute | solution.py:823
  68.2 0.0 copy-start.4
  68.2 0.7 copy-done.4
  68.9 1.9 %shard_map.356 = (f32[416,128]{1,0:T(8,128)}, bf16[448,128]{1,0:T(8,128)(2,1)}, f32[16,128]{1,0:T(8,128)}) custom-call(s32[2]{0:T(128)} %pad_add_fusion.pos_ref, f32[800,128]{1,0:T(8,128)} %get-tuple-element.66.keep_ref, bf16[832,128]{1,0:T(8,128)(2,1)} %copy-done.4, f32[16,128]{1,0:T(8,128)} %get-tuple-element.68.sums_ref), custom_call_target="tpu_custom_call" | custom-call | tf_op jit(solution)/shard_map/pallas_call | solution.py:713
  70.8 1.7 %collective-permute-start.5 = (bf16[448,128]{1,0:T(8,128)(2,1)}, bf16[448,128]{1,0:T(8,128)(2,1)S(1)}, u32[]{:S(2)}, u32[]{:S(2)}) collective-permute-start(bf16[448,128]{1,0:T(8,128)(2,1)} %get-tuple-element.70), channel_id=1, source_target_pairs={{0,4},{4,0},{8,12},{12,8},{16,20},{20,16},{24,28},{28,24},{1,5},{5... | collective-permute-start | bytes 344072 | tf_op jit(solution)/shard_map/ppermute | solution.py:823
  72.5 3.3 %collective-permute-done.5.got_ref = bf16[448,128]{1,0:T(8,128)(2,1)S(1)} collective-permute-done((bf16[448,128]{1,0:T(8,128)(2,1)}, bf16[448,128]{1,0:T(8,128)(2,1)S(1)}, u32[]{:S(2)}, u32[]{:S(2)}) %collective-permute-start.5) | collective-permute-done | bytes 114720 | tf_op jit(solution)/shard_map/ppermute | solution.py:823
  75.8 0.0 copy-start.5
  75.8 0.6 copy-done.5
  76.4 1.7 %shard_map.357 = (f32[416,128]{1,0:T(8,128)}, bf16[448,128]{1,0:T(8,128)(2,1)}, f32[16,128]{1,0:T(8,128)}) custom-call(f32[416,128]{1,0:T(8,128)} %get-tuple-element.69.keep_ref, bf16[448,128]{1,0:T(8,128)(2,1)} %copy-done.5, f32[16,128]{1,0:T(8,128)} %get-tuple-element.71.sums_ref), custom_call_target="tpu_custom_call" | custom-call | tf_op jit(solution)/shard_map/pallas_call | solution.py:713
  78.2 1.8 %collective-permute-start.6 = (bf16[448,128]{1,0:T(8,128)(2,1)}, bf16[448,128]{1,0:T(8,128)(2,1)S(1)}, u32[]{:S(2)}, u32[]{:S(2)}) collective-permute-start(bf16[448,128]{1,0:T(8,128)(2,1)} %get-tuple-element.73), channel_id=1, source_target_pairs={{0,8},{4,12},{8,0},{12,4},{16,24},{20,28},{24,16},{28,20},{1,9},{5... | collective-permute-start | bytes 344072 | tf_op jit(solution)/shard_map/ppermute | solution.py:823
  80.0 3.2 %collective-permute-done.6.got_ref = bf16[448,128]{1,0:T(8,128)(2,1)S(1)} collective-permute-done((bf16[448,128]{1,0:T(8,128)(2,1)}, bf16[448,128]{1,0:T(8,128)(2,1)S(1)}, u32[]{:S(2)}, u32[]{:S(2)}) %collective-permute-start.6) | collective-permute-done | bytes 114720 | tf_op jit(solution)/shard_map/ppermute | solution.py:823
  83.2 0.0 copy-start.6
  83.2 0.6 copy-done.6
  83.8 1.7 %shard_map.358 = (f32[416,128]{1,0:T(8,128)}, bf16[448,128]{1,0:T(8,128)(2,1)}, f32[16,128]{1,0:T(8,128)}) custom-call(f32[416,128]{1,0:T(8,128)} %get-tuple-element.72.keep_ref, bf16[448,128]{1,0:T(8,128)(2,1)} %copy-done.6, f32[16,128]{1,0:T(8,128)} %get-tuple-element.74.sums_ref), custom_call_target="tpu_custom_call" | custom-call | tf_op jit(solution)/shard_map/pallas_call | solution.py:713
  85.5 3.8 %collective-permute-start.7 = (bf16[448,128]{1,0:T(8,128)(2,1)}, bf16[448,128]{1,0:T(8,128)(2,1)S(1)}, u32[]{:S(2)}, u32[]{:S(2)}) collective-permute-start(bf16[448,128]{1,0:T(8,128)(2,1)} %get-tuple-element.76), channel_id=1, source_target_pairs={{0,24},{4,28},{8,16},{12,20},{16,8},{20,12},{24,0},{28,4},{1,25},{... | collective-permute-start | bytes 344072 | tf_op jit(solution)/shard_map/ppermute | solution.py:823
  89.4 3.1 %collective-permute-done.7.got_ref = bf16[448,128]{1,0:T(8,128)(2,1)S(1)} collective-permute-done((bf16[448,128]{1,0:T(8,128)(2,1)}, bf16[448,128]{1,0:T(8,128)(2,1)S(1)}, u32[]{:S(2)}, u32[]{:S(2)}) %collective-permute-start.7) | collective-permute-done | bytes 114720 | tf_op jit(solution)/shard_map/ppermute | solution.py:823
  92.5 0.6 copy-done.7
  93.1 1.7 %shard_map.359 = (bf16[416,128]{1,0:T(8,128)(2,1)}, f32[16,128]{1,0:T(8,128)}) custom-call(f32[416,128]{1,0:T(8,128)} %get-tuple-element.75.keep_ref, bf16[448,128]{1,0:T(8,128)(2,1)} %copy-done.7, f32[16,128]{1,0:T(8,128)} %get-tuple-element.77.sums_ref), custom_call_target="tpu_custom_call" | custom-call | tf_op jit(solution)/shard_map/pallas_call | solution.py:713
  94.8 1.7 %collective-permute-start.8 = (bf16[416,128]{1,0:T(8,128)(2,1)}, bf16[416,128]{1,0:T(8,128)(2,1)S(1)}, u32[]{:S(2)}, u32[]{:S(2)}) collective-permute-start(bf16[416,128]{1,0:T(8,128)(2,1)} %get-tuple-element.78.own_ref), channel_id=1, source_target_pairs={{0,4},{4,0},{8,12},{12,8},{16,20},{20,16},{24,28},{28,24},{1,5},{5... | collective-permute-start | bytes 319496 | tf_op jit(solution)/shard_map/ppermute | solution.py:823
  96.5 3.2 %collective-permute-done.8.got_ref = bf16[416,128]{1,0:T(8,128)(2,1)S(1)} collective-permute-done((bf16[416,128]{1,0:T(8,128)(2,1)}, bf16[416,128]{1,0:T(8,128)(2,1)S(1)}, u32[]{:S(2)}, u32[]{:S(2)}) %collective-permute-start.8) | collective-permute-done | bytes 106528 | tf_op jit(solution)/shard_map/ppermute | solution.py:823
  99.7 0.0 copy-start.2
  99.7 0.9 slice_select_fusion.refs_0_
  100.6 0.0 copy-start.3
  100.6 1.8 %collective-permute-start.10 = (bf16[384,128]{1,0:T(8,128)(2,1)S(1)}, bf16[384,128]{1,0:T(8,128)(2,1)S(1)}, u32[]{:S(2)}, u32[]{:S(2)}) collective-permute-start(bf16[384,128]{1,0:T(8,128)(2,1)S(1)} %slice_select_fusion.refs_0_), channel_id=1, source_target_pairs={{0,2},{1,3},{2,0},{3,1},{4,6},{5,7},{6,4},{7,5},{8,10},{9,11},{10,... | collective-permute-start | bytes 294920 | tf_op jit(solution)/shard_map/ppermute | solution.py:823
  102.4 0.0 collective-permute-start.9
  102.4 2.9 %collective-permute-done.10.refs_2_ = bf16[384,128]{1,0:T(8,128)(2,1)S(1)} collective-permute-done((bf16[384,128]{1,0:T(8,128)(2,1)S(1)}, bf16[384,128]{1,0:T(8,128)(2,1)S(1)}, u32[]{:S(2)}, u32[]{:S(2)}) %collective-permute-start.10) | collective-permute-done | bytes 98336 | tf_op jit(solution)/shard_map/ppermute | solution.py:823
  105.3 0.0 collective-permute-start.11
  105.3 0.0 copy-done.2
  105.3 2.3 %shard_map.361 = (f32[128,384]{1,0:T(8,128)}, f32[128,384]{1,0:T(8,128)}, f32[128,384]{1,0:T(8,128)}, bf16[128,384]{1,0:T(8,128)(2,1)}, f32[32,128]{1,0:T(8,128)...) custom-call(s32[2]{0:T(128)} %pad_add_fusion.pos_ref, ...), custom_call_target="tpu_custom_call" | custom-call | tf_op jit(solution)/shard_map/pallas_call | solution.py:713
  107.6 0.0 collective-permute-done.9.refs_1_
  107.6 0.0 copy-start.12
  107.6 0.0 collective-permute-done.11.refs_3_
  107.6 0.0 copy-done.3
  107.6 0.0 copy-done.11
  107.7 0.6 copy-done.12
  108.3 0.6 copy-done.13
  108.9 3.6 %shard_map.360 = (f32[128,1024]{1,0:T(8,128)}, f32[128,1024]{1,0:T(8,128)}, f32[128,1024]{1,0:T(8,128)}, bf16[128,1024]{1,0:T(8,128)(2,1)}, f32[512,128]{1,0:T(8...) custom-call(s32[2]{0:T(128)} %pad_add_fusion.pos_ref, bf16[384,128]{1,0:T(8,128)(2,1)} %copy-done.3, ...), custom_call_target="tpu_custom_call" | custom-call | tf_op jit(solution)/shard_map/pallas_call | solution.py:713
  (5 shorter events, 0.0 us)
Async XLA Ops:
  2.4 8.0 %copy-start = (bf16[416,128]{1,0:T(8,128)(2,1)}, bf16[416,128]{1,0:T(8,128)(2,1)S(1)}, u32[]{:S(2)}) copy-start(bf16[416,128]{1,0:T(8,128)(2,1)S(1)} %pad_maximum_fusion.own_ref) | copy-start | bytes 319492
  2.4 7.3 %collective-permute-start = (bf16[416,128]{1,0:T(8,128)(2,1)S(1)}, bf16[416,128]{1,0:T(8,128)(2,1)S(1)}, u32[]{:S(2)}, u32[]{:S(2)}) collective-permute-start(bf16[416,128]{1,0:T(8,128)(2,1)S(1)} %pad_maximum_fusion.own_ref), channel_id=1, source_target_pairs={{0,1},{1,0},{2,3},{3,2},{4,5},{5,4},{6,7},{7,6},{8,9},{9,8},{10,11... | collective-permute-start | bytes 319496 | tf_op jit(solution)/shard_map/ppermute | solution.py:823
  2.9 6.2 %collective-permute-start.1 = (bf16[416,128]{1,0:T(8,128)(2,1)S(1)}, bf16[416,128]{1,0:T(8,128)(2,1)S(1)}, u32[]{:S(2)}, u32[]{:S(2)}) collective-permute-start(bf16[416,128]{1,0:T(8,128)(2,1)S(1)} %pad_maximum_fusion.own_ref), channel_id=1, source_target_pairs={{0,2},{1,3},{2,0},{3,1},{4,6},{5,7},{6,4},{7,5},{8,10},{9,11},{10,... | collective-permute-start | bytes 319496 | tf_op jit(solution)/shard_map/ppermute | solution.py:823
  9.1 1.3 %copy-start.9 = (bf16[416,128]{1,0:T(8,128)(2,1)}, bf16[416,128]{1,0:T(8,128)(2,1)S(1)}, u32[]{:S(2)}) copy-start(bf16[416,128]{1,0:T(8,128)(2,1)S(1)} %collective-permute-done.1.two_ref) | copy-start | bytes 319492
  9.1 1.3 %collective-permute-start.2 = (bf16[416,128]{1,0:T(8,128)(2,1)S(1)}, bf16[416,128]{1,0:T(8,128)(2,1)S(1)}, u32[]{:S(2)}, u32[]{:S(2)}) collective-permute-start(bf16[416,128]{1,0:T(8,128)(2,1)S(1)} %collective-permute-done.1.two_ref), channel_id=1, source_target_pairs={{0,1},{1,0},{2,3},{3,2},{4,5},{5,4},{6,7},{7,6},{8,9},{9,8},{10,11... | collective-permute-start | bytes 319496 | tf_op jit(solution)/shard_map/ppermute | solution.py:823
  9.7 0.7 copy-start.8
  10.4 0.6 copy-start.10
  55.7 2.0 %collective-permute-start.3 = (bf16[1632,128]{1,0:T(8,128)(2,1)}, bf16[1632,128]{1,0:T(8,128)(2,1)S(1)}, u32[]{:S(2)}, u32[]{:S(2)}) collective-permute-start(bf16[1632,128]{1,0:T(8,128)(2,1)} %get-tuple-element.64), channel_id=1, source_target_pairs={{0,1},{1,0},{2,3},{3,2},{4,5},{5,4},{6,7},{7,6},{8,9},{9,8},{10,11... | collective-permute-start | bytes 1253384 | tf_op jit(solution)/shard_map/ppermute | solution.py:823
  57.8 0.8 copy-start.1
  60.7 7.5 %collective-permute-start.4 = (bf16[832,128]{1,0:T(8,128)(2,1)}, bf16[832,128]{1,0:T(8,128)(2,1)S(1)}, u32[]{:S(2)}, u32[]{:S(2)}) collective-permute-start(bf16[832,128]{1,0:T(8,128)(2,1)} %get-tuple-element.67), channel_id=1, source_target_pairs={{0,2},{1,3},{2,0},{3,1},{4,6},{5,7},{6,4},{7,5},{8,10},{9,11},{10,... | collective-permute-start | bytes 638984 | tf_op jit(solution)/shard_map/ppermute | solution.py:823
  68.2 0.7 copy-start.4
  70.8 5.0 %collective-permute-start.5 = (bf16[448,128]{1,0:T(8,128)(2,1)}, bf16[448,128]{1,0:T(8,128)(2,1)S(1)}, u32[]{:S(2)}, u32[]{:S(2)}) collective-permute-start(bf16[448,128]{1,0:T(8,128)(2,1)} %get-tuple-element.70), channel_id=1, source_target_pairs={{0,4},{4,0},{8,12},{12,8},{16,20},{20,16},{24,28},{28,24},{1,5},{5... | collective-permute-start | bytes 344072 | tf_op jit(solution)/shard_map/ppermute | solution.py:823
  75.8 0.6 copy-start.5
  78.2 5.0 %collective-permute-start.6 = (bf16[448,128]{1,0:T(8,128)(2,1)}, bf16[448,128]{1,0:T(8,128)(2,1)S(1)}, u32[]{:S(2)}, u32[]{:S(2)}) collective-permute-start(bf16[448,128]{1,0:T(8,128)(2,1)} %get-tuple-element.73), channel_id=1, source_target_pairs={{0,8},{4,12},{8,0},{12,4},{16,24},{20,28},{24,16},{28,20},{1,9},{5... | collective-permute-start | bytes 344072 | tf_op jit(solution)/shard_map/ppermute | solution.py:823
  83.2 0.6 copy-start.6
  85.5 6.9 %collective-permute-start.7 = (bf16[448,128]{1,0:T(8,128)(2,1)}, bf16[448,128]{1,0:T(8,128)(2,1)S(1)}, u32[]{:S(2)}, u32[]{:S(2)}) collective-permute-start(bf16[448,128]{1,0:T(8,128)(2,1)} %get-tuple-element.76), channel_id=1, source_target_pairs={{0,24},{4,28},{8,16},{12,20},{16,8},{20,12},{24,0},{28,4},{1,25},{... | collective-permute-start | bytes 344072 | tf_op jit(solution)/shard_map/ppermute | solution.py:823
  92.5 0.6 copy-start.7
  94.8 4.9 %collective-permute-start.8 = (bf16[416,128]{1,0:T(8,128)(2,1)}, bf16[416,128]{1,0:T(8,128)(2,1)S(1)}, u32[]{:S(2)}, u32[]{:S(2)}) collective-permute-start(bf16[416,128]{1,0:T(8,128)(2,1)} %get-tuple-element.78.own_ref), channel_id=1, source_target_pairs={{0,4},{4,0},{8,12},{12,8},{16,20},{20,16},{24,28},{28,24},{1,5},{5... | collective-permute-start | bytes 319496 | tf_op jit(solution)/shard_map/ppermute | solution.py:823
  99.7 5.6 %copy-start.2 = (bf16[416,128]{1,0:T(8,128)(2,1)}, bf16[416,128]{1,0:T(8,128)(2,1)S(1)}, u32[]{:S(2)}) copy-start(bf16[416,128]{1,0:T(8,128)(2,1)S(1)} %collective-permute-done.8.got_ref) | copy-start | bytes 319492
  100.6 7.0 %copy-start.3 = (bf16[384,128]{1,0:T(8,128)(2,1)}, bf16[384,128]{1,0:T(8,128)(2,1)S(1)}, u32[]{:S(2)}) copy-start(bf16[384,128]{1,0:T(8,128)(2,1)S(1)} %slice_select_fusion.refs_0_) | copy-start | bytes 294916
  100.6 4.7 %collective-permute-start.10 = (bf16[384,128]{1,0:T(8,128)(2,1)S(1)}, bf16[384,128]{1,0:T(8,128)(2,1)S(1)}, u32[]{:S(2)}, u32[]{:S(2)}) collective-permute-start(bf16[384,128]{1,0:T(8,128)(2,1)S(1)} %slice_select_fusion.refs_0_), channel_id=1, source_target_pairs={{0,2},{1,3},{2,0},{3,1},{4,6},{5,7},{6,4},{7,5},{8,10},{9,11},{10,... | collective-permute-start | bytes 294920 | tf_op jit(solution)/shard_map/ppermute | solution.py:823
  102.4 5.2 %collective-permute-start.9 = (bf16[384,128]{1,0:T(8,128)(2,1)S(1)}, bf16[384,128]{1,0:T(8,128)(2,1)S(1)}, u32[]{:S(2)}, u32[]{:S(2)}) collective-permute-start(bf16[384,128]{1,0:T(8,128)(2,1)S(1)} %slice_select_fusion.refs_0_), channel_id=1, source_target_pairs={{0,1},{1,0},{2,3},{3,2},{4,5},{5,4},{6,7},{7,6},{8,9},{9,8},{10,11... | collective-permute-start | bytes 294920 | tf_op jit(solution)/shard_map/ppermute | solution.py:823
  105.3 2.3 %copy-start.11 = (bf16[384,128]{1,0:T(8,128)(2,1)}, bf16[384,128]{1,0:T(8,128)(2,1)S(1)}, u32[]{:S(2)}) copy-start(bf16[384,128]{1,0:T(8,128)(2,1)S(1)} %collective-permute-done.10.refs_2_) | copy-start | bytes 294916
  105.3 2.3 %collective-permute-start.11 = (bf16[384,128]{1,0:T(8,128)(2,1)S(1)}, bf16[384,128]{1,0:T(8,128)(2,1)S(1)}, u32[]{:S(2)}, u32[]{:S(2)}) collective-permute-start(bf16[384,128]{1,0:T(8,128)(2,1)S(1)} %collective-permute-done.10.refs_2_), channel_id=1, source_target_pairs={{0,1},{1,0},{2,3},{3,2},{4,5},{5,4},{6,7},{7,6},{8,9},{9,8},{10,11... | collective-permute-start | bytes 294920 | tf_op jit(solution)/shard_map/ppermute | solution.py:823
  107.6 0.6 copy-start.12
  108.3 0.6 copy-start.13

commit v4 on v3

--- a/solution.py
+++ b/solution.py
@@ -34,7 +34,7 @@
 
 BF = jnp.bfloat16
 F32 = jnp.float32
-VMEM_LIMIT = 56 * 1024 * 1024
+VMEM_LIMIT = 54 * 1024 * 1024
 
 
 def mm(a, b):
@@ -70,6 +70,29 @@
     two = source[32 * j + 16 : 32 * j + 32]
     return jnp.concatenate(
         [jnp.concatenate([one, zero], axis=1), jnp.concatenate([zero, two], axis=1)], axis=0
+    )
+
+
+def turn_pair(both):
+    return jnp.concatenate([both[:, :128].T, both[:, 128:].T], axis=0)
+
+
+def turn_square(square):
+    return jnp.concatenate(
+        [jnp.concatenate([square[:128, c : c + 128].T, square[128:, c : c + 128].T], axis=1) for c in (0, 128)],
+        axis=0,
+    )
+
+
+def turn_all(wide):
+    return jnp.concatenate(
+        [turn_rows(wide[:, c : c + 128]) for c in range(0, wide.shape[1], 128)], axis=0
+    )
+
+
+def turn_rows(tall):
+    return jnp.concatenate(
+        [tall[i : i + 128].T for i in range(0, tall.shape[0], 128)], axis=1
     )
 
 
@@ -185,7 +208,13 @@
     zero = jnp.zeros((16, 128), BF)
     c0 = math.sqrt(2.0 / math.pi)
     c1 = c0 * 0.044715
+    LOW_M0, LOW_M1, LOW_ONE, LOW_2C0, LOW_6C1 = [
+        jnp.bfloat16(value)
+        for value in (-2.0 * LOG2E * c0, -2.0 * LOG2E * c1, 1.0, 2.0 * c0, 6.0 * c1)
+    ]
     masks = [(lane_block == c).astype(BF) for c in range(4)]
+    lane_head = lax.broadcasted_iota(jnp.int32, (1, 128), 1) // 16
+    head_lanes = [(lane_head == h).astype(BF) for h in range(HEADS)]
     at_block = [lane_block == c for c in range(4)]
     kept = {name: [] for name in ("normed", "gradp", "mixed", "branch", "normed2", "inner", "cot", "active", "sums")}
 
@@ -338,14 +367,14 @@
         for r in range(0, FF, 16):
             active_cols, grad_cols = [], []
             for b in every:
-                inner = inner_all[r : r + 16, lanes[b]]
+                inner = inner_all[r : r + 16, lanes[b]].astype(BF)
                 square = inner * inner
-                bend = jnp.tanh(inner * (c0 + c1 * square))
-                rise = 0.5 + 0.5 * bend
+                bend = jnp.exp2(inner * (LOW_M0 + LOW_M1 * square))
+                rise = pl.reciprocal(LOW_ONE + bend, approx=True)
                 active = inner * rise
-                slope = rise + (active - active * rise) * (2.0 * c0 + (6.0 * c1) * square)
-                active_cols.append(active.astype(BF))
-                grad_cols.append((grad_all[r : r + 16, lanes[b]] * slope).astype(BF))
+                slope = rise + (active - active * rise) * (LOW_2C0 + LOW_6C1 * square)
+                active_cols.append(active)
+                grad_cols.append(grad_all[r : r + 16, lanes[b]].astype(BF) * slope)
             active_rows.append(jnp.concatenate(active_cols, axis=1))
             grad_rows.append(jnp.concatenate(grad_cols, axis=1))
         active = jnp.concatenate(active_rows, axis=0)
@@ -353,6 +382,7 @@
         yield
         grad_all = mm(t_in[...], grad_inner)
         output_all = mm(t_dnT[...], active)
+        turn_inner, turn_active = turn_all(grad_inner), turn_all(active)
         yield
 
         grad_hidden = []
@@ -388,7 +418,7 @@
         yield
         grad_probs = [[mm(values[b], head_pair(grad_T[b], j)) for j in range(PAIRS)] for b in every]
         grad_values = [
-            [mm_nt(pair_rows(grad_T[b], j), raised[b][j]) for j in range(PAIRS)] for b in every
+            [mm(pair_rows(grad_T[b], j), turn_pair(raised[b][j])) for j in range(PAIRS)] for b in every
         ]
         yield
         grad_scores = []
@@ -407,7 +437,7 @@
             for b in every
         ]
         grad_keys = [
-            [mm_nt(pair_rows(query_T[b], j), grad_scores[b][j]) for j in range(PAIRS)] for b in every
+            [mm(pair_rows(query_T[b], j), turn_pair(grad_scores[b][j])) for j in range(PAIRS)] for b in every
         ]
         grad_list = []
         for b in every:
@@ -426,13 +456,13 @@
         grad_all = mm(t_qkv[...], grad_projected)
         for name, value in (
             ("normed", normed),
-            ("gradp", grad_projected),
+            ("gradp", turn_all(grad_projected)),
             ("mixed", mixed),
             ("branch", grad_branch),
             ("normed2", normed_two),
-            ("inner", grad_inner),
+            ("inner", turn_inner),
             ("cot", cot),
-            ("active", active),
+            ("active", turn_active),
         ):
             kept[name].append(value)
         yield
@@ -446,9 +476,19 @@
         for b in every:
             a_out[rels[b]] += mm_nt(stem_mixed[b], grad_tokens[b])
         yield
-        spread = []
+        spread, tall = [], []
         for b in every:
             spread.append([])
+            mixed_tok = grad_mixed[b].astype(BF).T
+            tall.append(
+                [
+                    jnp.concatenate(
+                        [mixed_tok[32 * s : 32 * s + 32] * head_lanes[h] for h in range(HEADS)],
+                        axis=0,
+                    )
+                    for s in range(STEPS)
+                ]
+            )
             turned = [grad_mixed[b].astype(BF)] + [
                 pltpu.roll(grad_mixed[b], 32 * k, 1).astype(BF) for k in range(1, 4)
             ]
@@ -469,7 +509,7 @@
         grad_values = [
             jnp.concatenate(
                 [
-                    mm_nt(jnp.concatenate(probs_low[b][s], axis=1), spread[b][s]).astype(BF)
+                    mm(jnp.concatenate(probs_low[b][s], axis=1), tall[b][s]).astype(BF)
                     for s in range(STEPS)
                 ],
                 axis=0,
@@ -494,7 +534,7 @@
         yield
         for i, b in enumerate(seqs):
             e = rels[i]
-            made = mm_nt(s_a[e], grad_scores[i]) + mm_nt(s_v[e], grad_values[i])
+            made = mm(s_a[e], turn_square(grad_scores[i])) + mm_nt(s_v[e], grad_values[i])
             rgrad_ref[b] = made.astype(BF).T
         yield
         for i, b in enumerate(seqs):
@@ -522,10 +562,13 @@
     def side(name):
         return jnp.concatenate(kept[name], axis=1)
 
-    a_dn[...] += mm_nt(side("cot"), side("active"))
-    a_in[...] += mm_nt(side("normed2"), side("inner"))
+    def stack(name):
+        return jnp.concatenate(kept[name], axis=0)
+
+    a_dn[...] += mm(side("cot"), stack("active"))
+    a_in[...] += mm(side("normed2"), stack("inner"))
     a_o[...] += mm_nt(side("mixed"), side("branch"))
-    a_qkv[...] += mm_nt(side("normed"), side("gradp"))
+    a_qkv[...] += mm(side("normed"), stack("gradp"))
     for c in range(3):
         total = kept["sums"][0][c]
         for sums in kept["sums"][1:]:
@@ -717,7 +760,7 @@
             + [in_vmem] * (len(args) - scalars),
             out_specs=jax.tree.map(lambda _: in_vmem, outs),
             scratch_shapes=list(scratch),
-            compiler_params=pltpu.CompilerParams(vmem_limit_bytes=VMEM_LIMIT),
+            compiler_params=pltpu.CompilerParams(vmem_limit_bytes=8 * 1024 * 1024),
         )(*args)
 
     return call
@@ -725,7 +768,7 @@
 
 def run_main(rel, segments, pos, rows, cot, stems, mats, down, vectors, emb_count):
     seqs = rows.shape[0]
-    group = 8
+    group = 16
     grid = seqs // group
 
     def whole(shape):

time: 113 us -> 88.9 us (0.79)
  Pallas kernels: 59.8 us -> 39.9 us
  local copies, waits for them, and re-layouts: 6.65 us -> 3.98 us
    pallas_call x7, Pallas kernels: 15.1 us -> 4.7 us  [call(): pl.pallas_call(kernel, out_shape=outs, in_specs=[pl.BlockSpec(memory_spac...]
    pallas_call x1, Pallas kernels: 44.7 us -> 35.2 us  [run_main(): pl.pallas_call(functools.partial(main_kernel, group), out_shape=(jax.Shap...]
    unnamed x29 -> x45, local copies, waits for them, and re-layouts: 6.02 us -> 3.34 us
  transfers between devices with their start and end apart: 12 -> 12, of which waited for: 9 -> 9; matrix products, arithmetic and copies ran while one was open for 3% -> 4% of each run, Pallas kernels for 2% -> 2%
where the time goes in v4:
time: 88.9 us; the launch traced here: 88.5 us
  Pallas kernels  39.9 us (45%)
  waiting for transfers between devices  24 us (27%)
  starting transfers between devices  16.3 us (18%)
  local copies, waits for them, and re-layouts  3.98 us (4%)
  other arithmetic  3.44 us (4%)
  between operations  0.95 us (1%)
    pallas_call x1, Pallas kernels, run_main(): pl.pallas_call(functools.partial(main_kernel, group), out_shape=(jax.Shap...  35.2 us
    ppermute x12, waiting for transfers between devices, swap(): return lax.ppermute(value, axis, [(i, i ^ mask) for i in range(count)])  24 us
    ppermute x12, starting transfers between devices, swap(): return lax.ppermute(value, axis, [(i, i ^ mask) for i in range(count)])  16.3 us
    pallas_call x7, Pallas kernels, call(): pl.pallas_call(kernel, out_shape=outs, in_specs=[pl.BlockSpec(memory_spac...  4.7 us
    unnamed x45, local copies, waits for them, and re-layouts  3.34 us
  transfers between devices with their start and end apart: 12, of which 9 were waited for; matrix products, arithmetic and copies ran while one was open for 4% of the time, Pallas kernels for 2%

profile of v4, /device:TPU:0, one launch (start us, length us, event | category | flops | bytes accessed | tf_op | source)
XLA Modules:
  0.0 88.5 jit_solution(17589694787235645312)
XLA Ops:
  0.7 0.7 bitcast_convert_fusion
  1.4 0.9 %bitcast_convert_fusion.1 = bf16[128,384]{1,0:T(8,128)(2,1)S(1)} fusion(f32[1,128,384]{2,1,0:T(8,128)} %param.32), kind=kLoop, calls=%fused_computation.5 | loop fusion | flops 49152 | bytes 294912 | tf_op jit(solution)/shard_map/convert_element_type | solution.py:872
  2.4 0.0 copy-start.18
  2.4 0.5 collective-permute-start
  2.9 2.6 %collective-permute-start.1 = (bf16[416,128]{1,0:T(8,128)(2,1)S(1)}, bf16[416,128]{1,0:T(8,128)(2,1)S(1)}, u32[]{:S(2)}, u32[]{:S(2)}) collective-permute-start(bf16[416,128]{1,0:T(8,128)(2,1)S(1)} %pad_maximum_fusion.own_ref), channel_id=1, source_target_pairs={{0,2},{1,3},{2,0},{3,1},{4,6},{5,7},{6,4},{7,5},{8,10},{9,11},{10,... | collective-permute-start | bytes 319496 | tf_op jit(solution)/shard_map/ppermute | solution.py:866
  5.5 1.2 %xor_bitcast_fusion.rel_ref = s32[32]{0:T(128)} fusion(s32[32,1]{0,1:T(1,128)} %param.20, s32[]{:T(128)} %axis_index.22), kind=kLoop, calls=%fused_computation.3 | loop fusion | flops 32 | bytes 260 | tf_op jit(solution)/shard_map/xor | solution.py:862
  6.7 0.8 copy.42
  7.4 0.6 reshape.55.seg_ref
  8.0 1.0 %collective-permute-done.1.two_ref = bf16[416,128]{1,0:T(8,128)(2,1)S(1)} collective-permute-done((bf16[416,128]{1,0:T(8,128)(2,1)S(1)}, bf16[416,128]{1,0:T(8,128)(2,1)S(1)}, u32[]{:S(2)}, u32[]{:S(2)}) %collective-permute-start.1) | collective-permute-done | bytes 106528 | tf_op jit(solution)/shard_map/ppermute | solution.py:866
  9.1 0.0 collective-permute-start.2
  9.1 0.6 pad_add_fusion.pos_ref
  9.6 0.0 collective-permute-done.one_ref
  9.7 0.7 collective-permute-done.2.three_ref
  10.4 0.0 copy-done.18
  10.4 0.0 copy-done.20
  10.4 0.0 copy-done.19
  10.4 0.6 copy-done.21
  11.0 0.0 copy-start.10
  11.0 0.0 copy-start.11
  11.0 0.0 copy-start.12
  11.1 0.0 copy-start.13
  11.1 0.0 copy-start.14
  11.1 0.0 copy-start.15
  11.1 0.0 copy-start.4
  11.1 0.0 copy-start.5
  11.1 0.0 copy-start.6
  11.1 0.0 copy-start.7
  11.1 35.2 %shard_map.354 = (bf16[32,128,128]{2,1,0:T(8,128)(2,1)}, bf16[32,256,128]{2,1,0:T(8,128)(2,1)}, f32[1600,128]{1,0:T(8,128)}, bf16[1632,128]{1,0:T(8,128)(2,1)}, f32[16,128]{1,0:T(8,128)}) custom-call(s32[32]{0:T(128)} %xor_bitcast_fusion.rel_ref, s32[128]{0:T(128)} %reshape.55.seg_ref, s32[2]{0:T(128)} %pad_add_fusion.pos_ref, ...), custom_call_target="tpu_custom_call" | custom-call | tf_op jit(solution)/shard_map/pallas_call | solution.py:804
  46.4 0.0 copy-start
  46.4 0.0 copy-start.1
  46.4 0.2 collective-permute-start.3
  46.6 1.8 %collective-permute-done.3.got_ref = bf16[1632,128]{1,0:T(8,128)(2,1)S(1)} collective-permute-done((bf16[1632,128]{1,0:T(8,128)(2,1)}, bf16[1632,128]{1,0:T(8,128)(2,1)S(1)}, u32[]{:S(2)}, u32[]{:S(2)}) %collective-permute-start.3) | collective-permute-done | bytes 417824 | tf_op jit(solution)/shard_map/ppermute | solution.py:866
  48.4 1.1 %copy-done.2 = f32[1600,128]{1,0:T(8,128)S(1)} copy-done((f32[1600,128]{1,0:T(8,128)S(1)}, f32[1600,128]{1,0:T(8,128)}, u32[]{:S(2)}) %copy-start.2) | copy-done | bytes 819224
  49.6 0.7 copy-done.16
  50.3 0.1 shard_map.355
  50.4 1.8 %collective-permute-start.4 = (bf16[832,128]{1,0:T(8,128)(2,1)S(1)}, bf16[832,128]{1,0:T(8,128)(2,1)S(1)}, u32[]{:S(2)}, u32[]{:S(2)}) collective-permute-start(bf16[832,128]{1,0:T(8,128)(2,1)S(1)} %get-tuple-element.67), channel_id=1, source_target_pairs={{0,2},{1,3},{2,0},{3,1},{4,6},{5,7},{6,4},{7,5},{8,10},{9,11},{10,... | collective-permute-start | bytes 638984 | tf_op jit(solution)/shard_map/ppermute | solution.py:866
  52.2 5.6 %collective-permute-done.4.got_ref = bf16[832,128]{1,0:T(8,128)(2,1)S(1)} collective-permute-done((bf16[832,128]{1,0:T(8,128)(2,1)S(1)}, bf16[832,128]{1,0:T(8,128)(2,1)S(1)}, u32[]{:S(2)}, u32[]{:S(2)}) %collective-permute-start.4) | collective-permute-done | bytes 213024 | tf_op jit(solution)/shard_map/ppermute | solution.py:866
  57.8 0.0 copy-done.17
  57.8 0.6 shard_map.356
  58.4 1.8 %collective-permute-start.5 = (bf16[448,128]{1,0:T(8,128)(2,1)S(1)}, bf16[448,128]{1,0:T(8,128)(2,1)S(1)}, u32[]{:S(2)}, u32[]{:S(2)}) collective-permute-start(bf16[448,128]{1,0:T(8,128)(2,1)S(1)} %get-tuple-element.70), channel_id=1, source_target_pairs={{0,4},{4,0},{8,12},{12,8},{16,20},{20,16},{24,28},{28,24},{1,5},{5... | collective-permute-start | bytes 344072 | tf_op jit(solution)/shard_map/ppermute | solution.py:866
  60.2 3.1 %collective-permute-done.5.got_ref = bf16[448,128]{1,0:T(8,128)(2,1)S(1)} collective-permute-done((bf16[448,128]{1,0:T(8,128)(2,1)S(1)}, bf16[448,128]{1,0:T(8,128)(2,1)S(1)}, u32[]{:S(2)}, u32[]{:S(2)}) %collective-permute-start.5) | collective-permute-done | bytes 114720 | tf_op jit(solution)/shard_map/ppermute | solution.py:866
  63.3 1.9 %collective-permute-start.6 = (bf16[448,128]{1,0:T(8,128)(2,1)S(1)}, bf16[448,128]{1,0:T(8,128)(2,1)S(1)}, u32[]{:S(2)}, u32[]{:S(2)}) collective-permute-start(bf16[448,128]{1,0:T(8,128)(2,1)S(1)} %get-tuple-element.73), channel_id=1, source_target_pairs={{0,8},{4,12},{8,0},{12,4},{16,24},{20,28},{24,16},{28,20},{1,9},{5... | collective-permute-start | bytes 344072 | tf_op jit(solution)/shard_map/ppermute | solution.py:866
  65.1 3.0 %collective-permute-done.6.got_ref = bf16[448,128]{1,0:T(8,128)(2,1)S(1)} collective-permute-done((bf16[448,128]{1,0:T(8,128)(2,1)S(1)}, bf16[448,128]{1,0:T(8,128)(2,1)S(1)}, u32[]{:S(2)}, u32[]{:S(2)}) %collective-permute-start.6) | collective-permute-done | bytes 114720 | tf_op jit(solution)/shard_map/ppermute | solution.py:866
  68.2 3.9 %collective-permute-start.7 = (bf16[448,128]{1,0:T(8,128)(2,1)S(1)}, bf16[448,128]{1,0:T(8,128)(2,1)S(1)}, u32[]{:S(2)}, u32[]{:S(2)}) collective-permute-start(bf16[448,128]{1,0:T(8,128)(2,1)S(1)} %get-tuple-element.76), channel_id=1, source_target_pairs={{0,24},{4,28},{8,16},{12,20},{16,8},{20,12},{24,0},{28,4},{1,25},{... | collective-permute-start | bytes 344072 | tf_op jit(solution)/shard_map/ppermute | solution.py:866
  72.1 2.9 %collective-permute-done.7.got_ref = bf16[448,128]{1,0:T(8,128)(2,1)S(1)} collective-permute-done((bf16[448,128]{1,0:T(8,128)(2,1)S(1)}, bf16[448,128]{1,0:T(8,128)(2,1)S(1)}, u32[]{:S(2)}, u32[]{:S(2)}) %collective-permute-start.7) | collective-permute-done | bytes 114720 | tf_op jit(solution)/shard_map/ppermute | solution.py:866
  75.0 1.8 %collective-permute-start.8 = (bf16[416,128]{1,0:T(8,128)(2,1)S(1)}, bf16[416,128]{1,0:T(8,128)(2,1)S(1)}, u32[]{:S(2)}, u32[]{:S(2)}) collective-permute-start(bf16[416,128]{1,0:T(8,128)(2,1)S(1)} %get-tuple-element.78.own_ref), channel_id=1, source_target_pairs={{0,4},{4,0},{8,12},{12,8},{16,20},{20,16},{24,28},{28,24},{1,5},{5... | collective-permute-start | bytes 319496 | tf_op jit(solution)/shard_map/ppermute | solution.py:866
  76.7 3.0 %collective-permute-done.8.got_ref = bf16[416,128]{1,0:T(8,128)(2,1)S(1)} collective-permute-done((bf16[416,128]{1,0:T(8,128)(2,1)S(1)}, bf16[416,128]{1,0:T(8,128)(2,1)S(1)}, u32[]{:S(2)}, u32[]{:S(2)}) %collective-permute-start.8) | collective-permute-done | bytes 106528 | tf_op jit(solution)/shard_map/ppermute | solution.py:866
  79.8 1.8 %collective-permute-start.10 = (bf16[384,128]{1,0:T(8,128)(2,1)S(1)}, bf16[384,128]{1,0:T(8,128)(2,1)S(1)}, u32[]{:S(2)}, u32[]{:S(2)}) collective-permute-start(bf16[384,128]{1,0:T(8,128)(2,1)S(1)} %slice_select_fusion.refs_0_), channel_id=1, source_target_pairs={{0,2},{1,3},{2,0},{3,1},{4,6},{5,7},{6,4},{7,5},{8,10},{9,11},{10,... | collective-permute-start | bytes 294920 | tf_op jit(solution)/shard_map/ppermute | solution.py:866
  81.6 0.0 collective-permute-start.9
  81.6 2.9 %collective-permute-done.10.refs_2_ = bf16[384,128]{1,0:T(8,128)(2,1)S(1)} collective-permute-done((bf16[384,128]{1,0:T(8,128)(2,1)S(1)}, bf16[384,128]{1,0:T(8,128)(2,1)S(1)}, u32[]{:S(2)}, u32[]{:S(2)}) %collective-permute-start.10) | collective-permute-done | bytes 98336 | tf_op jit(solution)/shard_map/ppermute | solution.py:866
  84.4 0.0 collective-permute-start.11
  84.4 0.0 copy-done.3
  84.4 0.0 copy-done.8
  84.5 0.0 copy-done.9
  84.5 0.0 copy-done.10
  84.5 0.0 copy-done.11
  84.5 0.0 copy-done.12
  84.5 0.0 copy-done.13
  84.5 0.0 copy-done.14
  84.5 0.0 copy-done.15
  84.5 1.5 %shard_map.361 = (f32[128,384]{1,0:T(8,128)}, f32[128,384]{1,0:T(8,128)}, f32[128,384]{1,0:T(8,128)}, bf16[128,384]{1,0:T(8,128)(2,1)}, f32[32,128]{1,0:T(8,128)...) custom-call(s32[2]{0:T(128)S(1)} %copy-done.17, ...), custom_call_target="tpu_custom_call" | custom-call | tf_op jit(solution)/shard_map/pallas_call | solution.py:756
  86.0 0.0 collective-permute-done.9.refs_1_
  86.0 0.0 collective-permute-done.11.refs_3_
  86.1 2.4 %shard_map.360 = (f32[128,1024]{1,0:T(8,128)}, f32[128,1024]{1,0:T(8,128)}, f32[128,1024]{1,0:T(8,128)}, bf16[128,1024]{1,0:T(8,128)(2,1)}, f32[512,128]{1,0:T(8...) custom-call(s32[2]{0:T(128)S(1)} %copy-done.17, ...), custom_call_target="tpu_custom_call" | custom-call | tf_op jit(solution)/shard_map/pallas_call | solution.py:756
  (21 shorter events, 0.2 us)
Async XLA Ops:
  2.4 8.0 %copy-start.18 = (bf16[416,128]{1,0:T(8,128)(2,1)}, bf16[416,128]{1,0:T(8,128)(2,1)S(1)}, u32[]{:S(2)}) copy-start(bf16[416,128]{1,0:T(8,128)(2,1)S(1)} %pad_maximum_fusion.own_ref) | copy-start | bytes 319492
  2.4 7.3 %collective-permute-start = (bf16[416,128]{1,0:T(8,128)(2,1)S(1)}, bf16[416,128]{1,0:T(8,128)(2,1)S(1)}, u32[]{:S(2)}, u32[]{:S(2)}) collective-permute-start(bf16[416,128]{1,0:T(8,128)(2,1)S(1)} %pad_maximum_fusion.own_ref), channel_id=1, source_target_pairs={{0,1},{1,0},{2,3},{3,2},{4,5},{5,4},{6,7},{7,6},{8,9},{9,8},{10,11... | collective-permute-start | bytes 319496 | tf_op jit(solution)/shard_map/ppermute | solution.py:866
  2.9 6.2 %collective-permute-start.1 = (bf16[416,128]{1,0:T(8,128)(2,1)S(1)}, bf16[416,128]{1,0:T(8,128)(2,1)S(1)}, u32[]{:S(2)}, u32[]{:S(2)}) collective-permute-start(bf16[416,128]{1,0:T(8,128)(2,1)S(1)} %pad_maximum_fusion.own_ref), channel_id=1, source_target_pairs={{0,2},{1,3},{2,0},{3,1},{4,6},{5,7},{6,4},{7,5},{8,10},{9,11},{10,... | collective-permute-start | bytes 319496 | tf_op jit(solution)/shard_map/ppermute | solution.py:866
  9.1 1.3 %copy-start.20 = (bf16[416,128]{1,0:T(8,128)(2,1)}, bf16[416,128]{1,0:T(8,128)(2,1)S(1)}, u32[]{:S(2)}) copy-start(bf16[416,128]{1,0:T(8,128)(2,1)S(1)} %collective-permute-done.1.two_ref) | copy-start | bytes 319492
  9.1 1.3 %collective-permute-start.2 = (bf16[416,128]{1,0:T(8,128)(2,1)S(1)}, bf16[416,128]{1,0:T(8,128)(2,1)S(1)}, u32[]{:S(2)}, u32[]{:S(2)}) collective-permute-start(bf16[416,128]{1,0:T(8,128)(2,1)S(1)} %collective-permute-done.1.two_ref), channel_id=1, source_target_pairs={{0,1},{1,0},{2,3},{3,2},{4,5},{5,4},{6,7},{7,6},{8,9},{9,8},{10,11... | collective-permute-start | bytes 319496 | tf_op jit(solution)/shard_map/ppermute | solution.py:866
  9.6 0.7 copy-start.19
  10.4 0.6 copy-start.21
  11.0 46.8 %copy-start.17 = (s32[2]{0:T(128)S(1)}, s32[2]{0:T(128)}, u32[]{:S(2)}) copy-start(s32[2]{0:T(128)} %pad_add_fusion.pos_ref) | copy-start | bytes 28
  11.0 73.4 %copy-start.3 = (f32[1,128,384]{2,1,0:T(8,128)S(1)}, f32[1,128,384]{2,1,0:T(8,128)}, u32[]{:S(2)}) copy-start(f32[1,128,384]{2,1,0:T(8,128)} %param.32) | copy-start | bytes 589828
  11.0 73.4 %copy-start.8 = (f32[1,128,384]{2,1,0:T(8,128)S(1)}, f32[1,128,384]{2,1,0:T(8,128)}, u32[]{:S(2)}) copy-start(f32[1,128,384]{2,1,0:T(8,128)} %param.33) | copy-start | bytes 589828
  11.0 73.4 %copy-start.9 = (f32[1,128,384]{2,1,0:T(8,128)S(1)}, f32[1,128,384]{2,1,0:T(8,128)}, u32[]{:S(2)}) copy-start(f32[1,128,384]{2,1,0:T(8,128)} %param.34) | copy-start | bytes 589828
  11.0 73.4 %copy-start.10 = (f32[1,32,128]{2,1,0:T(8,128)S(1)}, f32[1,32,128]{2,1,0:T(8,128)}, u32[]{:S(2)}) copy-start(f32[1,32,128]{2,1,0:T(8,128)} %param.35) | copy-start | bytes 49156
  11.0 73.4 %copy-start.11 = (f32[9,128]{1,0:T(8,128)S(1)}, f32[9,128]{1,0:T(8,128)}, u32[]{:S(2)}) copy-start(f32[9,128]{1,0:T(8,128)} %refs_6_.3) | copy-start | bytes 13828
  11.0 73.4 %copy-start.12 = (f32[1,32,128]{2,1,0:T(8,128)S(1)}, f32[1,32,128]{2,1,0:T(8,128)}, u32[]{:S(2)}) copy-start(f32[1,32,128]{2,1,0:T(8,128)} %param.36) | copy-start | bytes 49156
  11.1 73.4 %copy-start.13 = (f32[1,32,128]{2,1,0:T(8,128)S(1)}, f32[1,32,128]{2,1,0:T(8,128)}, u32[]{:S(2)}) copy-start(f32[1,32,128]{2,1,0:T(8,128)} %param.37) | copy-start | bytes 49156
  11.1 73.4 %copy-start.14 = (f32[9,128]{1,0:T(8,128)S(1)}, f32[9,128]{1,0:T(8,128)}, u32[]{:S(2)}) copy-start(f32[9,128]{1,0:T(8,128)} %refs_7_.3) | copy-start | bytes 13828
  11.1 73.4 %copy-start.15 = (f32[9,128]{1,0:T(8,128)S(1)}, f32[9,128]{1,0:T(8,128)}, u32[]{:S(2)}) copy-start(f32[9,128]{1,0:T(8,128)} %refs_8_.3) | copy-start | bytes 13828
  11.1 74.9 %copy-start.4 = (f32[128,1024]{1,0:T(8,128)S(1)}, f32[128,1024]{1,0:T(8,128)}, u32[]{:S(2)}) copy-start(f32[128,1024]{1,0:T(8,128)} %refs_5_.1) | copy-start | bytes 1572868
  11.1 74.9 %copy-start.5 = (f32[128,1024]{1,0:T(8,128)S(1)}, f32[128,1024]{1,0:T(8,128)}, u32[]{:S(2)}) copy-start(f32[128,1024]{1,0:T(8,128)} %refs_6_.2) | copy-start | bytes 1572868
  11.1 74.9 %copy-start.6 = (f32[512,128]{1,0:T(8,128)S(1)}, f32[512,128]{1,0:T(8,128)}, u32[]{:S(2)}) copy-start(f32[512,128]{1,0:T(8,128)} %refs_8_.2) | copy-start | bytes 786436
  11.1 74.9 %copy-start.7 = (f32[512,128]{1,0:T(8,128)S(1)}, f32[512,128]{1,0:T(8,128)}, u32[]{:S(2)}) copy-start(f32[512,128]{1,0:T(8,128)} %refs_9_.1) | copy-start | bytes 786436
  46.4 39.7 %copy-start = (f32[128,1024]{1,0:T(8,128)S(1)}, f32[128,1024]{1,0:T(8,128)}, u32[]{:S(2)}) copy-start(f32[128,1024]{1,0:T(8,128)} %refs_4_.1) | copy-start | bytes 1572868
  46.4 39.7 %copy-start.1 = (f32[512,128]{1,0:T(8,128)S(1)}, f32[512,128]{1,0:T(8,128)}, u32[]{:S(2)}) copy-start(f32[512,128]{1,0:T(8,128)} %refs_7_.2) | copy-start | bytes 786436
  46.4 2.0 %collective-permute-start.3 = (bf16[1632,128]{1,0:T(8,128)(2,1)}, bf16[1632,128]{1,0:T(8,128)(2,1)S(1)}, u32[]{:S(2)}, u32[]{:S(2)}) collective-permute-start(bf16[1632,128]{1,0:T(8,128)(2,1)} %get-tuple-element.64), channel_id=1, source_target_pairs={{0,1},{1,0},{2,3},{3,2},{4,5},{5,4},{6,7},{7,6},{8,9},{9,8},{10,11... | collective-permute-start | bytes 1253384 | tf_op jit(solution)/shard_map/ppermute | solution.py:866
  48.4 1.1 %copy-start.2 = (f32[1600,128]{1,0:T(8,128)S(1)}, f32[1600,128]{1,0:T(8,128)}, u32[]{:S(2)}) copy-start(f32[1600,128]{1,0:T(8,128)} %get-tuple-element.63.keep_ref) | copy-start | bytes 2457604
  49.6 0.7 copy-start.16
  50.4 7.4 %collective-permute-start.4 = (bf16[832,128]{1,0:T(8,128)(2,1)S(1)}, bf16[832,128]{1,0:T(8,128)(2,1)S(1)}, u32[]{:S(2)}, u32[]{:S(2)}) collective-permute-start(bf16[832,128]{1,0:T(8,128)(2,1)S(1)} %get-tuple-element.67), channel_id=1, source_target_pairs={{0,2},{1,3},{2,0},{3,1},{4,6},{5,7},{6,4},{7,5},{8,10},{9,11},{10,... | collective-permute-start | bytes 638984 | tf_op jit(solution)/shard_map/ppermute | solution.py:866
  58.4 4.9 %collective-permute-start.5 = (bf16[448,128]{1,0:T(8,128)(2,1)S(1)}, bf16[448,128]{1,0:T(8,128)(2,1)S(1)}, u32[]{:S(2)}, u32[]{:S(2)}) collective-permute-start(bf16[448,128]{1,0:T(8,128)(2,1)S(1)} %get-tuple-element.70), channel_id=1, source_target_pairs={{0,4},{4,0},{8,12},{12,8},{16,20},{20,16},{24,28},{28,24},{1,5},{5... | collective-permute-start | bytes 344072 | tf_op jit(solution)/shard_map/ppermute | solution.py:866
  63.3 4.9 %collective-permute-start.6 = (bf16[448,128]{1,0:T(8,128)(2,1)S(1)}, bf16[448,128]{1,0:T(8,128)(2,1)S(1)}, u32[]{:S(2)}, u32[]{:S(2)}) collective-permute-start(bf16[448,128]{1,0:T(8,128)(2,1)S(1)} %get-tuple-element.73), channel_id=1, source_target_pairs={{0,8},{4,12},{8,0},{12,4},{16,24},{20,28},{24,16},{28,20},{1,9},{5... | collective-permute-start | bytes 344072 | tf_op jit(solution)/shard_map/ppermute | solution.py:866
  68.2 6.8 %collective-permute-start.7 = (bf16[448,128]{1,0:T(8,128)(2,1)S(1)}, bf16[448,128]{1,0:T(8,128)(2,1)S(1)}, u32[]{:S(2)}, u32[]{:S(2)}) collective-permute-start(bf16[448,128]{1,0:T(8,128)(2,1)S(1)} %get-tuple-element.76), channel_id=1, source_target_pairs={{0,24},{4,28},{8,16},{12,20},{16,8},{20,12},{24,0},{28,4},{1,25},{... | collective-permute-start | bytes 344072 | tf_op jit(solution)/shard_map/ppermute | solution.py:866
  75.0 4.8 %collective-permute-start.8 = (bf16[416,128]{1,0:T(8,128)(2,1)S(1)}, bf16[416,128]{1,0:T(8,128)(2,1)S(1)}, u32[]{:S(2)}, u32[]{:S(2)}) collective-permute-start(bf16[416,128]{1,0:T(8,128)(2,1)S(1)} %get-tuple-element.78.own_ref), channel_id=1, source_target_pairs={{0,4},{4,0},{8,12},{12,8},{16,20},{20,16},{24,28},{28,24},{1,5},{5... | collective-permute-start | bytes 319496 | tf_op jit(solution)/shard_map/ppermute | solution.py:866
  79.8 4.7 %collective-permute-start.10 = (bf16[384,128]{1,0:T(8,128)(2,1)S(1)}, bf16[384,128]{1,0:T(8,128)(2,1)S(1)}, u32[]{:S(2)}, u32[]{:S(2)}) collective-permute-start(bf16[384,128]{1,0:T(8,128)(2,1)S(1)} %slice_select_fusion.refs_0_), channel_id=1, source_target_pairs={{0,2},{1,3},{2,0},{3,1},{4,6},{5,7},{6,4},{7,5},{8,10},{9,11},{10,... | collective-permute-start | bytes 294920 | tf_op jit(solution)/shard_map/ppermute | solution.py:866
  81.6 4.5 %collective-permute-start.9 = (bf16[384,128]{1,0:T(8,128)(2,1)S(1)}, bf16[384,128]{1,0:T(8,128)(2,1)S(1)}, u32[]{:S(2)}, u32[]{:S(2)}) collective-permute-start(bf16[384,128]{1,0:T(8,128)(2,1)S(1)} %slice_select_fusion.refs_0_), channel_id=1, source_target_pairs={{0,1},{1,0},{2,3},{3,2},{4,5},{5,4},{6,7},{7,6},{8,9},{9,8},{10,11... | collective-permute-start | bytes 294920 | tf_op jit(solution)/shard_map/ppermute | solution.py:866
  84.4 1.6 %collective-permute-start.11 = (bf16[384,128]{1,0:T(8,128)(2,1)S(1)}, bf16[384,128]{1,0:T(8,128)(2,1)S(1)}, u32[]{:S(2)}, u32[]{:S(2)}) collective-permute-start(bf16[384,128]{1,0:T(8,128)(2,1)S(1)} %collective-permute-done.10.refs_2_), channel_id=1, source_target_pairs={{0,1},{1,0},{2,3},{3,2},{4,5},{5,4},{6,7},{7,6},{8,9},{9,8},{10,11... | collective-permute-start | bytes 294920 | tf_op jit(solution)/shard_map/ppermute | solution.py:866

commit v5 on v4

--- a/solution.py
+++ b/solution.py
@@ -34,7 +34,7 @@
 
 BF = jnp.bfloat16
 F32 = jnp.float32
-VMEM_LIMIT = 54 * 1024 * 1024
+VMEM_LIMIT = 44 * 1024 * 1024
 
 
 def mm(a, b):
@@ -77,13 +77,6 @@
     return jnp.concatenate([both[:, :128].T, both[:, 128:].T], axis=0)
 
 
-def turn_square(square):
-    return jnp.concatenate(
-        [jnp.concatenate([square[:128, c : c + 128].T, square[128:, c : c + 128].T], axis=1) for c in (0, 128)],
-        axis=0,
-    )
-
-
 def turn_all(wide):
     return jnp.concatenate(
         [turn_rows(wide[:, c : c + 128]) for c in range(0, wide.shape[1], 128)], axis=0
@@ -100,33 +93,12 @@
     return jnp.concatenate([both[:16, :128], both[16:, 128:]], axis=0)
 
 
-def main_kernel(
-    group,
-    rel_ref,
-    seg_ref,
-    pos_ref,
-    rows_ref,
-    cot_ref,
-    own_ref,
-    one_ref,
-    two_ref,
-    three_ref,
+def ready_kernel(
     mats_ref,
     down_ref,
     vec_ref,
-    out_ref,
-    rgrad_ref,
-    keep_ref,
-    give_ref,
-    sums_ref,
-    s_k,
-    s_qb,
-    s_a,
-    s_a2,
-    s_v,
-    s_vT,
-    s_out,
-    s_outT,
+    rel_ref,
+    seg_ref,
     t_qkvT,
     t_qkv,
     t_o,
@@ -136,6 +108,81 @@
     t_dn,
     t_dnT,
     vecs,
+    done_ref,
+):
+    done_ref[...] = jnp.zeros_like(done_ref)
+    mats = mats_ref[...].astype(BF)
+    for c in range(5):
+        vecs[c] = jnp.broadcast_to(vec_ref[c : c + 1], (128, 128)).T
+    corner = lax.broadcasted_iota(jnp.int32, (128, 16), 1)
+
+    def beside(column):
+        column = jnp.broadcast_to(column, (128, 16))
+        high = column.astype(BF).astype(F32)
+        return jnp.where(corner == 0, high, jnp.where(corner == 1, column - high, 0.0)).astype(BF)
+
+    for c in range(7):
+        where = 128 * c if c < 3 else 128 * (c + 1)
+        block = mats[:, where : where + 128].astype(F32)
+        gain, bias = (vecs[0], vecs[1]) if c < 3 else (vecs[2], vecs[3])
+        scaled = (block * gain).astype(BF)
+        shift = jnp.sum((block * bias).T, axis=1, keepdims=True)
+        if c < 3:
+            t_qkv[:, 128 * c : 128 * c + 128] = scaled
+            t_qkvT[128 * c : 128 * c + 128, 0:128] = scaled.T
+            t_qkvT[128 * c : 128 * c + 128, 128:144] = beside(shift)
+        else:
+            d = c - 3
+            shift = shift + jnp.broadcast_to(vec_ref[5 + d : 6 + d], (128, 128)).T[:, 0:1]
+            t_in[:, 128 * d : 128 * d + 128] = scaled
+            t_inT[128 * d : 128 * d + 128, 0:128] = scaled.T
+            t_inT[128 * d : 128 * d + 128, 128:144] = beside(shift)
+    t_o[...] = mats[:, 384:512]
+    t_oT[...] = mats[:, 384:512].T
+    down = down_ref[...].astype(BF)
+    t_dn[...] = down
+    for c in range(4):
+        t_dnT[:, 128 * c : 128 * c + 128] = down[128 * c : 128 * c + 128].T
+
+
+def own_kernel(mats_ref, queries_ref, own_ref):
+    for c in range(3):
+        own_ref[128 * c : 128 * c + 128] = mats_ref[:, 128 * c : 128 * c + 128].astype(BF)
+    own_ref[384:416] = queries_ref[...].astype(BF)
+
+
+def main_kernel(
+    group,
+    rel_ref,
+    seg_ref,
+    rows_hbm,
+    cot_hbm,
+    own_ref,
+    one_ref,
+    two_ref,
+    three_ref,
+    mats_ref,
+    t_qkvT,
+    t_qkv,
+    t_o,
+    t_oT,
+    t_in,
+    t_inT,
+    t_dn,
+    t_dnT,
+    vecs,
+    out_hbm,
+    late_hbm,
+    back_ref,
+    keep_ref,
+    give_ref,
+    sums_ref,
+    s_k,
+    s_qb,
+    s_a2,
+    s_vT,
+    s_out,
+    s_outT,
     a_qkv,
     a_o,
     a_in,
@@ -144,8 +191,35 @@
     a_a,
     a_v,
     a_out,
+    pieces,
+    rows_ref,
+    cot_ref,
+    out_ref,
+    late_ref,
+    sems,
 ):
     step = pl.program_id(0)
+    steps = rows_ref.shape[0] // group
+
+    def moves(g):
+        here = pl.ds(g * group, group)
+        ends = (
+            (rows_hbm, rows_ref),
+            (cot_hbm, cot_ref),
+            (out_ref, out_hbm),
+            (late_ref, late_hbm),
+        )
+        return [
+            pltpu.make_async_copy(one.at[here], two.at[here], sems.at[i, g])
+            for i, (one, two) in enumerate(ends)
+        ]
+
+    @pl.when(step == 0)
+    def _():
+        for g in range(steps):
+            for move in moves(g)[:2]:
+                move.start()
+
 
     head_mask = (
         lax.broadcasted_iota(jnp.int32, (256, 128), 0) // 32
@@ -162,47 +236,18 @@
             both = mm(wk, block) * SCALE
             s_k[k] = wk
             s_qb[k] = block
-            s_a[k] = both.astype(BF)
+            back_ref[k, 0:256] = both.T.astype(BF)
+            back_ref[k, 256:384] = wv.T
             s_a2[k] = (both * LOG2E).astype(BF)
-            s_v[k] = wv
             s_vT[k] = wv.T
             s_out[k] = wo
             s_outT[k] = wo.T
-        mats = mats_ref[...].astype(BF)
-        for c in range(5):
-            vecs[c] = jnp.broadcast_to(vec_ref[c : c + 1], (128, 128)).T
-        corner = lax.broadcasted_iota(jnp.int32, (128, 16), 1)
-
-        def beside(column):
-            column = jnp.broadcast_to(column, (128, 16))
-            high = column.astype(BF).astype(F32)
-            return jnp.where(corner == 0, high, jnp.where(corner == 1, column - high, 0.0)).astype(BF)
-
-        for c in range(7):
-            where = 128 * c if c < 3 else 128 * (c + 1)
-            block = mats[:, where : where + 128].astype(F32)
-            gain, bias = (vecs[0], vecs[1]) if c < 3 else (vecs[2], vecs[3])
-            scaled = (block * gain).astype(BF)
-            shift = jnp.sum((block * bias).T, axis=1, keepdims=True)
-            if c < 3:
-                t_qkv[:, 128 * c : 128 * c + 128] = scaled
-                t_qkvT[128 * c : 128 * c + 128, 0:128] = scaled.T
-                t_qkvT[128 * c : 128 * c + 128, 128:144] = beside(shift)
-            else:
-                d = c - 3
-                shift = shift + jnp.broadcast_to(vec_ref[5 + d : 6 + d], (128, 128)).T[:, 0:1]
-                t_in[:, 128 * d : 128 * d + 128] = scaled
-                t_inT[128 * d : 128 * d + 128, 0:128] = scaled.T
-                t_inT[128 * d : 128 * d + 128, 128:144] = beside(shift)
-        t_o[...] = mats[:, 384:512]
-        t_oT[...] = mats[:, 384:512].T
-        down = down_ref[...].astype(BF)
-        t_dn[...] = down
-        for c in range(4):
-            t_dnT[:, 128 * c : 128 * c + 128] = down[128 * c : 128 * c + 128].T
         for ref in (a_qkv, a_o, a_in, a_dn, a_vec, a_a, a_v, a_out):
             ref[...] = jnp.zeros_like(ref)
 
+    for move in moves(step)[:2]:
+        move.wait()
+    first = step * group
     lane_block = lax.broadcasted_iota(jnp.int32, (1, 128), 1) // 32
     ones = jnp.ones((16, 128), BF)
     zero = jnp.zeros((16, 128), BF)
@@ -220,10 +265,10 @@
 
     def flow(seqs):
         every = range(len(seqs))
-        rels = [rel_ref[step * group + b] for b in seqs]
+        rels = [rel_ref[first + b] for b in seqs]
         lanes = [slice(128 * b, 128 * b + 128) for b in every]
-        scores = [mm(rows_ref[b], s_a2[e]) for b, e in zip(seqs, rels)]
-        rows_T = [rows_ref[b].T for b in seqs]
+        scores = [mm(rows_ref[first + b], s_a2[e]) for b, e in zip(seqs, rels)]
+        rows_T = [rows_ref[first + b].T for b in seqs]
         value_T = [mm(s_vT[e], rows_T[i]).astype(BF) for i, e in enumerate(rels)]
         yield
         probs, probs_low = [], []
@@ -304,8 +349,7 @@
         values = [value_T[b].T for b in every]
         hide = []
         for b in seqs:
-            base = (step * group + b) * STEPS
-            marks = [seg_ref[base + s] for s in range(STEPS)]
+            marks = [seg_ref[(first + b) * STEPS + s] for s in range(STEPS)]
             lane_marks = jnp.where(
                 at_block[0],
                 marks[0],
@@ -314,7 +358,7 @@
             hide.append([jnp.where(lane_marks == marks[s], 0.0, HIDDEN_SCORE) for s in range(STEPS)])
         yield
         scores = [[mm(keys[b], head_pair(query_T[b], j)) for j in range(PAIRS)] for b in every]
-        cot_list = [cot_ref[b].T for b in seqs]
+        cot_list = [cot_ref[first + b].T for b in seqs]
         yield
         raised = []
         for b in every:
@@ -397,7 +441,7 @@
         sums = [jnp.zeros((128, 128), F32)] * 3
         for i, b in enumerate(seqs):
             output = hidden[i] + output_all[:, lanes[i]] + vecs[4]
-            out_ref[b] = output.astype(BF).T
+            out_ref[first + b] = output.astype(BF).T
             sums = [
                 sums[0] + cot_list[i].astype(F32),
                 sums[1] + output,
@@ -534,12 +578,9 @@
         yield
         for i, b in enumerate(seqs):
             e = rels[i]
-            made = mm(s_a[e], turn_square(grad_scores[i])) + mm_nt(s_v[e], grad_values[i])
-            rgrad_ref[b] = made.astype(BF).T
-        yield
-        for i, b in enumerate(seqs):
-            e = rels[i]
-            rows_T = rows_ref[b].T
+            late_ref[first + b, :, 0:256] = grad_scores[i]
+            late_ref[first + b, :, 256:384] = grad_values[i]
+            rows_T = rows_ref[first + b].T
             a_a[e] += mm(rows_T, grad_scores[i])
             a_v[e] += mm(rows_T, grad_values[i])
 
@@ -559,6 +600,9 @@
                 pass
         wave += 1
 
+    for move in moves(step)[2:]:
+        move.start()
+
     def side(name):
         return jnp.concatenate(kept[name], axis=1)
 
@@ -577,7 +621,7 @@
 
     @pl.when(step == pl.num_programs(0) - 1)
     def _():
-        me = pos_ref[0]
+        me = lax.axis_index("emb")
 
         def exact(left, right):
             high = left.astype(BF)
@@ -601,22 +645,16 @@
         blocks += [a_dn[:, 128 * c : 128 * c + 128].T for c in range(4)]
         count, per = 4, len(blocks) // 4
 
-        def put(place, where, value):
-            rows = value.shape[0]
-            base = PIECE_ROWS * lax.div(place, 2)
-
-            @pl.when(lax.rem(place, 2) == 0)
-            def _():
-                keep_ref[pl.ds(base + where, rows)] = value
-
-            @pl.when(lax.rem(place, 2) == 1)
-            def _():
-                give_ref[pl.ds(base + where, rows)] = value.astype(BF)
-
         for j in range(count):
             place = jnp.bitwise_xor(me, j)
             for i in range(per):
-                put(place, 128 * i, blocks[per * j + i])
+                pieces[place, 128 * i : 128 * i + 128] = blocks[per * j + i]
+        for k in range(count):
+            here = slice(PIECE_ROWS * (k // 2), PIECE_ROWS * (k // 2) + TRUNK_ROWS)
+            if k % 2:
+                give_ref[here] = pieces[k].astype(BF)
+            else:
+                keep_ref[here] = pieces[k]
         columns = [gains[0], biases[0], gains[1], biases[1], a_vec[0]]
         sums = [jnp.sum(column.T, axis=0, keepdims=True) for column in columns]
         sums += [a_in[128:129, 128 * c : 128 * c + 128] for c in range(4)]
@@ -650,6 +688,45 @@
                     give_ref[here] = value.astype(BF)
                 else:
                     keep_ref[here] = value
+        for g in range(steps):
+            for move in moves(g)[2:]:
+                move.wait()
+
+
+def rows_kernel(group, rel_ref, late_ref, back_ref, after_ref, out_ref, done_ref):
+    step = pl.program_id(0)
+    done_ref[...] = jnp.zeros_like(done_ref)
+    for b in range(group):
+        out_ref[b] = mm(late_ref[b], back_ref[rel_ref[step * group + b]]).astype(BF)
+
+
+def run_rows(rel, late, back, after, group=8):
+    seqs = late.shape[0]
+    flops = 2 * seqs * ROWS_SEQ * 3 * D * D
+    return pl.pallas_call(
+        functools.partial(rows_kernel, group),
+        out_shape=(
+            jax.ShapeDtypeStruct((seqs, ROWS_SEQ, D), BF),
+            jax.ShapeDtypeStruct((8, D), F32),
+        ),
+        grid_spec=pltpu.PrefetchScalarGridSpec(
+            num_scalar_prefetch=1,
+            grid=(seqs // group,),
+            in_specs=[
+                pl.BlockSpec((group, ROWS_SEQ, 3 * D), lambda i, *_: (i, 0, 0)),
+                pl.BlockSpec(back.shape, lambda i, *_: (0, 0, 0)),
+                pl.BlockSpec(memory_space=pl.ANY),
+            ],
+            out_specs=(
+                pl.BlockSpec((group, ROWS_SEQ, D), lambda i, *_: (i, 0, 0)),
+                pl.BlockSpec((8, D), lambda i, *_: (0, 0)),
+            ),
+        ),
+        cost_estimate=pl.CostEstimate(flops=flops, bytes_accessed=16 * 1024 * 1024, transcendentals=0),
+        compiler_params=pltpu.CompilerParams(
+            vmem_limit_bytes=16 * 1024 * 1024, dimension_semantics=("arbitrary",)
+        ),
+    )(rel, late, back, after)
 
 
 def split_sum(sums):
@@ -676,8 +753,8 @@
     add_sums(sums_ref, got_ref, 2 * PIECE_ROWS, next_ref, give_ref, PIECE_ROWS)
 
 
-def halve_kernel(pos_ref, keep_ref, got_ref, sums_ref, own_ref, give_ref, next_ref):
-    odd = lax.rem(pos_ref[1], 2)
+def halve_kernel(keep_ref, got_ref, sums_ref, after_ref, own_ref, give_ref, next_ref):
+    odd = lax.rem(lax.axis_index("dp"), 2)
     trunk = keep_ref[0:TRUNK_ROWS] + got_ref[0:TRUNK_ROWS].astype(F32)
     stem = keep_ref[TRUNK_ROWS:] + got_ref[TRUNK_ROWS:PIECE_ROWS].astype(F32)
     rest = jnp.zeros((STEM_ROWS - TRUNK_ROWS, D), F32)
@@ -712,11 +789,12 @@
         outs[3][where] = made[2].astype(BF)
 
 
-def renew_stem(token_total, pos_ref, own_ref, got_ref, sums_ref, *refs):
+def renew_stem(token_total, own_ref, got_ref, sums_ref, *refs):
     stem_in, quer_in, vec_in = refs[0:3], refs[3:6], refs[6:9]
     stem_o, quer_o, vec_o, stats_o = refs[9:13], refs[13:17], refs[17:20], refs[20]
+    refs[21][...] = jnp.zeros_like(refs[21])
     rate = BASE_RATE / math.sqrt(token_total)
-    odd = lax.rem(pos_ref[1], 2) == 1
+    odd = lax.rem(lax.axis_index("dp"), 2) == 1
     full = (slice(None), slice(None))
     for i in range(3):
         where = (slice(None), slice(128 * i, 128 * i + 128))
@@ -731,12 +809,16 @@
     stats_o[1:2] = sums_ref[10:11] / token_total - mean * mean
 
 
-def renew_trunk(token_total, pos_ref, *refs):
+def pass_kernel(in_ref, after_ref, out_ref):
+    out_ref[...] = in_ref[...]
+
+
+def renew_trunk(token_total, *refs):
     trunk_refs, mats_in, down_in = refs[0:4], refs[4:7], refs[7:10]
     mats_o, down_o, pieces = refs[10:14], refs[14:18], refs[18]
     rate = BASE_RATE / math.sqrt(token_total)
     for k, ref in enumerate(trunk_refs):
-        pieces[jnp.bitwise_xor(pos_ref[0], k)] = ref[...].astype(F32)
+        pieces[jnp.bitwise_xor(lax.axis_index("emb"), k)] = ref[...].astype(F32)
 
     def block(i):
         return pieces[i // 3, 128 * (i % 3) : 128 * (i % 3) + 128]
@@ -749,7 +831,7 @@
         put_new(down_o, where, renew(*[ref[where] for ref in down_in], block(8 + i), rate))
 
 
-def vmem_call(kernel, outs, scratch=(), scalars=0):
+def vmem_call(kernel, outs, scratch=(), scalars=0, cost=None, after=0):
     in_vmem = pl.BlockSpec(memory_space=pltpu.VMEM)
 
     def call(*args):
@@ -757,32 +839,23 @@
             kernel,
             out_shape=outs,
             in_specs=[pl.BlockSpec(memory_space=pltpu.SMEM)] * scalars
-            + [in_vmem] * (len(args) - scalars),
+            + [in_vmem] * (len(args) - scalars - after)
+            + [pl.BlockSpec(memory_space=pl.ANY)] * after,
             out_specs=jax.tree.map(lambda _: in_vmem, outs),
             scratch_shapes=list(scratch),
+            cost_estimate=cost,
             compiler_params=pltpu.CompilerParams(vmem_limit_bytes=8 * 1024 * 1024),
         )(*args)
 
     return call
 
 
-def run_main(rel, segments, pos, rows, cot, stems, mats, down, vectors, emb_count):
-    seqs = rows.shape[0]
-    group = 16
-    grid = seqs // group
-
-    def whole(shape):
-        return pl.BlockSpec(shape, lambda i, *_: (0,) * len(shape))
-
-    scratch = [
-        ((4, 128, 128), BF),
-        ((4, 128, 256), BF),
-        ((4, 128, 256), BF),
-        ((4, 128, 256), BF),
-        ((4, 128, 128), BF),
-        ((4, 128, 128), BF),
-        ((4, 128, 128), BF),
-        ((4, 128, 128), BF),
+def in_hbm(value):
+    return pltpu.with_memory_space_constraint(value, pltpu.HBM)
+
+
+def run_ready(mats, down, vectors, rel, segments):
+    shapes = [
         ((384, 144), BF),
         ((128, 384), BF),
         ((128, 128), BF),
@@ -792,6 +865,31 @@
         ((512, 128), BF),
         ((128, 512), BF),
         ((5, 128, 128), F32),
+        ((8, 128), F32),
+    ]
+    return vmem_call(
+        ready_kernel,
+        [jax.ShapeDtypeStruct(*shape) for shape in shapes],
+        cost=pl.CostEstimate(flops=0, bytes_accessed=8 * 1024 * 1024, transcendentals=0),
+        after=2,
+    )(in_hbm(mats), in_hbm(down), in_hbm(vectors), rel, segments)
+
+
+def run_main(rel, segments, rows, cot, stems, mats, ready, emb_count):
+    seqs = rows.shape[0]
+    group = 16
+    steps = seqs // group
+
+    def whole(shape, mode=None):
+        return pl.BlockSpec(shape, lambda i, *_: (0,) * len(shape), pipeline_mode=mode)
+
+    scratch = [
+        ((4, 128, 128), BF),
+        ((4, 128, 256), BF),
+        ((4, 128, 256), BF),
+        ((4, 128, 128), BF),
+        ((4, 128, 128), BF),
+        ((4, 128, 128), BF),
         ((144, 384), F32),
         ((128, 128), F32),
         ((144, 512), F32),
@@ -800,38 +898,45 @@
         ((4, 128, 256), F32),
         ((4, 128, 128), F32),
         ((4, 128, 128), F32),
+        ((4, TRUNK_ROWS, D), F32),
+        ((seqs, ROWS_SEQ, D), BF),
+        ((seqs, TOK_SEQ, D), BF),
+        ((seqs, TOK_SEQ, D), BF),
+        ((seqs, ROWS_SEQ, 3 * D), BF),
     ]
+    anywhere = pl.BlockSpec(memory_space=pl.ANY)
     return pl.pallas_call(
         functools.partial(main_kernel, group),
         out_shape=(
             jax.ShapeDtypeStruct((seqs, TOK_SEQ, D), BF),
-            jax.ShapeDtypeStruct((seqs, ROWS_SEQ, D), BF),
+            jax.ShapeDtypeStruct((seqs, ROWS_SEQ, 3 * D), BF),
+            jax.ShapeDtypeStruct((emb_count, 3 * D, D), BF),
             jax.ShapeDtypeStruct((2 * PIECE_ROWS, D), F32),
             jax.ShapeDtypeStruct((2 * PIECE_ROWS + VEC_ROWS, D), BF),
             jax.ShapeDtypeStruct((16, D), F32),
         ),
         grid_spec=pltpu.PrefetchScalarGridSpec(
-            num_scalar_prefetch=3,
-            grid=(grid,),
-            in_specs=[
-                pl.BlockSpec((group, ROWS_SEQ, D), lambda i, *_: (i, 0, 0)),
-                pl.BlockSpec((group, TOK_SEQ, D), lambda i, *_: (i, 0, 0)),
-            ]
+            num_scalar_prefetch=2,
+            grid=(steps,),
+            in_specs=[anywhere, anywhere]
             + [whole((STEM_ROWS, D))] * 4
-            + [whole((D, 1024)), whole((FF, D)), whole((9, D))],
+            + [whole((D, 1024))]
+            + [whole(value.shape, pl.Buffered(1)) for value in ready],
             out_specs=(
-                pl.BlockSpec((group, TOK_SEQ, D), lambda i, *_: (i, 0, 0)),
-                pl.BlockSpec((group, ROWS_SEQ, D), lambda i, *_: (i, 0, 0)),
+                anywhere,
+                anywhere,
+                whole((emb_count, 3 * D, D)),
                 whole((2 * PIECE_ROWS, D)),
                 whole((2 * PIECE_ROWS + VEC_ROWS, D)),
                 whole((16, D)),
             ),
-            scratch_shapes=[pltpu.VMEM(shape, dtype) for shape, dtype in scratch],
+            scratch_shapes=[pltpu.VMEM(shape, dtype) for shape, dtype in scratch]
+            + [pltpu.SemaphoreType.DMA((4, steps))],
         ),
         compiler_params=pltpu.CompilerParams(
             vmem_limit_bytes=VMEM_LIMIT, dimension_semantics=("arbitrary",)
         ),
-    )(rel, segments, pos, rows, cot, *stems, mats, down, vectors)
+    )(rel, segments, in_hbm(rows), in_hbm(cot), *stems, in_hbm(mats), *ready)
 
 
 def local(
@@ -857,34 +962,29 @@
 ):
     seqs = stem_rows.shape[0]
     emb_count, dp_count = lax.axis_size("emb"), lax.axis_size("dp")
-    emb_me, dp_me = lax.axis_index("emb"), lax.axis_index("dp")
-    pos = jnp.stack([emb_me, dp_me]).astype(jnp.int32)
-    rel = emb_ids[:, 0] ^ emb_me
+    rel = emb_ids[:, 0] ^ lax.axis_index("emb")
     token_total = seqs * TOK_SEQ * dp_count * emb_count
 
     def swap(value, axis, count, mask):
         return lax.ppermute(value, axis, [(i, i ^ mask) for i in range(count)])
 
-    def spread(value):
-        far = swap(value, "emb", emb_count, 2)
-        return [value, swap(value, "emb", emb_count, 1), far, swap(far, "emb", emb_count, 1)]
-
-    low = stem_mats[0].astype(BF)
-    own = jnp.concatenate(
-        [low[:, :D], low[:, D : 2 * D], low[:, 2 * D :], stem_queries[0].astype(BF)], axis=0
-    )
-    stems = spread(own)
-
-    output, rows_grad, keep, give, sums = run_main(
+    own = vmem_call(own_kernel, jax.ShapeDtypeStruct((STEM_ROWS, D), BF))(
+        in_hbm(stem_mats[0]), in_hbm(stem_queries[0])
+    )
+    segments = segments.reshape(-1)
+    *ready, ready_done = run_ready(trunk_mats, trunk_down, trunk_vectors, rel, segments)
+    near, far = swap(own, "emb", emb_count, 1), swap(own, "emb", emb_count, 2)
+    far = vmem_call(pass_kernel, jax.ShapeDtypeStruct(far.shape, BF), after=1)(far, ready_done)
+    stems = [own, near, far, swap(far, "emb", emb_count, 1)]
+
+    output, late, back, keep, give, sums = run_main(
         rel,
-        segments.reshape(-1),
-        pos,
+        segments,
         stem_rows.reshape(seqs, ROWS_SEQ, D),
         cotangent,
         stems,
         trunk_mats,
-        trunk_down,
-        trunk_vectors,
+        ready,
         emb_count,
     )
 
@@ -898,8 +998,11 @@
         core_kernel, (shape(PIECE_ROWS, f32), shape(PIECE_ROWS + VEC_ROWS, bf16), shape(16, f32))
     )(keep, got, sums)
     got = swap(give, "emb", emb_count, 2)
+    rows_grad, rows_done = run_rows(rel, late, back, give)
     half = (shape(STEM_ROWS, f32), shape(STEM_ROWS + VEC_ROWS, bf16), shape(16, f32))
-    own, give, sums = vmem_call(halve_kernel, half, scalars=1)(pos, own, got, sums)
+    own, give, sums = vmem_call(halve_kernel, half, after=1)(
+        own, got, sums, rows_done
+    )
     got = swap(give, "dp", dp_count, 1)
     bits = [1 << i for i in range(1, dp_count.bit_length() - 1)]
     if len(bits) == 2:
@@ -909,8 +1012,9 @@
         got = swap(give, "dp", dp_count, mask)
     own, sums = vmem_call(last_kernel, (shape(STEM_ROWS, bf16), shape(16, f32)))(own, got, sums)
     other = swap(own, "dp", dp_count, 1)
-    trunk = jnp.where(dp_me % 2 == 0, own[:TRUNK_ROWS], other[:TRUNK_ROWS])
-    trunks = spread(trunk)
+    trunk = jnp.where(lax.axis_index("dp") % 2 == 0, own[:TRUNK_ROWS], other[:TRUNK_ROWS])
+    far = swap(trunk, "emb", emb_count, 2)
+    near = swap(trunk, "emb", emb_count, 1)
 
     def like(array, copy):
         made = [jax.ShapeDtypeStruct(array.shape, F32)] * 3
@@ -921,10 +1025,9 @@
         like(stem_mats[0], True)
         + like(stem_queries[0], True)
         + like(trunk_vectors, False)
-        + [jax.ShapeDtypeStruct((2, D), F32)],
-        scalars=1,
+        + [jax.ShapeDtypeStruct((2, D), F32), jax.ShapeDtypeStruct((8, D), F32)],
+        cost=pl.CostEstimate(flops=0, bytes_accessed=6 * 1024 * 1024, transcendentals=0),
     )(
-        pos,
         own,
         other,
         sums,
@@ -938,13 +1041,15 @@
         vectors_momentum,
         vectors_average,
     )
+    far = vmem_call(pass_kernel, jax.ShapeDtypeStruct(far.shape, far.dtype), after=1)(
+        far, stem_made[12]
+    )
+    trunks = [trunk, near, far, swap(far, "emb", emb_count, 1)]
     trunk_made = vmem_call(
         functools.partial(renew_trunk, token_total),
         like(trunk_mats, True) + like(trunk_down, True),
         [pltpu.VMEM((emb_count, TRUNK_ROWS, D), F32)],
-        scalars=1,
     )(
-        pos,
         *trunks,
         trunk_mats,
         mats_momentum,

time: 88.9 us -> 81.5 us (0.917)
  local copies, waits for them, and re-layouts: 3.98 us -> 0.94 us
  other arithmetic: 3.44 us -> 0.67 us
  Pallas kernels: 39.9 us -> 42.5 us
  waiting for transfers between devices: 24 us -> 21.6 us
  starting transfers between devices: 16.3 us -> 14.6 us
    pallas_call x0 -> x1, Pallas kernels: none -> 3.86 us  [run_rows(): pl.pallas_call(functools.partial(rows_kernel, group), out_shape=(jax.Shap...]
    pallas_call x1, Pallas kernels: 35.2 us -> 32.7 us  [run_main(): pl.pallas_call(functools.partial(main_kernel, group), out_shape=(jax.Shap...]
    unnamed x45 -> x31, local copies, waits for them, and re-layouts: 3.34 us -> 0.84 us
    ppermute x12, waiting for transfers between devices: 24 us -> 21.6 us  [swap(): return lax.ppermute(value, axis, [(i, i ^ mask) for i in range(count)])]
    convert_element_type x2 -> x0, other arithmetic: 1.66 us -> none  [the longest x1 0.94 us: local(): low = stem_mats[0].astype(BF)]
    ppermute x12, starting transfers between devices: 16.3 us -> 14.6 us  [swap(): return lax.ppermute(value, axis, [(i, i ^ mask) for i in range(count)])]
    pallas_call x7 -> x11, Pallas kernels: 4.7 us -> 5.99 us  [call(): pl.pallas_call(kernel, out_shape=outs, in_specs=[pl.BlockSpec(memory_spac...]
  transfers between devices with their start and end apart: 12 -> 12, of which waited for: 9 -> 9; matrix products, arithmetic and copies ran while one was open for 4% -> 2% of each run, Pallas kernels for 2% -> 8%
where the time goes in v5:
time: 81.5 us; the launch traced here: 81.3 us
  Pallas kernels  42.5 us (52%)
  waiting for transfers between devices  21.6 us (27%)
  starting transfers between devices  14.6 us (18%)
  local copies, waits for them, and re-layouts  0.94 us (1%)
  between operations  0.89 us (1%)
    pallas_call x1, Pallas kernels, run_main(): pl.pallas_call(functools.partial(main_kernel, group), out_shape=(jax.Shap...  32.7 us
    ppermute x12, waiting for transfers between devices, swap(): return lax.ppermute(value, axis, [(i, i ^ mask) for i in range(count)])  21.6 us
    ppermute x12, starting transfers between devices, swap(): return lax.ppermute(value, axis, [(i, i ^ mask) for i in range(count)])  14.6 us
    pallas_call x11, Pallas kernels, call(): pl.pallas_call(kernel, out_shape=outs, in_specs=[pl.BlockSpec(memory_spac...  5.99 us
    pallas_call x1, Pallas kernels, run_rows(): pl.pallas_call(functools.partial(rows_kernel, group), out_shape=(jax.Shap...  3.86 us
  transfers between devices with their start and end apart: 12, of which 9 were waited for; matrix products, arithmetic and copies ran while one was open for 2% of the time, Pallas kernels for 8%

profile of v5, /device:TPU:0, one launch (start us, length us, event | category | flops | bytes accessed | tf_op | source)
XLA Modules:
  0.0 81.3 jit_solution(7693118974293377897)
XLA Ops:
  0.7 0.9 %shard_map.354.own_ref = bf16[416,128]{1,0:T(8,128)(2,1)S(1)} custom-call(f32[128,384]{1,0:T(8,128)} %bitcast.18, f32[32,128]{1,0:T(8,128)} %bitcast.22), custom_call_target="tpu_custom_call" | custom-call | tf_op jit(solution)/shard_map/pallas_call | solution.py:838
  1.6 3.0 %collective-permute-start.1 = (bf16[416,128]{1,0:T(8,128)(2,1)S(1)}, bf16[416,128]{1,0:T(8,128)(2,1)S(1)}, u32[]{:S(2)}, u32[]{:S(2)}) collective-permute-start(bf16[416,128]{1,0:T(8,128)(2,1)S(1)} %shard_map.354.own_ref), channel_id=1, source_target_pairs={{0,2},{1,3},{2,0},{3,1},{4,6},{5,7},{6,4},{7,5},{8,10},{9,11},{10,... | collective-permute-start | bytes 319496 | tf_op jit(solution)/shard_map/ppermute | solution.py:969
  4.6 0.0 collective-permute-start
  4.6 0.7 xor_bitcast_fusion.rel_ref
  5.3 0.8 copy.42
  6.1 0.1 reshape.55.seg_ref
  6.2 1.9 %shard_map.355 = (bf16[384,144]{1,0:T(8,128)(2,1)S(1)}, bf16[128,384]{1,0:T(8,128)(2,1)S(1)}, bf16[128,128]{1,0:T(8,128)(2,1)S(1)}, bf16[128,128]{1,0:T(8,128)(2...) custom-call(f32[128,1024]{1,0:T(8,128)} %refs_4_.1, ...), custom_call_target="tpu_custom_call" | custom-call | bytes 8388608 | tf_op jit(solution)/shard_map/pallas_call | solution.py:838
  8.1 0.0 collective-permute-done.1.in_ref
  8.1 0.6 collective-permute-start.2
  8.7 0.0 collective-permute-done.one_ref
  8.7 1.0 %collective-permute-done.2.three_ref = bf16[416,128]{1,0:T(8,128)(2,1)S(1)} collective-permute-done((bf16[416,128]{1,0:T(8,128)(2,1)S(1)}, bf16[416,128]{1,0:T(8,128)(2,1)S(1)}, u32[]{:S(2)}, u32[]{:S(2)}) %collective-permute-start.2) | collective-permute-done | bytes 106528 | tf_op jit(solution)/shard_map/ppermute | solution.py:969
  9.7 32.7 %shard_map.357 = (bf16[32,128,128]{2,1,0:T(8,128)(2,1)}, bf16[32,256,384]{2,1,0:T(8,128)(2,1)S(1)}, bf16[4,384,128]{2,1,0:T(8,128)(2,1)S(1)}, f32[1600,128]{1,0:...) custom-call(s32[32]{0:T(128)S(1)} %xor_bitcast_fusion.rel_ref, s32[128]{0:T(128)S(1)} %reshape.55.seg_ref, ...), custom_call_target="tpu_custom_call" | custom-call | tf_op jit(solution)/shard_map/pallas_call | solution.py:908
  42.3 0.4 collective-permute-start.3
  42.8 1.4 %collective-permute-done.3.got_ref = bf16[1632,128]{1,0:T(8,128)(2,1)S(1)} collective-permute-done((bf16[1632,128]{1,0:T(8,128)(2,1)S(1)}, bf16[1632,128]{1,0:T(8,128)(2,1)S(1)}, u32[]{:S(2)}, u32[]{:S(2)}) %collective-permute-start.3) | collective-permute-done | bytes 417824 | tf_op jit(solution)/shard_map/ppermute | solution.py:969
  44.2 0.1 shard_map.358
  44.3 1.1 %collective-permute-start.4 = (bf16[832,128]{1,0:T(8,128)(2,1)S(1)}, bf16[832,128]{1,0:T(8,128)(2,1)S(1)}, u32[]{:S(2)}, u32[]{:S(2)}) collective-permute-start(bf16[832,128]{1,0:T(8,128)(2,1)S(1)} %get-tuple-element.91.after_ref), channel_id=1, source_target_pairs={{0,2},{1,3},{2,0},{3,1},{4,6},{5,7},{6,4},{7,5},{8,10},{9,11},{10,... | collective-permute-start | bytes 638984 | tf_op jit(solution)/shard_map/ppermute | solution.py:969
  45.4 0.0 copy-start.7
  45.4 0.0 copy-start.8
  45.4 0.0 copy-start.9
  45.4 0.0 copy-start.10
  45.4 0.0 copy-start.11
  45.4 0.0 copy-start.12
  45.5 0.0 copy-start.13
  45.5 0.0 copy-start.14
  45.5 3.9 %shard_map.359 = (bf16[32,256,128]{2,1,0:T(8,128)(2,1)}, f32[8,128]{1,0:T(8,128)S(1)}) custom-call(s32[32]{0:T(128)S(1)} %xor_bitcast_fusion.rel_ref, bf16[32,256,384]{2,1,0:T(8,128)(2,1)S(1)} %get-tuple-element.86.late_ref, bf16[4,384,128]{2,1,0:T(8,128)(2,1)S(1)} %get-tuple-element.87.back_ref, bf16[832,128]{1,0:T(8,128)(2,1)S(1)} %get-tuple-element.91.after_ref), custom_call_target="tpu_custom_call" | custom-call | flops 805306368 | bytes 16777216 | tf_op jit(solution)/shard_map/pallas_call | solution.py:706
  49.3 0.0 copy-start.2
  49.3 0.0 copy-start
  49.3 0.0 copy-start.3
  49.3 0.0 copy-start.4
  49.4 0.0 copy-start.5
  49.4 0.0 copy-start.6
  49.4 2.5 %collective-permute-done.4.got_ref = bf16[832,128]{1,0:T(8,128)(2,1)S(1)} collective-permute-done((bf16[832,128]{1,0:T(8,128)(2,1)S(1)}, bf16[832,128]{1,0:T(8,128)(2,1)S(1)}, u32[]{:S(2)}, u32[]{:S(2)}) %collective-permute-start.4) | collective-permute-done | bytes 213024 | tf_op jit(solution)/shard_map/ppermute | solution.py:969
  51.9 0.1 shard_map.360
  51.9 1.6 %collective-permute-start.5 = (bf16[448,128]{1,0:T(8,128)(2,1)S(1)}, bf16[448,128]{1,0:T(8,128)(2,1)S(1)}, u32[]{:S(2)}, u32[]{:S(2)}) collective-permute-start(bf16[448,128]{1,0:T(8,128)(2,1)S(1)} %get-tuple-element.97), channel_id=1, source_target_pairs={{0,4},{4,0},{8,12},{12,8},{16,20},{20,16},{24,28},{28,24},{1,5},{5... | collective-permute-start | bytes 344072 | tf_op jit(solution)/shard_map/ppermute | solution.py:969
  53.5 3.3 %collective-permute-done.5.got_ref = bf16[448,128]{1,0:T(8,128)(2,1)S(1)} collective-permute-done((bf16[448,128]{1,0:T(8,128)(2,1)S(1)}, bf16[448,128]{1,0:T(8,128)(2,1)S(1)}, u32[]{:S(2)}, u32[]{:S(2)}) %collective-permute-start.5) | collective-permute-done | bytes 114720 | tf_op jit(solution)/shard_map/ppermute | solution.py:969
  56.8 1.6 %collective-permute-start.6 = (bf16[448,128]{1,0:T(8,128)(2,1)S(1)}, bf16[448,128]{1,0:T(8,128)(2,1)S(1)}, u32[]{:S(2)}, u32[]{:S(2)}) collective-permute-start(bf16[448,128]{1,0:T(8,128)(2,1)S(1)} %get-tuple-element.100), channel_id=1, source_target_pairs={{0,8},{4,12},{8,0},{12,4},{16,24},{20,28},{24,16},{28,20},{1,9},{5... | collective-permute-start | bytes 344072 | tf_op jit(solution)/shard_map/ppermute | solution.py:969
  58.5 3.2 %collective-permute-done.6.got_ref = bf16[448,128]{1,0:T(8,128)(2,1)S(1)} collective-permute-done((bf16[448,128]{1,0:T(8,128)(2,1)S(1)}, bf16[448,128]{1,0:T(8,128)(2,1)S(1)}, u32[]{:S(2)}, u32[]{:S(2)}) %collective-permute-start.6) | collective-permute-done | bytes 114720 | tf_op jit(solution)/shard_map/ppermute | solution.py:969
  61.7 3.7 %collective-permute-start.7 = (bf16[448,128]{1,0:T(8,128)(2,1)S(1)}, bf16[448,128]{1,0:T(8,128)(2,1)S(1)}, u32[]{:S(2)}, u32[]{:S(2)}) collective-permute-start(bf16[448,128]{1,0:T(8,128)(2,1)S(1)} %get-tuple-element.103), channel_id=1, source_target_pairs={{0,24},{4,28},{8,16},{12,20},{16,8},{20,12},{24,0},{28,4},{1,25},{... | collective-permute-start | bytes 344072 | tf_op jit(solution)/shard_map/ppermute | solution.py:969
  65.4 3.1 %collective-permute-done.7.got_ref = bf16[448,128]{1,0:T(8,128)(2,1)S(1)} collective-permute-done((bf16[448,128]{1,0:T(8,128)(2,1)S(1)}, bf16[448,128]{1,0:T(8,128)(2,1)S(1)}, u32[]{:S(2)}, u32[]{:S(2)}) %collective-permute-start.7) | collective-permute-done | bytes 114720 | tf_op jit(solution)/shard_map/ppermute | solution.py:969
  68.5 1.6 %collective-permute-start.8 = (bf16[416,128]{1,0:T(8,128)(2,1)S(1)}, bf16[416,128]{1,0:T(8,128)(2,1)S(1)}, u32[]{:S(2)}, u32[]{:S(2)}) collective-permute-start(bf16[416,128]{1,0:T(8,128)(2,1)S(1)} %get-tuple-element.105.own_ref), channel_id=1, source_target_pairs={{0,4},{4,0},{8,12},{12,8},{16,20},{20,16},{24,28},{28,24},{1,5},{5... | collective-permute-start | bytes 319496 | tf_op jit(solution)/shard_map/ppermute | solution.py:969
  70.1 3.2 %collective-permute-done.8.got_ref = bf16[416,128]{1,0:T(8,128)(2,1)S(1)} collective-permute-done((bf16[416,128]{1,0:T(8,128)(2,1)S(1)}, bf16[416,128]{1,0:T(8,128)(2,1)S(1)}, u32[]{:S(2)}, u32[]{:S(2)}) %collective-permute-start.8) | collective-permute-done | bytes 106528 | tf_op jit(solution)/shard_map/ppermute | solution.py:969
  73.3 0.9 %collective-permute-start.10 = (bf16[384,128]{1,0:T(8,128)(2,1)S(1)}, bf16[384,128]{1,0:T(8,128)(2,1)S(1)}, u32[]{:S(2)}, u32[]{:S(2)}) collective-permute-start(bf16[384,128]{1,0:T(8,128)(2,1)S(1)} %slice_select_fusion.refs_0_), channel_id=1, source_target_pairs={{0,2},{1,3},{2,0},{3,1},{4,6},{5,7},{6,4},{7,5},{8,10},{9,11},{10,... | collective-permute-start | bytes 294920 | tf_op jit(solution)/shard_map/ppermute | solution.py:969
  74.2 0.0 collective-permute-start.9
  74.2 0.0 copy-done.7
  74.3 0.0 copy-done.8
  74.3 0.0 copy-done.9
  74.3 0.0 copy-done.10
  74.3 0.0 copy-done.11
  74.3 0.0 copy-done.12
  74.3 0.0 copy-done.13
  74.3 0.0 copy-done.14
  74.3 0.0 copy-done.2
  74.3 1.0 %shard_map.364 = (f32[128,384]{1,0:T(8,128)}, f32[128,384]{1,0:T(8,128)}, f32[128,384]{1,0:T(8,128)}, bf16[128,384]{1,0:T(8,128)(2,1)}, f32[32,128]{1,0:T(8,128)...) custom-call(bf16[416,128]{1,0:T(8,128)(2,1)S(1)} %get-tuple-element., ...), custom_call_target="tpu_custom_call" | custom-call | bytes 6291456 | tf_op jit(solution)/shard_map/pallas_call | solution.py:838
  75.3 2.7 %collective-permute-done.10.in_ref = bf16[384,128]{1,0:T(8,128)(2,1)S(1)} collective-permute-done((bf16[384,128]{1,0:T(8,128)(2,1)S(1)}, bf16[384,128]{1,0:T(8,128)(2,1)S(1)}, u32[]{:S(2)}, u32[]{:S(2)}) %collective-permute-start.10) | collective-permute-done | bytes 98336 | tf_op jit(solution)/shard_map/ppermute | solution.py:969
  78.0 0.1 collective-permute-start.11
  78.1 0.0 collective-permute-done.9.refs_1_
  78.1 1.3 %collective-permute-done.11.refs_3_ = bf16[384,128]{1,0:T(8,128)(2,1)S(1)} collective-permute-done((bf16[384,128]{1,0:T(8,128)(2,1)S(1)}, bf16[384,128]{1,0:T(8,128)(2,1)S(1)}, u32[]{:S(2)}, u32[]{:S(2)}) %collective-permute-start.11) | collective-permute-done | bytes 98336 | tf_op jit(solution)/shard_map/ppermute | solution.py:969
  79.4 0.0 copy-done
  79.4 0.0 copy-done.1
  79.4 0.0 copy-done.3
  79.4 0.0 copy-done.4
  79.4 0.0 copy-done.5
  79.4 0.0 copy-done.6
  79.4 1.8 %shard_map.366 = (f32[128,1024]{1,0:T(8,128)}, f32[128,1024]{1,0:T(8,128)}, f32[128,1024]{1,0:T(8,128)}, bf16[128,1024]{1,0:T(8,128)(2,1)}, f32[512,128]{1,0:T(8...) custom-call(bf16[384,128]{1,0:T(8,128)(2,1)S(1)} %slice_select_fusion.refs_0_, ...), custom_call_target="tpu_custom_call" | custom-call | tf_op jit(solution)/shard_map/pallas_call | solution.py:838
  (7 shorter events, 0.1 us)
Async XLA Ops:
  1.6 6.5 %collective-permute-start.1 = (bf16[416,128]{1,0:T(8,128)(2,1)S(1)}, bf16[416,128]{1,0:T(8,128)(2,1)S(1)}, u32[]{:S(2)}, u32[]{:S(2)}) collective-permute-start(bf16[416,128]{1,0:T(8,128)(2,1)S(1)} %shard_map.354.own_ref), channel_id=1, source_target_pairs={{0,2},{1,3},{2,0},{3,1},{4,6},{5,7},{6,4},{7,5},{8,10},{9,11},{10,... | collective-permute-start | bytes 319496 | tf_op jit(solution)/shard_map/ppermute | solution.py:969
  4.6 4.1 %collective-permute-start = (bf16[416,128]{1,0:T(8,128)(2,1)S(1)}, bf16[416,128]{1,0:T(8,128)(2,1)S(1)}, u32[]{:S(2)}, u32[]{:S(2)}) collective-permute-start(bf16[416,128]{1,0:T(8,128)(2,1)S(1)} %shard_map.354.own_ref), channel_id=1, source_target_pairs={{0,1},{1,0},{2,3},{3,2},{4,5},{5,4},{6,7},{7,6},{8,9},{9,8},{10,11... | collective-permute-start | bytes 319496 | tf_op jit(solution)/shard_map/ppermute | solution.py:969
  8.1 1.5 %collective-permute-start.2 = (bf16[416,128]{1,0:T(8,128)(2,1)S(1)}, bf16[416,128]{1,0:T(8,128)(2,1)S(1)}, u32[]{:S(2)}, u32[]{:S(2)}) collective-permute-start(bf16[416,128]{1,0:T(8,128)(2,1)S(1)} %shard_map.356.two_ref), channel_id=1, source_target_pairs={{0,1},{1,0},{2,3},{3,2},{4,5},{5,4},{6,7},{7,6},{8,9},{9,8},{10,11... | collective-permute-start | bytes 319496 | tf_op jit(solution)/shard_map/ppermute | solution.py:969
  42.3 1.8 %collective-permute-start.3 = (bf16[1632,128]{1,0:T(8,128)(2,1)S(1)}, bf16[1632,128]{1,0:T(8,128)(2,1)S(1)}, u32[]{:S(2)}, u32[]{:S(2)}) collective-permute-start(bf16[1632,128]{1,0:T(8,128)(2,1)S(1)} %get-tuple-element.89), channel_id=1, source_target_pairs={{0,1},{1,0},{2,3},{3,2},{4,5},{5,4},{6,7},{7,6},{8,9},{9,8},{10,11... | collective-permute-start | bytes 1253384 | tf_op jit(solution)/shard_map/ppermute | solution.py:969
  44.3 7.6 %collective-permute-start.4 = (bf16[832,128]{1,0:T(8,128)(2,1)S(1)}, bf16[832,128]{1,0:T(8,128)(2,1)S(1)}, u32[]{:S(2)}, u32[]{:S(2)}) collective-permute-start(bf16[832,128]{1,0:T(8,128)(2,1)S(1)} %get-tuple-element.91.after_ref), channel_id=1, source_target_pairs={{0,2},{1,3},{2,0},{3,1},{4,6},{5,7},{6,4},{7,5},{8,10},{9,11},{10,... | collective-permute-start | bytes 638984 | tf_op jit(solution)/shard_map/ppermute | solution.py:969
  45.4 28.8 %copy-start.7 = (f32[1,128,384]{2,1,0:T(8,128)S(1)}, f32[1,128,384]{2,1,0:T(8,128)}, u32[]{:S(2)}) copy-start(f32[1,128,384]{2,1,0:T(8,128)} %param.33) | copy-start | bytes 589828
  45.4 28.8 %copy-start.8 = (f32[1,128,384]{2,1,0:T(8,128)S(1)}, f32[1,128,384]{2,1,0:T(8,128)}, u32[]{:S(2)}) copy-start(f32[1,128,384]{2,1,0:T(8,128)} %param.34) | copy-start | bytes 589828
  45.4 28.8 %copy-start.9 = (f32[1,32,128]{2,1,0:T(8,128)S(1)}, f32[1,32,128]{2,1,0:T(8,128)}, u32[]{:S(2)}) copy-start(f32[1,32,128]{2,1,0:T(8,128)} %param.35) | copy-start | bytes 49156
  45.4 28.8 %copy-start.10 = (f32[9,128]{1,0:T(8,128)S(1)}, f32[9,128]{1,0:T(8,128)}, u32[]{:S(2)}) copy-start(f32[9,128]{1,0:T(8,128)} %refs_6_.2) | copy-start | bytes 13828
  45.4 28.8 %copy-start.11 = (f32[1,32,128]{2,1,0:T(8,128)S(1)}, f32[1,32,128]{2,1,0:T(8,128)}, u32[]{:S(2)}) copy-start(f32[1,32,128]{2,1,0:T(8,128)} %param.36) | copy-start | bytes 49156
  45.4 28.8 %copy-start.12 = (f32[1,32,128]{2,1,0:T(8,128)S(1)}, f32[1,32,128]{2,1,0:T(8,128)}, u32[]{:S(2)}) copy-start(f32[1,32,128]{2,1,0:T(8,128)} %param.37) | copy-start | bytes 49156
  45.5 28.8 %copy-start.13 = (f32[9,128]{1,0:T(8,128)S(1)}, f32[9,128]{1,0:T(8,128)}, u32[]{:S(2)}) copy-start(f32[9,128]{1,0:T(8,128)} %refs_7_.2) | copy-start | bytes 13828
  45.5 28.8 %copy-start.14 = (f32[9,128]{1,0:T(8,128)S(1)}, f32[9,128]{1,0:T(8,128)}, u32[]{:S(2)}) copy-start(f32[9,128]{1,0:T(8,128)} %refs_8_.2) | copy-start | bytes 13828
  49.3 25.0 %copy-start.2 = (f32[1,128,384]{2,1,0:T(8,128)S(1)}, f32[1,128,384]{2,1,0:T(8,128)}, u32[]{:S(2)}) copy-start(f32[1,128,384]{2,1,0:T(8,128)} %param.32) | copy-start | bytes 589828
  49.3 30.0 %copy-start = (f32[128,1024]{1,0:T(8,128)S(1)}, f32[128,1024]{1,0:T(8,128)}, u32[]{:S(2)}) copy-start(f32[128,1024]{1,0:T(8,128)} %refs_4_.1) | copy-start | bytes 1572868
  49.3 30.0 %copy-start.1 = (f32[512,128]{1,0:T(8,128)S(1)}, f32[512,128]{1,0:T(8,128)}, u32[]{:S(2)}) copy-start(f32[512,128]{1,0:T(8,128)} %refs_7_.3) | copy-start | bytes 786436
  49.3 30.0 %copy-start.3 = (f32[128,1024]{1,0:T(8,128)S(1)}, f32[128,1024]{1,0:T(8,128)}, u32[]{:S(2)}) copy-start(f32[128,1024]{1,0:T(8,128)} %refs_5_.1) | copy-start | bytes 1572868
  49.3 30.0 %copy-start.4 = (f32[128,1024]{1,0:T(8,128)S(1)}, f32[128,1024]{1,0:T(8,128)}, u32[]{:S(2)}) copy-start(f32[128,1024]{1,0:T(8,128)} %refs_6_.3) | copy-start | bytes 1572868
  49.4 30.0 %copy-start.5 = (f32[512,128]{1,0:T(8,128)S(1)}, f32[512,128]{1,0:T(8,128)}, u32[]{:S(2)}) copy-start(f32[512,128]{1,0:T(8,128)} %refs_8_.3) | copy-start | bytes 786436
  49.4 30.0 %copy-start.6 = (f32[512,128]{1,0:T(8,128)S(1)}, f32[512,128]{1,0:T(8,128)}, u32[]{:S(2)}) copy-start(f32[512,128]{1,0:T(8,128)} %refs_9_.1) | copy-start | bytes 786436
  51.9 4.9 %collective-permute-start.5 = (bf16[448,128]{1,0:T(8,128)(2,1)S(1)}, bf16[448,128]{1,0:T(8,128)(2,1)S(1)}, u32[]{:S(2)}, u32[]{:S(2)}) collective-permute-start(bf16[448,128]{1,0:T(8,128)(2,1)S(1)} %get-tuple-element.97), channel_id=1, source_target_pairs={{0,4},{4,0},{8,12},{12,8},{16,20},{20,16},{24,28},{28,24},{1,5},{5... | collective-permute-start | bytes 344072 | tf_op jit(solution)/shard_map/ppermute | solution.py:969
  56.8 4.9 %collective-permute-start.6 = (bf16[448,128]{1,0:T(8,128)(2,1)S(1)}, bf16[448,128]{1,0:T(8,128)(2,1)S(1)}, u32[]{:S(2)}, u32[]{:S(2)}) collective-permute-start(bf16[448,128]{1,0:T(8,128)(2,1)S(1)} %get-tuple-element.100), channel_id=1, source_target_pairs={{0,8},{4,12},{8,0},{12,4},{16,24},{20,28},{24,16},{28,20},{1,9},{5... | collective-permute-start | bytes 344072 | tf_op jit(solution)/shard_map/ppermute | solution.py:969
  61.7 6.8 %collective-permute-start.7 = (bf16[448,128]{1,0:T(8,128)(2,1)S(1)}, bf16[448,128]{1,0:T(8,128)(2,1)S(1)}, u32[]{:S(2)}, u32[]{:S(2)}) collective-permute-start(bf16[448,128]{1,0:T(8,128)(2,1)S(1)} %get-tuple-element.103), channel_id=1, source_target_pairs={{0,24},{4,28},{8,16},{12,20},{16,8},{20,12},{24,0},{28,4},{1,25},{... | collective-permute-start | bytes 344072 | tf_op jit(solution)/shard_map/ppermute | solution.py:969
  68.5 4.8 %collective-permute-start.8 = (bf16[416,128]{1,0:T(8,128)(2,1)S(1)}, bf16[416,128]{1,0:T(8,128)(2,1)S(1)}, u32[]{:S(2)}, u32[]{:S(2)}) collective-permute-start(bf16[416,128]{1,0:T(8,128)(2,1)S(1)} %get-tuple-element.105.own_ref), channel_id=1, source_target_pairs={{0,4},{4,0},{8,12},{12,8},{16,20},{20,16},{24,28},{28,24},{1,5},{5... | collective-permute-start | bytes 319496 | tf_op jit(solution)/shard_map/ppermute | solution.py:969
  73.3 4.7 %collective-permute-start.10 = (bf16[384,128]{1,0:T(8,128)(2,1)S(1)}, bf16[384,128]{1,0:T(8,128)(2,1)S(1)}, u32[]{:S(2)}, u32[]{:S(2)}) collective-permute-start(bf16[384,128]{1,0:T(8,128)(2,1)S(1)} %slice_select_fusion.refs_0_), channel_id=1, source_target_pairs={{0,2},{1,3},{2,0},{3,1},{4,6},{5,7},{6,4},{7,5},{8,10},{9,11},{10,... | collective-permute-start | bytes 294920 | tf_op jit(solution)/shard_map/ppermute | solution.py:969
  74.2 3.8 %collective-permute-start.9 = (bf16[384,128]{1,0:T(8,128)(2,1)S(1)}, bf16[384,128]{1,0:T(8,128)(2,1)S(1)}, u32[]{:S(2)}, u32[]{:S(2)}) collective-permute-start(bf16[384,128]{1,0:T(8,128)(2,1)S(1)} %slice_select_fusion.refs_0_), channel_id=1, source_target_pairs={{0,1},{1,0},{2,3},{3,2},{4,5},{5,4},{6,7},{7,6},{8,9},{9,8},{10,11... | collective-permute-start | bytes 294920 | tf_op jit(solution)/shard_map/ppermute | solution.py:969
  78.0 1.4 %collective-permute-start.11 = (bf16[384,128]{1,0:T(8,128)(2,1)S(1)}, bf16[384,128]{1,0:T(8,128)(2,1)S(1)}, u32[]{:S(2)}, u32[]{:S(2)}) collective-permute-start(bf16[384,128]{1,0:T(8,128)(2,1)S(1)} %shard_map.365.refs_2_), channel_id=1, source_target_pairs={{0,1},{1,0},{2,3},{3,2},{4,5},{5,4},{6,7},{7,6},{8,9},{9,8},{10,11... | collective-permute-start | bytes 294920 | tf_op jit(solution)/shard_map/ppermute | solution.py:969

commit v6 on v5

--- a/solution.py
+++ b/solution.py
@@ -89,8 +89,24 @@
     )
 
 
+def aslant(one, two):
+    gap = jnp.zeros_like(one)
+    return jnp.concatenate(
+        [jnp.concatenate([one, gap], axis=1), jnp.concatenate([gap, two], axis=1)], axis=0
+    )
+
+
 def pair_pick(both):
     return jnp.concatenate([both[:16, :128], both[16:, 128:]], axis=0)
+
+
+def query_block(ref):
+    head_mask = (
+        lax.broadcasted_iota(jnp.int32, (256, 128), 0) // 32
+        == lax.broadcasted_iota(jnp.int32, (256, 128), 1) // 16
+    )
+    queries = ref[384:416].astype(F32)
+    return jnp.where(head_mask, jnp.concatenate([queries] * HEADS, axis=0), 0.0).T.astype(BF)
 
 
 def ready_kernel(
@@ -161,24 +177,21 @@
     one_ref,
     two_ref,
     three_ref,
-    mats_ref,
-    t_qkvT,
-    t_qkv,
-    t_o,
-    t_oT,
-    t_in,
-    t_inT,
-    t_dn,
-    t_dnT,
-    vecs,
+    mats_any,
+    t_qkvT_any,
+    t_qkv_any,
+    t_o_any,
+    t_oT_any,
+    t_in_any,
+    t_inT_any,
+    t_dn_any,
+    t_dnT_any,
+    vecs_any,
     out_hbm,
     late_hbm,
-    back_ref,
     keep_ref,
     give_ref,
     sums_ref,
-    s_k,
-    s_qb,
     s_a2,
     s_vT,
     s_out,
@@ -196,9 +209,35 @@
     cot_ref,
     out_ref,
     late_ref,
+    mats_ref,
+    t_qkvT,
+    t_qkv,
+    t_o,
+    t_oT,
+    t_in,
+    t_inT,
+    t_dn,
+    t_dnT,
+    vecs,
     sems,
+    more_sems,
 ):
     step = pl.program_id(0)
+    ends = (
+        (mats_any, mats_ref),
+        (t_qkvT_any, t_qkvT),
+        (t_qkv_any, t_qkv),
+        (t_o_any, t_o),
+        (t_oT_any, t_oT),
+        (t_in_any, t_in),
+        (t_inT_any, t_inT),
+        (t_dn_any, t_dn),
+        (t_dnT_any, t_dnT),
+        (vecs_any, vecs),
+    )
+    weights = [
+        pltpu.make_async_copy(one, two, more_sems.at[i]) for i, (one, two) in enumerate(ends)
+    ]
     steps = rows_ref.shape[0] // group
 
     def moves(g):
@@ -216,9 +255,12 @@
 
     @pl.when(step == 0)
     def _():
-        for g in range(steps):
+        for move in moves(0)[:2] + weights[1:]:
+            move.start()
+        for g in range(1, steps):
             for move in moves(g)[:2]:
                 move.start()
+        weights[0].start()
 
 
     head_mask = (
@@ -230,20 +272,14 @@
     def _():
         for k, ref in enumerate((own_ref, one_ref, two_ref, three_ref)):
             wk, wv, wo = ref[0:128], ref[128:256], ref[256:384]
-            queries = ref[384:416].astype(F32)
-            tiled = jnp.where(head_mask, jnp.concatenate([queries] * HEADS, axis=0), 0.0)
-            block = tiled.T.astype(BF)
-            both = mm(wk, block) * SCALE
-            s_k[k] = wk
-            s_qb[k] = block
-            back_ref[k, 0:256] = both.T.astype(BF)
-            back_ref[k, 256:384] = wv.T
-            s_a2[k] = (both * LOG2E).astype(BF)
+            s_a2[k] = (mm(wk, query_block(ref)) * (SCALE * LOG2E)).astype(BF)
             s_vT[k] = wv.T
             s_out[k] = wo
             s_outT[k] = wo.T
         for ref in (a_qkv, a_o, a_in, a_dn, a_vec, a_a, a_v, a_out):
             ref[...] = jnp.zeros_like(ref)
+        for move in weights[1:]:
+            move.wait()
 
     for move in moves(step)[:2]:
         move.wait()
@@ -319,7 +355,10 @@
                 rows.append(row)
             stem_mixed.append(jnp.concatenate(rows, axis=0).astype(BF))
         yield
-        residual = [mm(s_outT[rels[b]], stem_mixed[b]) for b in every]
+        both = mm(
+            jnp.concatenate([s_outT[e] for e in rels], axis=1), aslant(*stem_mixed)
+        )
+        residual = [both[:, lanes[b]] for b in every]
         yield
 
         def norm(values):
@@ -516,9 +555,13 @@
         ]
         yield
 
-        grad_mixed = [mm(s_out[rels[b]], grad_tokens[b]) for b in every]
+        both = mm(jnp.concatenate([s_out[e] for e in rels], axis=1), aslant(*grad_tokens))
+        grad_mixed = [both[:, lanes[b]] for b in every]
+        both = mm(
+            jnp.concatenate(stem_mixed, axis=1), aslant(*[grad.T for grad in grad_tokens])
+        )
         for b in every:
-            a_out[rels[b]] += mm_nt(stem_mixed[b], grad_tokens[b])
+            a_out[rels[b]] += both[:, lanes[b]]
         yield
         spread, tall = [], []
         for b in every:
@@ -622,6 +665,7 @@
     @pl.when(step == pl.num_programs(0) - 1)
     def _():
         me = lax.axis_index("emb")
+        weights[0].wait()
 
         def exact(left, right):
             high = left.astype(BF)
@@ -665,18 +709,19 @@
         sums_ref[...] = sums
         give_ref[2 * PIECE_ROWS : 2 * PIECE_ROWS + 16] = high
         give_ref[2 * PIECE_ROWS + 16 : 2 * PIECE_ROWS + 32] = low
-        for k in range(count):
+        for k, ref in enumerate((own_ref, one_ref, two_ref, three_ref)):
+            block = query_block(ref)
             grad = a_a[k] * SCALE
             grad_high = grad.astype(BF)
             grad_low = (grad - grad_high.astype(F32)).astype(BF)
-            key_T = s_k[k].T
+            key_T = ref[0:128].T
             spread = (mm(key_T, grad_high) + mm(key_T, grad_low)).T
             spread = jnp.where(head_mask, spread, 0.0)
             query = spread[0:32]
             for h in range(1, HEADS):
                 query = query + spread[32 * h : 32 * h + 32]
             parts = [
-                mm_nt(grad_high, s_qb[k]) + mm_nt(grad_low, s_qb[k]),
+                mm_nt(grad_high, block) + mm_nt(grad_low, block),
                 a_v[k],
                 a_out[k],
                 query,
@@ -693,18 +738,27 @@
                 move.wait()
 
 
-def rows_kernel(group, rel_ref, late_ref, back_ref, after_ref, out_ref, done_ref):
+def rows_kernel(group, count, rel_ref, late_ref, *refs):
+    stems, (after_ref, out_ref, done_ref, back_ref) = refs[:count], refs[count:]
     step = pl.program_id(0)
+
+    @pl.when(step == 0)
+    def _():
+        for k, ref in enumerate(stems):
+            both = mm(ref[0:128], query_block(ref)) * SCALE
+            back_ref[k, 0:256] = both.T.astype(BF)
+            back_ref[k, 256:384] = ref[128:256].T
+
     done_ref[...] = jnp.zeros_like(done_ref)
     for b in range(group):
         out_ref[b] = mm(late_ref[b], back_ref[rel_ref[step * group + b]]).astype(BF)
 
 
-def run_rows(rel, late, back, after, group=8):
+def run_rows(rel, late, stems, after, group=8):
     seqs = late.shape[0]
     flops = 2 * seqs * ROWS_SEQ * 3 * D * D
     return pl.pallas_call(
-        functools.partial(rows_kernel, group),
+        functools.partial(rows_kernel, group, len(stems)),
         out_shape=(
             jax.ShapeDtypeStruct((seqs, ROWS_SEQ, D), BF),
             jax.ShapeDtypeStruct((8, D), F32),
@@ -714,9 +768,10 @@
             grid=(seqs // group,),
             in_specs=[
                 pl.BlockSpec((group, ROWS_SEQ, 3 * D), lambda i, *_: (i, 0, 0)),
-                pl.BlockSpec(back.shape, lambda i, *_: (0, 0, 0)),
-                pl.BlockSpec(memory_space=pl.ANY),
-            ],
+            ]
+            + [pl.BlockSpec(stem.shape, lambda i, *_: (0, 0)) for stem in stems]
+            + [pl.BlockSpec(memory_space=pl.ANY)],
+            scratch_shapes=[pltpu.VMEM((len(stems), 3 * D, D), BF)],
             out_specs=(
                 pl.BlockSpec((group, ROWS_SEQ, D), lambda i, *_: (i, 0, 0)),
                 pl.BlockSpec((8, D), lambda i, *_: (0, 0)),
@@ -726,7 +781,7 @@
         compiler_params=pltpu.CompilerParams(
             vmem_limit_bytes=16 * 1024 * 1024, dimension_semantics=("arbitrary",)
         ),
-    )(rel, late, back, after)
+    )(rel, late, *stems, after)
 
 
 def split_sum(sums):
@@ -880,12 +935,10 @@
     group = 16
     steps = seqs // group
 
-    def whole(shape, mode=None):
-        return pl.BlockSpec(shape, lambda i, *_: (0,) * len(shape), pipeline_mode=mode)
+    def whole(shape):
+        return pl.BlockSpec(shape, lambda i, *_: (0,) * len(shape))
 
     scratch = [
-        ((4, 128, 128), BF),
-        ((4, 128, 256), BF),
         ((4, 128, 256), BF),
         ((4, 128, 128), BF),
         ((4, 128, 128), BF),
@@ -910,7 +963,6 @@
         out_shape=(
             jax.ShapeDtypeStruct((seqs, TOK_SEQ, D), BF),
             jax.ShapeDtypeStruct((seqs, ROWS_SEQ, 3 * D), BF),
-            jax.ShapeDtypeStruct((emb_count, 3 * D, D), BF),
             jax.ShapeDtypeStruct((2 * PIECE_ROWS, D), F32),
             jax.ShapeDtypeStruct((2 * PIECE_ROWS + VEC_ROWS, D), BF),
             jax.ShapeDtypeStruct((16, D), F32),
@@ -920,18 +972,18 @@
             grid=(steps,),
             in_specs=[anywhere, anywhere]
             + [whole((STEM_ROWS, D))] * 4
-            + [whole((D, 1024))]
-            + [whole(value.shape, pl.Buffered(1)) for value in ready],
+            + [anywhere] * (1 + len(ready)),
             out_specs=(
                 anywhere,
                 anywhere,
-                whole((emb_count, 3 * D, D)),
                 whole((2 * PIECE_ROWS, D)),
                 whole((2 * PIECE_ROWS + VEC_ROWS, D)),
                 whole((16, D)),
             ),
             scratch_shapes=[pltpu.VMEM(shape, dtype) for shape, dtype in scratch]
-            + [pltpu.SemaphoreType.DMA((4, steps))],
+            + [pltpu.VMEM(mats.shape, F32)]
+            + [pltpu.VMEM(value.shape, value.dtype) for value in ready]
+            + [pltpu.SemaphoreType.DMA((4, steps)), pltpu.SemaphoreType.DMA((1 + len(ready),))],
         ),
         compiler_params=pltpu.CompilerParams(
             vmem_limit_bytes=VMEM_LIMIT, dimension_semantics=("arbitrary",)
@@ -977,7 +1029,7 @@
     far = vmem_call(pass_kernel, jax.ShapeDtypeStruct(far.shape, BF), after=1)(far, ready_done)
     stems = [own, near, far, swap(far, "emb", emb_count, 1)]
 
-    output, late, back, keep, give, sums = run_main(
+    output, late, keep, give, sums = run_main(
         rel,
         segments,
         stem_rows.reshape(seqs, ROWS_SEQ, D),
@@ -998,7 +1050,7 @@
         core_kernel, (shape(PIECE_ROWS, f32), shape(PIECE_ROWS + VEC_ROWS, bf16), shape(16, f32))
     )(keep, got, sums)
     got = swap(give, "emb", emb_count, 2)
-    rows_grad, rows_done = run_rows(rel, late, back, give)
+    rows_grad, rows_done = run_rows(rel, late, stems, give)
     half = (shape(STEM_ROWS, f32), shape(STEM_ROWS + VEC_ROWS, bf16), shape(16, f32))
     own, give, sums = vmem_call(halve_kernel, half, after=1)(
         own, got, sums, rows_done

time: 81.5 us -> 80.9 us (level)
  transfers between devices with their start and end apart: 12 -> 12, of which waited for: 9 -> 9; matrix products, arithmetic and copies ran while one was open for 2% -> 2% of each run, Pallas kernels for 8% -> 9%
where the time goes in v6:
time: 80.9 us; the launch traced here: 80.7 us
  Pallas kernels  42.6 us (53%)
  waiting for transfers between devices  21 us (26%)
  starting transfers between devices  14.6 us (18%)
  local copies, waits for them, and re-layouts  0.94 us (1%)
  between operations  0.89 us (1%)
    pallas_call x1, Pallas kernels, run_main(): pl.pallas_call(functools.partial(main_kernel, group), out_shape=(jax.Shap...  32.2 us
    ppermute x12, waiting for transfers between devices, swap(): return lax.ppermute(value, axis, [(i, i ^ mask) for i in range(count)])  21 us
    ppermute x12, starting transfers between devices, swap(): return lax.ppermute(value, axis, [(i, i ^ mask) for i in range(count)])  14.6 us
    pallas_call x11, Pallas kernels, call(): pl.pallas_call(kernel, out_shape=outs, in_specs=[pl.BlockSpec(memory_spac...  5.98 us
    pallas_call x1, Pallas kernels, run_rows(): pl.pallas_call(functools.partial(rows_kernel, group, len(stems)), out_sha...  4.5 us
  transfers between devices with their start and end apart: 12, of which 9 were waited for; matrix products, arithmetic and copies ran while one was open for 2% of the time, Pallas kernels for 9%

profile of v6, /device:TPU:0, one launch (start us, length us, event | category | flops | bytes accessed | tf_op | source)
XLA Modules:
  0.0 80.7 jit_solution(5229369377622909881)
XLA Ops:
  0.7 0.9 %shard_map.354.own_ref.refs_0_ = bf16[416,128]{1,0:T(8,128)(2,1)S(1)} custom-call(f32[128,384]{1,0:T(8,128)} %bitcast.18, f32[32,128]{1,0:T(8,128)} %bitcast.22), custom_call_target="tpu_custom_call" | custom-call | tf_op jit(solution)/shard_map/pallas_call | solution.py:893
  1.6 3.0 %collective-permute-start.1 = (bf16[416,128]{1,0:T(8,128)(2,1)S(1)}, bf16[416,128]{1,0:T(8,128)(2,1)S(1)}, u32[]{:S(2)}, u32[]{:S(2)}) collective-permute-start(bf16[416,128]{1,0:T(8,128)(2,1)S(1)} %shard_map.354.own_ref.refs_0_), channel_id=1, source_target_pairs={{0,2},{1,3},{2,0},{3,1},{4,6},{5,7},{6,4},{7,5},{8,10},{9,11},{10,... | collective-permute-start | bytes 319496 | tf_op jit(solution)/shard_map/ppermute | solution.py:1021
  4.6 0.0 collective-permute-start
  4.6 0.7 xor_bitcast_fusion.rel_ref
  5.3 0.8 copy.42
  6.1 0.1 reshape.55.seg_ref
  6.2 1.9 %shard_map.355 = (bf16[384,144]{1,0:T(8,128)(2,1)S(1)}, bf16[128,384]{1,0:T(8,128)(2,1)S(1)}, bf16[128,128]{1,0:T(8,128)(2,1)S(1)}, bf16[128,128]{1,0:T(8,128)(2...) custom-call(f32[128,1024]{1,0:T(8,128)} %refs_4_.1, ...), custom_call_target="tpu_custom_call" | custom-call | bytes 8388608 | tf_op jit(solution)/shard_map/pallas_call | solution.py:893
  8.1 0.0 collective-permute-done.1.in_ref
  8.1 0.6 collective-permute-start.2
  8.7 0.0 collective-permute-done.one_ref.refs_1_
  8.7 1.0 %collective-permute-done.2.three_ref.refs_3_ = bf16[416,128]{1,0:T(8,128)(2,1)S(1)} collective-permute-done((bf16[416,128]{1,0:T(8,128)(2,1)S(1)}, bf16[416,128]{1,0:T(8,128)(2,1)S(1)}, u32[]{:S(2)}, u32[]{:S(2)}) %collective-permute-start.2) | collective-permute-done | bytes 106528 | tf_op jit(solution)/shard_map/ppermute | solution.py:1021
  9.7 32.2 %shard_map.357 = (bf16[32,128,128]{2,1,0:T(8,128)(2,1)}, bf16[32,256,384]{2,1,0:T(8,128)(2,1)S(1)}, f32[1600,128]{1,0:T(8,128)S(1)}, bf16[1632,128]{1,0:T(8,128)(2,1)S(1)}, f32[16,128]{1,0:T(8,128)S(1)}) custom-call(s32[32]{0:T(128)S(1)} %xor_bitcast_fusion.rel_ref, s32[128]{0:T(128)S(1)} %reshape.55.seg_ref, bf16[32,256,128]{2,1,0:T(8,128)(2,1)} %bitcast.26, ...), custom_call_target="tpu_custom_call" | custom-call | tf_op jit(solution)/shard_map/pallas_call | solution.py:961
  41.8 0.4 collective-permute-start.3
  42.3 1.4 %collective-permute-done.3.got_ref = bf16[1632,128]{1,0:T(8,128)(2,1)S(1)} collective-permute-done((bf16[1632,128]{1,0:T(8,128)(2,1)S(1)}, bf16[1632,128]{1,0:T(8,128)(2,1)S(1)}, u32[]{:S(2)}, u32[]{:S(2)}) %collective-permute-start.3) | collective-permute-done | bytes 417824 | tf_op jit(solution)/shard_map/ppermute | solution.py:1021
  43.7 0.1 shard_map.358
  43.8 1.1 %collective-permute-start.4 = (bf16[832,128]{1,0:T(8,128)(2,1)S(1)}, bf16[832,128]{1,0:T(8,128)(2,1)S(1)}, u32[]{:S(2)}, u32[]{:S(2)}) collective-permute-start(bf16[832,128]{1,0:T(8,128)(2,1)S(1)} %get-tuple-element.89.refs_4_), channel_id=1, source_target_pairs={{0,2},{1,3},{2,0},{3,1},{4,6},{5,7},{6,4},{7,5},{8,10},{9,11},{10,... | collective-permute-start | bytes 638984 | tf_op jit(solution)/shard_map/ppermute | solution.py:1021
  44.9 0.0 copy-start.7
  44.9 0.0 copy-start.8
  44.9 0.0 copy-start.9
  44.9 0.0 copy-start.10
  44.9 0.0 copy-start.11
  44.9 0.0 copy-start.12
  44.9 0.0 copy-start.13
  45.0 0.0 copy-start.14
  45.0 4.5 %shard_map.359 = (bf16[32,256,128]{2,1,0:T(8,128)(2,1)}, f32[8,128]{1,0:T(8,128)S(1)}) custom-call(s32[32]{0:T(128)S(1)} %xor_bitcast_fusion.rel_ref, bf16[32,256,384]{2,1,0:T(8,128)(2,1)S(1)} %get-tuple-element.85.late_ref, bf16[416,128]{1,0:T(8,128)(2,1)S(1)} %shard_map.354.own_ref.refs_0_, bf16[416,128]{1,0:T(8,128)(2,1)S(1)} %collective-permute-done.one_ref.refs_1_, ...), custom_call_target="tpu_custom_call" | custom-call | flops 805306368 | bytes 16777216 | tf_op jit(solution)/shard_map/pallas_call | solution.py:760
  49.5 0.0 copy-start.2
  49.5 0.0 copy-start
  49.5 0.0 copy-start.1
  49.5 0.0 copy-start.4
  49.5 0.0 copy-start.5
  49.5 0.0 copy-start.6
  49.5 1.8 %collective-permute-done.4.got_ref = bf16[832,128]{1,0:T(8,128)(2,1)S(1)} collective-permute-done((bf16[832,128]{1,0:T(8,128)(2,1)S(1)}, bf16[832,128]{1,0:T(8,128)(2,1)S(1)}, u32[]{:S(2)}, u32[]{:S(2)}) %collective-permute-start.4) | collective-permute-done | bytes 213024 | tf_op jit(solution)/shard_map/ppermute | solution.py:1021
  51.3 0.1 shard_map.360
  51.4 1.6 %collective-permute-start.5 = (bf16[448,128]{1,0:T(8,128)(2,1)S(1)}, bf16[448,128]{1,0:T(8,128)(2,1)S(1)}, u32[]{:S(2)}, u32[]{:S(2)}) collective-permute-start(bf16[448,128]{1,0:T(8,128)(2,1)S(1)} %get-tuple-element.95), channel_id=1, source_target_pairs={{0,4},{4,0},{8,12},{12,8},{16,20},{20,16},{24,28},{28,24},{1,5},{5... | collective-permute-start | bytes 344072 | tf_op jit(solution)/shard_map/ppermute | solution.py:1021
  53.0 3.3 %collective-permute-done.5.got_ref = bf16[448,128]{1,0:T(8,128)(2,1)S(1)} collective-permute-done((bf16[448,128]{1,0:T(8,128)(2,1)S(1)}, bf16[448,128]{1,0:T(8,128)(2,1)S(1)}, u32[]{:S(2)}, u32[]{:S(2)}) %collective-permute-start.5) | collective-permute-done | bytes 114720 | tf_op jit(solution)/shard_map/ppermute | solution.py:1021
  56.3 1.6 %collective-permute-start.6 = (bf16[448,128]{1,0:T(8,128)(2,1)S(1)}, bf16[448,128]{1,0:T(8,128)(2,1)S(1)}, u32[]{:S(2)}, u32[]{:S(2)}) collective-permute-start(bf16[448,128]{1,0:T(8,128)(2,1)S(1)} %get-tuple-element.98), channel_id=1, source_target_pairs={{0,8},{4,12},{8,0},{12,4},{16,24},{20,28},{24,16},{28,20},{1,9},{5... | collective-permute-start | bytes 344072 | tf_op jit(solution)/shard_map/ppermute | solution.py:1021
  57.9 3.2 %collective-permute-done.6.got_ref = bf16[448,128]{1,0:T(8,128)(2,1)S(1)} collective-permute-done((bf16[448,128]{1,0:T(8,128)(2,1)S(1)}, bf16[448,128]{1,0:T(8,128)(2,1)S(1)}, u32[]{:S(2)}, u32[]{:S(2)}) %collective-permute-start.6) | collective-permute-done | bytes 114720 | tf_op jit(solution)/shard_map/ppermute | solution.py:1021
  61.2 3.7 %collective-permute-start.7 = (bf16[448,128]{1,0:T(8,128)(2,1)S(1)}, bf16[448,128]{1,0:T(8,128)(2,1)S(1)}, u32[]{:S(2)}, u32[]{:S(2)}) collective-permute-start(bf16[448,128]{1,0:T(8,128)(2,1)S(1)} %get-tuple-element.101), channel_id=1, source_target_pairs={{0,24},{4,28},{8,16},{12,20},{16,8},{20,12},{24,0},{28,4},{1,25},{... | collective-permute-start | bytes 344072 | tf_op jit(solution)/shard_map/ppermute | solution.py:1021
  64.9 3.1 %collective-permute-done.7.got_ref = bf16[448,128]{1,0:T(8,128)(2,1)S(1)} collective-permute-done((bf16[448,128]{1,0:T(8,128)(2,1)S(1)}, bf16[448,128]{1,0:T(8,128)(2,1)S(1)}, u32[]{:S(2)}, u32[]{:S(2)}) %collective-permute-start.7) | collective-permute-done | bytes 114720 | tf_op jit(solution)/shard_map/ppermute | solution.py:1021
  68.0 1.6 %collective-permute-start.8 = (bf16[416,128]{1,0:T(8,128)(2,1)S(1)}, bf16[416,128]{1,0:T(8,128)(2,1)S(1)}, u32[]{:S(2)}, u32[]{:S(2)}) collective-permute-start(bf16[416,128]{1,0:T(8,128)(2,1)S(1)} %get-tuple-element.103.own_ref), channel_id=1, source_target_pairs={{0,4},{4,0},{8,12},{12,8},{16,20},{20,16},{24,28},{28,24},{1,5},{5... | collective-permute-start | bytes 319496 | tf_op jit(solution)/shard_map/ppermute | solution.py:1021
  69.6 3.2 %collective-permute-done.8.got_ref = bf16[416,128]{1,0:T(8,128)(2,1)S(1)} collective-permute-done((bf16[416,128]{1,0:T(8,128)(2,1)S(1)}, bf16[416,128]{1,0:T(8,128)(2,1)S(1)}, u32[]{:S(2)}, u32[]{:S(2)}) %collective-permute-start.8) | collective-permute-done | bytes 106528 | tf_op jit(solution)/shard_map/ppermute | solution.py:1021
  72.8 0.9 %collective-permute-start.10 = (bf16[384,128]{1,0:T(8,128)(2,1)S(1)}, bf16[384,128]{1,0:T(8,128)(2,1)S(1)}, u32[]{:S(2)}, u32[]{:S(2)}) collective-permute-start(bf16[384,128]{1,0:T(8,128)(2,1)S(1)} %slice_select_fusion.refs_0_), channel_id=1, source_target_pairs={{0,2},{1,3},{2,0},{3,1},{4,6},{5,7},{6,4},{7,5},{8,10},{9,11},{10,... | collective-permute-start | bytes 294920 | tf_op jit(solution)/shard_map/ppermute | solution.py:1021
  73.7 0.0 collective-permute-start.9
  73.7 0.0 copy-done.7
  73.7 0.0 copy-done.8
  73.7 0.0 copy-done.9
  73.7 0.0 copy-done.10
  73.8 0.0 copy-done.11
  73.8 0.0 copy-done.12
  73.8 0.0 copy-done.13
  73.8 0.0 copy-done.14
  73.8 0.0 copy-done.2
  73.8 1.0 %shard_map.364 = (f32[128,384]{1,0:T(8,128)}, f32[128,384]{1,0:T(8,128)}, f32[128,384]{1,0:T(8,128)}, bf16[128,384]{1,0:T(8,128)(2,1)}, f32[32,128]{1,0:T(8,128)...) custom-call(bf16[416,128]{1,0:T(8,128)(2,1)S(1)} %get-tuple-element., ...), custom_call_target="tpu_custom_call" | custom-call | bytes 6291456 | tf_op jit(solution)/shard_map/pallas_call | solution.py:893
  74.8 2.7 %collective-permute-done.10.in_ref = bf16[384,128]{1,0:T(8,128)(2,1)S(1)} collective-permute-done((bf16[384,128]{1,0:T(8,128)(2,1)S(1)}, bf16[384,128]{1,0:T(8,128)(2,1)S(1)}, u32[]{:S(2)}, u32[]{:S(2)}) %collective-permute-start.10) | collective-permute-done | bytes 98336 | tf_op jit(solution)/shard_map/ppermute | solution.py:1021
  77.5 0.1 collective-permute-start.11
  77.6 0.0 collective-permute-done.9.refs_1_
  77.6 1.3 %collective-permute-done.11.refs_3_ = bf16[384,128]{1,0:T(8,128)(2,1)S(1)} collective-permute-done((bf16[384,128]{1,0:T(8,128)(2,1)S(1)}, bf16[384,128]{1,0:T(8,128)(2,1)S(1)}, u32[]{:S(2)}, u32[]{:S(2)}) %collective-permute-start.11) | collective-permute-done | bytes 98336 | tf_op jit(solution)/shard_map/ppermute | solution.py:1021
  78.9 0.0 copy-done
  78.9 0.0 copy-done.1
  78.9 0.0 copy-done.3
  78.9 0.0 copy-done.4
  78.9 0.0 copy-done.5
  78.9 0.0 copy-done.6
  78.9 1.8 %shard_map.366 = (f32[128,1024]{1,0:T(8,128)}, f32[128,1024]{1,0:T(8,128)}, f32[128,1024]{1,0:T(8,128)}, bf16[128,1024]{1,0:T(8,128)(2,1)}, f32[512,128]{1,0:T(8...) custom-call(bf16[384,128]{1,0:T(8,128)(2,1)S(1)} %slice_select_fusion.refs_0_, ...), custom_call_target="tpu_custom_call" | custom-call | tf_op jit(solution)/shard_map/pallas_call | solution.py:893
  (7 shorter events, 0.1 us)
Async XLA Ops:
  1.6 6.5 %collective-permute-start.1 = (bf16[416,128]{1,0:T(8,128)(2,1)S(1)}, bf16[416,128]{1,0:T(8,128)(2,1)S(1)}, u32[]{:S(2)}, u32[]{:S(2)}) collective-permute-start(bf16[416,128]{1,0:T(8,128)(2,1)S(1)} %shard_map.354.own_ref.refs_0_), channel_id=1, source_target_pairs={{0,2},{1,3},{2,0},{3,1},{4,6},{5,7},{6,4},{7,5},{8,10},{9,11},{10,... | collective-permute-start | bytes 319496 | tf_op jit(solution)/shard_map/ppermute | solution.py:1021
  4.6 4.1 %collective-permute-start = (bf16[416,128]{1,0:T(8,128)(2,1)S(1)}, bf16[416,128]{1,0:T(8,128)(2,1)S(1)}, u32[]{:S(2)}, u32[]{:S(2)}) collective-permute-start(bf16[416,128]{1,0:T(8,128)(2,1)S(1)} %shard_map.354.own_ref.refs_0_), channel_id=1, source_target_pairs={{0,1},{1,0},{2,3},{3,2},{4,5},{5,4},{6,7},{7,6},{8,9},{9,8},{10,11... | collective-permute-start | bytes 319496 | tf_op jit(solution)/shard_map/ppermute | solution.py:1021
  8.1 1.5 %collective-permute-start.2 = (bf16[416,128]{1,0:T(8,128)(2,1)S(1)}, bf16[416,128]{1,0:T(8,128)(2,1)S(1)}, u32[]{:S(2)}, u32[]{:S(2)}) collective-permute-start(bf16[416,128]{1,0:T(8,128)(2,1)S(1)} %shard_map.356.two_ref.refs_2_), channel_id=1, source_target_pairs={{0,1},{1,0},{2,3},{3,2},{4,5},{5,4},{6,7},{7,6},{8,9},{9,8},{10,11... | collective-permute-start | bytes 319496 | tf_op jit(solution)/shard_map/ppermute | solution.py:1021
  41.8 1.8 %collective-permute-start.3 = (bf16[1632,128]{1,0:T(8,128)(2,1)S(1)}, bf16[1632,128]{1,0:T(8,128)(2,1)S(1)}, u32[]{:S(2)}, u32[]{:S(2)}) collective-permute-start(bf16[1632,128]{1,0:T(8,128)(2,1)S(1)} %get-tuple-element.87), channel_id=1, source_target_pairs={{0,1},{1,0},{2,3},{3,2},{4,5},{5,4},{6,7},{7,6},{8,9},{9,8},{10,11... | collective-permute-start | bytes 1253384 | tf_op jit(solution)/shard_map/ppermute | solution.py:1021
  43.8 7.6 %collective-permute-start.4 = (bf16[832,128]{1,0:T(8,128)(2,1)S(1)}, bf16[832,128]{1,0:T(8,128)(2,1)S(1)}, u32[]{:S(2)}, u32[]{:S(2)}) collective-permute-start(bf16[832,128]{1,0:T(8,128)(2,1)S(1)} %get-tuple-element.89.refs_4_), channel_id=1, source_target_pairs={{0,2},{1,3},{2,0},{3,1},{4,6},{5,7},{6,4},{7,5},{8,10},{9,11},{10,... | collective-permute-start | bytes 638984 | tf_op jit(solution)/shard_map/ppermute | solution.py:1021
  44.9 28.8 %copy-start.7 = (f32[1,128,384]{2,1,0:T(8,128)S(1)}, f32[1,128,384]{2,1,0:T(8,128)}, u32[]{:S(2)}) copy-start(f32[1,128,384]{2,1,0:T(8,128)} %param.33) | copy-start | bytes 589828
  44.9 28.8 %copy-start.8 = (f32[1,128,384]{2,1,0:T(8,128)S(1)}, f32[1,128,384]{2,1,0:T(8,128)}, u32[]{:S(2)}) copy-start(f32[1,128,384]{2,1,0:T(8,128)} %param.34) | copy-start | bytes 589828
  44.9 28.8 %copy-start.9 = (f32[1,32,128]{2,1,0:T(8,128)S(1)}, f32[1,32,128]{2,1,0:T(8,128)}, u32[]{:S(2)}) copy-start(f32[1,32,128]{2,1,0:T(8,128)} %param.35) | copy-start | bytes 49156
  44.9 28.8 %copy-start.10 = (f32[9,128]{1,0:T(8,128)S(1)}, f32[9,128]{1,0:T(8,128)}, u32[]{:S(2)}) copy-start(f32[9,128]{1,0:T(8,128)} %refs_6_.2) | copy-start | bytes 13828
  44.9 28.8 %copy-start.11 = (f32[1,32,128]{2,1,0:T(8,128)S(1)}, f32[1,32,128]{2,1,0:T(8,128)}, u32[]{:S(2)}) copy-start(f32[1,32,128]{2,1,0:T(8,128)} %param.36) | copy-start | bytes 49156
  44.9 28.8 %copy-start.12 = (f32[1,32,128]{2,1,0:T(8,128)S(1)}, f32[1,32,128]{2,1,0:T(8,128)}, u32[]{:S(2)}) copy-start(f32[1,32,128]{2,1,0:T(8,128)} %param.37) | copy-start | bytes 49156
  44.9 28.8 %copy-start.13 = (f32[9,128]{1,0:T(8,128)S(1)}, f32[9,128]{1,0:T(8,128)}, u32[]{:S(2)}) copy-start(f32[9,128]{1,0:T(8,128)} %refs_7_.2) | copy-start | bytes 13828
  45.0 28.8 %copy-start.14 = (f32[9,128]{1,0:T(8,128)S(1)}, f32[9,128]{1,0:T(8,128)}, u32[]{:S(2)}) copy-start(f32[9,128]{1,0:T(8,128)} %refs_8_.2) | copy-start | bytes 13828
  49.5 24.3 %copy-start.2 = (f32[1,128,384]{2,1,0:T(8,128)S(1)}, f32[1,128,384]{2,1,0:T(8,128)}, u32[]{:S(2)}) copy-start(f32[1,128,384]{2,1,0:T(8,128)} %param.32) | copy-start | bytes 589828
  49.5 29.4 %copy-start = (f32[128,1024]{1,0:T(8,128)S(1)}, f32[128,1024]{1,0:T(8,128)}, u32[]{:S(2)}) copy-start(f32[128,1024]{1,0:T(8,128)} %refs_4_.1) | copy-start | bytes 1572868
  49.5 29.4 %copy-start.1 = (f32[512,128]{1,0:T(8,128)S(1)}, f32[512,128]{1,0:T(8,128)}, u32[]{:S(2)}) copy-start(f32[512,128]{1,0:T(8,128)} %refs_7_.3) | copy-start | bytes 786436
  49.5 29.4 %copy-start.3 = (f32[128,1024]{1,0:T(8,128)S(1)}, f32[128,1024]{1,0:T(8,128)}, u32[]{:S(2)}) copy-start(f32[128,1024]{1,0:T(8,128)} %refs_5_.1) | copy-start | bytes 1572868
  49.5 29.4 %copy-start.4 = (f32[128,1024]{1,0:T(8,128)S(1)}, f32[128,1024]{1,0:T(8,128)}, u32[]{:S(2)}) copy-start(f32[128,1024]{1,0:T(8,128)} %refs_6_.3) | copy-start | bytes 1572868
  49.5 29.4 %copy-start.5 = (f32[512,128]{1,0:T(8,128)S(1)}, f32[512,128]{1,0:T(8,128)}, u32[]{:S(2)}) copy-start(f32[512,128]{1,0:T(8,128)} %refs_8_.3) | copy-start | bytes 786436
  49.5 29.4 %copy-start.6 = (f32[512,128]{1,0:T(8,128)S(1)}, f32[512,128]{1,0:T(8,128)}, u32[]{:S(2)}) copy-start(f32[512,128]{1,0:T(8,128)} %refs_9_.1) | copy-start | bytes 786436
  51.4 4.9 %collective-permute-start.5 = (bf16[448,128]{1,0:T(8,128)(2,1)S(1)}, bf16[448,128]{1,0:T(8,128)(2,1)S(1)}, u32[]{:S(2)}, u32[]{:S(2)}) collective-permute-start(bf16[448,128]{1,0:T(8,128)(2,1)S(1)} %get-tuple-element.95), channel_id=1, source_target_pairs={{0,4},{4,0},{8,12},{12,8},{16,20},{20,16},{24,28},{28,24},{1,5},{5... | collective-permute-start | bytes 344072 | tf_op jit(solution)/shard_map/ppermute | solution.py:1021
  56.3 4.9 %collective-permute-start.6 = (bf16[448,128]{1,0:T(8,128)(2,1)S(1)}, bf16[448,128]{1,0:T(8,128)(2,1)S(1)}, u32[]{:S(2)}, u32[]{:S(2)}) collective-permute-start(bf16[448,128]{1,0:T(8,128)(2,1)S(1)} %get-tuple-element.98), channel_id=1, source_target_pairs={{0,8},{4,12},{8,0},{12,4},{16,24},{20,28},{24,16},{28,20},{1,9},{5... | collective-permute-start | bytes 344072 | tf_op jit(solution)/shard_map/ppermute | solution.py:1021
  61.2 6.8 %collective-permute-start.7 = (bf16[448,128]{1,0:T(8,128)(2,1)S(1)}, bf16[448,128]{1,0:T(8,128)(2,1)S(1)}, u32[]{:S(2)}, u32[]{:S(2)}) collective-permute-start(bf16[448,128]{1,0:T(8,128)(2,1)S(1)} %get-tuple-element.101), channel_id=1, source_target_pairs={{0,24},{4,28},{8,16},{12,20},{16,8},{20,12},{24,0},{28,4},{1,25},{... | collective-permute-start | bytes 344072 | tf_op jit(solution)/shard_map/ppermute | solution.py:1021
  68.0 4.8 %collective-permute-start.8 = (bf16[416,128]{1,0:T(8,128)(2,1)S(1)}, bf16[416,128]{1,0:T(8,128)(2,1)S(1)}, u32[]{:S(2)}, u32[]{:S(2)}) collective-permute-start(bf16[416,128]{1,0:T(8,128)(2,1)S(1)} %get-tuple-element.103.own_ref), channel_id=1, source_target_pairs={{0,4},{4,0},{8,12},{12,8},{16,20},{20,16},{24,28},{28,24},{1,5},{5... | collective-permute-start | bytes 319496 | tf_op jit(solution)/shard_map/ppermute | solution.py:1021
  72.8 4.7 %collective-permute-start.10 = (bf16[384,128]{1,0:T(8,128)(2,1)S(1)}, bf16[384,128]{1,0:T(8,128)(2,1)S(1)}, u32[]{:S(2)}, u32[]{:S(2)}) collective-permute-start(bf16[384,128]{1,0:T(8,128)(2,1)S(1)} %slice_select_fusion.refs_0_), channel_id=1, source_target_pairs={{0,2},{1,3},{2,0},{3,1},{4,6},{5,7},{6,4},{7,5},{8,10},{9,11},{10,... | collective-permute-start | bytes 294920 | tf_op jit(solution)/shard_map/ppermute | solution.py:1021
  73.7 3.8 %collective-permute-start.9 = (bf16[384,128]{1,0:T(8,128)(2,1)S(1)}, bf16[384,128]{1,0:T(8,128)(2,1)S(1)}, u32[]{:S(2)}, u32[]{:S(2)}) collective-permute-start(bf16[384,128]{1,0:T(8,128)(2,1)S(1)} %slice_select_fusion.refs_0_), channel_id=1, source_target_pairs={{0,1},{1,0},{2,3},{3,2},{4,5},{5,4},{6,7},{7,6},{8,9},{9,8},{10,11... | collective-permute-start | bytes 294920 | tf_op jit(solution)/shard_map/ppermute | solution.py:1021
  77.5 1.4 %collective-permute-start.11 = (bf16[384,128]{1,0:T(8,128)(2,1)S(1)}, bf16[384,128]{1,0:T(8,128)(2,1)S(1)}, u32[]{:S(2)}, u32[]{:S(2)}) collective-permute-start(bf16[384,128]{1,0:T(8,128)(2,1)S(1)} %shard_map.365.refs_2_), channel_id=1, source_target_pairs={{0,1},{1,0},{2,3},{3,2},{4,5},{5,4},{6,7},{7,6},{8,9},{9,8},{10,11... | collective-permute-start | bytes 294920 | tf_op jit(solution)/shard_map/ppermute | solution.py:1021

commit v7 on v6

--- a/solution.py
+++ b/solution.py
@@ -24,6 +24,7 @@
 BASE_RATE = 0.1
 HIDDEN_SCORE = -1e30
 LAG = 1
+FLUSH = 4
 SCALE = 1.0 / math.sqrt(HEAD_DIM)
 LOG2E = math.log2(math.e)
 
@@ -45,9 +46,9 @@
     return lax.dot_general(a, b, (((1,), (1,)), ((), ())), preferred_element_type=F32)
 
 
-def scores_back(probs, grad, axis):
-    product = probs * grad
-    return (product - probs * jnp.sum(product, axis=axis, keepdims=True)).astype(BF)
+def scores_back(probs, low, grad, axis):
+    drop = jnp.sum(probs * grad, axis=axis, keepdims=True)
+    return (grad - drop).astype(BF) * low
 
 
 def head_pair(source, j):
@@ -465,7 +466,13 @@
         yield
         grad_all = mm(t_in[...], grad_inner)
         output_all = mm(t_dnT[...], active)
-        turn_inner, turn_active = turn_all(grad_inner), turn_all(active)
+        for name, value in (
+            ("normed2", normed_two),
+            ("inner", turn_all(grad_inner)),
+            ("cot", cot),
+            ("active", turn_all(active)),
+        ):
+            kept[name].append(value)
         yield
 
         grad_hidden = []
@@ -542,10 +549,6 @@
             ("gradp", turn_all(grad_projected)),
             ("mixed", mixed),
             ("branch", grad_branch),
-            ("normed2", normed_two),
-            ("inner", turn_inner),
-            ("cot", cot),
-            ("active", turn_active),
         ):
             kept[name].append(value)
         yield
@@ -611,7 +614,7 @@
                 steps.append(
                     jnp.concatenate(
                         [
-                            scores_back(probs[b][s][u], grad_probs[b][s][:, 128 * u : 128 * u + 128], 0)
+                            scores_back(probs[b][s][u], probs_low[b][s][u], grad_probs[b][s][:, 128 * u : 128 * u + 128], 0)
                             for u in range(2)
                         ],
                         axis=1,
@@ -626,6 +629,24 @@
             rows_T = rows_ref[first + b].T
             a_a[e] += mm(rows_T, grad_scores[i])
             a_v[e] += mm(rows_T, grad_values[i])
+
+    def side(name):
+        return jnp.concatenate(kept[name], axis=1)
+
+    def stack(name):
+        return jnp.concatenate(kept[name], axis=0)
+
+    def flush(least):
+        if len(kept["active"]) >= least:
+            a_dn[...] += mm(side("cot"), stack("active"))
+            a_in[...] += mm(side("normed2"), stack("inner"))
+            for name in ("cot", "active", "normed2", "inner"):
+                kept[name].clear()
+        if len(kept["gradp"]) >= least:
+            a_o[...] += mm_nt(side("mixed"), side("branch"))
+            a_qkv[...] += mm(side("normed"), stack("gradp"))
+            for name in ("mixed", "branch", "normed", "gradp"):
+                kept[name].clear()
 
     part = 2
     flows = [flow(range(part * g, part * g + part)) for g in range(group // part)]
@@ -642,20 +663,11 @@
             except StopIteration:
                 pass
         wave += 1
+        flush(FLUSH)
 
     for move in moves(step)[2:]:
         move.start()
 
-    def side(name):
-        return jnp.concatenate(kept[name], axis=1)
-
-    def stack(name):
-        return jnp.concatenate(kept[name], axis=0)
-
-    a_dn[...] += mm(side("cot"), stack("active"))
-    a_in[...] += mm(side("normed2"), stack("inner"))
-    a_o[...] += mm_nt(side("mixed"), side("branch"))
-    a_qkv[...] += mm(side("normed"), stack("gradp"))
     for c in range(3):
         total = kept["sums"][0][c]
         for sums in kept["sums"][1:]:

time: 80.9 us -> 80 us (0.989)
    pallas_call x1, Pallas kernels: 32.2 us -> 31.3 us  [run_main(): pl.pallas_call(functools.partial(main_kernel, group), out_shape=(jax.Shap...]
where the time goes in v7:
time: 80 us; the launch traced here: 79.8 us
  Pallas kernels  41.8 us (52%)
  waiting for transfers between devices  21 us (26%)
  starting transfers between devices  14.6 us (18%)
  local copies, waits for them, and re-layouts  0.94 us (1%)
  between operations  0.89 us (1%)
    pallas_call x1, Pallas kernels, run_main(): pl.pallas_call(functools.partial(main_kernel, group), out_shape=(jax.Shap...  31.3 us
    ppermute x12, waiting for transfers between devices, swap(): return lax.ppermute(value, axis, [(i, i ^ mask) for i in range(count)])  21 us
    ppermute x12, starting transfers between devices, swap(): return lax.ppermute(value, axis, [(i, i ^ mask) for i in range(count)])  14.6 us
    pallas_call x11, Pallas kernels, call(): pl.pallas_call(kernel, out_shape=outs, in_specs=[pl.BlockSpec(memory_spac...  5.98 us
    pallas_call x1, Pallas kernels, run_rows(): pl.pallas_call(functools.partial(rows_kernel, group, len(stems)), out_sha...  4.5 us
  transfers between devices with their start and end apart: 12, of which 9 were waited for; matrix products, arithmetic and copies ran while one was open for 2% of the time, Pallas kernels for 9%

profile of v7, /device:TPU:0, one launch (start us, length us, event | category | flops | bytes accessed | tf_op | source)
XLA Modules:
  0.0 79.8 jit_solution(17655940638910699451)
XLA Ops:
  0.7 0.9 %shard_map.354.own_ref.refs_0_ = bf16[416,128]{1,0:T(8,128)(2,1)S(1)} custom-call(f32[128,384]{1,0:T(8,128)} %bitcast.18, f32[32,128]{1,0:T(8,128)} %bitcast.22), custom_call_target="tpu_custom_call" | custom-call | tf_op jit(solution)/shard_map/pallas_call | solution.py:905
  1.6 3.0 %collective-permute-start.1 = (bf16[416,128]{1,0:T(8,128)(2,1)S(1)}, bf16[416,128]{1,0:T(8,128)(2,1)S(1)}, u32[]{:S(2)}, u32[]{:S(2)}) collective-permute-start(bf16[416,128]{1,0:T(8,128)(2,1)S(1)} %shard_map.354.own_ref.refs_0_), channel_id=1, source_target_pairs={{0,2},{1,3},{2,0},{3,1},{4,6},{5,7},{6,4},{7,5},{8,10},{9,11},{10,... | collective-permute-start | bytes 319496 | tf_op jit(solution)/shard_map/ppermute | solution.py:1033
  4.6 0.0 collective-permute-start
  4.6 0.7 xor_bitcast_fusion.rel_ref
  5.3 0.8 copy.42
  6.1 0.1 reshape.55.seg_ref
  6.2 1.9 %shard_map.355 = (bf16[384,144]{1,0:T(8,128)(2,1)S(1)}, bf16[128,384]{1,0:T(8,128)(2,1)S(1)}, bf16[128,128]{1,0:T(8,128)(2,1)S(1)}, bf16[128,128]{1,0:T(8,128)(2...) custom-call(f32[128,1024]{1,0:T(8,128)} %refs_4_.1, ...), custom_call_target="tpu_custom_call" | custom-call | bytes 8388608 | tf_op jit(solution)/shard_map/pallas_call | solution.py:905
  8.1 0.0 collective-permute-done.1.in_ref
  8.1 0.6 collective-permute-start.2
  8.7 0.0 collective-permute-done.one_ref.refs_1_
  8.7 1.0 %collective-permute-done.2.three_ref.refs_3_ = bf16[416,128]{1,0:T(8,128)(2,1)S(1)} collective-permute-done((bf16[416,128]{1,0:T(8,128)(2,1)S(1)}, bf16[416,128]{1,0:T(8,128)(2,1)S(1)}, u32[]{:S(2)}, u32[]{:S(2)}) %collective-permute-start.2) | collective-permute-done | bytes 106528 | tf_op jit(solution)/shard_map/ppermute | solution.py:1033
  9.7 31.3 %shard_map.357 = (bf16[32,128,128]{2,1,0:T(8,128)(2,1)}, bf16[32,256,384]{2,1,0:T(8,128)(2,1)S(1)}, f32[1600,128]{1,0:T(8,128)S(1)}, bf16[1632,128]{1,0:T(8,128)(2,1)S(1)}, f32[16,128]{1,0:T(8,128)S(1)}) custom-call(s32[32]{0:T(128)S(1)} %xor_bitcast_fusion.rel_ref, s32[128]{0:T(128)S(1)} %reshape.55.seg_ref, bf16[32,256,128]{2,1,0:T(8,128)(2,1)} %bitcast.26, ...), custom_call_target="tpu_custom_call" | custom-call | tf_op jit(solution)/shard_map/pallas_call | solution.py:973
  40.9 0.4 collective-permute-start.3
  41.4 1.4 %collective-permute-done.3.got_ref = bf16[1632,128]{1,0:T(8,128)(2,1)S(1)} collective-permute-done((bf16[1632,128]{1,0:T(8,128)(2,1)S(1)}, bf16[1632,128]{1,0:T(8,128)(2,1)S(1)}, u32[]{:S(2)}, u32[]{:S(2)}) %collective-permute-start.3) | collective-permute-done | bytes 417824 | tf_op jit(solution)/shard_map/ppermute | solution.py:1033
  42.8 0.1 shard_map.358
  42.9 1.1 %collective-permute-start.4 = (bf16[832,128]{1,0:T(8,128)(2,1)S(1)}, bf16[832,128]{1,0:T(8,128)(2,1)S(1)}, u32[]{:S(2)}, u32[]{:S(2)}) collective-permute-start(bf16[832,128]{1,0:T(8,128)(2,1)S(1)} %get-tuple-element.89.refs_4_), channel_id=1, source_target_pairs={{0,2},{1,3},{2,0},{3,1},{4,6},{5,7},{6,4},{7,5},{8,10},{9,11},{10,... | collective-permute-start | bytes 638984 | tf_op jit(solution)/shard_map/ppermute | solution.py:1033
  44.0 0.0 copy-start.7
  44.0 0.0 copy-start.8
  44.0 0.0 copy-start.9
  44.0 0.0 copy-start.10
  44.0 0.0 copy-start.11
  44.0 0.0 copy-start.12
  44.0 0.0 copy-start.13
  44.1 0.0 copy-start.14
  44.1 4.5 %shard_map.359 = (bf16[32,256,128]{2,1,0:T(8,128)(2,1)}, f32[8,128]{1,0:T(8,128)S(1)}) custom-call(s32[32]{0:T(128)S(1)} %xor_bitcast_fusion.rel_ref, bf16[32,256,384]{2,1,0:T(8,128)(2,1)S(1)} %get-tuple-element.85.late_ref, bf16[416,128]{1,0:T(8,128)(2,1)S(1)} %shard_map.354.own_ref.refs_0_, bf16[416,128]{1,0:T(8,128)(2,1)S(1)} %collective-permute-done.one_ref.refs_1_, ...), custom_call_target="tpu_custom_call" | custom-call | flops 805306368 | bytes 16777216 | tf_op jit(solution)/shard_map/pallas_call | solution.py:772
  48.6 0.0 copy-start.2
  48.6 0.0 copy-start
  48.6 0.0 copy-start.1
  48.6 0.0 copy-start.4
  48.6 0.0 copy-start.5
  48.6 0.0 copy-start.6
  48.6 1.8 %collective-permute-done.4.got_ref = bf16[832,128]{1,0:T(8,128)(2,1)S(1)} collective-permute-done((bf16[832,128]{1,0:T(8,128)(2,1)S(1)}, bf16[832,128]{1,0:T(8,128)(2,1)S(1)}, u32[]{:S(2)}, u32[]{:S(2)}) %collective-permute-start.4) | collective-permute-done | bytes 213024 | tf_op jit(solution)/shard_map/ppermute | solution.py:1033
  50.5 0.1 shard_map.360
  50.5 1.6 %collective-permute-start.5 = (bf16[448,128]{1,0:T(8,128)(2,1)S(1)}, bf16[448,128]{1,0:T(8,128)(2,1)S(1)}, u32[]{:S(2)}, u32[]{:S(2)}) collective-permute-start(bf16[448,128]{1,0:T(8,128)(2,1)S(1)} %get-tuple-element.95), channel_id=1, source_target_pairs={{0,4},{4,0},{8,12},{12,8},{16,20},{20,16},{24,28},{28,24},{1,5},{5... | collective-permute-start | bytes 344072 | tf_op jit(solution)/shard_map/ppermute | solution.py:1033
  52.1 3.3 %collective-permute-done.5.got_ref = bf16[448,128]{1,0:T(8,128)(2,1)S(1)} collective-permute-done((bf16[448,128]{1,0:T(8,128)(2,1)S(1)}, bf16[448,128]{1,0:T(8,128)(2,1)S(1)}, u32[]{:S(2)}, u32[]{:S(2)}) %collective-permute-start.5) | collective-permute-done | bytes 114720 | tf_op jit(solution)/shard_map/ppermute | solution.py:1033
  55.4 1.6 %collective-permute-start.6 = (bf16[448,128]{1,0:T(8,128)(2,1)S(1)}, bf16[448,128]{1,0:T(8,128)(2,1)S(1)}, u32[]{:S(2)}, u32[]{:S(2)}) collective-permute-start(bf16[448,128]{1,0:T(8,128)(2,1)S(1)} %get-tuple-element.98), channel_id=1, source_target_pairs={{0,8},{4,12},{8,0},{12,4},{16,24},{20,28},{24,16},{28,20},{1,9},{5... | collective-permute-start | bytes 344072 | tf_op jit(solution)/shard_map/ppermute | solution.py:1033
  57.1 3.2 %collective-permute-done.6.got_ref = bf16[448,128]{1,0:T(8,128)(2,1)S(1)} collective-permute-done((bf16[448,128]{1,0:T(8,128)(2,1)S(1)}, bf16[448,128]{1,0:T(8,128)(2,1)S(1)}, u32[]{:S(2)}, u32[]{:S(2)}) %collective-permute-start.6) | collective-permute-done | bytes 114720 | tf_op jit(solution)/shard_map/ppermute | solution.py:1033
  60.3 3.7 %collective-permute-start.7 = (bf16[448,128]{1,0:T(8,128)(2,1)S(1)}, bf16[448,128]{1,0:T(8,128)(2,1)S(1)}, u32[]{:S(2)}, u32[]{:S(2)}) collective-permute-start(bf16[448,128]{1,0:T(8,128)(2,1)S(1)} %get-tuple-element.101), channel_id=1, source_target_pairs={{0,24},{4,28},{8,16},{12,20},{16,8},{20,12},{24,0},{28,4},{1,25},{... | collective-permute-start | bytes 344072 | tf_op jit(solution)/shard_map/ppermute | solution.py:1033
  64.0 3.1 %collective-permute-done.7.got_ref = bf16[448,128]{1,0:T(8,128)(2,1)S(1)} collective-permute-done((bf16[448,128]{1,0:T(8,128)(2,1)S(1)}, bf16[448,128]{1,0:T(8,128)(2,1)S(1)}, u32[]{:S(2)}, u32[]{:S(2)}) %collective-permute-start.7) | collective-permute-done | bytes 114720 | tf_op jit(solution)/shard_map/ppermute | solution.py:1033
  67.1 1.6 %collective-permute-start.8 = (bf16[416,128]{1,0:T(8,128)(2,1)S(1)}, bf16[416,128]{1,0:T(8,128)(2,1)S(1)}, u32[]{:S(2)}, u32[]{:S(2)}) collective-permute-start(bf16[416,128]{1,0:T(8,128)(2,1)S(1)} %get-tuple-element.103.own_ref), channel_id=1, source_target_pairs={{0,4},{4,0},{8,12},{12,8},{16,20},{20,16},{24,28},{28,24},{1,5},{5... | collective-permute-start | bytes 319496 | tf_op jit(solution)/shard_map/ppermute | solution.py:1033
  68.7 3.2 %collective-permute-done.8.got_ref = bf16[416,128]{1,0:T(8,128)(2,1)S(1)} collective-permute-done((bf16[416,128]{1,0:T(8,128)(2,1)S(1)}, bf16[416,128]{1,0:T(8,128)(2,1)S(1)}, u32[]{:S(2)}, u32[]{:S(2)}) %collective-permute-start.8) | collective-permute-done | bytes 106528 | tf_op jit(solution)/shard_map/ppermute | solution.py:1033
  71.9 0.9 %collective-permute-start.10 = (bf16[384,128]{1,0:T(8,128)(2,1)S(1)}, bf16[384,128]{1,0:T(8,128)(2,1)S(1)}, u32[]{:S(2)}, u32[]{:S(2)}) collective-permute-start(bf16[384,128]{1,0:T(8,128)(2,1)S(1)} %slice_select_fusion.refs_0_), channel_id=1, source_target_pairs={{0,2},{1,3},{2,0},{3,1},{4,6},{5,7},{6,4},{7,5},{8,10},{9,11},{10,... | collective-permute-start | bytes 294920 | tf_op jit(solution)/shard_map/ppermute | solution.py:1033
  72.8 0.0 collective-permute-start.9
  72.8 0.0 copy-done.7
  72.8 0.0 copy-done.8
  72.8 0.0 copy-done.9
  72.9 0.0 copy-done.10
  72.9 0.0 copy-done.11
  72.9 0.0 copy-done.12
  72.9 0.0 copy-done.13
  72.9 0.0 copy-done.14
  72.9 0.0 copy-done.2
  72.9 1.0 %shard_map.364 = (f32[128,384]{1,0:T(8,128)}, f32[128,384]{1,0:T(8,128)}, f32[128,384]{1,0:T(8,128)}, bf16[128,384]{1,0:T(8,128)(2,1)}, f32[32,128]{1,0:T(8,128)...) custom-call(bf16[416,128]{1,0:T(8,128)(2,1)S(1)} %get-tuple-element., ...), custom_call_target="tpu_custom_call" | custom-call | bytes 6291456 | tf_op jit(solution)/shard_map/pallas_call | solution.py:905
  73.9 2.7 %collective-permute-done.10.in_ref = bf16[384,128]{1,0:T(8,128)(2,1)S(1)} collective-permute-done((bf16[384,128]{1,0:T(8,128)(2,1)S(1)}, bf16[384,128]{1,0:T(8,128)(2,1)S(1)}, u32[]{:S(2)}, u32[]{:S(2)}) %collective-permute-start.10) | collective-permute-done | bytes 98336 | tf_op jit(solution)/shard_map/ppermute | solution.py:1033
  76.6 0.1 collective-permute-start.11
  76.7 0.0 collective-permute-done.9.refs_1_
  76.7 1.3 %collective-permute-done.11.refs_3_ = bf16[384,128]{1,0:T(8,128)(2,1)S(1)} collective-permute-done((bf16[384,128]{1,0:T(8,128)(2,1)S(1)}, bf16[384,128]{1,0:T(8,128)(2,1)S(1)}, u32[]{:S(2)}, u32[]{:S(2)}) %collective-permute-start.11) | collective-permute-done | bytes 98336 | tf_op jit(solution)/shard_map/ppermute | solution.py:1033
  78.0 0.0 copy-done
  78.0 0.0 copy-done.1
  78.0 0.0 copy-done.3
  78.0 0.0 copy-done.4
  78.0 0.0 copy-done.5
  78.0 0.0 copy-done.6
  78.0 1.8 %shard_map.366 = (f32[128,1024]{1,0:T(8,128)}, f32[128,1024]{1,0:T(8,128)}, f32[128,1024]{1,0:T(8,128)}, bf16[128,1024]{1,0:T(8,128)(2,1)}, f32[512,128]{1,0:T(8...) custom-call(bf16[384,128]{1,0:T(8,128)(2,1)S(1)} %slice_select_fusion.refs_0_, ...), custom_call_target="tpu_custom_call" | custom-call | tf_op jit(solution)/shard_map/pallas_call | solution.py:905
  (7 shorter events, 0.1 us)
Async XLA Ops:
  1.6 6.5 %collective-permute-start.1 = (bf16[416,128]{1,0:T(8,128)(2,1)S(1)}, bf16[416,128]{1,0:T(8,128)(2,1)S(1)}, u32[]{:S(2)}, u32[]{:S(2)}) collective-permute-start(bf16[416,128]{1,0:T(8,128)(2,1)S(1)} %shard_map.354.own_ref.refs_0_), channel_id=1, source_target_pairs={{0,2},{1,3},{2,0},{3,1},{4,6},{5,7},{6,4},{7,5},{8,10},{9,11},{10,... | collective-permute-start | bytes 319496 | tf_op jit(solution)/shard_map/ppermute | solution.py:1033
  4.6 4.1 %collective-permute-start = (bf16[416,128]{1,0:T(8,128)(2,1)S(1)}, bf16[416,128]{1,0:T(8,128)(2,1)S(1)}, u32[]{:S(2)}, u32[]{:S(2)}) collective-permute-start(bf16[416,128]{1,0:T(8,128)(2,1)S(1)} %shard_map.354.own_ref.refs_0_), channel_id=1, source_target_pairs={{0,1},{1,0},{2,3},{3,2},{4,5},{5,4},{6,7},{7,6},{8,9},{9,8},{10,11... | collective-permute-start | bytes 319496 | tf_op jit(solution)/shard_map/ppermute | solution.py:1033
  8.1 1.5 %collective-permute-start.2 = (bf16[416,128]{1,0:T(8,128)(2,1)S(1)}, bf16[416,128]{1,0:T(8,128)(2,1)S(1)}, u32[]{:S(2)}, u32[]{:S(2)}) collective-permute-start(bf16[416,128]{1,0:T(8,128)(2,1)S(1)} %shard_map.356.two_ref.refs_2_), channel_id=1, source_target_pairs={{0,1},{1,0},{2,3},{3,2},{4,5},{5,4},{6,7},{7,6},{8,9},{9,8},{10,11... | collective-permute-start | bytes 319496 | tf_op jit(solution)/shard_map/ppermute | solution.py:1033
  40.9 1.8 %collective-permute-start.3 = (bf16[1632,128]{1,0:T(8,128)(2,1)S(1)}, bf16[1632,128]{1,0:T(8,128)(2,1)S(1)}, u32[]{:S(2)}, u32[]{:S(2)}) collective-permute-start(bf16[1632,128]{1,0:T(8,128)(2,1)S(1)} %get-tuple-element.87), channel_id=1, source_target_pairs={{0,1},{1,0},{2,3},{3,2},{4,5},{5,4},{6,7},{7,6},{8,9},{9,8},{10,11... | collective-permute-start | bytes 1253384 | tf_op jit(solution)/shard_map/ppermute | solution.py:1033
  42.9 7.6 %collective-permute-start.4 = (bf16[832,128]{1,0:T(8,128)(2,1)S(1)}, bf16[832,128]{1,0:T(8,128)(2,1)S(1)}, u32[]{:S(2)}, u32[]{:S(2)}) collective-permute-start(bf16[832,128]{1,0:T(8,128)(2,1)S(1)} %get-tuple-element.89.refs_4_), channel_id=1, source_target_pairs={{0,2},{1,3},{2,0},{3,1},{4,6},{5,7},{6,4},{7,5},{8,10},{9,11},{10,... | collective-permute-start | bytes 638984 | tf_op jit(solution)/shard_map/ppermute | solution.py:1033
  44.0 28.8 %copy-start.7 = (f32[1,128,384]{2,1,0:T(8,128)S(1)}, f32[1,128,384]{2,1,0:T(8,128)}, u32[]{:S(2)}) copy-start(f32[1,128,384]{2,1,0:T(8,128)} %param.33) | copy-start | bytes 589828
  44.0 28.8 %copy-start.8 = (f32[1,128,384]{2,1,0:T(8,128)S(1)}, f32[1,128,384]{2,1,0:T(8,128)}, u32[]{:S(2)}) copy-start(f32[1,128,384]{2,1,0:T(8,128)} %param.34) | copy-start | bytes 589828
  44.0 28.8 %copy-start.9 = (f32[1,32,128]{2,1,0:T(8,128)S(1)}, f32[1,32,128]{2,1,0:T(8,128)}, u32[]{:S(2)}) copy-start(f32[1,32,128]{2,1,0:T(8,128)} %param.35) | copy-start | bytes 49156
  44.0 28.8 %copy-start.10 = (f32[9,128]{1,0:T(8,128)S(1)}, f32[9,128]{1,0:T(8,128)}, u32[]{:S(2)}) copy-start(f32[9,128]{1,0:T(8,128)} %refs_6_.2) | copy-start | bytes 13828
  44.0 28.8 %copy-start.11 = (f32[1,32,128]{2,1,0:T(8,128)S(1)}, f32[1,32,128]{2,1,0:T(8,128)}, u32[]{:S(2)}) copy-start(f32[1,32,128]{2,1,0:T(8,128)} %param.36) | copy-start | bytes 49156
  44.0 28.8 %copy-start.12 = (f32[1,32,128]{2,1,0:T(8,128)S(1)}, f32[1,32,128]{2,1,0:T(8,128)}, u32[]{:S(2)}) copy-start(f32[1,32,128]{2,1,0:T(8,128)} %param.37) | copy-start | bytes 49156
  44.0 28.8 %copy-start.13 = (f32[9,128]{1,0:T(8,128)S(1)}, f32[9,128]{1,0:T(8,128)}, u32[]{:S(2)}) copy-start(f32[9,128]{1,0:T(8,128)} %refs_7_.2) | copy-start | bytes 13828
  44.1 28.8 %copy-start.14 = (f32[9,128]{1,0:T(8,128)S(1)}, f32[9,128]{1,0:T(8,128)}, u32[]{:S(2)}) copy-start(f32[9,128]{1,0:T(8,128)} %refs_8_.2) | copy-start | bytes 13828
  48.6 24.3 %copy-start.2 = (f32[1,128,384]{2,1,0:T(8,128)S(1)}, f32[1,128,384]{2,1,0:T(8,128)}, u32[]{:S(2)}) copy-start(f32[1,128,384]{2,1,0:T(8,128)} %param.32) | copy-start | bytes 589828
  48.6 29.4 %copy-start = (f32[128,1024]{1,0:T(8,128)S(1)}, f32[128,1024]{1,0:T(8,128)}, u32[]{:S(2)}) copy-start(f32[128,1024]{1,0:T(8,128)} %refs_4_.1) | copy-start | bytes 1572868
  48.6 29.4 %copy-start.1 = (f32[512,128]{1,0:T(8,128)S(1)}, f32[512,128]{1,0:T(8,128)}, u32[]{:S(2)}) copy-start(f32[512,128]{1,0:T(8,128)} %refs_7_.3) | copy-start | bytes 786436
  48.6 29.4 %copy-start.3 = (f32[128,1024]{1,0:T(8,128)S(1)}, f32[128,1024]{1,0:T(8,128)}, u32[]{:S(2)}) copy-start(f32[128,1024]{1,0:T(8,128)} %refs_5_.1) | copy-start | bytes 1572868
  48.6 29.4 %copy-start.4 = (f32[128,1024]{1,0:T(8,128)S(1)}, f32[128,1024]{1,0:T(8,128)}, u32[]{:S(2)}) copy-start(f32[128,1024]{1,0:T(8,128)} %refs_6_.3) | copy-start | bytes 1572868
  48.6 29.4 %copy-start.5 = (f32[512,128]{1,0:T(8,128)S(1)}, f32[512,128]{1,0:T(8,128)}, u32[]{:S(2)}) copy-start(f32[512,128]{1,0:T(8,128)} %refs_8_.3) | copy-start | bytes 786436
  48.6 29.4 %copy-start.6 = (f32[512,128]{1,0:T(8,128)S(1)}, f32[512,128]{1,0:T(8,128)}, u32[]{:S(2)}) copy-start(f32[512,128]{1,0:T(8,128)} %refs_9_.1) | copy-start | bytes 786436
  50.5 4.9 %collective-permute-start.5 = (bf16[448,128]{1,0:T(8,128)(2,1)S(1)}, bf16[448,128]{1,0:T(8,128)(2,1)S(1)}, u32[]{:S(2)}, u32[]{:S(2)}) collective-permute-start(bf16[448,128]{1,0:T(8,128)(2,1)S(1)} %get-tuple-element.95), channel_id=1, source_target_pairs={{0,4},{4,0},{8,12},{12,8},{16,20},{20,16},{24,28},{28,24},{1,5},{5... | collective-permute-start | bytes 344072 | tf_op jit(solution)/shard_map/ppermute | solution.py:1033
  55.4 4.9 %collective-permute-start.6 = (bf16[448,128]{1,0:T(8,128)(2,1)S(1)}, bf16[448,128]{1,0:T(8,128)(2,1)S(1)}, u32[]{:S(2)}, u32[]{:S(2)}) collective-permute-start(bf16[448,128]{1,0:T(8,128)(2,1)S(1)} %get-tuple-element.98), channel_id=1, source_target_pairs={{0,8},{4,12},{8,0},{12,4},{16,24},{20,28},{24,16},{28,20},{1,9},{5... | collective-permute-start | bytes 344072 | tf_op jit(solution)/shard_map/ppermute | solution.py:1033
  60.3 6.8 %collective-permute-start.7 = (bf16[448,128]{1,0:T(8,128)(2,1)S(1)}, bf16[448,128]{1,0:T(8,128)(2,1)S(1)}, u32[]{:S(2)}, u32[]{:S(2)}) collective-permute-start(bf16[448,128]{1,0:T(8,128)(2,1)S(1)} %get-tuple-element.101), channel_id=1, source_target_pairs={{0,24},{4,28},{8,16},{12,20},{16,8},{20,12},{24,0},{28,4},{1,25},{... | collective-permute-start | bytes 344072 | tf_op jit(solution)/shard_map/ppermute | solution.py:1033
  67.1 4.8 %collective-permute-start.8 = (bf16[416,128]{1,0:T(8,128)(2,1)S(1)}, bf16[416,128]{1,0:T(8,128)(2,1)S(1)}, u32[]{:S(2)}, u32[]{:S(2)}) collective-permute-start(bf16[416,128]{1,0:T(8,128)(2,1)S(1)} %get-tuple-element.103.own_ref), channel_id=1, source_target_pairs={{0,4},{4,0},{8,12},{12,8},{16,20},{20,16},{24,28},{28,24},{1,5},{5... | collective-permute-start | bytes 319496 | tf_op jit(solution)/shard_map/ppermute | solution.py:1033
  71.9 4.7 %collective-permute-start.10 = (bf16[384,128]{1,0:T(8,128)(2,1)S(1)}, bf16[384,128]{1,0:T(8,128)(2,1)S(1)}, u32[]{:S(2)}, u32[]{:S(2)}) collective-permute-start(bf16[384,128]{1,0:T(8,128)(2,1)S(1)} %slice_select_fusion.refs_0_), channel_id=1, source_target_pairs={{0,2},{1,3},{2,0},{3,1},{4,6},{5,7},{6,4},{7,5},{8,10},{9,11},{10,... | collective-permute-start | bytes 294920 | tf_op jit(solution)/shard_map/ppermute | solution.py:1033
  72.8 3.8 %collective-permute-start.9 = (bf16[384,128]{1,0:T(8,128)(2,1)S(1)}, bf16[384,128]{1,0:T(8,128)(2,1)S(1)}, u32[]{:S(2)}, u32[]{:S(2)}) collective-permute-start(bf16[384,128]{1,0:T(8,128)(2,1)S(1)} %slice_select_fusion.refs_0_), channel_id=1, source_target_pairs={{0,1},{1,0},{2,3},{3,2},{4,5},{5,4},{6,7},{7,6},{8,9},{9,8},{10,11... | collective-permute-start | bytes 294920 | tf_op jit(solution)/shard_map/ppermute | solution.py:1033
  76.6 1.4 %collective-permute-start.11 = (bf16[384,128]{1,0:T(8,128)(2,1)S(1)}, bf16[384,128]{1,0:T(8,128)(2,1)S(1)}, u32[]{:S(2)}, u32[]{:S(2)}) collective-permute-start(bf16[384,128]{1,0:T(8,128)(2,1)S(1)} %shard_map.365.refs_2_), channel_id=1, source_target_pairs={{0,1},{1,0},{2,3},{3,2},{4,5},{5,4},{6,7},{7,6},{8,9},{9,8},{10,11... | collective-permute-start | bytes 294920 | tf_op jit(solution)/shard_map/ppermute | solution.py:1033
